TPU v7x, 32 devices: a whole 2x2x4 slice. The times are simulated.
32 devices in a mesh: wide: 8 (over z, x), narrow: 4 (over y, core).
Axes of the slice: x: 2, y: 2, z: 4, core: 2. Of those that a mesh axis runs over, the one named last changes fastest.
Arguments:
- particles_first: bfloat16 [32, 384, 1536], P(('wide', 'narrow')), may hold values from -24 to 24
- particles_second: bfloat16 [32, 1536, 384], P(('wide', 'narrow')), may hold values from -24 to 24
- pool_images: bfloat16 [8, 197, 384], replicated, may hold values from -6 to 6
- pool_targets: bfloat16 [8, 197, 384], replicated, may hold values from -6 to 6
- batch_index: int32 [32, 8], P(('wide', 'narrow')), may hold values from 0 to 7
- kernel_scale: float32 [1], replicated, may hold values from 589824 to 1179648
Outputs:
- attract_first: bfloat16 [32, 384, 1536], P(('wide', 'narrow'))
- attract_second: bfloat16 [32, 1536, 384], P(('wide', 'narrow'))
- spread_first: bfloat16 [32, 384, 1536], P(('wide', 'narrow'))
- spread_second: bfloat16 [32, 1536, 384], P(('wide', 'narrow'))
All inputs are finite; a program needn't handle non-finite values.
Results may differ from a plain program's by a relative error of at most 0.005.
Values may be sent and summed in bfloat16 or wider, within the bound.
No kernel may reach another device: no remote copies, remote signals or barrier semaphores. Data moves between devices by JAX's collectives and lax.ppermute only.
A program may use at most 128 MiB of HBM per device.

v0:
```python
import functools
import math

import jax
import jax.numpy as jnp
from jax import lax
from jax.experimental import pallas as pl
from jax.experimental.pallas import tpu as pltpu
from jax.sharding import PartitionSpec as P

D = 384
FF = 1536
S = 197
DATA = 10000
AXES = ("wide", "narrow")
PAD = 208
EDGE = 48
BLOCKS = D * FF // (EDGE * D)
COLS = FF // D
TILE = 16

gelu_c = math.sqrt(2.0 / math.pi)
isd = 1.0 / math.sqrt(D)
isf = 1.0 / math.sqrt(FF)


def dot(a, b, dims):
    return lax.dot_general(a, b, (dims, ((), ())), preferred_element_type=jnp.float32)


def score_kernel(
    factor, picks, image, target, first, second, out, xs, ts, normed, hidden, deriv, delta, back
):
    step = pl.program_id(0)
    images = pl.num_programs(0)
    rows = pl.ds(pl.multiple_of(step * PAD, PAD), PAD)

    @pl.when(step == 0)
    def _():
        xs[...] = jnp.zeros_like(xs)
        ts[...] = jnp.zeros_like(ts)

    xs[0:S, :] = image[0].astype(jnp.float32)
    ts[0:S, :] = target[0].astype(jnp.float32)
    xf = xs[...]
    mean = jnp.mean(xf, axis=1, keepdims=True)
    centered = xf - mean
    var = jnp.mean(centered * centered, axis=1, keepdims=True)
    nrm = (centered * lax.rsqrt(var + 1e-06)).astype(jnp.bfloat16)
    normed[rows, :] = nrm
    for c in range(COLS):
        cols = pl.ds(c * D, D)
        pre = dot(nrm, first[:, cols], ((1,), (0,))) * isd
        sq = pre * pre
        tval = jnp.tanh(pre * (gelu_c + (gelu_c * 0.044715) * sq))
        gate = 0.5 + 0.5 * tval
        hid = pre * gate
        hidden[rows, cols] = hid.astype(jnp.bfloat16)
        deriv[:, cols] = gate + hid * (1.0 - gate) * (
            2.0 * gelu_c + (6.0 * gelu_c * 0.044715) * sq
        )
    prod = dot(hidden[rows, :], second[...], ((1,), (0,))) * isf
    dlt = ((xs[...] + prod - ts[...]) * (1.0 / S)).astype(jnp.bfloat16)
    delta[rows, :] = dlt
    for c in range(COLS):
        cols = pl.ds(c * D, D)
        dhid = dot(dlt, second[cols, :], ((1,), (1,))) * isf
        back[rows, cols] = (dhid * deriv[:, cols]).astype(jnp.bfloat16)

    @pl.when(step == images - 1)
    def _():
        for c in range(COLS):
            cols = pl.ds(c * D, D)
            grad = dot(normed[...], back[:, cols], ((0,), (0,))) * (-factor * isd)
            score = (grad - first[:, cols].astype(jnp.float32)).astype(jnp.bfloat16)
            for r in range(D // EDGE):
                out[r * COLS + c, 0:EDGE, :] = score[r * EDGE : (r + 1) * EDGE, :]
            grad = dot(hidden[:, cols], delta[...], ((0,), (0,))) * (-factor * isf)
            score = (grad - second[cols, :].astype(jnp.float32)).astype(jnp.bfloat16)
            for r in range(D // EDGE):
                out[c * (D // EDGE) + r, EDGE : 2 * EDGE, :] = score[
                    r * EDGE : (r + 1) * EDGE, :
                ]


def particle_scores(first, second, images, targets, picks):
    count = picks.shape[0]
    rows = count * PAD
    bf = jnp.bfloat16
    return pl.pallas_call(
        functools.partial(score_kernel, DATA / count),
        out_shape=jax.ShapeDtypeStruct((BLOCKS, 2 * EDGE, D), bf),
        grid_spec=pltpu.PrefetchScalarGridSpec(
            num_scalar_prefetch=1,
            grid=(count,),
            in_specs=[
                pl.BlockSpec((1, S, D), lambda b, picks: (picks[b], 0, 0)),
                pl.BlockSpec((1, S, D), lambda b, picks: (picks[b], 0, 0)),
                pl.BlockSpec((D, FF), lambda b, picks: (0, 0)),
                pl.BlockSpec((FF, D), lambda b, picks: (0, 0)),
            ],
            out_specs=pl.BlockSpec((BLOCKS, 2 * EDGE, D), lambda b, picks: (0, 0, 0)),
            scratch_shapes=[
                pltpu.VMEM((PAD, D), jnp.float32),
                pltpu.VMEM((PAD, D), jnp.float32),
                pltpu.VMEM((rows, D), bf),
                pltpu.VMEM((rows, FF), bf),
                pltpu.VMEM((PAD, FF), jnp.float32),
                pltpu.VMEM((rows, D), bf),
                pltpu.VMEM((rows, FF), bf),
            ],
        ),
        compiler_params=pltpu.CompilerParams(vmem_limit_bytes=48 * 1024 * 1024),
        cost_estimate=pl.CostEstimate(
            flops=10 * count * PAD * D * FF,
            bytes_accessed=4 * (2 * D * FF + count * S * D),
            transcendentals=count * PAD * FF,
        ),
        name="score",
    )(picks, images, targets, first, second)


def gram_kernel(params, gram, total):
    members, rows, _ = params.shape
    wide = members * TILE
    total[...] = jnp.zeros_like(total)
    for r in range(rows // TILE):
        part = params[:, r * TILE : (r + 1) * TILE, :].reshape(wide, D)
        total[...] += dot(part, part, ((1,), (1,)))
    at = lax.broadcasted_iota(jnp.int32, (wide, wide), 0) % TILE
    to = lax.broadcasted_iota(jnp.int32, (wide, wide), 1) % TILE
    kept = jnp.where(at == to, total[...], 0.0)
    summed = jnp.sum(kept.reshape(members, TILE, wide), axis=1)
    turned = summed.T
    gram[...] = jnp.sum(turned.reshape(members, TILE, members), axis=1)


def pair_products(params):
    members, rows, _ = params.shape
    wide = members * TILE
    return pl.pallas_call(
        gram_kernel,
        out_shape=jax.ShapeDtypeStruct((members, members), jnp.float32),
        scratch_shapes=[pltpu.VMEM((wide, wide), jnp.float32)],
        compiler_params=pltpu.CompilerParams(vmem_limit_bytes=32 * 1024 * 1024),
        cost_estimate=pl.CostEstimate(
            flops=2 * wide * wide * rows // TILE * D,
            bytes_accessed=2 * members * rows * D,
            transcendentals=0,
        ),
        name="gram",
    )(params)


def spreading(kernel):
    members = kernel.shape[0]
    wide = members * TILE
    at = lax.broadcasted_iota(jnp.int32, (wide, members), 0) // TILE
    which = lax.broadcasted_iota(jnp.int32, (wide, members), 1)
    pick = jnp.where(at == which, 1.0, 0.0).astype(jnp.bfloat16)
    tall = dot(pick, kernel, ((1,), (0,))).astype(jnp.bfloat16)
    full = dot(tall, pick, ((1,), (1,)))
    row = lax.broadcasted_iota(jnp.int32, (wide, wide), 0) % TILE
    col = lax.broadcasted_iota(jnp.int32, (wide, wide), 1) % TILE
    return jnp.where(row == col, full, 0.0)


def mix_kernel(kernel, params, scores, attract, spread):
    members, rows, _ = params.shape
    wide = members * TILE
    full = spreading(kernel[...])
    ksum = jnp.sum(full, axis=1, keepdims=True)
    mixer = full.astype(jnp.bfloat16)
    for r in range(rows // TILE):
        here = slice(r * TILE, (r + 1) * TILE)
        got = scores[:, here, :].reshape(wide, D)
        pulled = dot(mixer, got, ((1,), (0,))) * (1.0 / members)
        attract[:, here, :] = pulled.astype(jnp.bfloat16).reshape(members, TILE, D)
        own = params[:, here, :].reshape(wide, D)
        mixed = dot(mixer, own, ((1,), (0,)))
        pushed = (ksum * own.astype(jnp.float32) - mixed) * (1.0 / members)
        spread[:, here, :] = pushed.astype(jnp.bfloat16).reshape(members, TILE, D)


def weighted(kernel, params, scores):
    members, rows, _ = params.shape
    wide = members * TILE
    shape = jax.ShapeDtypeStruct(params.shape, jnp.bfloat16)
    return pl.pallas_call(
        mix_kernel,
        out_shape=(shape, shape),
        compiler_params=pltpu.CompilerParams(vmem_limit_bytes=48 * 1024 * 1024),
        cost_estimate=pl.CostEstimate(
            flops=4 * wide * wide * rows // TILE * D,
            bytes_accessed=8 * members * rows * D,
            transcendentals=0,
        ),
        name="mix",
    )(kernel, params, scores)


def plain_products(params):
    flat = params.reshape(params.shape[0], -1)
    return dot(flat, flat, ((1,), (1,)))


def plain_weighted(kernel, params, scores):
    members = params.shape[0]
    flat = params.reshape(members, -1)
    ksum = jnp.sum(kernel.astype(jnp.float32), axis=1, keepdims=True)
    attract = dot(kernel, scores.reshape(members, -1), ((1,), (0,))) / members
    mixed = dot(kernel, flat, ((1,), (0,)))
    spread = (flat.astype(jnp.float32) * ksum - mixed) / members
    return tuple(x.astype(jnp.bfloat16).reshape(params.shape) for x in (attract, spread))


def to_blocks(first, second):
    a = first.reshape(D // EDGE, EDGE, COLS, D).transpose(0, 2, 1, 3).reshape(BLOCKS, EDGE, D)
    return jnp.concatenate([a, second.reshape(BLOCKS, EDGE, D)], axis=1)


def from_blocks(blocks):
    a = blocks[:, :EDGE].reshape(D // EDGE, COLS, EDGE, D).transpose(0, 2, 1, 3)
    return a.reshape(1, D, FF), blocks[:, EDGE:].reshape(1, FF, D)


def exchange(blocks):
    return lax.all_to_all(blocks, AXES, split_axis=0, concat_axis=0, tiled=True)


def on_device(
    particles_first, particles_second, pool_images, pool_targets, batch_index, kernel_scale
):
    members = lax.axis_size("wide") * lax.axis_size("narrow")
    cut = (members, BLOCKS * 2 * EDGE // members, D)
    first = particles_first[0]
    second = particles_second[0]
    params = exchange(to_blocks(first, second).reshape(cut))
    scores = particle_scores(first, second, pool_images, pool_targets, batch_index[0])
    scores = exchange(scores.reshape(cut))
    tiled = cut[1] % TILE == 0
    gram = pair_products(params) if tiled else plain_products(params)
    gram = lax.psum(gram, AXES)
    norms = jnp.diagonal(gram)
    dist = norms[:, None] + norms[None, :] - 2.0 * gram
    kernel = jnp.exp(-dist / kernel_scale[0]).astype(jnp.bfloat16)
    attract, spread = (weighted if tiled else plain_weighted)(kernel, params, scores)
    whole = (BLOCKS, 2 * EDGE, D)
    attract = from_blocks(exchange(attract).reshape(whole))
    spread = from_blocks(exchange(spread).reshape(whole))
    return (*attract, *spread)


def solution(mesh):
    split = P(AXES, None, None)
    return jax.shard_map(
        on_device,
        mesh=mesh,
        in_specs=(split, split, P(), P(), P(AXES, None), P()),
        out_specs=(split, split, split, split),
        check_vma=False,
    )
```

profile of v0, /device:TPU:0, one launch (start us, length us, event | category | flops | bytes accessed | tf_op | source)
XLA Modules:
  0.0 275.4 jit_solution(5733800601994866905)
XLA Ops:
  0.6 2.5 reshape_squeeze.6
  3.2 0.0 copy-start.2
  3.2 0.2 copy.15
  3.3 1.1 copy-done.2
  4.4 1.7 pad_maximum_fusion
  6.1 7.3 %all-to-all-start = ((bf16[32,96,384]{2,1,0:T(8,128)(2,1)}), bf16[32,96,384]{2,1,0:T(8,128)(2,1)S(1)}, u32[]{:S(2)}, u32[]{:S(2)}) async-start(bf16[32,96,384]{2,1,0:T(8,128)(2,1)} %pad_maximum_fusion), calls=%async_computation | async-start | bytes 4718592 | tf_op jit(solution)/shard_map/all_to_all | solution.py:228
  13.4 0.0 copy-start.4
  13.4 1.5 copy.16.image
  14.9 0.1 copy-done.4
  15.0 0.0 copy-start.1
  15.0 0.0 copy-start.3
  15.0 0.2 copy.17.target
  15.2 1.1 copy-done.1
  16.3 0.0 copy-done.3
  16.3 23.1 %score.1 = bf16[32,96,384]{2,1,0:T(8,128)(2,1)} custom-call(s32[8]{0:T(128)S(1)} %bitcast.22, bf16[8,197,384]{2,1,0:T(8,128)(2,1)S(1)} %copy.16.image, bf16[8,197,384]{2,1,0:T(8,128)(2,1)S(1)} %copy.17.target, bf16[384,1536]{1,0:T(8,128)(2,1)S(1)} %bitcast.19, bf16[1536,384]{1,0:T(8,128)(2,1)S(1)} %bitcast.21), custom_call_target="tpu_custom_call" | custom-call | flops 9814671360 | bytes 7139328 | tf_op jit(solution)/shard_map/score/pallas_call | solution.py:90
  39.4 28.4 %all-to-all-done.params = bf16[32,96,384]{2,1,0:T(8,128)(2,1)S(1)} async-done(((bf16[32,96,384]{2,1,0:T(8,128)(2,1)}), bf16[32,96,384]{2,1,0:T(8,128)(2,1)S(1)}, u32[]{:S(2)}, u32[]{:S(2)}) %all-to-all-start) | async-done | bytes 2359328 | tf_op jit(solution)/shard_map/all_to_all | solution.py:228
  67.8 0.0 copy-start
  67.8 4.4 %all-to-all-start.1 = ((bf16[32,96,384]{2,1,0:T(8,128)(2,1)}), bf16[32,96,384]{2,1,0:T(8,128)(2,1)}, u32[]{:S(2)}, u32[]{:S(2)}) async-start(bf16[32,96,384]{2,1,0:T(8,128)(2,1)} %score.1), calls=%async_computation.1 | async-start | bytes 4718592 | tf_op jit(solution)/shard_map/all_to_all | solution.py:228
  72.9 0.0 copy-done
  72.9 2.0 gram.1
  74.9 72.5 %psum.7 = f32[32,32]{1,0:T(8,128)S(1)} all-reduce(f32[32,32]{1,0:T(8,128)S(1)} %gram.1), channel_id=1, replica_groups=mesh['wide'=8,'narrow'=4] {'wide','narrow'}, use_global_device_ids=true, to_apply=%region_0.0 | all-reduce | flops 1024 | bytes 8192 | tf_op jit(solution)/shard_map/psum | solution.py:243
  147.4 0.7 gather_fusion
  148.1 0.1 exponential_convert_fusion.kernel
  148.2 0.0 all-to-all-done.1.scores
  148.2 7.5 %mix.1 = (bf16[32,96,384]{2,1,0:T(8,128)(2,1)S(1)}, bf16[32,96,384]{2,1,0:T(8,128)(2,1)}) custom-call(bf16[32,32]{1,0:T(8,128)(2,1)S(1)} %exponential_convert_fusion.kernel, bf16[32,96,384]{2,1,0:T(8,128)(2,1)} %copy-done, bf16[32,96,384]{2,1,0:T(8,128)(2,1)} %all-to-all-done.1.scores), custom_call_target="tpu_custom_call" | custom-call | flops 2415919104 | bytes 9437184 | tf_op jit(solution)/shard_map/mix/pallas_call | solution.py:189
  155.7 59.4 %all_to_all.20 = bf16[32,96,384]{2,1,0:T(8,128)(2,1)} all-to-all(bf16[32,96,384]{2,1,0:T(8,128)(2,1)S(1)} %get-tuple-element.6), channel_id=1, replica_groups=mesh['wide'=8,'narrow'=4] {'wide','narrow'}, dimensions={0} | all-to-all | bytes 4718592 | tf_op jit(solution)/shard_map/all_to_all | solution.py:228
  215.1 2.8 %all-to-all-start.3 = ((bf16[32,96,384]{2,1,0:T(8,128)(2,1)}), bf16[32,96,384]{2,1,0:T(8,128)(2,1)S(1)}, u32[]{:S(2)}, u32[]{:S(2)}) async-start(bf16[32,96,384]{2,1,0:T(8,128)(2,1)} %get-tuple-element.7), calls=%async_computation.3 | async-start | bytes 4718592 | tf_op jit(solution)/shard_map/all_to_all | solution.py:228
  217.8 2.9 %fusion.1 = (bf16[32,48,384]{2,1,0:T(8,128)(2,1)}, bf16[32,48,384]{2,1,0:T(8,128)(2,1)S(1)}) fusion(bf16[32,96,384]{2,1,0:T(8,128)(2,1)} %all_to_all.20), kind=kLoop, calls=%fused_computation.5 | loop fusion | bytes 4718592 | tf_op jit(solution)/shard_map/slice | solution.py:224
  220.7 0.5 copy.18
  221.2 1.3 reshape.33
  222.5 49.8 %all-to-all-done.3 = bf16[32,96,384]{2,1,0:T(8,128)(2,1)S(1)} async-done(((bf16[32,96,384]{2,1,0:T(8,128)(2,1)}), bf16[32,96,384]{2,1,0:T(8,128)(2,1)S(1)}, u32[]{:S(2)}, u32[]{:S(2)}) %all-to-all-start.3) | async-done | bytes 2359328 | tf_op jit(solution)/shard_map/all_to_all | solution.py:228
  272.3 1.2 fusion
  273.6 0.5 copy.19
  274.1 1.3 reshape.36
  (1 shorter events, 0.0 us)
Async XLA Ops:
  3.2 1.3 copy-start.2
  6.1 61.7 %all-to-all-start = ((bf16[32,96,384]{2,1,0:T(8,128)(2,1)}), bf16[32,96,384]{2,1,0:T(8,128)(2,1)S(1)}, u32[]{:S(2)}, u32[]{:S(2)}) async-start(bf16[32,96,384]{2,1,0:T(8,128)(2,1)} %pad_maximum_fusion), calls=%async_computation | async-start | bytes 4718592 | tf_op jit(solution)/shard_map/all_to_all | solution.py:228
  13.4 1.6 copy-start.4
  15.0 1.3 copy-start.1
  15.0 1.3 copy-start.3
  67.8 5.1 %copy-start = (bf16[32,96,384]{2,1,0:T(8,128)(2,1)}, bf16[32,96,384]{2,1,0:T(8,128)(2,1)S(1)}, u32[]{:S(2)}) copy-start(bf16[32,96,384]{2,1,0:T(8,128)(2,1)S(1)} %all-to-all-done.params) | copy-start | bytes 7077892
  67.8 80.4 %all-to-all-start.1 = ((bf16[32,96,384]{2,1,0:T(8,128)(2,1)}), bf16[32,96,384]{2,1,0:T(8,128)(2,1)}, u32[]{:S(2)}, u32[]{:S(2)}) async-start(bf16[32,96,384]{2,1,0:T(8,128)(2,1)} %score.1), calls=%async_computation.1 | async-start | bytes 4718592 | tf_op jit(solution)/shard_map/all_to_all | solution.py:228
  215.1 57.3 %all-to-all-start.3 = ((bf16[32,96,384]{2,1,0:T(8,128)(2,1)}), bf16[32,96,384]{2,1,0:T(8,128)(2,1)S(1)}, u32[]{:S(2)}, u32[]{:S(2)}) async-start(bf16[32,96,384]{2,1,0:T(8,128)(2,1)} %get-tuple-element.7), calls=%async_computation.3 | async-start | bytes 4718592 | tf_op jit(solution)/shard_map/all_to_all | solution.py:228
where the time goes:
time: 276 us; the launch traced here: 275 us
  blocking collectives  132 us (48%)
  waiting for transfers between devices  78.2 us (28%)
  Pallas kernels  32.6 us (12%)
  local copies, waits for them, and re-layouts  15.1 us (5%)
  starting transfers between devices  14.5 us (5%)
    all_to_all x3, waiting for transfers between devices, exchange(): return lax.all_to_all(blocks, AXES, split_axis=0, concat_axis=0, tiled=True)  78.2 us
    psum x1, blocking collectives, on_device(): gram = lax.psum(gram, AXES)  72.5 us
    all_to_all x1, blocking collectives, exchange(): return lax.all_to_all(blocks, AXES, split_axis=0, concat_axis=0, tiled=True)  59.4 us
    pallas_call x1, Pallas kernels, particle_scores(): pl.pallas_call(functools.partial(score_kernel, DATA / count), out_shape=j...  23.1 us
    all_to_all x3, starting transfers between devices, exchange(): return lax.all_to_all(blocks, AXES, split_axis=0, concat_axis=0, tiled=True)  14.5 us
    pallas_call x1, Pallas kernels, weighted(): pl.pallas_call(mix_kernel, out_shape=(shape, shape), compiler_params=pltp...  7.47 us
  transfers between devices with their start and end apart: 3, of which 2 were waited for; matrix products, arithmetic and copies ran while one was open for 3% of the time, Pallas kernels for 9%

commit v1 on v0

--- a/solution.py
+++ b/solution.py
@@ -132,7 +132,9 @@
     kept = jnp.where(at == to, total[...], 0.0)
     summed = jnp.sum(kept.reshape(members, TILE, wide), axis=1)
     turned = summed.T
-    gram[...] = jnp.sum(turned.reshape(members, TILE, members), axis=1)
+    small = jnp.sum(turned.reshape(members, TILE, members), axis=1)
+    packed = jnp.concatenate([small[8 * q : 8 * q + 8] for q in range(members // 8)], axis=1)
+    gram[...] = jnp.broadcast_to(packed[None], gram.shape)
 
 
 def pair_products(params):
@@ -140,7 +142,7 @@
     wide = members * TILE
     return pl.pallas_call(
         gram_kernel,
-        out_shape=jax.ShapeDtypeStruct((members, members), jnp.float32),
+        out_shape=jax.ShapeDtypeStruct((members, 8, members * members // 8), jnp.float32),
         scratch_shapes=[pltpu.VMEM((wide, wide), jnp.float32)],
         compiler_params=pltpu.CompilerParams(vmem_limit_bytes=32 * 1024 * 1024),
         cost_estimate=pl.CostEstimate(
@@ -150,6 +152,19 @@
         ),
         name="gram",
     )(params)
+
+
+def kernel_of(scale, partials):
+    members = partials.shape[0]
+    packed = jnp.sum(partials[...], axis=0)
+    gram = jnp.concatenate(
+        [packed[:, members * q : members * (q + 1)] for q in range(members // 8)], axis=0
+    )
+    row = lax.broadcasted_iota(jnp.int32, gram.shape, 0)
+    col = lax.broadcasted_iota(jnp.int32, gram.shape, 1)
+    own = jnp.where(row == col, gram, 0.0)
+    dist = jnp.sum(own, axis=1, keepdims=True) + jnp.sum(own, axis=0, keepdims=True) - 2.0 * gram
+    return jnp.exp(-dist / scale[0]).astype(jnp.bfloat16)
 
 
 def spreading(kernel):
@@ -165,38 +180,50 @@
     return jnp.where(row == col, full, 0.0)
 
 
-def mix_kernel(kernel, params, scores, attract, spread):
+def spread_kernel(scale, partials, params, spread):
     members, rows, _ = params.shape
     wide = members * TILE
-    full = spreading(kernel[...])
+    full = spreading(kernel_of(scale, partials))
     ksum = jnp.sum(full, axis=1, keepdims=True)
     mixer = full.astype(jnp.bfloat16)
+    for r in range(rows // TILE):
+        here = slice(r * TILE, (r + 1) * TILE)
+        own = params[:, here, :].reshape(wide, D)
+        mixed = dot(mixer, own, ((1,), (0,)))
+        pushed = (ksum * own.astype(jnp.float32) - mixed) * (1.0 / members)
+        spread[:, here, :] = pushed.astype(jnp.bfloat16).reshape(members, TILE, D)
+
+
+def attract_kernel(scale, partials, scores, attract):
+    members, rows, _ = scores.shape
+    wide = members * TILE
+    mixer = spreading(kernel_of(scale, partials)).astype(jnp.bfloat16)
     for r in range(rows // TILE):
         here = slice(r * TILE, (r + 1) * TILE)
         got = scores[:, here, :].reshape(wide, D)
         pulled = dot(mixer, got, ((1,), (0,))) * (1.0 / members)
         attract[:, here, :] = pulled.astype(jnp.bfloat16).reshape(members, TILE, D)
-        own = params[:, here, :].reshape(wide, D)
-        mixed = dot(mixer, own, ((1,), (0,)))
-        pushed = (ksum * own.astype(jnp.float32) - mixed) * (1.0 / members)
-        spread[:, here, :] = pushed.astype(jnp.bfloat16).reshape(members, TILE, D)
-
-
-def weighted(kernel, params, scores):
-    members, rows, _ = params.shape
-    wide = members * TILE
-    shape = jax.ShapeDtypeStruct(params.shape, jnp.bfloat16)
-    return pl.pallas_call(
-        mix_kernel,
-        out_shape=(shape, shape),
-        compiler_params=pltpu.CompilerParams(vmem_limit_bytes=48 * 1024 * 1024),
+
+
+def weighted(body, name, scale, partials, held):
+    members, rows, _ = held.shape
+    wide = members * TILE
+    return pl.pallas_call(
+        body,
+        out_shape=jax.ShapeDtypeStruct(held.shape, jnp.bfloat16),
+        in_specs=[
+            pl.BlockSpec(memory_space=pltpu.SMEM),
+            pl.BlockSpec(memory_space=pltpu.VMEM),
+            pl.BlockSpec(memory_space=pltpu.VMEM),
+        ],
+        compiler_params=pltpu.CompilerParams(vmem_limit_bytes=32 * 1024 * 1024),
         cost_estimate=pl.CostEstimate(
-            flops=4 * wide * wide * rows // TILE * D,
-            bytes_accessed=8 * members * rows * D,
+            flops=2 * wide * wide * rows // TILE * D,
+            bytes_accessed=4 * members * rows * D,
             transcendentals=0,
         ),
-        name="mix",
-    )(kernel, params, scores)
+        name=name,
+    )(scale, partials, held)
 
 
 def plain_products(params):
@@ -204,8 +231,11 @@
     return dot(flat, flat, ((1,), (1,)))
 
 
-def plain_weighted(kernel, params, scores):
+def plain_weighted(gram, scale, params, scores):
     members = params.shape[0]
+    norms = jnp.diagonal(gram)
+    dist = norms[:, None] + norms[None, :] - 2.0 * gram
+    kernel = jnp.exp(-dist / scale[0]).astype(jnp.bfloat16)
     flat = params.reshape(members, -1)
     ksum = jnp.sum(kernel.astype(jnp.float32), axis=1, keepdims=True)
     attract = dot(kernel, scores.reshape(members, -1), ((1,), (0,))) / members
@@ -214,14 +244,43 @@
     return tuple(x.astype(jnp.bfloat16).reshape(params.shape) for x in (attract, spread))
 
 
+def pack_kernel(first, second, out):
+    for r in range(D // EDGE):
+        for c in range(COLS):
+            b = r * COLS + c
+            out[b, 0:EDGE, :] = first[0, r * EDGE : (r + 1) * EDGE, c * D : (c + 1) * D]
+            out[b, EDGE : 2 * EDGE, :] = second[0, b * EDGE : (b + 1) * EDGE, :]
+
+
 def to_blocks(first, second):
-    a = first.reshape(D // EDGE, EDGE, COLS, D).transpose(0, 2, 1, 3).reshape(BLOCKS, EDGE, D)
-    return jnp.concatenate([a, second.reshape(BLOCKS, EDGE, D)], axis=1)
+    return pl.pallas_call(
+        pack_kernel,
+        out_shape=jax.ShapeDtypeStruct((BLOCKS, 2 * EDGE, D), jnp.bfloat16),
+        compiler_params=pltpu.CompilerParams(vmem_limit_bytes=16 * 1024 * 1024),
+        cost_estimate=pl.CostEstimate(flops=0, bytes_accessed=8 * D * FF, transcendentals=0),
+        name="pack",
+    )(first, second)
+
+
+def unpack_kernel(blocks, first, second):
+    for r in range(D // EDGE):
+        for c in range(COLS):
+            b = r * COLS + c
+            first[0, r * EDGE : (r + 1) * EDGE, c * D : (c + 1) * D] = blocks[b, 0:EDGE, :]
+            second[0, b * EDGE : (b + 1) * EDGE, :] = blocks[b, EDGE : 2 * EDGE, :]
 
 
 def from_blocks(blocks):
-    a = blocks[:, :EDGE].reshape(D // EDGE, COLS, EDGE, D).transpose(0, 2, 1, 3)
-    return a.reshape(1, D, FF), blocks[:, EDGE:].reshape(1, FF, D)
+    return pl.pallas_call(
+        unpack_kernel,
+        out_shape=(
+            jax.ShapeDtypeStruct((1, D, FF), jnp.bfloat16),
+            jax.ShapeDtypeStruct((1, FF, D), jnp.bfloat16),
+        ),
+        compiler_params=pltpu.CompilerParams(vmem_limit_bytes=16 * 1024 * 1024),
+        cost_estimate=pl.CostEstimate(flops=0, bytes_accessed=8 * D * FF, transcendentals=0),
+        name="unpack",
+    )(blocks)
 
 
 def exchange(blocks):
@@ -233,21 +292,23 @@
 ):
     members = lax.axis_size("wide") * lax.axis_size("narrow")
     cut = (members, BLOCKS * 2 * EDGE // members, D)
-    first = particles_first[0]
-    second = particles_second[0]
-    params = exchange(to_blocks(first, second).reshape(cut))
-    scores = particle_scores(first, second, pool_images, pool_targets, batch_index[0])
+    whole = (BLOCKS, 2 * EDGE, D)
+    params = exchange(to_blocks(particles_first, particles_second).reshape(cut))
+    scores = particle_scores(
+        particles_first[0], particles_second[0], pool_images, pool_targets, batch_index[0]
+    )
+    params, scores = lax.optimization_barrier((params, scores))
     scores = exchange(scores.reshape(cut))
-    tiled = cut[1] % TILE == 0
-    gram = pair_products(params) if tiled else plain_products(params)
-    gram = lax.psum(gram, AXES)
-    norms = jnp.diagonal(gram)
-    dist = norms[:, None] + norms[None, :] - 2.0 * gram
-    kernel = jnp.exp(-dist / kernel_scale[0]).astype(jnp.bfloat16)
-    attract, spread = (weighted if tiled else plain_weighted)(kernel, params, scores)
-    whole = (BLOCKS, 2 * EDGE, D)
+    if cut[1] % TILE == 0:
+        partials = exchange(pair_products(params))
+        spread = weighted(spread_kernel, "spread", kernel_scale, partials, params)
+        spread, scores = lax.optimization_barrier((spread, scores))
+        attract = weighted(attract_kernel, "attract", kernel_scale, partials, scores)
+    else:
+        gram = lax.psum(plain_products(params), AXES)
+        attract, spread = plain_weighted(gram, kernel_scale, params, scores)
+    spread = from_blocks(exchange(spread).reshape(whole))
     attract = from_blocks(exchange(attract).reshape(whole))
-    spread = from_blocks(exchange(spread).reshape(whole))
     return (*attract, *spread)
 
 

time: 276 us -> 262 us (0.949)
  blocking collectives: 132 us -> 72.1 us
  waiting for transfers between devices: 78.2 us -> 129 us
  local copies, waits for them, and re-layouts: 15.1 us -> 8.87 us
  Pallas kernels: 32.6 us -> 36.2 us
    psum x1 -> x0, blocking collectives: 72.5 us -> none  [on_device(): gram = lax.psum(gram, AXES)]
    all_to_all x3, waiting for transfers between devices: 78.2 us -> 129 us  [exchange(): return lax.all_to_all(blocks, AXES, split_axis=0, concat_axis=0, tiled=True)]
    all_to_all x1 -> x2, blocking collectives: 59.4 us -> 72.1 us  [exchange(): return lax.all_to_all(blocks, AXES, split_axis=0, concat_axis=0, tiled=True)]
    unnamed x12 -> x18, local copies, waits for them, and re-layouts: 4.01 us -> 8.87 us
    slice x2 -> x0, local copies, waits for them, and re-layouts: 4.14 us -> none  [from_blocks(): return (a.reshape(1, D, FF), blocks[:, EDGE:].reshape(1, FF, D))]
    pallas_call x2 -> x6, Pallas kernels: 9.5 us -> 13.1 us  [the longest x2 7.57 us: weighted(): pl.pallas_call(body, out_shape=jax.ShapeDtypeStruct(held.shape, jnp.bfloa...]
  transfers between devices with their start and end apart: 3 -> 3, of which waited for: 2 -> 3; matrix products, arithmetic and copies ran while one was open for 3% -> 1% of each run, Pallas kernels for 9% -> 11%
where the time goes in v1:
time: 262 us; the launch traced here: 261 us
  waiting for transfers between devices  129 us (49%)
  blocking collectives  72.1 us (28%)
  Pallas kernels  36.2 us (14%)
  starting transfers between devices  13.8 us (5%)
  local copies, waits for them, and re-layouts  8.87 us (3%)
    all_to_all x3, waiting for transfers between devices, exchange(): return lax.all_to_all(blocks, AXES, split_axis=0, concat_axis=0, tiled=True)  129 us
    all_to_all x2, blocking collectives, exchange(): return lax.all_to_all(blocks, AXES, split_axis=0, concat_axis=0, tiled=True)  72.1 us
    pallas_call x1, Pallas kernels, particle_scores(): pl.pallas_call(functools.partial(score_kernel, DATA / count), out_shape=j...  23.1 us
    all_to_all x3, starting transfers between devices, exchange(): return lax.all_to_all(blocks, AXES, split_axis=0, concat_axis=0, tiled=True)  13.8 us
    unnamed x18, local copies, waits for them, and re-layouts  8.87 us
    pallas_call x2, Pallas kernels, weighted(): pl.pallas_call(body, out_shape=jax.ShapeDtypeStruct(held.shape, jnp.bfloa...  7.57 us
  transfers between devices with their start and end apart: 3, of which 3 were waited for; matrix products, arithmetic and copies ran while one was open for 1% of the time, Pallas kernels for 11%

profile of v1, /device:TPU:0, one launch (start us, length us, event | category | flops | bytes accessed | tf_op | source)
XLA Modules:
  0.0 261.5 jit_solution(1325611660712634798)
XLA Ops:
  0.6 0.0 copy-start.2
  0.6 1.3 copy-done.2
  1.9 0.0 copy-start.4
  1.9 1.3 copy-done.4
  3.2 0.2 pack.1
  3.4 0.0 copy-start
  3.4 1.4 copy-done
  4.8 7.3 %all-to-all-start = ((bf16[32,96,384]{2,1,0:T(8,128)(2,1)}), bf16[32,96,384]{2,1,0:T(8,128)(2,1)S(1)}, u32[]{:S(2)}, u32[]{:S(2)}) async-start(bf16[32,96,384]{2,1,0:T(8,128)(2,1)} %copy-done), calls=%async_computation | async-start | bytes 4718592 | tf_op jit(solution)/shard_map/all_to_all | solution.py:287
  12.1 0.0 copy-start.7
  12.1 1.5 copy.10.image
  13.7 0.1 copy-done.7
  13.8 0.0 copy-start.3
  13.8 0.0 copy-start.5
  13.8 0.0 copy-start.6
  13.8 0.2 copy.11.target
  13.9 1.1 copy-done.3
  15.0 0.4 copy-done.5
  15.4 0.0 copy-done.6
  15.4 23.1 %score.1 = bf16[32,96,384]{2,1,0:T(8,128)(2,1)} custom-call(s32[8]{0:T(128)S(1)} %bitcast.5, bf16[8,197,384]{2,1,0:T(8,128)(2,1)S(1)} %copy.10.image, bf16[8,197,384]{2,1,0:T(8,128)(2,1)S(1)} %copy.11.target, bf16[384,1536]{1,0:T(8,128)(2,1)S(1)} %bitcast.3, bf16[1536,384]{1,0:T(8,128)(2,1)S(1)} %bitcast.4), custom_call_target="tpu_custom_call" | custom-call | flops 9814671360 | bytes 7139328 | tf_op jit(solution)/shard_map/score/pallas_call | solution.py:90
  38.5 28.0 %all-to-all-done.params = bf16[32,96,384]{2,1,0:T(8,128)(2,1)S(1)} async-done(((bf16[32,96,384]{2,1,0:T(8,128)(2,1)}), bf16[32,96,384]{2,1,0:T(8,128)(2,1)S(1)}, u32[]{:S(2)}, u32[]{:S(2)}) %all-to-all-start) | async-done | bytes 2359328 | tf_op jit(solution)/shard_map/all_to_all | solution.py:287
  66.5 2.1 gram.1
  68.6 12.3 %all_to_all.25.partials = f32[32,8,128]{2,1,0:T(8,128)S(1)} all-to-all(f32[32,8,128]{2,1,0:T(8,128)S(1)} %gram.1), channel_id=1, replica_groups=mesh['wide'=8,'narrow'=4] {'wide','narrow'}, dimensions={0} | all-to-all | bytes 262144 | tf_op jit(solution)/shard_map/all_to_all | solution.py:287
  80.9 3.7 %all-to-all-start.2 = ((bf16[32,96,384]{2,1,0:T(8,128)(2,1)}), bf16[32,96,384]{2,1,0:T(8,128)(2,1)}, u32[]{:S(2)}, u32[]{:S(2)}) async-start(bf16[32,96,384]{2,1,0:T(8,128)(2,1)} %score.1), calls=%async_computation.2 | async-start | bytes 4718592 | tf_op jit(solution)/shard_map/all_to_all | solution.py:287
  85.3 3.7 %spread.1 = bf16[32,96,384]{2,1,0:T(8,128)(2,1)} custom-call(f32[1]{0:T(128)S(6)} %copy.12.scale, f32[32,8,128]{2,1,0:T(8,128)S(1)} %all_to_all.25.partials, bf16[32,96,384]{2,1,0:T(8,128)(2,1)S(1)} %all-to-all-done.params), custom_call_target="tpu_custom_call" | custom-call | flops 1207959552 | bytes 4718592 | tf_op jit(solution)/shard_map/spread/pallas_call | solution.py:211
  89.0 50.0 %all-to-all-done.2.scores = bf16[32,96,384]{2,1,0:T(8,128)(2,1)} async-done(((bf16[32,96,384]{2,1,0:T(8,128)(2,1)}), bf16[32,96,384]{2,1,0:T(8,128)(2,1)}, u32[]{:S(2)}, u32[]{:S(2)}) %all-to-all-start.2) | async-done | bytes 2359328 | tf_op jit(solution)/shard_map/all_to_all | solution.py:287
  138.9 3.9 %attract.1 = bf16[32,96,384]{2,1,0:T(8,128)(2,1)S(1)} custom-call(f32[1]{0:T(128)S(6)} %copy.12.scale, f32[32,8,128]{2,1,0:T(8,128)S(1)} %all_to_all.25.partials, bf16[32,96,384]{2,1,0:T(8,128)(2,1)} %all-to-all-done.2.scores), custom_call_target="tpu_custom_call" | custom-call | flops 1207959552 | bytes 4718592 | tf_op jit(solution)/shard_map/attract/pallas_call | solution.py:211
  142.8 59.8 %all_to_all.26.blocks = bf16[32,96,384]{2,1,0:T(8,128)(2,1)} all-to-all(bf16[32,96,384]{2,1,0:T(8,128)(2,1)S(1)} %attract.1), channel_id=1, replica_groups=mesh['wide'=8,'narrow'=4] {'wide','narrow'}, dimensions={0} | all-to-all | bytes 4718592 | tf_op jit(solution)/shard_map/all_to_all | solution.py:287
  202.6 2.8 %all-to-all-start.4 = ((bf16[32,96,384]{2,1,0:T(8,128)(2,1)}), bf16[32,96,384]{2,1,0:T(8,128)(2,1)S(1)}, u32[]{:S(2)}, u32[]{:S(2)}) async-start(bf16[32,96,384]{2,1,0:T(8,128)(2,1)} %spread.1), calls=%async_computation.4 | async-start | bytes 4718592 | tf_op jit(solution)/shard_map/all_to_all | solution.py:287
  205.4 0.0 copy-start.1
  205.4 1.7 copy-done.1
  207.0 1.6 unpack.2
  208.6 51.2 %all-to-all-done.4.blocks = bf16[32,96,384]{2,1,0:T(8,128)(2,1)S(1)} async-done(((bf16[32,96,384]{2,1,0:T(8,128)(2,1)}), bf16[32,96,384]{2,1,0:T(8,128)(2,1)S(1)}, u32[]{:S(2)}, u32[]{:S(2)}) %all-to-all-start.4) | async-done | bytes 2359328 | tf_op jit(solution)/shard_map/all_to_all | solution.py:287
  259.9 1.6 unpack.3
Async XLA Ops:
  0.6 1.3 copy-start.2
  1.9 1.3 copy-start.4
  3.4 1.4 copy-start
  4.8 61.7 %all-to-all-start = ((bf16[32,96,384]{2,1,0:T(8,128)(2,1)}), bf16[32,96,384]{2,1,0:T(8,128)(2,1)S(1)}, u32[]{:S(2)}, u32[]{:S(2)}) async-start(bf16[32,96,384]{2,1,0:T(8,128)(2,1)} %copy-done), calls=%async_computation | async-start | bytes 4718592 | tf_op jit(solution)/shard_map/all_to_all | solution.py:287
  12.1 1.6 copy-start.7
  13.8 1.3 copy-start.3
  13.8 1.6 copy-start.5
  13.8 1.6 copy-start.6
  80.9 58.0 %all-to-all-start.2 = ((bf16[32,96,384]{2,1,0:T(8,128)(2,1)}), bf16[32,96,384]{2,1,0:T(8,128)(2,1)}, u32[]{:S(2)}, u32[]{:S(2)}) async-start(bf16[32,96,384]{2,1,0:T(8,128)(2,1)} %score.1), calls=%async_computation.2 | async-start | bytes 4718592 | tf_op jit(solution)/shard_map/all_to_all | solution.py:287
  202.6 57.3 %all-to-all-start.4 = ((bf16[32,96,384]{2,1,0:T(8,128)(2,1)}), bf16[32,96,384]{2,1,0:T(8,128)(2,1)S(1)}, u32[]{:S(2)}, u32[]{:S(2)}) async-start(bf16[32,96,384]{2,1,0:T(8,128)(2,1)} %spread.1), calls=%async_computation.4 | async-start | bytes 4718592 | tf_op jit(solution)/shard_map/all_to_all | solution.py:287
  205.4 1.7 copy-start.1

commit v2 on v0

v2 whole, which is shorter than its diff:
```python
import functools
import math

import jax
import jax.numpy as jnp
from jax import lax
from jax.experimental import pallas as pl
from jax.experimental.pallas import tpu as pltpu
from jax.sharding import Mesh
from jax.sharding import PartitionSpec as P

D = 384
FF = 1536
S = 197
DATA = 10000
AXES = ("half", "rest")
PAD = 208
EDGE = 48
BLOCKS = D * FF // (EDGE * D)
COLS = FF // D
TILE = 16
GROUPS = 16
PER = BLOCKS // GROUPS
SIDE = PER * EDGE
ROWS = 2 * SIDE
EXTRA = 16

gelu_c = math.sqrt(2.0 / math.pi)
isd = 1.0 / math.sqrt(D)
isf = 1.0 / math.sqrt(FF)


def dot(a, b, dims):
    return lax.dot_general(a, b, (dims, ((), ())), preferred_element_type=jnp.float32)


def place(block):
    return block // PER, block % PER * EDGE


def score_kernel(
    factor, picks, image, target, first, second, out, xs, ts, normed, hidden, deriv, delta, back
):
    step = pl.program_id(0)
    images = pl.num_programs(0)
    rows = pl.ds(pl.multiple_of(step * PAD, PAD), PAD)

    @pl.when(step == 0)
    def _():
        xs[...] = jnp.zeros_like(xs)
        ts[...] = jnp.zeros_like(ts)

    xs[0:S, :] = image[0].astype(jnp.float32)
    ts[0:S, :] = target[0].astype(jnp.float32)
    xf = xs[...]
    mean = jnp.mean(xf, axis=1, keepdims=True)
    centered = xf - mean
    var = jnp.mean(centered * centered, axis=1, keepdims=True)
    nrm = (centered * lax.rsqrt(var + 1e-06)).astype(jnp.bfloat16)
    normed[rows, :] = nrm
    for c in range(COLS):
        cols = pl.ds(c * D, D)
        pre = dot(nrm, first[:, cols], ((1,), (0,))) * isd
        sq = pre * pre
        tval = jnp.tanh(pre * (gelu_c + (gelu_c * 0.044715) * sq))
        gate = 0.5 + 0.5 * tval
        hid = pre * gate
        hidden[rows, cols] = hid.astype(jnp.bfloat16)
        deriv[:, cols] = gate + hid * (1.0 - gate) * (
            2.0 * gelu_c + (6.0 * gelu_c * 0.044715) * sq
        )
    prod = dot(hidden[rows, :], second[...], ((1,), (0,))) * isf
    dlt = ((xs[...] + prod - ts[...]) * (1.0 / S)).astype(jnp.bfloat16)
    delta[rows, :] = dlt
    for c in range(COLS):
        cols = pl.ds(c * D, D)
        dhid = dot(dlt, second[cols, :], ((1,), (1,))) * isf
        back[rows, cols] = (dhid * deriv[:, cols]).astype(jnp.bfloat16)

    @pl.when(step == images - 1)
    def _():
        for c in range(COLS):
            cols = pl.ds(c * D, D)
            grad = dot(normed[...], back[:, cols], ((0,), (0,))) * (-factor * isd)
            score = (grad - first[:, cols].astype(jnp.float32)).astype(jnp.bfloat16)
            for r in range(D // EDGE):
                g, at = place(r * COLS + c)
                out[g, at : at + EDGE, :] = score[r * EDGE : (r + 1) * EDGE, :]
            grad = dot(hidden[:, cols], delta[...], ((0,), (0,))) * (-factor * isf)
            score = (grad - second[cols, :].astype(jnp.float32)).astype(jnp.bfloat16)
            for r in range(D // EDGE):
                g, at = place(c * (D // EDGE) + r)
                out[g, SIDE + at : SIDE + at + EDGE, :] = score[r * EDGE : (r + 1) * EDGE, :]


def particle_scores(first, second, images, targets, picks, extra=0):
    count = picks.shape[0]
    rows = count * PAD
    bf = jnp.bfloat16
    return pl.pallas_call(
        functools.partial(score_kernel, DATA / count),
        out_shape=jax.ShapeDtypeStruct((GROUPS, ROWS + extra, D), bf),
        grid_spec=pltpu.PrefetchScalarGridSpec(
            num_scalar_prefetch=1,
            grid=(count,),
            in_specs=[
                pl.BlockSpec((1, S, D), lambda b, picks: (picks[b], 0, 0)),
                pl.BlockSpec((1, S, D), lambda b, picks: (picks[b], 0, 0)),
                pl.BlockSpec((D, FF), lambda b, picks: (0, 0)),
                pl.BlockSpec((FF, D), lambda b, picks: (0, 0)),
            ],
            out_specs=pl.BlockSpec((GROUPS, ROWS, D), lambda b, picks: (0, 0, 0)),
            scratch_shapes=[
                pltpu.VMEM((PAD, D), jnp.float32),
                pltpu.VMEM((PAD, D), jnp.float32),
                pltpu.VMEM((rows, D), bf),
                pltpu.VMEM((rows, FF), bf),
                pltpu.VMEM((PAD, FF), jnp.float32),
                pltpu.VMEM((rows, D), bf),
                pltpu.VMEM((rows, FF), bf),
            ],
        ),
        compiler_params=pltpu.CompilerParams(vmem_limit_bytes=48 * 1024 * 1024),
        cost_estimate=pl.CostEstimate(
            flops=10 * count * PAD * D * FF,
            bytes_accessed=4 * (2 * D * FF + count * S * D),
            transcendentals=count * PAD * FF,
        ),
        name="score",
    )(picks, images, targets, first, second)


def gram_kernel(own, other_first, other_second, scores, out, total, parts, sem):
    half = own.shape[0]
    members = 2 * half
    wide = members * TILE
    total[...] = jnp.zeros_like(total)
    for r in range(0, ROWS, TILE):
        there = other_first if r < SIDE else other_second
        at = r % SIDE
        part = jnp.concatenate([own[:, r : r + TILE, :], there[:, at : at + TILE, :]], axis=0)
        part = part.reshape(wide, D)
        total[...] += dot(part, part, ((1,), (1,)))
    row = lax.broadcasted_iota(jnp.int32, (wide, wide), 0) % TILE
    col = lax.broadcasted_iota(jnp.int32, (wide, wide), 1) % TILE
    kept = jnp.where(row == col, total[...], 0.0)
    summed = jnp.sum(kept.reshape(members, TILE, wide), axis=1)
    turned = summed.T
    small = jnp.sum(turned.reshape(members, TILE, members), axis=1)
    packed = jnp.concatenate([small[8 * q : 8 * q + 8] for q in range(members // 8)], axis=1)
    high = packed.astype(jnp.bfloat16).astype(jnp.float32)
    middle = (packed - high).astype(jnp.bfloat16).astype(jnp.float32)
    low = packed - high - middle
    three = jnp.concatenate([high, middle, low], axis=1)
    three = jnp.concatenate([three, jnp.zeros_like(three)], axis=0).astype(jnp.bfloat16)
    parts[...] = jnp.broadcast_to(three[None], parts.shape)
    copy = pltpu.make_async_copy(parts, out.at[:, pl.ds(ROWS, EXTRA), :], sem)
    copy.start()
    copy.wait()


def add_products(own, other_first, other_second, scores):
    half = own.shape[0]
    wide = 2 * half * TILE
    vmem = pl.BlockSpec(memory_space=pltpu.VMEM)
    return pl.pallas_call(
        gram_kernel,
        out_shape=jax.ShapeDtypeStruct(scores.shape, scores.dtype),
        in_specs=[vmem, vmem, vmem, pl.BlockSpec(memory_space=pl.ANY)],
        out_specs=pl.BlockSpec(memory_space=pl.ANY),
        input_output_aliases={3: 0},
        scratch_shapes=[
            pltpu.VMEM((wide, wide), jnp.float32),
            pltpu.VMEM((half, EXTRA, D), jnp.bfloat16),
            pltpu.SemaphoreType.DMA,
        ],
        compiler_params=pltpu.CompilerParams(vmem_limit_bytes=32 * 1024 * 1024),
        cost_estimate=pl.CostEstimate(
            flops=2 * wide * wide * ROWS // TILE * D,
            bytes_accessed=4 * half * ROWS * D,
            transcendentals=0,
        ),
        name="gram",
    )(own, other_first, other_second, scores)


def kernel_of(scale, gram):
    row = lax.broadcasted_iota(jnp.int32, gram.shape, 0)
    col = lax.broadcasted_iota(jnp.int32, gram.shape, 1)
    own = jnp.where(row == col, gram, 0.0)
    dist = jnp.sum(own, axis=1, keepdims=True) + jnp.sum(own, axis=0, keepdims=True) - 2.0 * gram
    return jnp.exp(-dist / scale[0]).astype(jnp.bfloat16)


def one_hot(members):
    at = lax.broadcasted_iota(jnp.int32, (members * TILE, members), 0) // TILE
    which = lax.broadcasted_iota(jnp.int32, (members * TILE, members), 1)
    return jnp.where(at == which, 1.0, 0.0).astype(jnp.bfloat16)


def mix_kernel(scale, other_scores, own_scores, own, other_first, other_second, out):
    half = own.shape[0]
    members = 2 * half
    wide = half * TILE
    three = jnp.sum(other_scores[:, ROWS : ROWS + EXTRA, :].astype(jnp.float32), axis=0)
    lanes = members * members // 8
    packed = three[0:8, 0:lanes] + three[0:8, lanes : 2 * lanes] + three[0:8, 2 * lanes :]
    gram = jnp.concatenate(
        [packed[:, members * q : members * (q + 1)] for q in range(members // 8)], axis=0
    )
    kernel = kernel_of(scale, gram)
    tall = dot(one_hot(half), kernel[0:half], ((1,), (0,))).astype(jnp.bfloat16)
    full = dot(tall, one_hot(members), ((1,), (1,)))
    row = lax.broadcasted_iota(jnp.int32, full.shape, 0) % TILE
    col = lax.broadcasted_iota(jnp.int32, full.shape, 1) % TILE
    full = jnp.where(row == col, full, 0.0)
    ksum = jnp.sum(full, axis=1, keepdims=True)
    near = full[:, :wide].astype(jnp.bfloat16)
    far = full[:, wide:].astype(jnp.bfloat16)
    for r in range(0, ROWS, TILE):
        here = slice(r, r + TILE)
        pulled = dot(near, own_scores[:, here, :].reshape(wide, D), ((1,), (0,)))
        pulled += dot(far, other_scores[:, here, :].reshape(wide, D), ((1,), (0,)))
        pulled *= 1.0 / members
        out[:, here, :] = pulled.astype(jnp.bfloat16).reshape(half, TILE, D)
        there = other_first if r < SIDE else other_second
        at = r % SIDE
        mine = own[:, here, :].reshape(wide, D)
        mixed = dot(near, mine, ((1,), (0,)))
        mixed += dot(far, there[:, at : at + TILE, :].reshape(wide, D), ((1,), (0,)))
        pushed = (ksum * mine.astype(jnp.float32) - mixed) * (1.0 / members)
        out[:, ROWS + r : ROWS + r + TILE, :] = pushed.astype(jnp.bfloat16).reshape(half, TILE, D)


def weighted(scale, other_scores, own_scores, own, other_first, other_second):
    half = own.shape[0]
    vmem = pl.BlockSpec(memory_space=pltpu.VMEM)
    return pl.pallas_call(
        mix_kernel,
        out_shape=jax.ShapeDtypeStruct((half, 2 * ROWS, D), jnp.bfloat16),
        in_specs=[pl.BlockSpec(memory_space=pltpu.SMEM)] + [vmem] * 5,
        compiler_params=pltpu.CompilerParams(vmem_limit_bytes=48 * 1024 * 1024),
        cost_estimate=pl.CostEstimate(
            flops=8 * half * half * TILE * ROWS * D,
            bytes_accessed=12 * half * ROWS * D,
            transcendentals=0,
        ),
        name="mix",
    )(scale, other_scores, own_scores, own, other_first, other_second)


def plain_mix(scale, params, scores):
    members = params.shape[0]
    half = members // 2
    flat = params.reshape(members, -1)
    gram = lax.psum(dot(flat, flat, ((1,), (1,))), "rest")
    kernel = kernel_of(scale, gram)[:half]
    ksum = jnp.sum(kernel.astype(jnp.float32), axis=1, keepdims=True)
    attract = dot(kernel, scores.reshape(members, -1), ((1,), (0,))) / members
    mixed = dot(kernel, flat, ((1,), (0,)))
    spread = (flat[:half].astype(jnp.float32) * ksum - mixed) / members
    shape = (half, *params.shape[1:])
    return tuple(x.astype(jnp.bfloat16).reshape(shape) for x in (attract, spread))


def pack_kernel(first, second, out):
    for b in range(BLOCKS):
        g, at = place(b)
        r, c = b // COLS * EDGE, b % COLS * D
        out[g, at : at + EDGE, :] = first[0, r : r + EDGE, c : c + D]
        out[g, SIDE + at : SIDE + at + EDGE, :] = second[0, b * EDGE : (b + 1) * EDGE, :]


def pack_first_kernel(first, out):
    for b in range(BLOCKS):
        g, at = place(b)
        r, c = b // COLS * EDGE, b % COLS * D
        out[g, at : at + EDGE, :] = first[0, r : r + EDGE, c : c + D]


def pack(*arrays):
    return pl.pallas_call(
        pack_kernel if len(arrays) == 2 else pack_first_kernel,
        out_shape=jax.ShapeDtypeStruct((GROUPS, len(arrays) * SIDE, D), jnp.bfloat16),
        compiler_params=pltpu.CompilerParams(vmem_limit_bytes=16 * 1024 * 1024),
        cost_estimate=pl.CostEstimate(
            flops=0, bytes_accessed=4 * len(arrays) * D * FF, transcendentals=0
        ),
        name="pack",
    )(*arrays)


def unpack_kernel(blocks, *outs):
    for which in range(2):
        first, second = outs[2 * which : 2 * which + 2]
        for b in range(BLOCKS):
            g, at = place(b)
            at += which * ROWS
            r, c = b // COLS * EDGE, b % COLS * D
            first[0, r : r + EDGE, c : c + D] = blocks[g, at : at + EDGE, :]
            second[0, b * EDGE : (b + 1) * EDGE, :] = blocks[g, SIDE + at : SIDE + at + EDGE, :]


def unpack(blocks):
    shapes = (
        jax.ShapeDtypeStruct((1, D, FF), jnp.bfloat16),
        jax.ShapeDtypeStruct((1, FF, D), jnp.bfloat16),
    )
    return pl.pallas_call(
        unpack_kernel,
        out_shape=shapes + shapes,
        compiler_params=pltpu.CompilerParams(vmem_limit_bytes=24 * 1024 * 1024),
        cost_estimate=pl.CostEstimate(flops=0, bytes_accessed=16 * D * FF, transcendentals=0),
        name="unpack",
    )(blocks)


def exchange(blocks):
    return lax.all_to_all(blocks, "rest", split_axis=0, concat_axis=0, tiled=True)


def after(value, *others):
    return lax.optimization_barrier((value, *others))[0]


def on_device(first, second, images, targets, picks, scale):
    half = lax.axis_size("rest")
    over = [(0, 1), (1, 0)]
    far_first = lax.ppermute(first, "half", over)
    far_second = lax.ppermute(second, "half", over)
    far_picks = lax.ppermute(picks, "half", over)
    own_scores = particle_scores(first[0], second[0], images, targets, picks[0])
    if half == GROUPS:
        own = exchange(pack(first, second))
        own_scores = exchange(after(own_scores, own))
        other_second = exchange(after(far_second.reshape(half, SIDE, D), own_scores))
        other_first = exchange(after(pack(far_first), other_second))
        scores = particle_scores(
            far_first[0], far_second[0], images, targets, far_picks[0], EXTRA
        )
        scores = exchange(add_products(own, other_first, other_second, scores))
        mixed = exchange(weighted(scale, scores, own_scores, own, other_first, other_second))
    else:
        cut = (half, GROUPS * ROWS // half, D)
        scores = particle_scores(far_first[0], far_second[0], images, targets, far_picks[0])
        params = [pack(first, second), pack(far_first, far_second)]
        params = jnp.concatenate([exchange(x.reshape(cut)) for x in params])
        scores = jnp.concatenate([exchange(x.reshape(cut)) for x in (own_scores, scores)])
        mixed = [exchange(x) for x in plain_mix(scale, params, scores)]
        mixed = jnp.concatenate([x.reshape(GROUPS, ROWS, D) for x in mixed], axis=1)
    return unpack(mixed)


def solution(mesh):
    halves = Mesh(mesh.devices.reshape(2, -1), AXES)
    split = P(AXES, None, None)
    return jax.shard_map(
        on_device,
        mesh=halves,
        in_specs=(split, split, P(), P(), P(AXES, None), P()),
        out_specs=(split, split, split, split),
        check_vma=False,
    )
```

time: 276 us -> 339 us (1.23)
  waiting for transfers between devices: 78.2 us -> 161 us
  blocking collectives: 132 us -> 60 us
  Pallas kernels: 32.6 us -> 63.5 us
  starting transfers between devices: 14.5 us -> 33.2 us
  local copies, waits for them, and re-layouts: 15.1 us -> 19.1 us
    ppermute x0 -> x3, waiting for transfers between devices: none -> 118 us  [the longest x1 54.6 us: on_device(): far_first = lax.ppermute(first, 'half', over)]
    psum x1 -> x0, blocking collectives: 72.5 us -> none  [on_device(): gram = lax.psum(gram, AXES)]
    all_to_all x3 -> x5, waiting for transfers between devices: 78.2 us -> 43 us  [exchange(): lax.all_to_all(blocks, 'rest', split_axis=0, concat_axis=0, tiled=True)]
    pallas_call x1 -> x2, Pallas kernels: 23.1 us -> 46.2 us  [particle_scores(): pl.pallas_call(functools.partial(score_kernel, DATA / count), out_shape=j...]
    all_to_all x3 -> x5, starting transfers between devices: 14.5 us -> 29.8 us  [exchange(): lax.all_to_all(blocks, 'rest', split_axis=0, concat_axis=0, tiled=True)]
    unnamed x12 -> x40, local copies, waits for them, and re-layouts: 4.01 us -> 19.1 us
    pallas_call x2 -> x5, Pallas kernels: 9.5 us -> 17.4 us  [the longest x1 9.47 us: weighted(): pl.pallas_call(mix_kernel, out_shape=jax.ShapeDtypeStruct((half, 2 * ROWS...]
    slice x2 -> x0, local copies, waits for them, and re-layouts: 4.14 us -> none  [from_blocks(): return (a.reshape(1, D, FF), blocks[:, EDGE:].reshape(1, FF, D))]
  transfers between devices with their start and end apart: 3 -> 8, of which waited for: 2 -> 6; matrix products, arithmetic and copies ran while one was open for 3% -> 1% of each run, Pallas kernels for 9% -> 14%
where the time goes in v2:
time: 339 us; the launch traced here: 338 us
  waiting for transfers between devices  161 us (47%)
  Pallas kernels  63.5 us (19%)
  blocking collectives  60 us (18%)
  starting transfers between devices  33.2 us (10%)
  local copies, waits for them, and re-layouts  19.1 us (6%)
    all_to_all x1, blocking collectives, exchange(): lax.all_to_all(blocks, 'rest', split_axis=0, concat_axis=0, tiled=True)  60 us
    ppermute x1, waiting for transfers between devices, on_device(): far_first = lax.ppermute(first, 'half', over)  54.6 us
    ppermute x1, waiting for transfers between devices, on_device(): far_second = lax.ppermute(second, 'half', over)  50.8 us
    pallas_call x2, Pallas kernels, particle_scores(): pl.pallas_call(functools.partial(score_kernel, DATA / count), out_shape=j...  46.2 us
    all_to_all x5, waiting for transfers between devices, exchange(): lax.all_to_all(blocks, 'rest', split_axis=0, concat_axis=0, tiled=True)  43 us
    all_to_all x5, starting transfers between devices, exchange(): lax.all_to_all(blocks, 'rest', split_axis=0, concat_axis=0, tiled=True)  29.8 us
    unnamed x40, local copies, waits for them, and re-layouts  19.1 us
    ppermute x1, waiting for transfers between devices, on_device(): far_picks = lax.ppermute(picks, 'half', over)  12.8 us
  transfers between devices with their start and end apart: 8, of which 6 were waited for; matrix products, arithmetic and copies ran while one was open for 1% of the time, Pallas kernels for 14%

profile of v2, /device:TPU:0, one launch (start us, length us, event | category | flops | bytes accessed | tf_op | source)
XLA Modules:
  0.0 338.4 jit_solution(10659682353127150818)
XLA Ops:
  0.6 0.0 copy-start.13
  0.6 1.3 copy-done.13
  1.9 1.3 copy-done.15
  3.2 0.2 pack.2
  3.4 0.0 copy-start.3
  3.4 1.4 copy-done.3
  4.8 6.3 %all-to-all-start = ((bf16[16,192,384]{2,1,0:T(8,128)(2,1)}), bf16[16,192,384]{2,1,0:T(8,128)(2,1)S(1)}, u32[]{:S(2)}, u32[]{:S(2)}) async-start(bf16[16,192,384]{2,1,0:T(8,128)(2,1)} %copy-done.3), calls=%async_computation | async-start | bytes 4718592 | tf_op jit(solution)/shard_map/all_to_all | solution.py:319
  11.1 0.0 copy-start.18
  11.1 1.5 copy.11.image
  12.7 0.1 copy-done.18
  12.8 0.2 copy.12.target
  13.0 0.9 copy-done.5
  13.8 0.7 copy-done.14
  14.5 0.4 copy-done.16
  14.8 0.0 copy-done.17
  14.9 23.1 %score.2 = bf16[16,192,384]{2,1,0:T(8,128)(2,1)} custom-call(s32[8]{0:T(128)S(1)} %bitcast.12, bf16[8,197,384]{2,1,0:T(8,128)(2,1)S(1)} %copy.11.image, bf16[8,197,384]{2,1,0:T(8,128)(2,1)S(1)} %copy.12.target, bf16[384,1536]{1,0:T(8,128)(2,1)S(1)} %bitcast.11, bf16[1536,384]{1,0:T(8,128)(2,1)S(1)} %bitcast.10), custom_call_target="tpu_custom_call" | custom-call | flops 9814671360 | bytes 7139328 | tf_op jit(solution)/shard_map/score/pallas_call | solution.py:100
  37.9 1.1 copy-done.7
  39.0 5.6 %all-to-all-done.own = bf16[16,192,384]{2,1,0:T(8,128)(2,1)S(1)} async-done(((bf16[16,192,384]{2,1,0:T(8,128)(2,1)}), bf16[16,192,384]{2,1,0:T(8,128)(2,1)S(1)}, u32[]{:S(2)}, u32[]{:S(2)}) %all-to-all-start) | async-done | bytes 2359328 | tf_op jit(solution)/shard_map/all_to_all | solution.py:319
  44.6 4.4 %all-to-all-start.1 = ((bf16[16,192,384]{2,1,0:T(8,128)(2,1)}), bf16[16,192,384]{2,1,0:T(8,128)(2,1)}, u32[]{:S(2)}, u32[]{:S(2)}) async-start(bf16[16,192,384]{2,1,0:T(8,128)(2,1)} %score.2), calls=%async_computation.1 | async-start | bytes 4718592 | tf_op jit(solution)/shard_map/all_to_all | solution.py:319
  49.1 2.7 collective-permute-start.1
  51.7 50.8 %collective-permute-done.1 = bf16[1,1536,384]{2,1,0:T(8,128)(2,1)S(1)} collective-permute-done((bf16[1,1536,384]{2,1,0:T(8,128)(2,1)}, bf16[1,1536,384]{2,1,0:T(8,128)(2,1)S(1)}, u32[]{:S(2)}, u32[]{:S(2)}) %collective-permute-start.1) | collective-permute-done | bytes 1179680 | tf_op jit(solution)/shard_map/ppermute | solution.py:330
  102.5 2.1 all-to-all-done.1.own_scores
  104.6 0.0 copy-done.9
  104.6 8.3 %all-to-all-start.2 = ((bf16[16,96,384]{2,1,0:T(8,128)(2,1)}), bf16[16,96,384]{2,1,0:T(8,128)(2,1)S(1)}, u32[]{:S(2)}, u32[]{:S(2)}) async-start(bf16[16,96,384]{2,1,0:T(8,128)(2,1)} %bitcast.7), calls=%async_computation.2 | async-start | bytes 2359296 | tf_op jit(solution)/shard_map/all_to_all | solution.py:319
  112.9 0.1 collective-permute-start
  113.0 54.6 %collective-permute-done.first = bf16[1,384,1536]{2,1,0:T(8,128)(2,1)S(1)} collective-permute-done((bf16[1,384,1536]{2,1,0:T(8,128)(2,1)}, bf16[1,384,1536]{2,1,0:T(8,128)(2,1)S(1)}, u32[]{:S(2)}, u32[]{:S(2)}) %collective-permute-start) | collective-permute-done | bytes 1179680 | tf_op jit(solution)/shard_map/ppermute | solution.py:329
  167.6 0.1 pack.3
  167.8 0.0 copy-start.4
  167.8 1.0 copy-done.4
  168.8 1.0 copy-done.11
  169.8 0.0 all-to-all-done.2.other_second
  169.8 4.6 %all-to-all-start.3 = ((bf16[16,96,384]{2,1,0:T(8,128)(2,1)}), bf16[16,96,384]{2,1,0:T(8,128)(2,1)}, u32[]{:S(2)}, u32[]{:S(2)}) async-start(bf16[16,96,384]{2,1,0:T(8,128)(2,1)} %copy-done.4), calls=%async_computation.3 | async-start | bytes 2359296 | tf_op jit(solution)/shard_map/all_to_all | solution.py:319
  174.4 0.7 collective-permute-start.2
  175.1 12.8 %collective-permute-done.2 = s32[1,8]{1,0:T(1,128)S(1)} collective-permute-done((s32[1,8]{1,0:T(1,128)S(1)}, s32[1,8]{1,0:T(1,128)S(1)}, u32[]{:S(2)}, u32[]{:S(2)}) %collective-permute-start.2) | collective-permute-done | bytes 64 | tf_op jit(solution)/shard_map/ppermute | solution.py:331
  187.9 1.3 copy-done.6
  189.2 1.3 copy-done.8
  190.4 1.3 copy-done.10
  191.7 1.3 copy-done.12
  193.0 23.1 %score.3.scores = bf16[16,208,384]{2,1,0:T(8,128)(2,1)} custom-call(s32[8]{0:T(128)S(1)} %bitcast.13, bf16[8,197,384]{2,1,0:T(8,128)(2,1)S(1)} %copy-done.6, bf16[8,197,384]{2,1,0:T(8,128)(2,1)S(1)} %copy-done.8, bf16[384,1536]{1,0:T(8,128)(2,1)S(1)} %bitcast.9, bf16[1536,384]{1,0:T(8,128)(2,1)S(1)} %bitcast.8), custom_call_target="tpu_custom_call" | custom-call | flops 9814671360 | bytes 7139328 | tf_op jit(solution)/shard_map/score/pallas_call | solution.py:100
  216.1 0.0 all-to-all-done.3.other_first
  216.1 1.7 copy-done.1
  217.8 5.0 %gram.1 = bf16[16,208,384]{2,1,0:T(8,128)(2,1)S(1)} custom-call(bf16[16,192,384]{2,1,0:T(8,128)(2,1)S(1)} %all-to-all-done.own, bf16[16,96,384]{2,1,0:T(8,128)(2,1)} %all-to-all-done.3.other_first, bf16[16,96,384]{2,1,0:T(8,128)(2,1)S(1)} %all-to-all-done.2.other_second, bf16[16,208,384]{2,1,0:T(8,128)(2,1)S(1)} %copy-done.1), custom_call_target="tpu_custom_call", output_to_operand_aliasing={{}: (3, {})} | custom-call | flops 2415919104 | bytes 4718592 | tf_op jit(solution)/shard_map/gram/pallas_call | solution.py:166
  222.8 1.5 copy-done.2
  224.3 6.2 %all-to-all-start.4 = ((bf16[16,208,384]{2,1,0:T(8,128)(2,1)}), bf16[16,208,384]{2,1,0:T(8,128)(2,1)}, u32[]{:S(2)}, u32[]{:S(2)}) async-start(bf16[16,208,384]{2,1,0:T(8,128)(2,1)} %copy-done.2), calls=%async_computation.4 | async-start | bytes 5111808 | tf_op jit(solution)/shard_map/all_to_all | solution.py:319
  231.2 35.2 %all-to-all-done.4.other_scores = bf16[16,208,384]{2,1,0:T(8,128)(2,1)} async-done(((bf16[16,208,384]{2,1,0:T(8,128)(2,1)}), bf16[16,208,384]{2,1,0:T(8,128)(2,1)}, u32[]{:S(2)}, u32[]{:S(2)}) %all-to-all-start.4) | async-done | bytes 2555936 | tf_op jit(solution)/shard_map/all_to_all | solution.py:319
  266.4 9.5 %mix.1 = bf16[16,384,384]{2,1,0:T(8,128)(2,1)} custom-call(f32[1]{0:T(128)S(6)} %copy.16.scale, bf16[16,208,384]{2,1,0:T(8,128)(2,1)} %all-to-all-done.4.other_scores, bf16[16,192,384]{2,1,0:T(8,128)(2,1)} %all-to-all-done.1.own_scores, bf16[16,192,384]{2,1,0:T(8,128)(2,1)} %copy-done, bf16[16,96,384]{2,1,0:T(8,128)(2,1)} %all-to-all-done.3.other_first, ...), custom_call_target="tpu_custom_call" | custom-call | flops 2415919104 | bytes 14155776 | tf_op jit(solution)/shard_map/mix/pallas_call | solution.py:238
  275.8 60.0 %all_to_all.30.blocks = bf16[16,384,384]{2,1,0:T(8,128)(2,1)S(1)} all-to-all(bf16[16,384,384]{2,1,0:T(8,128)(2,1)} %mix.1), channel_id=1, replica_groups=mesh['wide'=8,'narrow'=4] {'wide':(2)4,'narrow'}, dimensions={0} | all-to-all | bytes 9437184 | tf_op jit(solution)/shard_map/all_to_all | solution.py:319
  335.8 2.6 unpack.1
  (16 shorter events, 0.0 us)
Async XLA Ops:
  0.6 1.3 copy-start.13
  1.9 1.3 copy-start.15
  3.4 1.5 copy-start.3
  4.8 39.8 %all-to-all-start = ((bf16[16,192,384]{2,1,0:T(8,128)(2,1)}), bf16[16,192,384]{2,1,0:T(8,128)(2,1)S(1)}, u32[]{:S(2)}, u32[]{:S(2)}) async-start(bf16[16,192,384]{2,1,0:T(8,128)(2,1)} %copy-done.3), calls=%async_computation | async-start | bytes 4718592 | tf_op jit(solution)/shard_map/all_to_all | solution.py:319
  11.1 1.6 copy-start.18
  12.8 1.1 copy-start.5
  12.8 1.7 copy-start.14
  12.8 2.1 copy-start.16
  12.8 2.1 copy-start.17
  37.9 1.1 copy-start.7
  44.6 171.4 %copy-start = (bf16[16,192,384]{2,1,0:T(8,128)(2,1)}, bf16[16,192,384]{2,1,0:T(8,128)(2,1)S(1)}, u32[]{:S(2)}) copy-start(bf16[16,192,384]{2,1,0:T(8,128)(2,1)S(1)} %all-to-all-done.own) | copy-start | bytes 7077892
  44.6 60.0 %all-to-all-start.1 = ((bf16[16,192,384]{2,1,0:T(8,128)(2,1)}), bf16[16,192,384]{2,1,0:T(8,128)(2,1)}, u32[]{:S(2)}, u32[]{:S(2)}) async-start(bf16[16,192,384]{2,1,0:T(8,128)(2,1)} %score.2), calls=%async_computation.1 | async-start | bytes 4718592 | tf_op jit(solution)/shard_map/all_to_all | solution.py:319
  49.1 53.4 %collective-permute-start.1 = (bf16[1,1536,384]{2,1,0:T(8,128)(2,1)}, bf16[1,1536,384]{2,1,0:T(8,128)(2,1)S(1)}, u32[]{:S(2)}, u32[]{:S(2)}) collective-permute-start(bf16[1,1536,384]{2,1,0:T(8,128)(2,1)} %second.1), channel_id=1, source_target_pairs={{0,16},{16,0},{1,17},{17,1},{2,18},{18,2},{3,19},{19,3},{4,20},{20... | collective-permute-start | bytes 3538952 | tf_op jit(solution)/shard_map/ppermute | solution.py:330
  102.5 2.1 copy-start.9
  104.6 65.2 %all-to-all-start.2 = ((bf16[16,96,384]{2,1,0:T(8,128)(2,1)}), bf16[16,96,384]{2,1,0:T(8,128)(2,1)S(1)}, u32[]{:S(2)}, u32[]{:S(2)}) async-start(bf16[16,96,384]{2,1,0:T(8,128)(2,1)} %bitcast.7), calls=%async_computation.2 | async-start | bytes 2359296 | tf_op jit(solution)/shard_map/all_to_all | solution.py:319
  112.9 54.7 %collective-permute-start = (bf16[1,384,1536]{2,1,0:T(8,128)(2,1)}, bf16[1,384,1536]{2,1,0:T(8,128)(2,1)S(1)}, u32[]{:S(2)}, u32[]{:S(2)}) collective-permute-start(bf16[1,384,1536]{2,1,0:T(8,128)(2,1)} %first.1), channel_id=1, source_target_pairs={{0,16},{16,0},{1,17},{17,1},{2,18},{18,2},{3,19},{19,3},{4,20},{20... | collective-permute-start | bytes 3538952 | tf_op jit(solution)/shard_map/ppermute | solution.py:329
  167.8 1.0 copy-start.4
  168.8 1.0 copy-start.11
  169.8 46.3 %all-to-all-start.3 = ((bf16[16,96,384]{2,1,0:T(8,128)(2,1)}), bf16[16,96,384]{2,1,0:T(8,128)(2,1)}, u32[]{:S(2)}, u32[]{:S(2)}) async-start(bf16[16,96,384]{2,1,0:T(8,128)(2,1)} %copy-done.4), calls=%async_computation.3 | async-start | bytes 2359296 | tf_op jit(solution)/shard_map/all_to_all | solution.py:319
  174.4 13.5 %collective-permute-start.2 = (s32[1,8]{1,0:T(1,128)S(1)}, s32[1,8]{1,0:T(1,128)S(1)}, u32[]{:S(2)}, u32[]{:S(2)}) collective-permute-start(s32[1,8]{1,0:T(1,128)S(1)} %copy-done.17), channel_id=1, source_target_pairs={{0,16},{16,0},{1,17},{17,1},{2,18},{18,2},{3,19},{19,3},{4,20},{20... | collective-permute-start | bytes 104 | tf_op jit(solution)/shard_map/ppermute | solution.py:331
  187.9 1.3 copy-start.6
  189.1 1.3 copy-start.8
  190.4 1.3 copy-start.10
  191.7 1.3 copy-start.12
  216.1 1.7 copy-start.1
  222.8 1.5 copy-start.2
  224.3 42.1 %all-to-all-start.4 = ((bf16[16,208,384]{2,1,0:T(8,128)(2,1)}), bf16[16,208,384]{2,1,0:T(8,128)(2,1)}, u32[]{:S(2)}, u32[]{:S(2)}) async-start(bf16[16,208,384]{2,1,0:T(8,128)(2,1)} %copy-done.2), calls=%async_computation.4 | async-start | bytes 5111808 | tf_op jit(solution)/shard_map/all_to_all | solution.py:319

commit v3 on v1

--- a/solution.py
+++ b/solution.py
@@ -134,7 +134,7 @@
     turned = summed.T
     small = jnp.sum(turned.reshape(members, TILE, members), axis=1)
     packed = jnp.concatenate([small[8 * q : 8 * q + 8] for q in range(members // 8)], axis=1)
-    gram[...] = jnp.broadcast_to(packed[None], gram.shape)
+    gram[...] = packed
 
 
 def pair_products(params):
@@ -142,7 +142,7 @@
     wide = members * TILE
     return pl.pallas_call(
         gram_kernel,
-        out_shape=jax.ShapeDtypeStruct((members, 8, members * members // 8), jnp.float32),
+        out_shape=jax.ShapeDtypeStruct((8, members * members // 8), jnp.float32),
         scratch_shapes=[pltpu.VMEM((wide, wide), jnp.float32)],
         compiler_params=pltpu.CompilerParams(vmem_limit_bytes=32 * 1024 * 1024),
         cost_estimate=pl.CostEstimate(
@@ -180,50 +180,76 @@
     return jnp.where(row == col, full, 0.0)
 
 
-def spread_kernel(scale, partials, params, spread):
+def spread_kernel(scale, partials, params, out, mixing):
     members, rows, _ = params.shape
     wide = members * TILE
     full = spreading(kernel_of(scale, partials))
     ksum = jnp.sum(full, axis=1, keepdims=True)
     mixer = full.astype(jnp.bfloat16)
+    mixing[...] = mixer
     for r in range(rows // TILE):
         here = slice(r * TILE, (r + 1) * TILE)
         own = params[:, here, :].reshape(wide, D)
         mixed = dot(mixer, own, ((1,), (0,)))
         pushed = (ksum * own.astype(jnp.float32) - mixed) * (1.0 / members)
-        spread[:, here, :] = pushed.astype(jnp.bfloat16).reshape(members, TILE, D)
-
-
-def attract_kernel(scale, partials, scores, attract):
-    members, rows, _ = scores.shape
-    wide = members * TILE
-    mixer = spreading(kernel_of(scale, partials)).astype(jnp.bfloat16)
-    for r in range(rows // TILE):
-        here = slice(r * TILE, (r + 1) * TILE)
-        got = scores[:, here, :].reshape(wide, D)
-        pulled = dot(mixer, got, ((1,), (0,))) * (1.0 / members)
-        attract[:, here, :] = pulled.astype(jnp.bfloat16).reshape(members, TILE, D)
-
-
-def weighted(body, name, scale, partials, held):
-    members, rows, _ = held.shape
-    wide = members * TILE
-    return pl.pallas_call(
-        body,
-        out_shape=jax.ShapeDtypeStruct(held.shape, jnp.bfloat16),
-        in_specs=[
-            pl.BlockSpec(memory_space=pltpu.SMEM),
-            pl.BlockSpec(memory_space=pltpu.VMEM),
-            pl.BlockSpec(memory_space=pltpu.VMEM),
-        ],
+        out[:, here, :] = pushed.astype(jnp.bfloat16).reshape(members, TILE, D)
+
+
+def spread_part(scale, partials, params):
+    members, rows, _ = params.shape
+    wide = members * TILE
+    vmem = pl.BlockSpec(memory_space=pltpu.VMEM)
+    return pl.pallas_call(
+        spread_kernel,
+        out_shape=(
+            jax.ShapeDtypeStruct((members, 2 * rows, D), jnp.bfloat16),
+            jax.ShapeDtypeStruct((wide, wide), jnp.bfloat16),
+        ),
+        grid=(1,),
+        in_specs=[pl.BlockSpec(memory_space=pltpu.SMEM), vmem, vmem],
+        out_specs=(
+            pl.BlockSpec((members, rows, D), lambda i: (0, 1, 0)),
+            pl.BlockSpec((wide, wide), lambda i: (0, 0)),
+        ),
         compiler_params=pltpu.CompilerParams(vmem_limit_bytes=32 * 1024 * 1024),
         cost_estimate=pl.CostEstimate(
             flops=2 * wide * wide * rows // TILE * D,
             bytes_accessed=4 * members * rows * D,
             transcendentals=0,
         ),
-        name=name,
-    )(scale, partials, held)
+        name="spread",
+    )(scale, partials, params)
+
+
+def attract_kernel(mixing, scores, half_done, out):
+    members, rows, _ = scores.shape
+    wide = members * TILE
+    for r in range(rows // TILE):
+        here = slice(r * TILE, (r + 1) * TILE)
+        got = scores[:, here, :].reshape(wide, D)
+        pulled = dot(mixing[...], got, ((1,), (0,))) * (1.0 / members)
+        out[:, here, :] = pulled.astype(jnp.bfloat16).reshape(members, TILE, D)
+
+
+def attract_part(mixing, scores, half_done):
+    members, rows, _ = scores.shape
+    wide = members * TILE
+    vmem = pl.BlockSpec(memory_space=pltpu.VMEM)
+    return pl.pallas_call(
+        attract_kernel,
+        out_shape=jax.ShapeDtypeStruct(half_done.shape, half_done.dtype),
+        grid=(1,),
+        in_specs=[vmem, vmem, pl.BlockSpec(memory_space=pl.ANY)],
+        out_specs=pl.BlockSpec((members, rows, D), lambda i: (0, 0, 0)),
+        input_output_aliases={2: 0},
+        compiler_params=pltpu.CompilerParams(vmem_limit_bytes=32 * 1024 * 1024),
+        cost_estimate=pl.CostEstimate(
+            flops=2 * wide * wide * rows // TILE * D,
+            bytes_accessed=4 * members * rows * D,
+            transcendentals=0,
+        ),
+        name="attract",
+    )(mixing, scores, half_done)
 
 
 def plain_products(params):
@@ -245,40 +271,48 @@
 
 
 def pack_kernel(first, second, out):
-    for r in range(D // EDGE):
-        for c in range(COLS):
-            b = r * COLS + c
-            out[b, 0:EDGE, :] = first[0, r * EDGE : (r + 1) * EDGE, c * D : (c + 1) * D]
-            out[b, EDGE : 2 * EDGE, :] = second[0, b * EDGE : (b + 1) * EDGE, :]
+    for b in range(out.shape[0]):
+        r, c = b // COLS * EDGE, b % COLS * D
+        out[b, 0:EDGE, :] = first[0, r : r + EDGE, c : c + D]
+        out[b, EDGE : 2 * EDGE, :] = second[0, b * EDGE : (b + 1) * EDGE, :]
 
 
 def to_blocks(first, second):
+    steps = 4
     return pl.pallas_call(
         pack_kernel,
         out_shape=jax.ShapeDtypeStruct((BLOCKS, 2 * EDGE, D), jnp.bfloat16),
-        compiler_params=pltpu.CompilerParams(vmem_limit_bytes=16 * 1024 * 1024),
+        grid=(steps,),
+        in_specs=[
+            pl.BlockSpec((1, D // steps, FF), lambda i: (0, i, 0)),
+            pl.BlockSpec((1, FF // steps, D), lambda i: (0, i, 0)),
+        ],
+        out_specs=pl.BlockSpec((BLOCKS // steps, 2 * EDGE, D), lambda i: (i, 0, 0)),
+        compiler_params=pltpu.CompilerParams(vmem_limit_bytes=56 * 1024 * 1024),
         cost_estimate=pl.CostEstimate(flops=0, bytes_accessed=8 * D * FF, transcendentals=0),
         name="pack",
     )(first, second)
 
 
-def unpack_kernel(blocks, first, second):
-    for r in range(D // EDGE):
-        for c in range(COLS):
-            b = r * COLS + c
-            first[0, r * EDGE : (r + 1) * EDGE, c * D : (c + 1) * D] = blocks[b, 0:EDGE, :]
-            second[0, b * EDGE : (b + 1) * EDGE, :] = blocks[b, EDGE : 2 * EDGE, :]
+def unpack_kernel(blocks, first_a, second_a, first_s, second_s):
+    for b in range(BLOCKS):
+        r, c = b // COLS * EDGE, b % COLS * D
+        first_a[0, r : r + EDGE, c : c + D] = blocks[b, 0:EDGE, :]
+        second_a[0, b * EDGE : (b + 1) * EDGE, :] = blocks[b, EDGE : 2 * EDGE, :]
+        first_s[0, r : r + EDGE, c : c + D] = blocks[b, 2 * EDGE : 3 * EDGE, :]
+        second_s[0, b * EDGE : (b + 1) * EDGE, :] = blocks[b, 3 * EDGE : 4 * EDGE, :]
 
 
 def from_blocks(blocks):
+    shapes = (
+        jax.ShapeDtypeStruct((1, D, FF), jnp.bfloat16),
+        jax.ShapeDtypeStruct((1, FF, D), jnp.bfloat16),
+    )
     return pl.pallas_call(
         unpack_kernel,
-        out_shape=(
-            jax.ShapeDtypeStruct((1, D, FF), jnp.bfloat16),
-            jax.ShapeDtypeStruct((1, FF, D), jnp.bfloat16),
-        ),
-        compiler_params=pltpu.CompilerParams(vmem_limit_bytes=16 * 1024 * 1024),
-        cost_estimate=pl.CostEstimate(flops=0, bytes_accessed=8 * D * FF, transcendentals=0),
+        out_shape=shapes + shapes,
+        compiler_params=pltpu.CompilerParams(vmem_limit_bytes=24 * 1024 * 1024),
+        cost_estimate=pl.CostEstimate(flops=0, bytes_accessed=16 * D * FF, transcendentals=0),
         name="unpack",
     )(blocks)
 
@@ -297,19 +331,18 @@
     scores = particle_scores(
         particles_first[0], particles_second[0], pool_images, pool_targets, batch_index[0]
     )
-    params, scores = lax.optimization_barrier((params, scores))
-    scores = exchange(scores.reshape(cut))
-    if cut[1] % TILE == 0:
-        partials = exchange(pair_products(params))
-        spread = weighted(spread_kernel, "spread", kernel_scale, partials, params)
-        spread, scores = lax.optimization_barrier((spread, scores))
-        attract = weighted(attract_kernel, "attract", kernel_scale, partials, scores)
+    if members == BLOCKS:
+        partials = lax.all_gather(pair_products(params), AXES)
+        params, scores = lax.optimization_barrier((params, scores))
+        scores = exchange(scores)
+        spread, mixing = spread_part(kernel_scale, partials, params)
+        mixed = exchange(attract_part(mixing, scores, spread))
     else:
+        scores = exchange(scores.reshape(cut))
         gram = lax.psum(plain_products(params), AXES)
-        attract, spread = plain_weighted(gram, kernel_scale, params, scores)
-    spread = from_blocks(exchange(spread).reshape(whole))
-    attract = from_blocks(exchange(attract).reshape(whole))
-    return (*attract, *spread)
+        parts = plain_weighted(gram, kernel_scale, params, scores)
+        mixed = jnp.concatenate([exchange(x).reshape(whole) for x in parts], axis=1)
+    return from_blocks(mixed)
 
 
 def solution(mesh):

time: 262 us -> 272 us (1.038)
  blocking collectives: 72.1 us -> 184 us
  waiting for transfers between devices: 129 us -> 28 us
    all_to_all x3 -> x2, waiting for transfers between devices: 129 us -> 28 us  [exchange(): return lax.all_to_all(blocks, AXES, split_axis=0, concat_axis=0, tiled=True)]
    all_gather x0 -> x1, blocking collectives: none -> 69.8 us  [on_device(): partials = lax.all_gather(pair_products(params), AXES)]
    all_to_all x2 -> x1, blocking collectives: 72.1 us -> 114 us  [exchange(): return lax.all_to_all(blocks, AXES, split_axis=0, concat_axis=0, tiled=True)]
    pallas_call x1, Pallas kernels: 0.2 us -> 3.88 us  [to_blocks(): pl.pallas_call(pack_kernel, out_shape=jax.ShapeDtypeStruct((BLOCKS, 2 * E...]
    pallas_call x5 -> x4, Pallas kernels: 12.9 us -> 9.43 us  [the longest x1 2.62 us: spread_part(): pl.pallas_call(spread_kernel, out_shape=(jax.ShapeDtypeStruct((members, 2...]
    all_to_all x3 -> x2, starting transfers between devices: 13.8 us -> 11.6 us  [exchange(): return lax.all_to_all(blocks, AXES, split_axis=0, concat_axis=0, tiled=True)]
  transfers between devices with their start and end apart: 3 -> 2, of which waited for: 3 -> 1; matrix products, arithmetic and copies ran while one was open for 1% -> 1% of each run, Pallas kernels for 11% -> 10%
where the time goes in v3:
time: 272 us
  blocking collectives  184 us (68%)
  Pallas kernels  36.4 us (13%)
  waiting for transfers between devices  28 us (10%)
  starting transfers between devices  11.6 us (4%)
  local copies, waits for them, and re-layouts  10.8 us (4%)
    all_to_all x1, blocking collectives, exchange(): return lax.all_to_all(blocks, AXES, split_axis=0, concat_axis=0, tiled=True)  114 us
    all_gather x1, blocking collectives, on_device(): partials = lax.all_gather(pair_products(params), AXES)  69.8 us
    all_to_all x2, waiting for transfers between devices, exchange(): return lax.all_to_all(blocks, AXES, split_axis=0, concat_axis=0, tiled=True)  28 us
    pallas_call x1, Pallas kernels, particle_scores(): pl.pallas_call(functools.partial(score_kernel, DATA / count), out_shape=j...  23.1 us
    all_to_all x2, starting transfers between devices, exchange(): return lax.all_to_all(blocks, AXES, split_axis=0, concat_axis=0, tiled=True)  11.6 us
    unnamed x18, local copies, waits for them, and re-layouts  10.8 us
  transfers between devices with their start and end apart: 2, of which 1 were waited for; matrix products, arithmetic and copies ran while one was open for 1% of the time, Pallas kernels for 10%

profile of v3, /device:TPU:0, one launch (start us, length us, event | category | flops | bytes accessed | tf_op | source)
XLA Modules:
  0.0 271.8 jit_solution(15781466226409236104)
XLA Ops:
  0.6 3.9 %pack.1 = bf16[32,96,384]{2,1,0:T(8,128)(2,1)} custom-call(bf16[1,384,1536]{2,1,0:T(8,128)(2,1)} %first.1, bf16[1,1536,384]{2,1,0:T(8,128)(2,1)} %second.1), custom_call_target="tpu_custom_call" | custom-call | bytes 4718592 | tf_op jit(solution)/shard_map/pack/pallas_call | solution.py:282
  4.5 7.3 %all-to-all-start = ((bf16[32,96,384]{2,1,0:T(8,128)(2,1)}), bf16[32,96,384]{2,1,0:T(8,128)(2,1)S(1)}, u32[]{:S(2)}, u32[]{:S(2)}) async-start(bf16[32,96,384]{2,1,0:T(8,128)(2,1)} %pack.1), calls=%async_computation | async-start | bytes 4718592 | tf_op jit(solution)/shard_map/all_to_all | solution.py:321
  11.8 0.0 copy-start.7
  11.8 1.5 copy.11.image
  13.4 0.1 copy-done.7
  13.5 0.0 copy-start.4
  13.5 0.0 copy-start.5
  13.5 0.0 copy-start.6
  13.5 0.2 copy.12.target
  13.6 1.1 copy-done.4
  14.7 0.4 copy-done.5
  15.1 0.0 copy-done.6
  15.1 23.1 %score.1 = bf16[32,96,384]{2,1,0:T(8,128)(2,1)} custom-call(s32[8]{0:T(128)S(1)} %bitcast.7, bf16[8,197,384]{2,1,0:T(8,128)(2,1)S(1)} %copy.11.image, bf16[8,197,384]{2,1,0:T(8,128)(2,1)S(1)} %copy.12.target, bf16[384,1536]{1,0:T(8,128)(2,1)S(1)} %bitcast.4, bf16[1536,384]{1,0:T(8,128)(2,1)S(1)} %bitcast.5), custom_call_target="tpu_custom_call" | custom-call | flops 9814671360 | bytes 7139328 | tf_op jit(solution)/shard_map/score/pallas_call | solution.py:90
  38.2 28.0 %all-to-all-done.params = bf16[32,96,384]{2,1,0:T(8,128)(2,1)S(1)} async-done(((bf16[32,96,384]{2,1,0:T(8,128)(2,1)}), bf16[32,96,384]{2,1,0:T(8,128)(2,1)S(1)}, u32[]{:S(2)}, u32[]{:S(2)}) %all-to-all-start) | async-done | bytes 2359328 | tf_op jit(solution)/shard_map/all_to_all | solution.py:321
  66.2 0.0 copy-start.2
  66.2 1.4 copy-done.2
  67.7 4.3 %all-to-all-start.1 = ((bf16[32,96,384]{2,1,0:T(8,128)(2,1)}), bf16[32,96,384]{2,1,0:T(8,128)(2,1)S(1)}, u32[]{:S(2)}, u32[]{:S(2)}) async-start(bf16[32,96,384]{2,1,0:T(8,128)(2,1)} %score.1), calls=%async_computation.1 | async-start | bytes 4718592 | tf_op jit(solution)/shard_map/all_to_all | solution.py:321
  72.6 0.0 copy-start.3
  72.6 1.7 copy-done.3
  74.3 2.1 gram.1
  76.3 69.8 %all-gather = f32[256,128]{1,0:T(8,128)S(1)} all-gather(f32[8,128]{1,0:T(8,128)S(1)} %gram.1), channel_id=2, replica_groups=mesh['wide'=8,'narrow'=4] {'wide','narrow'}, dimensions={0}, use_global_device_ids=true | all-gather | bytes 135168 | tf_op jit(solution)/shard_map/all_gather | solution.py:335
  146.2 2.6 spread.1
  148.8 0.0 copy-start
  148.8 2.1 copy-done
  150.9 0.0 all-to-all-done.1.scores
  150.9 0.0 copy-start.1
  150.9 2.3 copy-done.1
  153.3 2.1 attract.1
  155.4 113.8 %all_to_all.15.blocks = bf16[32,192,384]{2,1,0:T(8,128)(2,1)S(1)} all-to-all(bf16[32,192,384]{2,1,0:T(8,128)(2,1)S(1)} %attract.1), channel_id=1, replica_groups=mesh['wide'=8,'narrow'=4] {'wide','narrow'}, dimensions={0} | all-to-all | bytes 9437184 | tf_op jit(solution)/shard_map/all_to_all | solution.py:321
  269.2 2.6 unpack.1
Async XLA Ops:
  4.5 61.7 %all-to-all-start = ((bf16[32,96,384]{2,1,0:T(8,128)(2,1)}), bf16[32,96,384]{2,1,0:T(8,128)(2,1)S(1)}, u32[]{:S(2)}, u32[]{:S(2)}) async-start(bf16[32,96,384]{2,1,0:T(8,128)(2,1)} %pack.1), calls=%async_computation | async-start | bytes 4718592 | tf_op jit(solution)/shard_map/all_to_all | solution.py:321
  11.8 1.6 copy-start.7
  13.5 1.3 copy-start.4
  13.5 1.6 copy-start.5
  13.5 1.6 copy-start.6
  66.2 1.4 copy-start.2
  67.7 83.3 %all-to-all-start.1 = ((bf16[32,96,384]{2,1,0:T(8,128)(2,1)}), bf16[32,96,384]{2,1,0:T(8,128)(2,1)S(1)}, u32[]{:S(2)}, u32[]{:S(2)}) async-start(bf16[32,96,384]{2,1,0:T(8,128)(2,1)} %score.1), calls=%async_computation.1 | async-start | bytes 4718592 | tf_op jit(solution)/shard_map/all_to_all | solution.py:321
  72.6 1.7 copy-start.3
  148.8 2.1 copy-start
  150.9 2.3 copy-start.1

commit v4 on v0

--- a/solution.py
+++ b/solution.py
@@ -18,6 +18,8 @@
 BLOCKS = D * FF // (EDGE * D)
 COLS = FF // D
 TILE = 16
+ROWS = 2 * EDGE
+EXTRA = 8
 
 gelu_c = math.sqrt(2.0 / math.pi)
 isd = 1.0 / math.sqrt(D)
@@ -83,13 +85,13 @@
                 ]
 
 
-def particle_scores(first, second, images, targets, picks):
+def particle_scores(first, second, images, targets, picks, extra):
     count = picks.shape[0]
     rows = count * PAD
     bf = jnp.bfloat16
     return pl.pallas_call(
         functools.partial(score_kernel, DATA / count),
-        out_shape=jax.ShapeDtypeStruct((BLOCKS, 2 * EDGE, D), bf),
+        out_shape=jax.ShapeDtypeStruct((BLOCKS, ROWS + extra, D), bf),
         grid_spec=pltpu.PrefetchScalarGridSpec(
             num_scalar_prefetch=1,
             grid=(count,),
@@ -99,7 +101,7 @@
                 pl.BlockSpec((D, FF), lambda b, picks: (0, 0)),
                 pl.BlockSpec((FF, D), lambda b, picks: (0, 0)),
             ],
-            out_specs=pl.BlockSpec((BLOCKS, 2 * EDGE, D), lambda b, picks: (0, 0, 0)),
+            out_specs=pl.BlockSpec((BLOCKS, ROWS, D), lambda b, picks: (0, 0, 0)),
             scratch_shapes=[
                 pltpu.VMEM((PAD, D), jnp.float32),
                 pltpu.VMEM((PAD, D), jnp.float32),
@@ -120,7 +122,7 @@
     )(picks, images, targets, first, second)
 
 
-def gram_kernel(params, gram, total):
+def gram_kernel(params, scores, out, total, parts, sem):
     members, rows, _ = params.shape
     wide = members * TILE
     total[...] = jnp.zeros_like(total)
@@ -132,16 +134,32 @@
     kept = jnp.where(at == to, total[...], 0.0)
     summed = jnp.sum(kept.reshape(members, TILE, wide), axis=1)
     turned = summed.T
-    gram[...] = jnp.sum(turned.reshape(members, TILE, members), axis=1)
-
-
-def pair_products(params):
+    small = jnp.sum(turned.reshape(members, TILE, members), axis=1)
+    packed = jnp.concatenate([small[8 * q : 8 * q + 8] for q in range(members // 8)], axis=1)
+    high = packed.astype(jnp.bfloat16).astype(jnp.float32)
+    middle = (packed - high).astype(jnp.bfloat16).astype(jnp.float32)
+    low = packed - high - middle
+    three = jnp.concatenate([high, middle, low], axis=1).astype(jnp.bfloat16)
+    parts[...] = jnp.broadcast_to(three[None], parts.shape)
+    copy = pltpu.make_async_copy(parts, out.at[:, pl.ds(rows, EXTRA), :], sem)
+    copy.start()
+    copy.wait()
+
+
+def add_products(params, scores):
     members, rows, _ = params.shape
     wide = members * TILE
     return pl.pallas_call(
         gram_kernel,
-        out_shape=jax.ShapeDtypeStruct((members, members), jnp.float32),
-        scratch_shapes=[pltpu.VMEM((wide, wide), jnp.float32)],
+        out_shape=jax.ShapeDtypeStruct(scores.shape, scores.dtype),
+        in_specs=[pl.BlockSpec(memory_space=pltpu.VMEM), pl.BlockSpec(memory_space=pl.ANY)],
+        out_specs=pl.BlockSpec(memory_space=pl.ANY),
+        input_output_aliases={1: 0},
+        scratch_shapes=[
+            pltpu.VMEM((wide, wide), jnp.float32),
+            pltpu.VMEM((members, EXTRA, D), jnp.bfloat16),
+            pltpu.SemaphoreType.DMA,
+        ],
         compiler_params=pltpu.CompilerParams(vmem_limit_bytes=32 * 1024 * 1024),
         cost_estimate=pl.CostEstimate(
             flops=2 * wide * wide * rows // TILE * D,
@@ -149,7 +167,22 @@
             transcendentals=0,
         ),
         name="gram",
-    )(params)
+    )(params, scores)
+
+
+def kernel_of(scale, parts):
+    members = parts.shape[0]
+    lanes = members * members // 8
+    three = jnp.sum(parts[...].astype(jnp.float32), axis=0)
+    packed = three[:, :lanes] + three[:, lanes : 2 * lanes] + three[:, 2 * lanes : 3 * lanes]
+    gram = jnp.concatenate(
+        [packed[:, members * q : members * (q + 1)] for q in range(members // 8)], axis=0
+    )
+    row = lax.broadcasted_iota(jnp.int32, gram.shape, 0)
+    col = lax.broadcasted_iota(jnp.int32, gram.shape, 1)
+    own = jnp.where(row == col, gram, 0.0)
+    dist = jnp.sum(own, axis=1, keepdims=True) + jnp.sum(own, axis=0, keepdims=True) - 2.0 * gram
+    return jnp.exp(-dist / scale[0]).astype(jnp.bfloat16)
 
 
 def spreading(kernel):
@@ -165,38 +198,51 @@
     return jnp.where(row == col, full, 0.0)
 
 
-def mix_kernel(kernel, params, scores, attract, spread):
+def mix_kernel(scale, parts, scores, params, out, mixing, ksum):
+    members = params.shape[0]
+    wide = members * TILE
+
+    @pl.when(pl.program_id(0) == 0)
+    def _():
+        full = spreading(kernel_of(scale, parts))
+        ksum[...] = jnp.sum(full, axis=1, keepdims=True)
+        mixing[...] = full.astype(jnp.bfloat16)
+
+    got = scores[...].reshape(wide, D)
+    pulled = dot(mixing[...], got, ((1,), (0,))) * (1.0 / members)
+    out[:, 0] = pulled.astype(jnp.bfloat16).reshape(members, TILE, D)
+    own = params[...].reshape(wide, D)
+    mixed = dot(mixing[...], own, ((1,), (0,)))
+    pushed = (ksum[...] * own.astype(jnp.float32) - mixed) * (1.0 / members)
+    out[:, 1] = pushed.astype(jnp.bfloat16).reshape(members, TILE, D)
+
+
+def weighted(scale, scores, params):
     members, rows, _ = params.shape
     wide = members * TILE
-    full = spreading(kernel[...])
-    ksum = jnp.sum(full, axis=1, keepdims=True)
-    mixer = full.astype(jnp.bfloat16)
-    for r in range(rows // TILE):
-        here = slice(r * TILE, (r + 1) * TILE)
-        got = scores[:, here, :].reshape(wide, D)
-        pulled = dot(mixer, got, ((1,), (0,))) * (1.0 / members)
-        attract[:, here, :] = pulled.astype(jnp.bfloat16).reshape(members, TILE, D)
-        own = params[:, here, :].reshape(wide, D)
-        mixed = dot(mixer, own, ((1,), (0,)))
-        pushed = (ksum * own.astype(jnp.float32) - mixed) * (1.0 / members)
-        spread[:, here, :] = pushed.astype(jnp.bfloat16).reshape(members, TILE, D)
-
-
-def weighted(kernel, params, scores):
-    members, rows, _ = params.shape
-    wide = members * TILE
-    shape = jax.ShapeDtypeStruct(params.shape, jnp.bfloat16)
     return pl.pallas_call(
         mix_kernel,
-        out_shape=(shape, shape),
-        compiler_params=pltpu.CompilerParams(vmem_limit_bytes=48 * 1024 * 1024),
+        out_shape=jax.ShapeDtypeStruct((members, 2, rows, D), jnp.bfloat16),
+        grid=(rows // TILE,),
+        in_specs=[
+            pl.BlockSpec(memory_space=pltpu.SMEM),
+            pl.BlockSpec((members, EXTRA, D), lambda r: (0, rows // EXTRA, 0)),
+            pl.BlockSpec((members, TILE, D), lambda r: (0, r, 0)),
+            pl.BlockSpec((members, TILE, D), lambda r: (0, r, 0)),
+        ],
+        out_specs=pl.BlockSpec((members, 2, TILE, D), lambda r: (0, 0, r, 0)),
+        scratch_shapes=[
+            pltpu.VMEM((wide, wide), jnp.bfloat16),
+            pltpu.VMEM((wide, 1), jnp.float32),
+        ],
+        compiler_params=pltpu.CompilerParams(vmem_limit_bytes=32 * 1024 * 1024),
         cost_estimate=pl.CostEstimate(
             flops=4 * wide * wide * rows // TILE * D,
             bytes_accessed=8 * members * rows * D,
             transcendentals=0,
         ),
         name="mix",
-    )(kernel, params, scores)
+    )(scale, scores, scores, params)
 
 
 def plain_products(params):
@@ -204,8 +250,11 @@
     return dot(flat, flat, ((1,), (1,)))
 
 
-def plain_weighted(kernel, params, scores):
+def plain_weighted(gram, scale, params, scores):
     members = params.shape[0]
+    norms = jnp.diagonal(gram)
+    dist = norms[:, None] + norms[None, :] - 2.0 * gram
+    kernel = jnp.exp(-dist / scale[0]).astype(jnp.bfloat16)
     flat = params.reshape(members, -1)
     ksum = jnp.sum(kernel.astype(jnp.float32), axis=1, keepdims=True)
     attract = dot(kernel, scores.reshape(members, -1), ((1,), (0,))) / members
@@ -214,14 +263,66 @@
     return tuple(x.astype(jnp.bfloat16).reshape(params.shape) for x in (attract, spread))
 
 
+def run(copies):
+    for copy in copies:
+        copy.start()
+    for copy in copies:
+        copy.wait()
+
+
+def pack_kernel(first, second, out, sems):
+    copies = [pltpu.make_async_copy(second, out.at[:, :, pl.ds(EDGE, EDGE), :], sems.at[COLS])]
+    for c in range(COLS):
+        here = first.at[:, :, pl.ds(c * D, D)]
+        copies.append(pltpu.make_async_copy(here, out.at[:, c, pl.ds(0, EDGE), :], sems.at[c]))
+    run(copies)
+
+
 def to_blocks(first, second):
-    a = first.reshape(D // EDGE, EDGE, COLS, D).transpose(0, 2, 1, 3).reshape(BLOCKS, EDGE, D)
-    return jnp.concatenate([a, second.reshape(BLOCKS, EDGE, D)], axis=1)
+    any_space = pl.BlockSpec(memory_space=pl.ANY)
+    deep = BLOCKS // COLS
+    packed = pl.pallas_call(
+        pack_kernel,
+        out_shape=jax.ShapeDtypeStruct((deep, COLS, ROWS, D), jnp.bfloat16),
+        in_specs=[any_space, any_space],
+        out_specs=any_space,
+        scratch_shapes=[pltpu.SemaphoreType.DMA((COLS + 1,))],
+        cost_estimate=pl.CostEstimate(flops=0, bytes_accessed=8 * D * FF, transcendentals=0),
+        name="pack",
+    )(first.reshape(deep, EDGE, FF), second.reshape(deep, COLS, EDGE, D))
+    return packed.reshape(BLOCKS, ROWS, D)
+
+
+def unpack_kernel(blocks, first_a, second_a, first_s, second_s, sems):
+    copies = []
+    for which, (first, second) in enumerate(((first_a, second_a), (first_s, second_s))):
+        at = which * ROWS
+        here = blocks.at[:, :, pl.ds(at + EDGE, EDGE), :]
+        copies.append(pltpu.make_async_copy(here, second, sems.at[which, COLS]))
+        for c in range(COLS):
+            here = blocks.at[:, c, pl.ds(at, EDGE), :]
+            there = first.at[:, :, pl.ds(c * D, D)]
+            copies.append(pltpu.make_async_copy(here, there, sems.at[which, c]))
+    run(copies)
 
 
 def from_blocks(blocks):
-    a = blocks[:, :EDGE].reshape(D // EDGE, COLS, EDGE, D).transpose(0, 2, 1, 3)
-    return a.reshape(1, D, FF), blocks[:, EDGE:].reshape(1, FF, D)
+    any_space = pl.BlockSpec(memory_space=pl.ANY)
+    deep = BLOCKS // COLS
+    shapes = (
+        jax.ShapeDtypeStruct((deep, EDGE, FF), jnp.bfloat16),
+        jax.ShapeDtypeStruct((deep, COLS, EDGE, D), jnp.bfloat16),
+    )
+    outs = pl.pallas_call(
+        unpack_kernel,
+        out_shape=shapes + shapes,
+        in_specs=[any_space],
+        out_specs=(any_space,) * 4,
+        scratch_shapes=[pltpu.SemaphoreType.DMA((2, COLS + 1))],
+        cost_estimate=pl.CostEstimate(flops=0, bytes_accessed=16 * D * FF, transcendentals=0),
+        name="unpack",
+    )(blocks.reshape(deep, COLS, 2 * ROWS, D))
+    return tuple(x.reshape(s) for x, s in zip(outs, ((1, D, FF), (1, FF, D)) * 2))
 
 
 def exchange(blocks):
@@ -232,23 +333,27 @@
     particles_first, particles_second, pool_images, pool_targets, batch_index, kernel_scale
 ):
     members = lax.axis_size("wide") * lax.axis_size("narrow")
-    cut = (members, BLOCKS * 2 * EDGE // members, D)
-    first = particles_first[0]
-    second = particles_second[0]
-    params = exchange(to_blocks(first, second).reshape(cut))
-    scores = particle_scores(first, second, pool_images, pool_targets, batch_index[0])
-    scores = exchange(scores.reshape(cut))
-    tiled = cut[1] % TILE == 0
-    gram = pair_products(params) if tiled else plain_products(params)
-    gram = lax.psum(gram, AXES)
-    norms = jnp.diagonal(gram)
-    dist = norms[:, None] + norms[None, :] - 2.0 * gram
-    kernel = jnp.exp(-dist / kernel_scale[0]).astype(jnp.bfloat16)
-    attract, spread = (weighted if tiled else plain_weighted)(kernel, params, scores)
-    whole = (BLOCKS, 2 * EDGE, D)
-    attract = from_blocks(exchange(attract).reshape(whole))
-    spread = from_blocks(exchange(spread).reshape(whole))
-    return (*attract, *spread)
+    cut = (members, BLOCKS * ROWS // members, D)
+    tiled = members == BLOCKS
+    params = exchange(to_blocks(particles_first, particles_second).reshape(cut))
+    scores = particle_scores(
+        particles_first[0],
+        particles_second[0],
+        pool_images,
+        pool_targets,
+        batch_index[0],
+        EXTRA if tiled else 0,
+    )
+    if tiled:
+        scores = exchange(add_products(params, scores))
+        mixed = exchange(weighted(kernel_scale, scores, params).reshape(members, 2 * ROWS, D))
+    else:
+        scores = exchange(scores.reshape(cut))
+        gram = lax.psum(plain_products(params), AXES)
+        parts = plain_weighted(gram, kernel_scale, params, scores)
+        mixed = [exchange(x).reshape(BLOCKS, ROWS, D) for x in parts]
+        mixed = jnp.concatenate(mixed, axis=1)
+    return from_blocks(mixed)
 
 
 def solution(mesh):

time: 276 us -> 465 us (1.68)
  Pallas kernels: 32.6 us -> 248 us
  blocking collectives: 132 us -> 110 us
  waiting for transfers between devices: 78.2 us -> 86.1 us
  local copies, waits for them, and re-layouts: 15.1 us -> 8.14 us
    pallas_call x2 -> x4, Pallas kernels: 9.5 us -> 225 us  [the longest x1 144 us: from_blocks(): pl.pallas_call(unpack_kernel, out_shape=shapes + shapes, in_specs=[any_sp...]
    psum x1 -> x0, blocking collectives: 72.5 us -> none  [on_device(): gram = lax.psum(gram, AXES)]
    all_to_all x1, blocking collectives: 59.4 us -> 110 us  [exchange(): return lax.all_to_all(blocks, AXES, split_axis=0, concat_axis=0, tiled=True)]
    all_to_all x3 -> x2, waiting for transfers between devices: 78.2 us -> 86.1 us  [exchange(): return lax.all_to_all(blocks, AXES, split_axis=0, concat_axis=0, tiled=True)]
    all_to_all x3 -> x2, starting transfers between devices: 14.5 us -> 11.6 us  [exchange(): return lax.all_to_all(blocks, AXES, split_axis=0, concat_axis=0, tiled=True)]
  transfers between devices with their start and end apart: 3 -> 2, of which waited for: 2 -> 2; matrix products, arithmetic and copies ran while one was open for 3% -> 0% of each run, Pallas kernels for 9% -> 5%
where the time goes in v4:
time: 465 us
  Pallas kernels  248 us (53%)
  blocking collectives  110 us (24%)
  waiting for transfers between devices  86.1 us (19%)
  starting transfers between devices  11.6 us (2%)
  local copies, waits for them, and re-layouts  8.14 us (2%)
    pallas_call x1, Pallas kernels, from_blocks(): pl.pallas_call(unpack_kernel, out_shape=shapes + shapes, in_specs=[any_sp...  144 us
    all_to_all x1, blocking collectives, exchange(): return lax.all_to_all(blocks, AXES, split_axis=0, concat_axis=0, tiled=True)  110 us
    all_to_all x2, waiting for transfers between devices, exchange(): return lax.all_to_all(blocks, AXES, split_axis=0, concat_axis=0, tiled=True)  86.1 us
    pallas_call x1, Pallas kernels, to_blocks(): pl.pallas_call(pack_kernel, out_shape=jax.ShapeDtypeStruct((deep, COLS, R...  72.6 us
    pallas_call x1, Pallas kernels, particle_scores(): pl.pallas_call(functools.partial(score_kernel, DATA / count), out_shape=j...  23.1 us
    all_to_all x2, starting transfers between devices, exchange(): return lax.all_to_all(blocks, AXES, split_axis=0, concat_axis=0, tiled=True)  11.6 us
  transfers between devices with their start and end apart: 2, of which 2 were waited for; matrix products, arithmetic and copies ran while one was open for 0% of the time, Pallas kernels for 5%

profile of v4, /device:TPU:0, one launch (start us, length us, event | category | flops | bytes accessed | tf_op | source)
XLA Modules:
  0.0 465.0 jit_solution(11062013981758417398)
XLA Ops:
  0.6 72.6 %pack.1 = bf16[8,4,96,384]{3,2,1,0:T(8,128)(2,1)} custom-call(bf16[8,48,1536]{2,1,0:T(8,128)(2,1)} %bitcast.13, bf16[8,4,48,384]{3,2,1,0:T(8,128)(2,1)} %bitcast.15), custom_call_target="tpu_custom_call" | custom-call | bytes 4718592 | tf_op jit(solution)/shard_map/pack/pallas_call | solution.py:284
  73.3 7.3 %all-to-all-start = ((bf16[32,96,384]{2,1,0:T(8,128)(2,1)}), bf16[32,96,384]{2,1,0:T(8,128)(2,1)S(1)}, u32[]{:S(2)}, u32[]{:S(2)}) async-start(bf16[32,96,384]{2,1,0:T(8,128)(2,1)} %bitcast.19), calls=%async_computation | async-start | bytes 4718592 | tf_op jit(solution)/shard_map/all_to_all | solution.py:329
  80.6 0.0 copy-start.7
  80.6 1.5 copy.11.image
  82.1 0.1 copy-done.7
  82.2 0.0 copy-start.4
  82.2 0.0 copy-start.5
  82.2 0.0 copy-start.6
  82.2 0.2 copy.12.target
  82.4 1.1 copy-done.4
  83.5 0.4 copy-done.5
  83.8 0.0 copy-done.6
  83.8 23.1 %score.1.scores = bf16[32,104,384]{2,1,0:T(8,128)(2,1)} custom-call(s32[8]{0:T(128)S(1)} %bitcast.17, bf16[8,197,384]{2,1,0:T(8,128)(2,1)S(1)} %copy.11.image, bf16[8,197,384]{2,1,0:T(8,128)(2,1)S(1)} %copy.12.target, bf16[384,1536]{1,0:T(8,128)(2,1)S(1)} %bitcast.14, bf16[1536,384]{1,0:T(8,128)(2,1)S(1)} %bitcast.16), custom_call_target="tpu_custom_call" | custom-call | flops 9814671360 | bytes 7139328 | tf_op jit(solution)/shard_map/score/pallas_call | solution.py:92
  107.0 28.0 %all-to-all-done.params = bf16[32,96,384]{2,1,0:T(8,128)(2,1)S(1)} async-done(((bf16[32,96,384]{2,1,0:T(8,128)(2,1)}), bf16[32,96,384]{2,1,0:T(8,128)(2,1)S(1)}, u32[]{:S(2)}, u32[]{:S(2)}) %all-to-all-start) | async-done | bytes 2359328 | tf_op jit(solution)/shard_map/all_to_all | solution.py:329
  135.0 0.0 copy-start.2
  135.0 1.7 copy-done.2
  136.7 0.0 copy-start
  136.7 2.1 gram.1
  138.9 0.0 copy-done
  138.9 0.0 copy-start.3
  138.9 1.5 copy-done.3
  140.4 4.3 all-to-all-start.1
  145.3 58.1 %all-to-all-done.1.parts.scores = bf16[32,104,384]{2,1,0:T(8,128)(2,1)S(1)} async-done(((bf16[32,104,384]{2,1,0:T(8,128)(2,1)}), bf16[32,104,384]{2,1,0:T(8,128)(2,1)S(1)}, u32[]{:S(2)}, u32[]{:S(2)}) %all-to-all-start.1) | async-done | bytes 2555936 | tf_op jit(solution)/shard_map/all_to_all | solution.py:329
  203.4 0.0 copy-start.1
  203.4 1.7 copy-done.1
  205.1 6.2 %mix.1 = bf16[32,2,96,384]{3,2,1,0:T(8,128)(2,1)S(1)} custom-call(f32[1]{0:T(128)S(6)} %copy.14.scale, bf16[32,104,384]{2,1,0:T(8,128)(2,1)S(1)} %all-to-all-done.1.parts.scores, bf16[32,104,384]{2,1,0:T(8,128)(2,1)S(1)} %all-to-all-done.1.parts.scores, bf16[32,96,384]{2,1,0:T(8,128)(2,1)S(1)} %copy-done.1), custom_call_target="tpu_custom_call" | custom-call | flops 2415919104 | bytes 9437184 | tf_op jit(solution)/shard_map/mix/pallas_call | solution.py:223
  211.2 109.7 %all_to_all.15 = bf16[32,192,384]{2,1,0:T(8,128)(2,1)} all-to-all(bf16[32,192,384]{2,1,0:T(8,128)(2,1)S(1)} %bitcast.12), channel_id=1, replica_groups=mesh['wide'=8,'narrow'=4] {'wide','narrow'}, dimensions={0} | all-to-all | bytes 9437184 | tf_op jit(solution)/shard_map/all_to_all | solution.py:329
  320.9 144.1 %unpack.1 = (bf16[8,48,1536]{2,1,0:T(8,128)(2,1)}, bf16[8,4,48,384]{3,2,1,0:T(8,128)(2,1)}, bf16[8,48,1536]{2,1,0:T(8,128)(2,1)}, bf16[8,4,48,384]{3,2,1,0:T(8,128)(2,1)}) custom-call(bf16[8,4,192,384]{3,2,1,0:T(8,128)(2,1)} %bitcast.18), custom_call_target="tpu_custom_call" | custom-call | bytes 9437184 | tf_op jit(solution)/shard_map/unpack/pallas_call | solution.py:316
Async XLA Ops:
  73.3 61.7 %all-to-all-start = ((bf16[32,96,384]{2,1,0:T(8,128)(2,1)}), bf16[32,96,384]{2,1,0:T(8,128)(2,1)S(1)}, u32[]{:S(2)}, u32[]{:S(2)}) async-start(bf16[32,96,384]{2,1,0:T(8,128)(2,1)} %bitcast.19), calls=%async_computation | async-start | bytes 4718592 | tf_op jit(solution)/shard_map/all_to_all | solution.py:329
  80.6 1.6 copy-start.7
  82.2 1.3 copy-start.4
  82.2 1.6 copy-start.5
  82.2 1.6 copy-start.6
  135.0 1.7 copy-start.2
  136.7 2.2 copy-start
  138.9 1.5 copy-start.3
  140.4 63.0 %all-to-all-start.1 = ((bf16[32,104,384]{2,1,0:T(8,128)(2,1)}), bf16[32,104,384]{2,1,0:T(8,128)(2,1)S(1)}, u32[]{:S(2)}, u32[]{:S(2)}) async-start(bf16[32,104,384]{2,1,0:T(8,128)(2,1)} %copy-done.3), calls=%async_computation.1 | async-start | bytes 5111808 | tf_op jit(solution)/shard_map/all_to_all | solution.py:329
  203.4 1.7 copy-start.1

commit v5 on v4

--- a/solution.py
+++ b/solution.py
@@ -152,15 +152,15 @@
     return pl.pallas_call(
         gram_kernel,
         out_shape=jax.ShapeDtypeStruct(scores.shape, scores.dtype),
-        in_specs=[pl.BlockSpec(memory_space=pltpu.VMEM), pl.BlockSpec(memory_space=pl.ANY)],
-        out_specs=pl.BlockSpec(memory_space=pl.ANY),
+        in_specs=[pl.BlockSpec(memory_space=pltpu.VMEM), pl.BlockSpec(memory_space=pltpu.HBM)],
+        out_specs=pl.BlockSpec(memory_space=pltpu.HBM),
         input_output_aliases={1: 0},
         scratch_shapes=[
             pltpu.VMEM((wide, wide), jnp.float32),
             pltpu.VMEM((members, EXTRA, D), jnp.bfloat16),
             pltpu.SemaphoreType.DMA,
         ],
-        compiler_params=pltpu.CompilerParams(vmem_limit_bytes=32 * 1024 * 1024),
+        compiler_params=pltpu.CompilerParams(vmem_limit_bytes=59 * 1024 * 1024),
         cost_estimate=pl.CostEstimate(
             flops=2 * wide * wide * rows // TILE * D,
             bytes_accessed=2 * members * rows * D,
@@ -235,7 +235,7 @@
             pltpu.VMEM((wide, wide), jnp.bfloat16),
             pltpu.VMEM((wide, 1), jnp.float32),
         ],
-        compiler_params=pltpu.CompilerParams(vmem_limit_bytes=32 * 1024 * 1024),
+        compiler_params=pltpu.CompilerParams(vmem_limit_bytes=59 * 1024 * 1024),
         cost_estimate=pl.CostEstimate(
             flops=4 * wide * wide * rows // TILE * D,
             bytes_accessed=8 * members * rows * D,
@@ -279,13 +279,12 @@
 
 
 def to_blocks(first, second):
-    any_space = pl.BlockSpec(memory_space=pl.ANY)
     deep = BLOCKS // COLS
     packed = pl.pallas_call(
         pack_kernel,
         out_shape=jax.ShapeDtypeStruct((deep, COLS, ROWS, D), jnp.bfloat16),
-        in_specs=[any_space, any_space],
-        out_specs=any_space,
+        in_specs=[pl.BlockSpec(memory_space=pltpu.HBM)] * 2,
+        out_specs=pl.BlockSpec(memory_space=pltpu.VMEM),
         scratch_shapes=[pltpu.SemaphoreType.DMA((COLS + 1,))],
         cost_estimate=pl.CostEstimate(flops=0, bytes_accessed=8 * D * FF, transcendentals=0),
         name="pack",
@@ -307,7 +306,6 @@
 
 
 def from_blocks(blocks):
-    any_space = pl.BlockSpec(memory_space=pl.ANY)
     deep = BLOCKS // COLS
     shapes = (
         jax.ShapeDtypeStruct((deep, EDGE, FF), jnp.bfloat16),
@@ -316,8 +314,8 @@
     outs = pl.pallas_call(
         unpack_kernel,
         out_shape=shapes + shapes,
-        in_specs=[any_space],
-        out_specs=(any_space,) * 4,
+        in_specs=[pl.BlockSpec(memory_space=pltpu.VMEM)],
+        out_specs=(pl.BlockSpec(memory_space=pltpu.HBM),) * 4,
         scratch_shapes=[pltpu.SemaphoreType.DMA((2, COLS + 1))],
         cost_estimate=pl.CostEstimate(flops=0, bytes_accessed=16 * D * FF, transcendentals=0),
         name="unpack",

time: 465 us -> 260 us (0.56)
  Pallas kernels: 248 us -> 44 us
    pallas_call x1, Pallas kernels: 144 us -> 4.59 us  [from_blocks(): pl.pallas_call(unpack_kernel, out_shape=shapes + shapes, in_specs=[pl.Blo...]
    pallas_call x1, Pallas kernels: 72.6 us -> 3.08 us  [to_blocks(): pl.pallas_call(pack_kernel, out_shape=jax.ShapeDtypeStruct((deep, COLS, R...]
  transfers between devices with their start and end apart: 2 -> 2, of which waited for: 2 -> 2; matrix products, arithmetic and copies ran while one was open for 0% -> 1% of each run, Pallas kernels for 5% -> 9%
where the time goes in v5:
time: 260 us; the launch traced here: 259 us
  blocking collectives  110 us (42%)
  waiting for transfers between devices  86.1 us (33%)
  Pallas kernels  44 us (17%)
  starting transfers between devices  11.6 us (4%)
  local copies, waits for them, and re-layouts  6.24 us (2%)
    all_to_all x1, blocking collectives, exchange(): return lax.all_to_all(blocks, AXES, split_axis=0, concat_axis=0, tiled=True)  110 us
    all_to_all x2, waiting for transfers between devices, exchange(): return lax.all_to_all(blocks, AXES, split_axis=0, concat_axis=0, tiled=True)  86.1 us
    pallas_call x1, Pallas kernels, particle_scores(): pl.pallas_call(functools.partial(score_kernel, DATA / count), out_shape=j...  23.2 us
    all_to_all x2, starting transfers between devices, exchange(): return lax.all_to_all(blocks, AXES, split_axis=0, concat_axis=0, tiled=True)  11.6 us
    pallas_call x1, Pallas kernels, weighted(): pl.pallas_call(mix_kernel, out_shape=jax.ShapeDtypeStruct((members, 2, ro...  8.64 us
    unnamed x14, local copies, waits for them, and re-layouts  6.24 us
  transfers between devices with their start and end apart: 2, of which 2 were waited for; matrix products, arithmetic and copies ran while one was open for 1% of the time, Pallas kernels for 9%

profile of v5, /device:TPU:0, one launch (start us, length us, event | category | flops | bytes accessed | tf_op | source)
XLA Modules:
  0.0 259.1 jit_solution(8696501539414174233)
XLA Ops:
  0.6 3.1 %pack.1 = bf16[8,4,96,384]{3,2,1,0:T(8,128)(2,1)} custom-call(bf16[8,48,1536]{2,1,0:T(8,128)(2,1)} %bitcast.12, bf16[8,4,48,384]{3,2,1,0:T(8,128)(2,1)} %bitcast.14), custom_call_target="tpu_custom_call" | custom-call | bytes 4718592 | tf_op jit(solution)/shard_map/pack/pallas_call | solution.py:283
  3.7 7.3 %all-to-all-start = ((bf16[32,96,384]{2,1,0:T(8,128)(2,1)}), bf16[32,96,384]{2,1,0:T(8,128)(2,1)S(1)}, u32[]{:S(2)}, u32[]{:S(2)}) async-start(bf16[32,96,384]{2,1,0:T(8,128)(2,1)} %bitcast.19), calls=%async_computation | async-start | bytes 4718592 | tf_op jit(solution)/shard_map/all_to_all | solution.py:327
  11.0 0.0 copy-start.5
  11.0 1.5 copy.11.image
  12.6 0.1 copy-done.5
  12.7 0.0 copy-start
  12.7 0.0 copy-start.1
  12.7 0.0 copy-start.2
  12.7 0.2 copy.12.target
  12.8 1.1 copy-done
  14.0 0.4 copy-done.1
  14.3 0.0 copy-done.2
  14.3 23.2 %score.1.scores = bf16[32,104,384]{2,1,0:T(8,128)(2,1)} custom-call(s32[8]{0:T(128)S(1)} %bitcast.16, bf16[8,197,384]{2,1,0:T(8,128)(2,1)S(1)} %copy.11.image, bf16[8,197,384]{2,1,0:T(8,128)(2,1)S(1)} %copy.12.target, bf16[384,1536]{1,0:T(8,128)(2,1)S(1)} %bitcast.13, bf16[1536,384]{1,0:T(8,128)(2,1)S(1)} %bitcast.15), custom_call_target="tpu_custom_call" | custom-call | flops 9814671360 | bytes 7139328 | tf_op jit(solution)/shard_map/score/pallas_call | solution.py:92
  37.5 28.0 %all-to-all-done.params = bf16[32,96,384]{2,1,0:T(8,128)(2,1)S(1)} async-done(((bf16[32,96,384]{2,1,0:T(8,128)(2,1)}), bf16[32,96,384]{2,1,0:T(8,128)(2,1)S(1)}, u32[]{:S(2)}, u32[]{:S(2)}) %all-to-all-start) | async-done | bytes 2359328 | tf_op jit(solution)/shard_map/all_to_all | solution.py:327
  65.5 0.0 copy-start.4
  65.5 1.5 copy-done.4
  66.9 4.5 %gram.1 = bf16[32,104,384]{2,1,0:T(8,128)(2,1)} custom-call(bf16[32,96,384]{2,1,0:T(8,128)(2,1)} %copy-done.4, bf16[32,104,384]{2,1,0:T(8,128)(2,1)} %score.1.scores), custom_call_target="tpu_custom_call", output_to_operand_aliasing={{}: (1, {})} | custom-call | flops 1207959552 | bytes 2359296 | tf_op jit(solution)/shard_map/gram/pallas_call | solution.py:152
  71.4 4.3 %all-to-all-start.1 = ((bf16[32,104,384]{2,1,0:T(8,128)(2,1)}), bf16[32,104,384]{2,1,0:T(8,128)(2,1)S(1)}, u32[]{:S(2)}, u32[]{:S(2)}) async-start(bf16[32,104,384]{2,1,0:T(8,128)(2,1)} %gram.1), calls=%async_computation.1 | async-start | bytes 5111808 | tf_op jit(solution)/shard_map/all_to_all | solution.py:327
  76.4 58.1 %all-to-all-done.1.parts.scores = bf16[32,104,384]{2,1,0:T(8,128)(2,1)S(1)} async-done(((bf16[32,104,384]{2,1,0:T(8,128)(2,1)}), bf16[32,104,384]{2,1,0:T(8,128)(2,1)S(1)}, u32[]{:S(2)}, u32[]{:S(2)}) %all-to-all-start.1) | async-done | bytes 2555936 | tf_op jit(solution)/shard_map/all_to_all | solution.py:327
  134.5 0.0 copy-start.3
  134.5 1.5 copy-done.3
  136.0 8.6 %mix.1 = bf16[32,2,96,384]{3,2,1,0:T(8,128)(2,1)} custom-call(f32[1]{0:T(128)S(6)} %copy.14.scale, bf16[32,104,384]{2,1,0:T(8,128)(2,1)} %copy-done.3, bf16[32,104,384]{2,1,0:T(8,128)(2,1)} %copy-done.3, bf16[32,96,384]{2,1,0:T(8,128)(2,1)} %copy-done.4), custom_call_target="tpu_custom_call" | custom-call | flops 2415919104 | bytes 9437184 | tf_op jit(solution)/shard_map/mix/pallas_call | solution.py:223
  144.6 109.9 %all_to_all.15 = bf16[32,192,384]{2,1,0:T(8,128)(2,1)} all-to-all(bf16[32,192,384]{2,1,0:T(8,128)(2,1)} %bitcast.18), channel_id=1, replica_groups=mesh['wide'=8,'narrow'=4] {'wide','narrow'}, dimensions={0} | all-to-all | bytes 9437184 | tf_op jit(solution)/shard_map/all_to_all | solution.py:327
  254.5 4.6 %unpack.1 = (bf16[8,48,1536]{2,1,0:T(8,128)(2,1)}, bf16[8,4,48,384]{3,2,1,0:T(8,128)(2,1)}, bf16[8,48,1536]{2,1,0:T(8,128)(2,1)}, bf16[8,4,48,384]{3,2,1,0:T(8,128)(2,1)}) custom-call(bf16[8,4,192,384]{3,2,1,0:T(8,128)(2,1)} %bitcast.17), custom_call_target="tpu_custom_call" | custom-call | bytes 9437184 | tf_op jit(solution)/shard_map/unpack/pallas_call | solution.py:314
Async XLA Ops:
  3.7 61.7 %all-to-all-start = ((bf16[32,96,384]{2,1,0:T(8,128)(2,1)}), bf16[32,96,384]{2,1,0:T(8,128)(2,1)S(1)}, u32[]{:S(2)}, u32[]{:S(2)}) async-start(bf16[32,96,384]{2,1,0:T(8,128)(2,1)} %bitcast.19), calls=%async_computation | async-start | bytes 4718592 | tf_op jit(solution)/shard_map/all_to_all | solution.py:327
  11.0 1.6 copy-start.5
  12.7 1.3 copy-start
  12.7 1.6 copy-start.1
  12.7 1.6 copy-start.2
  65.5 1.5 copy-start.4
  71.4 63.0 %all-to-all-start.1 = ((bf16[32,104,384]{2,1,0:T(8,128)(2,1)}), bf16[32,104,384]{2,1,0:T(8,128)(2,1)S(1)}, u32[]{:S(2)}, u32[]{:S(2)}) async-start(bf16[32,104,384]{2,1,0:T(8,128)(2,1)} %gram.1), calls=%async_computation.1 | async-start | bytes 5111808 | tf_op jit(solution)/shard_map/all_to_all | solution.py:327
  134.5 1.5 copy-start.3

commit v6 on v5

--- a/solution.py
+++ b/solution.py
@@ -6,13 +6,15 @@
 from jax import lax
 from jax.experimental import pallas as pl
 from jax.experimental.pallas import tpu as pltpu
+from jax.sharding import Mesh
 from jax.sharding import PartitionSpec as P
 
 D = 384
 FF = 1536
 S = 197
 DATA = 10000
-AXES = ("wide", "narrow")
+AXES = ("far", "near", "rest")
+ORDER = ("rest", "near", "far")
 PAD = 208
 EDGE = 48
 BLOCKS = D * FF // (EDGE * D)
@@ -112,7 +114,7 @@
                 pltpu.VMEM((rows, FF), bf),
             ],
         ),
-        compiler_params=pltpu.CompilerParams(vmem_limit_bytes=48 * 1024 * 1024),
+        compiler_params=pltpu.CompilerParams(vmem_limit_bytes=32 * 1024 * 1024),
         cost_estimate=pl.CostEstimate(
             flops=10 * count * PAD * D * FF,
             bytes_accessed=4 * (2 * D * FF + count * S * D),
@@ -160,7 +162,7 @@
             pltpu.VMEM((members, EXTRA, D), jnp.bfloat16),
             pltpu.SemaphoreType.DMA,
         ],
-        compiler_params=pltpu.CompilerParams(vmem_limit_bytes=59 * 1024 * 1024),
+        compiler_params=pltpu.CompilerParams(vmem_limit_bytes=16 * 1024 * 1024),
         cost_estimate=pl.CostEstimate(
             flops=2 * wide * wide * rows // TILE * D,
             bytes_accessed=2 * members * rows * D,
@@ -173,7 +175,7 @@
 def kernel_of(scale, parts):
     members = parts.shape[0]
     lanes = members * members // 8
-    three = jnp.sum(parts[...].astype(jnp.float32), axis=0)
+    three = jnp.sum(parts.astype(jnp.float32), axis=0)
     packed = three[:, :lanes] + three[:, lanes : 2 * lanes] + three[:, 2 * lanes : 3 * lanes]
     gram = jnp.concatenate(
         [packed[:, members * q : members * (q + 1)] for q in range(members // 8)], axis=0
@@ -198,51 +200,40 @@
     return jnp.where(row == col, full, 0.0)
 
 
-def mix_kernel(scale, parts, scores, params, out, mixing, ksum):
-    members = params.shape[0]
-    wide = members * TILE
-
-    @pl.when(pl.program_id(0) == 0)
-    def _():
-        full = spreading(kernel_of(scale, parts))
-        ksum[...] = jnp.sum(full, axis=1, keepdims=True)
-        mixing[...] = full.astype(jnp.bfloat16)
-
-    got = scores[...].reshape(wide, D)
-    pulled = dot(mixing[...], got, ((1,), (0,))) * (1.0 / members)
-    out[:, 0] = pulled.astype(jnp.bfloat16).reshape(members, TILE, D)
-    own = params[...].reshape(wide, D)
-    mixed = dot(mixing[...], own, ((1,), (0,)))
-    pushed = (ksum[...] * own.astype(jnp.float32) - mixed) * (1.0 / members)
-    out[:, 1] = pushed.astype(jnp.bfloat16).reshape(members, TILE, D)
+def mix_kernel(scale, scores, params, out):
+    members, rows, _ = params.shape
+    wide = members * TILE
+    full = spreading(kernel_of(scale, scores[:, rows : rows + EXTRA, :]))
+    ksum = jnp.sum(full, axis=1, keepdims=True)
+    mixer = full.astype(jnp.bfloat16)
+    for r in range(0, rows, TILE):
+        got = scores[:, r : r + TILE, :].reshape(wide, D)
+        pulled = dot(mixer, got, ((1,), (0,))) * (1.0 / members)
+        out[:, r : r + TILE, :] = pulled.astype(jnp.bfloat16).reshape(members, TILE, D)
+        own = params[:, r : r + TILE, :].reshape(wide, D)
+        mixed = dot(mixer, own, ((1,), (0,)))
+        pushed = (ksum * own.astype(jnp.float32) - mixed) * (1.0 / members)
+        out[:, rows + r : rows + r + TILE, :] = pushed.astype(jnp.bfloat16).reshape(
+            members, TILE, D
+        )
 
 
 def weighted(scale, scores, params):
     members, rows, _ = params.shape
     wide = members * TILE
+    vmem = pl.BlockSpec(memory_space=pltpu.VMEM)
     return pl.pallas_call(
         mix_kernel,
-        out_shape=jax.ShapeDtypeStruct((members, 2, rows, D), jnp.bfloat16),
-        grid=(rows // TILE,),
-        in_specs=[
-            pl.BlockSpec(memory_space=pltpu.SMEM),
-            pl.BlockSpec((members, EXTRA, D), lambda r: (0, rows // EXTRA, 0)),
-            pl.BlockSpec((members, TILE, D), lambda r: (0, r, 0)),
-            pl.BlockSpec((members, TILE, D), lambda r: (0, r, 0)),
-        ],
-        out_specs=pl.BlockSpec((members, 2, TILE, D), lambda r: (0, 0, r, 0)),
-        scratch_shapes=[
-            pltpu.VMEM((wide, wide), jnp.bfloat16),
-            pltpu.VMEM((wide, 1), jnp.float32),
-        ],
-        compiler_params=pltpu.CompilerParams(vmem_limit_bytes=59 * 1024 * 1024),
+        out_shape=jax.ShapeDtypeStruct((members, 2 * rows, D), jnp.bfloat16),
+        in_specs=[pl.BlockSpec(memory_space=pltpu.SMEM), vmem, vmem],
+        compiler_params=pltpu.CompilerParams(vmem_limit_bytes=24 * 1024 * 1024),
         cost_estimate=pl.CostEstimate(
             flops=4 * wide * wide * rows // TILE * D,
             bytes_accessed=8 * members * rows * D,
             transcendentals=0,
         ),
         name="mix",
-    )(scale, scores, scores, params)
+    )(scale, scores, params)
 
 
 def plain_products(params):
@@ -292,45 +283,37 @@
     return packed.reshape(BLOCKS, ROWS, D)
 
 
-def unpack_kernel(blocks, first_a, second_a, first_s, second_s, sems):
-    copies = []
-    for which, (first, second) in enumerate(((first_a, second_a), (first_s, second_s))):
-        at = which * ROWS
-        here = blocks.at[:, :, pl.ds(at + EDGE, EDGE), :]
-        copies.append(pltpu.make_async_copy(here, second, sems.at[which, COLS]))
-        for c in range(COLS):
-            here = blocks.at[:, c, pl.ds(at, EDGE), :]
-            there = first.at[:, :, pl.ds(c * D, D)]
-            copies.append(pltpu.make_async_copy(here, there, sems.at[which, c]))
-    run(copies)
+def unpack_kernel(blocks, first_a, second_a, first_s, second_s):
+    for b in range(BLOCKS):
+        r, c = b // COLS * EDGE, b % COLS * D
+        first_a[0, r : r + EDGE, c : c + D] = blocks[b, 0:EDGE, :]
+        second_a[0, b * EDGE : (b + 1) * EDGE, :] = blocks[b, EDGE : 2 * EDGE, :]
+        first_s[0, r : r + EDGE, c : c + D] = blocks[b, 2 * EDGE : 3 * EDGE, :]
+        second_s[0, b * EDGE : (b + 1) * EDGE, :] = blocks[b, 3 * EDGE : 4 * EDGE, :]
 
 
 def from_blocks(blocks):
-    deep = BLOCKS // COLS
     shapes = (
-        jax.ShapeDtypeStruct((deep, EDGE, FF), jnp.bfloat16),
-        jax.ShapeDtypeStruct((deep, COLS, EDGE, D), jnp.bfloat16),
+        jax.ShapeDtypeStruct((1, D, FF), jnp.bfloat16),
+        jax.ShapeDtypeStruct((1, FF, D), jnp.bfloat16),
     )
-    outs = pl.pallas_call(
+    return pl.pallas_call(
         unpack_kernel,
         out_shape=shapes + shapes,
-        in_specs=[pl.BlockSpec(memory_space=pltpu.VMEM)],
-        out_specs=(pl.BlockSpec(memory_space=pltpu.HBM),) * 4,
-        scratch_shapes=[pltpu.SemaphoreType.DMA((2, COLS + 1))],
+        compiler_params=pltpu.CompilerParams(vmem_limit_bytes=24 * 1024 * 1024),
         cost_estimate=pl.CostEstimate(flops=0, bytes_accessed=16 * D * FF, transcendentals=0),
         name="unpack",
-    )(blocks.reshape(deep, COLS, 2 * ROWS, D))
-    return tuple(x.reshape(s) for x, s in zip(outs, ((1, D, FF), (1, FF, D)) * 2))
+    )(blocks)
 
 
 def exchange(blocks):
-    return lax.all_to_all(blocks, AXES, split_axis=0, concat_axis=0, tiled=True)
+    return lax.all_to_all(blocks, ORDER, split_axis=0, concat_axis=0, tiled=True)
 
 
 def on_device(
     particles_first, particles_second, pool_images, pool_targets, batch_index, kernel_scale
 ):
-    members = lax.axis_size("wide") * lax.axis_size("narrow")
+    members = math.prod(lax.axis_size(name) for name in AXES)
     cut = (members, BLOCKS * ROWS // members, D)
     tiled = members == BLOCKS
     params = exchange(to_blocks(particles_first, particles_second).reshape(cut))
@@ -344,7 +327,7 @@
     )
     if tiled:
         scores = exchange(add_products(params, scores))
-        mixed = exchange(weighted(kernel_scale, scores, params).reshape(members, 2 * ROWS, D))
+        mixed = exchange(weighted(kernel_scale, scores, params))
     else:
         scores = exchange(scores.reshape(cut))
         gram = lax.psum(plain_products(params), AXES)
@@ -358,7 +341,7 @@
     split = P(AXES, None, None)
     return jax.shard_map(
         on_device,
-        mesh=mesh,
+        mesh=Mesh(mesh.devices.reshape(2, 2, -1), AXES),
         in_specs=(split, split, P(), P(), P(AXES, None), P()),
         out_specs=(split, split, split, split),
         check_vma=False,

time: 260 us -> 255 us (0.981)
  Pallas kernels: 44 us -> 35.3 us
  waiting for transfers between devices: 86.1 us -> 90.4 us
    pallas_call x2, Pallas kernels: 13.2 us -> 8.19 us  [the longest x1 5.6 us: weighted(): pl.pallas_call(mix_kernel, out_shape=jax.ShapeDtypeStruct((members, 2 * r...]
    all_to_all x2, waiting for transfers between devices: 86.1 us -> 90.4 us  [exchange(): lax.all_to_all(blocks, ORDER, split_axis=0, concat_axis=0, tiled=True)]
    unnamed x14 -> x16, local copies, waits for them, and re-layouts: 6.24 us -> 7.97 us
where the time goes in v6:
time: 255 us; the launch traced here: 254 us
  blocking collectives  108 us (42%)
  waiting for transfers between devices  90.4 us (35%)
  Pallas kernels  35.3 us (14%)
  starting transfers between devices  10.8 us (4%)
  local copies, waits for them, and re-layouts  7.97 us (3%)
    all_to_all x1, blocking collectives, exchange(): lax.all_to_all(blocks, ORDER, split_axis=0, concat_axis=0, tiled=True)  108 us
    all_to_all x2, waiting for transfers between devices, exchange(): lax.all_to_all(blocks, ORDER, split_axis=0, concat_axis=0, tiled=True)  90.4 us
    pallas_call x1, Pallas kernels, particle_scores(): pl.pallas_call(functools.partial(score_kernel, DATA / count), out_shape=j...  21.9 us
    all_to_all x2, starting transfers between devices, exchange(): lax.all_to_all(blocks, ORDER, split_axis=0, concat_axis=0, tiled=True)  10.8 us
    unnamed x16, local copies, waits for them, and re-layouts  7.97 us
    pallas_call x1, Pallas kernels, weighted(): pl.pallas_call(mix_kernel, out_shape=jax.ShapeDtypeStruct((members, 2 * r...  5.6 us
  transfers between devices with their start and end apart: 2, of which 2 were waited for; matrix products, arithmetic and copies ran while one was open for 1% of the time, Pallas kernels for 9%

profile of v6, /device:TPU:0, one launch (start us, length us, event | category | flops | bytes accessed | tf_op | source)
XLA Modules:
  0.0 254.3 jit_solution(12489105879609386314)
XLA Ops:
  0.6 3.1 %pack.1 = bf16[8,4,96,384]{3,2,1,0:T(8,128)(2,1)} custom-call(bf16[8,48,1536]{2,1,0:T(8,128)(2,1)} %bitcast.6, bf16[8,4,48,384]{3,2,1,0:T(8,128)(2,1)} %bitcast.8), custom_call_target="tpu_custom_call" | custom-call | bytes 4718592 | tf_op jit(solution)/shard_map/pack/pallas_call | solution.py:274
  3.7 7.3 %all-to-all-start = ((bf16[32,96,384]{2,1,0:T(8,128)(2,1)}), bf16[32,96,384]{2,1,0:T(8,128)(2,1)S(1)}, u32[]{:S(2)}, u32[]{:S(2)}) async-start(bf16[32,96,384]{2,1,0:T(8,128)(2,1)} %bitcast.11), calls=%async_computation | async-start | bytes 4718592 | tf_op jit(solution)/shard_map/all_to_all | solution.py:310
  11.0 0.0 copy-start.6
  11.0 1.5 copy.11.image
  12.6 0.1 copy-done.6
  12.7 0.0 copy-start.3
  12.7 0.0 copy-start.4
  12.7 0.0 copy-start.5
  12.7 0.2 copy.12.target
  12.8 1.1 copy-done.3
  14.0 0.4 copy-done.4
  14.3 0.0 copy-done.5
  14.3 21.9 %score.1.scores = bf16[32,104,384]{2,1,0:T(8,128)(2,1)S(1)} custom-call(s32[8]{0:T(128)S(1)} %bitcast.10, bf16[8,197,384]{2,1,0:T(8,128)(2,1)S(1)} %copy.11.image, bf16[8,197,384]{2,1,0:T(8,128)(2,1)S(1)} %copy.12.target, bf16[384,1536]{1,0:T(8,128)(2,1)S(1)} %bitcast.7, bf16[1536,384]{1,0:T(8,128)(2,1)S(1)} %bitcast.9), custom_call_target="tpu_custom_call" | custom-call | flops 9814671360 | bytes 7139328 | tf_op jit(solution)/shard_map/score/pallas_call | solution.py:94
  36.2 0.0 copy-start
  36.2 1.5 copy-done
  37.7 30.0 %all-to-all-done.params = bf16[32,96,384]{2,1,0:T(8,128)(2,1)S(1)} async-done(((bf16[32,96,384]{2,1,0:T(8,128)(2,1)}), bf16[32,96,384]{2,1,0:T(8,128)(2,1)S(1)}, u32[]{:S(2)}, u32[]{:S(2)}) %all-to-all-start) | async-done | bytes 2359328 | tf_op jit(solution)/shard_map/all_to_all | solution.py:310
  67.7 0.0 copy-start.1
  67.7 1.7 copy-done.1
  69.5 2.1 gram.1
  71.6 0.0 copy-start.2
  71.6 1.5 copy-done.2
  73.1 3.5 %all-to-all-start.1 = ((bf16[32,104,384]{2,1,0:T(8,128)(2,1)}), bf16[32,104,384]{2,1,0:T(8,128)(2,1)}, u32[]{:S(2)}, u32[]{:S(2)}) async-start(bf16[32,104,384]{2,1,0:T(8,128)(2,1)} %copy-done.2), calls=%async_computation.1 | async-start | bytes 5111808 | tf_op jit(solution)/shard_map/all_to_all | solution.py:310
  77.3 60.5 %all-to-all-done.1.scores = bf16[32,104,384]{2,1,0:T(8,128)(2,1)} async-done(((bf16[32,104,384]{2,1,0:T(8,128)(2,1)}), bf16[32,104,384]{2,1,0:T(8,128)(2,1)}, u32[]{:S(2)}, u32[]{:S(2)}) %all-to-all-start.1) | async-done | bytes 2555936 | tf_op jit(solution)/shard_map/all_to_all | solution.py:310
  137.7 5.6 %mix.1 = bf16[32,192,384]{2,1,0:T(8,128)(2,1)S(1)} custom-call(f32[1]{0:T(128)S(6)} %copy.14.scale, bf16[32,104,384]{2,1,0:T(8,128)(2,1)} %all-to-all-done.1.scores, bf16[32,96,384]{2,1,0:T(8,128)(2,1)S(1)} %all-to-all-done.params), custom_call_target="tpu_custom_call" | custom-call | flops 2415919104 | bytes 9437184 | tf_op jit(solution)/shard_map/mix/pallas_call | solution.py:225
  143.3 108.3 %all_to_all.15.blocks = bf16[32,192,384]{2,1,0:T(8,128)(2,1)S(1)} all-to-all(bf16[32,192,384]{2,1,0:T(8,128)(2,1)S(1)} %mix.1), channel_id=1, replica_groups=mesh['far'=2,'near'=2,'rest'=8] {'rest','near','far'}, dimensions={0} | all-to-all | bytes 9437184 | tf_op jit(solution)/shard_map/all_to_all | solution.py:310
  251.7 2.6 %unpack.1 = (bf16[1,384,1536]{2,1,0:T(8,128)(2,1)}, bf16[1,1536,384]{2,1,0:T(8,128)(2,1)}, bf16[1,384,1536]{2,1,0:T(8,128)(2,1)}, bf16[1,1536,384]{2,1,0:T(8,128)(2,1)}) custom-call(bf16[32,192,384]{2,1,0:T(8,128)(2,1)S(1)} %all_to_all.15.blocks), custom_call_target="tpu_custom_call" | custom-call | bytes 9437184 | tf_op jit(solution)/shard_map/unpack/pallas_call | solution.py:300
Async XLA Ops:
  3.7 64.0 %all-to-all-start = ((bf16[32,96,384]{2,1,0:T(8,128)(2,1)}), bf16[32,96,384]{2,1,0:T(8,128)(2,1)S(1)}, u32[]{:S(2)}, u32[]{:S(2)}) async-start(bf16[32,96,384]{2,1,0:T(8,128)(2,1)} %bitcast.11), calls=%async_computation | async-start | bytes 4718592 | tf_op jit(solution)/shard_map/all_to_all | solution.py:310
  11.0 1.6 copy-start.6
  12.7 1.3 copy-start.3
  12.7 1.6 copy-start.4
  12.7 1.6 copy-start.5
  36.2 1.5 copy-start
  67.7 1.7 copy-start.1
  71.6 1.5 copy-start.2
  73.1 64.6 %all-to-all-start.1 = ((bf16[32,104,384]{2,1,0:T(8,128)(2,1)}), bf16[32,104,384]{2,1,0:T(8,128)(2,1)}, u32[]{:S(2)}, u32[]{:S(2)}) async-start(bf16[32,104,384]{2,1,0:T(8,128)(2,1)} %copy-done.2), calls=%async_computation.1 | async-start | bytes 5111808 | tf_op jit(solution)/shard_map/all_to_all | solution.py:310

commit v7 on v6

v7 whole, which is shorter than its diff:
```python
import functools
import math

import jax
import jax.numpy as jnp
from jax import lax
from jax.experimental import pallas as pl
from jax.experimental.pallas import tpu as pltpu
from jax.sharding import PartitionSpec as P

D = 384
FF = 1536
S = 197
DATA = 10000
AXES = ("wide", "narrow")
PAD = 208
EDGE = 48
BLOCKS = D * FF // (EDGE * D)
COLS = FF // D
TILE = 16
LANES = 128
SIDE = 2 * EDGE
GROUPS = range(D // LANES)
ROWS = SIDE * len(GROUPS)
EXTRA = 8

gelu_c = math.sqrt(2.0 / math.pi)
isd = 1.0 / math.sqrt(D)
isf = 1.0 / math.sqrt(FF)


def dot(a, b, dims):
    return lax.dot_general(a, b, (dims, ((), ())), preferred_element_type=jnp.float32)


def put(out, block, row, value):
    for g in GROUPS:
        at = g * SIDE + row
        out[block, at : at + EDGE, :] = value[:, g * LANES : (g + 1) * LANES]


def tile(ref, r):
    members = ref.shape[0]
    parts = [ref[:, g * SIDE + r : g * SIDE + r + TILE, :] for g in GROUPS]
    return jnp.concatenate([p.reshape(members * TILE, LANES) for p in parts], axis=1)


def score_kernel(
    factor, picks, image, target, first, second, out, xs, ts, normed, hidden, deriv, delta, back
):
    step = pl.program_id(0)
    images = pl.num_programs(0)
    rows = pl.ds(pl.multiple_of(step * PAD, PAD), PAD)

    @pl.when(step == 0)
    def _():
        xs[...] = jnp.zeros_like(xs)
        ts[...] = jnp.zeros_like(ts)

    xs[0:S, :] = image[0].astype(jnp.float32)
    ts[0:S, :] = target[0].astype(jnp.float32)
    xf = xs[...]
    mean = jnp.mean(xf, axis=1, keepdims=True)
    centered = xf - mean
    var = jnp.mean(centered * centered, axis=1, keepdims=True)
    nrm = (centered * lax.rsqrt(var + 1e-06)).astype(jnp.bfloat16)
    normed[rows, :] = nrm
    for c in range(COLS):
        cols = pl.ds(c * D, D)
        pre = dot(nrm, first[:, cols], ((1,), (0,))) * isd
        sq = pre * pre
        tval = jnp.tanh(pre * (gelu_c + (gelu_c * 0.044715) * sq))
        gate = 0.5 + 0.5 * tval
        hid = pre * gate
        hidden[rows, cols] = hid.astype(jnp.bfloat16)
        deriv[:, cols] = gate + hid * (1.0 - gate) * (
            2.0 * gelu_c + (6.0 * gelu_c * 0.044715) * sq
        )
    prod = dot(hidden[rows, :], second[...], ((1,), (0,))) * isf
    dlt = ((xs[...] + prod - ts[...]) * (1.0 / S)).astype(jnp.bfloat16)
    delta[rows, :] = dlt
    for c in range(COLS):
        cols = pl.ds(c * D, D)
        dhid = dot(dlt, second[cols, :], ((1,), (1,))) * isf
        back[rows, cols] = (dhid * deriv[:, cols]).astype(jnp.bfloat16)

    @pl.when(step == images - 1)
    def _():
        for c in range(COLS):
            cols = pl.ds(c * D, D)
            grad = dot(normed[...], back[:, cols], ((0,), (0,))) * (-factor * isd)
            score = (grad - first[:, cols].astype(jnp.float32)).astype(jnp.bfloat16)
            for r in range(D // EDGE):
                put(out, r * COLS + c, 0, score[r * EDGE : (r + 1) * EDGE, :])
            grad = dot(hidden[:, cols], delta[...], ((0,), (0,))) * (-factor * isf)
            score = (grad - second[cols, :].astype(jnp.float32)).astype(jnp.bfloat16)
            for r in range(D // EDGE):
                put(out, c * (D // EDGE) + r, EDGE, score[r * EDGE : (r + 1) * EDGE, :])


def particle_scores(first, second, images, targets, picks, extra):
    count = picks.shape[0]
    rows = count * PAD
    bf = jnp.bfloat16
    return pl.pallas_call(
        functools.partial(score_kernel, DATA / count),
        out_shape=pltpu.HBM((BLOCKS, ROWS + extra, LANES), bf),
        grid_spec=pltpu.PrefetchScalarGridSpec(
            num_scalar_prefetch=1,
            grid=(count,),
            in_specs=[
                pl.BlockSpec((1, S, D), lambda b, picks: (picks[b], 0, 0)),
                pl.BlockSpec((1, S, D), lambda b, picks: (picks[b], 0, 0)),
                pl.BlockSpec((D, FF), lambda b, picks: (0, 0)),
                pl.BlockSpec((FF, D), lambda b, picks: (0, 0)),
            ],
            out_specs=pl.BlockSpec((BLOCKS, ROWS, LANES), lambda b, picks: (0, 0, 0)),
            scratch_shapes=[
                pltpu.VMEM((PAD, D), jnp.float32),
                pltpu.VMEM((PAD, D), jnp.float32),
                pltpu.VMEM((rows, D), bf),
                pltpu.VMEM((rows, FF), bf),
                pltpu.VMEM((PAD, FF), jnp.float32),
                pltpu.VMEM((rows, D), bf),
                pltpu.VMEM((rows, FF), bf),
            ],
        ),
        compiler_params=pltpu.CompilerParams(vmem_limit_bytes=32 * 1024 * 1024),
        cost_estimate=pl.CostEstimate(
            flops=10 * count * PAD * D * FF,
            bytes_accessed=4 * (2 * D * FF + count * S * D),
            transcendentals=count * PAD * FF,
        ),
        name="score",
    )(picks, images, targets, first, second)


def gram_kernel(params, scores, out, total, parts, sem):
    members, rows, _ = params.shape
    wide = members * TILE
    half = members // 2
    total[...] = jnp.zeros_like(total)
    for r in range(0, SIDE, TILE):
        part = tile(params, r)
        total[...] += dot(part, part, ((1,), (1,)))
    at = lax.broadcasted_iota(jnp.int32, (wide, wide), 0) % TILE
    to = lax.broadcasted_iota(jnp.int32, (wide, wide), 1) % TILE
    kept = jnp.where(at == to, total[...], 0.0)
    summed = jnp.sum(kept.reshape(members, TILE, wide), axis=1)
    turned = summed.T
    gram = jnp.sum(turned.reshape(members, TILE, members), axis=1)
    row = lax.broadcasted_iota(jnp.int32, gram.shape, 0)
    col = lax.broadcasted_iota(jnp.int32, gram.shape, 1)
    own = jnp.where(row == col, gram, 0.0)
    dist = jnp.sum(own, axis=1, keepdims=True) + jnp.sum(own, axis=0, keepdims=True) - 2.0 * gram
    low = jnp.concatenate([dist[half:, half:], dist[half:, :half]], axis=1)
    once = jnp.where(col[:half] > row[:half], dist[:half], low)
    high = once.astype(jnp.bfloat16).astype(jnp.float32)
    rest = once - high
    both = [x[q : q + EXTRA] for x in (high, rest) for q in range(0, half, EXTRA)]
    packed = jnp.concatenate(both, axis=1).astype(jnp.bfloat16)
    parts[...] = jnp.broadcast_to(packed[None], parts.shape)
    copy = pltpu.make_async_copy(parts, out.at[:, pl.ds(rows, EXTRA), :], sem)
    copy.start()
    copy.wait()


def add_distances(params, scores):
    members, rows, _ = params.shape
    wide = members * TILE
    return pl.pallas_call(
        gram_kernel,
        out_shape=pltpu.HBM(scores.shape, scores.dtype),
        in_specs=[pl.BlockSpec(memory_space=pltpu.VMEM), pl.BlockSpec(memory_space=pl.ANY)],
        out_specs=pl.BlockSpec(memory_space=pl.ANY),
        input_output_aliases={1: 0},
        scratch_shapes=[
            pltpu.VMEM((wide, wide), jnp.float32),
            pltpu.VMEM((members, EXTRA, LANES), jnp.bfloat16),
            pltpu.SemaphoreType.DMA,
        ],
        compiler_params=pltpu.CompilerParams(vmem_limit_bytes=16 * 1024 * 1024),
        cost_estimate=pl.CostEstimate(
            flops=2 * wide * wide * SIDE // TILE * D,
            bytes_accessed=2 * members * rows * LANES,
            transcendentals=0,
        ),
        name="gram",
    )(params, scores)


def kernel_of(scale, parts):
    members = parts.shape[0]
    half = members // 2
    packed = jnp.sum(parts.astype(jnp.float32), axis=0)
    both = [packed[:, q : q + members] for q in range(0, LANES, members)]
    once = jnp.concatenate(both[:2], axis=0) + jnp.concatenate(both[2:], axis=0)
    row = lax.broadcasted_iota(jnp.int32, once.shape, 0)
    col = lax.broadcasted_iota(jnp.int32, once.shape, 1)
    upper = jnp.where(col > row, once, 0.0)
    lower = jnp.where(col < row, once, 0.0)
    lower = jnp.concatenate([lower[:, half:], lower[:, :half]], axis=1)
    dist = jnp.concatenate([upper, lower], axis=0)
    return jnp.exp(-(dist + dist.T) / scale[0]).astype(jnp.bfloat16)


def spreading(kernel):
    members = kernel.shape[0]
    wide = members * TILE
    at = lax.broadcasted_iota(jnp.int32, (wide, members), 0) // TILE
    which = lax.broadcasted_iota(jnp.int32, (wide, members), 1)
    pick = jnp.where(at == which, 1.0, 0.0).astype(jnp.bfloat16)
    tall = dot(pick, kernel, ((1,), (0,))).astype(jnp.bfloat16)
    full = dot(tall, pick, ((1,), (1,)))
    row = lax.broadcasted_iota(jnp.int32, (wide, wide), 0) % TILE
    col = lax.broadcasted_iota(jnp.int32, (wide, wide), 1) % TILE
    return jnp.where(row == col, full, 0.0)


def mix_kernel(scale, scores, params, out):
    members, rows, _ = params.shape
    wide = members * TILE
    full = spreading(kernel_of(scale, scores[:, rows : rows + EXTRA, :]))
    ksum = jnp.sum(full, axis=1, keepdims=True)
    mixer = full.astype(jnp.bfloat16)
    for r in range(0, SIDE, TILE):
        own = tile(params, r)
        both = dot(mixer, jnp.concatenate([tile(scores, r), own], axis=1), ((1,), (0,)))
        pushed = ksum * own.astype(jnp.float32) - both[:, D:]
        both = jnp.concatenate([both[:, :D], pushed], axis=1) * (1.0 / members)
        both = both.astype(jnp.bfloat16)
        for g in range(2 * len(GROUPS)):
            at = g * SIDE + r
            out[:, at : at + TILE, :] = both[:, g * LANES : (g + 1) * LANES].reshape(
                members, TILE, LANES
            )


def weighted(scale, scores, params):
    members, rows, _ = params.shape
    wide = members * TILE
    vmem = pl.BlockSpec(memory_space=pltpu.VMEM)
    return pl.pallas_call(
        mix_kernel,
        out_shape=jax.ShapeDtypeStruct((members, 2 * rows, LANES), jnp.bfloat16),
        in_specs=[pl.BlockSpec(memory_space=pltpu.SMEM), vmem, vmem],
        compiler_params=pltpu.CompilerParams(vmem_limit_bytes=24 * 1024 * 1024),
        cost_estimate=pl.CostEstimate(
            flops=4 * wide * wide * SIDE // TILE * D,
            bytes_accessed=8 * members * rows * LANES,
            transcendentals=0,
        ),
        name="mix",
    )(scale, scores, params)


def plain_products(params):
    flat = params.reshape(params.shape[0], -1)
    return dot(flat, flat, ((1,), (1,)))


def plain_weighted(gram, scale, params, scores):
    members = params.shape[0]
    norms = jnp.diagonal(gram)
    dist = norms[:, None] + norms[None, :] - 2.0 * gram
    kernel = jnp.exp(-dist / scale[0]).astype(jnp.bfloat16)
    flat = params.reshape(members, -1)
    ksum = jnp.sum(kernel.astype(jnp.float32), axis=1, keepdims=True)
    attract = dot(kernel, scores.reshape(members, -1), ((1,), (0,))) / members
    mixed = dot(kernel, flat, ((1,), (0,)))
    spread = (flat.astype(jnp.float32) * ksum - mixed) / members
    return tuple(x.astype(jnp.bfloat16).reshape(params.shape) for x in (attract, spread))


STEPS = D // EDGE
TALL = FF // STEPS


def pack_kernel(first, second, out, wide, tall, packed, loads, stores):
    def load(d):
        return (
            pltpu.make_async_copy(
                first.at[0, pl.ds(d * EDGE, EDGE), :], wide.at[d], loads.at[0, d]
            ),
            pltpu.make_async_copy(
                second.at[0, pl.ds(d * TALL, TALL), :], tall.at[d], loads.at[1, d]
            ),
        )

    def store(d):
        here = pl.ds(d * COLS, COLS)
        return pltpu.make_async_copy(packed.at[here], out.at[here], stores.at[d])

    for d in range(STEPS):
        for copy in load(d):
            copy.start()
    for d in range(STEPS):
        for copy in load(d):
            copy.wait()
        for c in range(COLS):
            put(packed, d * COLS + c, 0, wide[d, :, c * D : (c + 1) * D])
            put(packed, d * COLS + c, EDGE, tall[d, c * EDGE : (c + 1) * EDGE, :])
        store(d).start()
    for d in range(STEPS):
        store(d).wait()


def to_blocks(first, second):
    bf = jnp.bfloat16
    return pl.pallas_call(
        pack_kernel,
        out_shape=pltpu.HBM((BLOCKS, ROWS, LANES), bf),
        in_specs=[pl.BlockSpec(memory_space=pl.ANY)] * 2,
        out_specs=pl.BlockSpec(memory_space=pl.ANY),
        scratch_shapes=[
            pltpu.VMEM((STEPS, EDGE, FF), bf),
            pltpu.VMEM((STEPS, TALL, D), bf),
            pltpu.VMEM((BLOCKS, ROWS, LANES), bf),
            pltpu.SemaphoreType.DMA((2, STEPS)),
            pltpu.SemaphoreType.DMA((STEPS,)),
        ],
        compiler_params=pltpu.CompilerParams(vmem_limit_bytes=56 * 1024 * 1024),
        cost_estimate=pl.CostEstimate(flops=0, bytes_accessed=8 * D * FF, transcendentals=0),
        name="pack",
    )(first, second)


def unpack_kernel(blocks, first_a, second_a, first_s, second_s, wide, tall, stores):
    def store(which, d):
        first, second = ((first_a, second_a), (first_s, second_s))[which]
        return (
            pltpu.make_async_copy(
                wide.at[which, d], first.at[0, pl.ds(d * EDGE, EDGE), :], stores.at[which, 0, d]
            ),
            pltpu.make_async_copy(
                tall.at[which, d], second.at[0, pl.ds(d * TALL, TALL), :], stores.at[which, 1, d]
            ),
        )

    for which in range(2):
        for d in range(STEPS):
            for c in range(COLS):
                for g in GROUPS:
                    at = which * ROWS + g * SIDE
                    lanes = slice(c * D + g * LANES, c * D + (g + 1) * LANES)
                    wide[which, d, :, lanes] = blocks[d * COLS + c, at : at + EDGE, :]
                    tall[which, d, c * EDGE : (c + 1) * EDGE, g * LANES : (g + 1) * LANES] = blocks[
                        d * COLS + c, at + EDGE : at + SIDE, :
                    ]
            for copy in store(which, d):
                copy.start()
    for which in range(2):
        for d in range(STEPS):
            for copy in store(which, d):
                copy.wait()


def from_blocks(blocks):
    bf = jnp.bfloat16
    return pl.pallas_call(
        unpack_kernel,
        out_shape=(pltpu.HBM((1, D, FF), bf), pltpu.HBM((1, FF, D), bf)) * 2,
        in_specs=[pl.BlockSpec(memory_space=pltpu.VMEM)],
        out_specs=(pl.BlockSpec(memory_space=pl.ANY),) * 4,
        scratch_shapes=[
            pltpu.VMEM((2, STEPS, EDGE, FF), bf),
            pltpu.VMEM((2, STEPS, TALL, D), bf),
            pltpu.SemaphoreType.DMA((2, 2, STEPS)),
        ],
        compiler_params=pltpu.CompilerParams(vmem_limit_bytes=24 * 1024 * 1024),
        cost_estimate=pl.CostEstimate(flops=0, bytes_accessed=16 * D * FF, transcendentals=0),
        name="unpack",
    )(blocks)


def exchange(blocks):
    return lax.all_to_all(blocks, AXES, split_axis=0, concat_axis=0, tiled=True)


def on_device(
    particles_first, particles_second, pool_images, pool_targets, batch_index, kernel_scale
):
    members = math.prod(lax.axis_size(name) for name in AXES)
    cut = (members, BLOCKS * ROWS // members, LANES)
    tiled = members == BLOCKS
    params = exchange(to_blocks(particles_first, particles_second).reshape(cut))
    scores = particle_scores(
        particles_first[0],
        particles_second[0],
        pool_images,
        pool_targets,
        batch_index[0],
        EXTRA if tiled else 0,
    )
    if tiled:
        scores = exchange(add_distances(params, scores))
        mixed = exchange(weighted(kernel_scale, scores, params))
    else:
        scores = exchange(scores.reshape(cut))
        gram = lax.psum(plain_products(params), AXES)
        parts = plain_weighted(gram, kernel_scale, params, scores)
        mixed = [exchange(x).reshape(BLOCKS, ROWS, LANES) for x in parts]
        mixed = jnp.concatenate(mixed, axis=1)
    return from_blocks(mixed)


def solution(mesh):
    split = P(AXES, None, None)
    return jax.shard_map(
        on_device,
        mesh=mesh,
        in_specs=(split, split, P(), P(), P(AXES, None), P()),
        out_specs=(split, split, split, split),
        check_vma=False,
    )
```

time: 255 us -> 245 us (0.961)
  waiting for transfers between devices: 90.4 us -> 83.2 us
  local copies, waits for them, and re-layouts: 7.97 us -> 3.26 us
    all_to_all x2, waiting for transfers between devices: 90.4 us -> 83.2 us  [exchange(): return lax.all_to_all(blocks, AXES, split_axis=0, concat_axis=0, tiled=True)]
    unnamed x16 -> x10, local copies, waits for them, and re-layouts: 7.97 us -> 3.26 us
where the time goes in v7:
time: 245 us
  blocking collectives  110 us (45%)
  waiting for transfers between devices  83.2 us (34%)
  Pallas kernels  36 us (15%)
  starting transfers between devices  11.7 us (5%)
  local copies, waits for them, and re-layouts  3.26 us (1%)
    all_to_all x1, blocking collectives, exchange(): return lax.all_to_all(blocks, AXES, split_axis=0, concat_axis=0, tiled=True)  110 us
    all_to_all x2, waiting for transfers between devices, exchange(): return lax.all_to_all(blocks, AXES, split_axis=0, concat_axis=0, tiled=True)  83.2 us
    pallas_call x1, Pallas kernels, particle_scores(): pl.pallas_call(functools.partial(score_kernel, DATA / count), out_shape=p...  23.1 us
    all_to_all x2, starting transfers between devices, exchange(): return lax.all_to_all(blocks, AXES, split_axis=0, concat_axis=0, tiled=True)  11.7 us
  transfers between devices with their start and end apart: 2, of which 2 were waited for; matrix products, arithmetic and copies ran while one was open for 1% of the time, Pallas kernels for 9%

profile of v7, /device:TPU:0, one launch (start us, length us, event | category | flops | bytes accessed | tf_op | source)
XLA Modules:
  0.0 245.1 jit_solution(5754319026593126652)
XLA Ops:
  0.6 2.7 %pack.1 = bf16[32,288,128]{2,1,0:T(8,128)(2,1)} custom-call(bf16[1,384,1536]{2,1,0:T(8,128)(2,1)} %first.1, bf16[1,1536,384]{2,1,0:T(8,128)(2,1)} %second.1), custom_call_target="tpu_custom_call" | custom-call | bytes 4718592 | tf_op jit(solution)/shard_map/pack/pallas_call | solution.py:310
  3.4 7.3 %all-to-all-start = ((bf16[32,288,128]{2,1,0:T(8,128)(2,1)}), bf16[32,288,128]{2,1,0:T(8,128)(2,1)S(1)}, u32[]{:S(2)}, u32[]{:S(2)}) async-start(bf16[32,288,128]{2,1,0:T(8,128)(2,1)} %pack.1), calls=%async_computation | async-start | bytes 4718592 | tf_op jit(solution)/shard_map/all_to_all | solution.py:377
  10.7 0.0 copy-start.3
  10.7 1.5 copy.11.image
  12.2 0.1 copy-done.3
  12.3 0.0 copy-start
  12.3 0.0 copy-start.1
  12.3 0.0 copy-start.2
  12.3 0.2 copy.12.target
  12.5 1.1 copy-done
  13.6 0.4 copy-done.1
  13.9 0.0 copy-done.2
  13.9 23.1 %score.1.scores = bf16[32,296,128]{2,1,0:T(8,128)(2,1)} custom-call(s32[8]{0:T(128)S(1)} %bitcast.5, bf16[8,197,384]{2,1,0:T(8,128)(2,1)S(1)} %copy.11.image, bf16[8,197,384]{2,1,0:T(8,128)(2,1)S(1)} %copy.12.target, bf16[384,1536]{1,0:T(8,128)(2,1)S(1)} %bitcast.3, bf16[1536,384]{1,0:T(8,128)(2,1)S(1)} %bitcast.4), custom_call_target="tpu_custom_call" | custom-call | flops 9814671360 | bytes 7139328 | tf_op jit(solution)/shard_map/score/pallas_call | solution.py:105
  37.0 28.0 %all-to-all-done.params = bf16[32,288,128]{2,1,0:T(8,128)(2,1)S(1)} async-done(((bf16[32,288,128]{2,1,0:T(8,128)(2,1)}), bf16[32,288,128]{2,1,0:T(8,128)(2,1)S(1)}, u32[]{:S(2)}, u32[]{:S(2)}) %all-to-all-start) | async-done | bytes 2359328 | tf_op jit(solution)/shard_map/all_to_all | solution.py:377
  65.1 2.8 %gram.1 = bf16[32,296,128]{2,1,0:T(8,128)(2,1)} custom-call(bf16[32,288,128]{2,1,0:T(8,128)(2,1)S(1)} %all-to-all-done.params, bf16[32,296,128]{2,1,0:T(8,128)(2,1)} %score.1.scores), custom_call_target="tpu_custom_call", output_to_operand_aliasing={{}: (1, {})} | custom-call | flops 1207959552 | bytes 2359296 | tf_op jit(solution)/shard_map/gram/pallas_call | solution.py:171
  67.9 4.4 %all-to-all-start.1 = ((bf16[32,296,128]{2,1,0:T(8,128)(2,1)}), bf16[32,296,128]{2,1,0:T(8,128)(2,1)}, u32[]{:S(2)}, u32[]{:S(2)}) async-start(bf16[32,296,128]{2,1,0:T(8,128)(2,1)} %gram.1), calls=%async_computation.1 | async-start | bytes 4849664 | tf_op jit(solution)/shard_map/all_to_all | solution.py:377
  73.0 55.2 %all-to-all-done.1.scores = bf16[32,296,128]{2,1,0:T(8,128)(2,1)} async-done(((bf16[32,296,128]{2,1,0:T(8,128)(2,1)}), bf16[32,296,128]{2,1,0:T(8,128)(2,1)}, u32[]{:S(2)}, u32[]{:S(2)}) %all-to-all-start.1) | async-done | bytes 2424864 | tf_op jit(solution)/shard_map/all_to_all | solution.py:377
  128.2 4.9 %mix.1 = bf16[32,576,128]{2,1,0:T(8,128)(2,1)S(1)} custom-call(f32[1]{0:T(128)S(6)} %copy.14.scale, bf16[32,296,128]{2,1,0:T(8,128)(2,1)} %all-to-all-done.1.scores, bf16[32,288,128]{2,1,0:T(8,128)(2,1)S(1)} %all-to-all-done.params), custom_call_target="tpu_custom_call" | custom-call | flops 2415919104 | bytes 9437184 | tf_op jit(solution)/shard_map/mix/pallas_call | solution.py:243
  133.0 109.5 %all_to_all.15.blocks = bf16[32,576,128]{2,1,0:T(8,128)(2,1)S(1)} all-to-all(bf16[32,576,128]{2,1,0:T(8,128)(2,1)S(1)} %mix.1), channel_id=1, replica_groups=mesh['wide'=8,'narrow'=4] {'wide','narrow'}, dimensions={0} | all-to-all | bytes 9437184 | tf_op jit(solution)/shard_map/all_to_all | solution.py:377
  242.6 2.5 %unpack.1 = (bf16[1,384,1536]{2,1,0:T(8,128)(2,1)}, bf16[1,1536,384]{2,1,0:T(8,128)(2,1)}, bf16[1,384,1536]{2,1,0:T(8,128)(2,1)}, bf16[1,1536,384]{2,1,0:T(8,128)(2,1)}) custom-call(bf16[32,576,128]{2,1,0:T(8,128)(2,1)S(1)} %all_to_all.15.blocks), custom_call_target="tpu_custom_call" | custom-call | bytes 9437184 | tf_op jit(solution)/shard_map/unpack/pallas_call | solution.py:360
Async XLA Ops:
  3.4 61.7 %all-to-all-start = ((bf16[32,288,128]{2,1,0:T(8,128)(2,1)}), bf16[32,288,128]{2,1,0:T(8,128)(2,1)S(1)}, u32[]{:S(2)}, u32[]{:S(2)}) async-start(bf16[32,288,128]{2,1,0:T(8,128)(2,1)} %pack.1), calls=%async_computation | async-start | bytes 4718592 | tf_op jit(solution)/shard_map/all_to_all | solution.py:377
  10.7 1.6 copy-start.3
  12.3 1.3 copy-start
  12.3 1.6 copy-start.1
  12.3 1.6 copy-start.2
  67.9 60.2 %all-to-all-start.1 = ((bf16[32,296,128]{2,1,0:T(8,128)(2,1)}), bf16[32,296,128]{2,1,0:T(8,128)(2,1)}, u32[]{:S(2)}, u32[]{:S(2)}) async-start(bf16[32,296,128]{2,1,0:T(8,128)(2,1)} %gram.1), calls=%async_computation.1 | async-start | bytes 4849664 | tf_op jit(solution)/shard_map/all_to_all | solution.py:377

commit v8 on v7

--- a/solution.py
+++ b/solution.py
@@ -22,7 +22,6 @@
 SIDE = 2 * EDGE
 GROUPS = range(D // LANES)
 ROWS = SIDE * len(GROUPS)
-EXTRA = 8
 
 gelu_c = math.sqrt(2.0 / math.pi)
 isd = 1.0 / math.sqrt(D)
@@ -98,13 +97,13 @@
                 put(out, c * (D // EDGE) + r, EDGE, score[r * EDGE : (r + 1) * EDGE, :])
 
 
-def particle_scores(first, second, images, targets, picks, extra):
+def particle_scores(first, second, images, targets, picks):
     count = picks.shape[0]
     rows = count * PAD
     bf = jnp.bfloat16
     return pl.pallas_call(
         functools.partial(score_kernel, DATA / count),
-        out_shape=pltpu.HBM((BLOCKS, ROWS + extra, LANES), bf),
+        out_shape=pltpu.HBM((BLOCKS, ROWS, LANES), bf),
         grid_spec=pltpu.PrefetchScalarGridSpec(
             num_scalar_prefetch=1,
             grid=(count,),
@@ -135,10 +134,9 @@
     )(picks, images, targets, first, second)
 
 
-def gram_kernel(params, scores, out, total, parts, sem):
+def gram_kernel(params, out, total):
     members, rows, _ = params.shape
     wide = members * TILE
-    half = members // 2
     total[...] = jnp.zeros_like(total)
     for r in range(0, SIDE, TILE):
         part = tile(params, r)
@@ -153,32 +151,16 @@
     col = lax.broadcasted_iota(jnp.int32, gram.shape, 1)
     own = jnp.where(row == col, gram, 0.0)
     dist = jnp.sum(own, axis=1, keepdims=True) + jnp.sum(own, axis=0, keepdims=True) - 2.0 * gram
-    low = jnp.concatenate([dist[half:, half:], dist[half:, :half]], axis=1)
-    once = jnp.where(col[:half] > row[:half], dist[:half], low)
-    high = once.astype(jnp.bfloat16).astype(jnp.float32)
-    rest = once - high
-    both = [x[q : q + EXTRA] for x in (high, rest) for q in range(0, half, EXTRA)]
-    packed = jnp.concatenate(both, axis=1).astype(jnp.bfloat16)
-    parts[...] = jnp.broadcast_to(packed[None], parts.shape)
-    copy = pltpu.make_async_copy(parts, out.at[:, pl.ds(rows, EXTRA), :], sem)
-    copy.start()
-    copy.wait()
-
-
-def add_distances(params, scores):
+    out[...] = jnp.concatenate([dist[q : q + 8] for q in range(0, members, 8)], axis=1)
+
+
+def distances(params):
     members, rows, _ = params.shape
     wide = members * TILE
     return pl.pallas_call(
         gram_kernel,
-        out_shape=pltpu.HBM(scores.shape, scores.dtype),
-        in_specs=[pl.BlockSpec(memory_space=pltpu.VMEM), pl.BlockSpec(memory_space=pl.ANY)],
-        out_specs=pl.BlockSpec(memory_space=pl.ANY),
-        input_output_aliases={1: 0},
-        scratch_shapes=[
-            pltpu.VMEM((wide, wide), jnp.float32),
-            pltpu.VMEM((members, EXTRA, LANES), jnp.bfloat16),
-            pltpu.SemaphoreType.DMA,
-        ],
+        out_shape=jax.ShapeDtypeStruct((8, members * members // 8), jnp.float32),
+        scratch_shapes=[pltpu.VMEM((wide, wide), jnp.float32)],
         compiler_params=pltpu.CompilerParams(vmem_limit_bytes=16 * 1024 * 1024),
         cost_estimate=pl.CostEstimate(
             flops=2 * wide * wide * SIDE // TILE * D,
@@ -186,22 +168,22 @@
             transcendentals=0,
         ),
         name="gram",
-    )(params, scores)
-
-
-def kernel_of(scale, parts):
-    members = parts.shape[0]
-    half = members // 2
-    packed = jnp.sum(parts.astype(jnp.float32), axis=0)
-    both = [packed[:, q : q + members] for q in range(0, LANES, members)]
-    once = jnp.concatenate(both[:2], axis=0) + jnp.concatenate(both[2:], axis=0)
-    row = lax.broadcasted_iota(jnp.int32, once.shape, 0)
-    col = lax.broadcasted_iota(jnp.int32, once.shape, 1)
-    upper = jnp.where(col > row, once, 0.0)
-    lower = jnp.where(col < row, once, 0.0)
-    lower = jnp.concatenate([lower[:, half:], lower[:, :half]], axis=1)
-    dist = jnp.concatenate([upper, lower], axis=0)
-    return jnp.exp(-(dist + dist.T) / scale[0]).astype(jnp.bfloat16)
+    )(params)
+
+
+def add_over(value, members, bits):
+    got = [
+        lax.ppermute(value, AXES, [(i, i ^ bit) for i in range(members)]) for bit in bits
+    ]
+    return sum(got, value)
+
+
+def kernel_of(scale, packed):
+    members = packed.shape[1] // 4
+    dist = jnp.concatenate(
+        [packed[:, members * q : members * (q + 1)] for q in range(members // 8)], axis=0
+    )
+    return jnp.exp(-dist / scale[0]).astype(jnp.bfloat16)
 
 
 def spreading(kernel):
@@ -217,41 +199,97 @@
     return jnp.where(row == col, full, 0.0)
 
 
-def mix_kernel(scale, scores, params, out):
+def spread_kernel(scale, packed, params, out, mixing):
     members, rows, _ = params.shape
-    wide = members * TILE
-    full = spreading(kernel_of(scale, scores[:, rows : rows + EXTRA, :]))
+    full = spreading(kernel_of(scale, packed[...]))
     ksum = jnp.sum(full, axis=1, keepdims=True)
     mixer = full.astype(jnp.bfloat16)
+    mixing[...] = mixer
     for r in range(0, SIDE, TILE):
         own = tile(params, r)
-        both = dot(mixer, jnp.concatenate([tile(scores, r), own], axis=1), ((1,), (0,)))
-        pushed = ksum * own.astype(jnp.float32) - both[:, D:]
-        both = jnp.concatenate([both[:, :D], pushed], axis=1) * (1.0 / members)
-        both = both.astype(jnp.bfloat16)
-        for g in range(2 * len(GROUPS)):
+        mixed = dot(mixer, own, ((1,), (0,)))
+        pushed = (ksum * own.astype(jnp.float32) - mixed) * (1.0 / members)
+        pushed = pushed.astype(jnp.bfloat16)
+        for g in GROUPS:
             at = g * SIDE + r
-            out[:, at : at + TILE, :] = both[:, g * LANES : (g + 1) * LANES].reshape(
+            out[:, at : at + TILE, :] = pushed[:, g * LANES : (g + 1) * LANES].reshape(
                 members, TILE, LANES
             )
 
 
-def weighted(scale, scores, params):
+def spread_part(scale, packed, params):
     members, rows, _ = params.shape
     wide = members * TILE
     vmem = pl.BlockSpec(memory_space=pltpu.VMEM)
     return pl.pallas_call(
-        mix_kernel,
-        out_shape=jax.ShapeDtypeStruct((members, 2 * rows, LANES), jnp.bfloat16),
+        spread_kernel,
+        out_shape=(
+            pltpu.HBM((members, 2 * rows, LANES), jnp.bfloat16),
+            jax.ShapeDtypeStruct((wide, wide), jnp.bfloat16),
+        ),
+        grid=(1,),
         in_specs=[pl.BlockSpec(memory_space=pltpu.SMEM), vmem, vmem],
+        out_specs=(pl.BlockSpec((members, rows, LANES), lambda i: (0, 1, 0)), vmem),
         compiler_params=pltpu.CompilerParams(vmem_limit_bytes=24 * 1024 * 1024),
         cost_estimate=pl.CostEstimate(
-            flops=4 * wide * wide * SIDE // TILE * D,
-            bytes_accessed=8 * members * rows * LANES,
+            flops=2 * wide * wide * SIDE // TILE * D,
+            bytes_accessed=4 * members * rows * LANES,
             transcendentals=0,
         ),
-        name="mix",
-    )(scale, scores, params)
+        name="spread",
+    )(scale, packed, params)
+
+
+def attract_kernel(mixing, scores, half_done, out, mixed, stores):
+    members, rows, _ = scores.shape
+    step = 2 * TILE
+
+    def store(r, g):
+        here = pl.ds(g * SIDE + r, step)
+        return pltpu.make_async_copy(
+            mixed.at[:, here, :], out.at[:, here, :], stores.at[r // step, g]
+        )
+
+    for r in range(0, SIDE, step):
+        got = jnp.concatenate([tile(scores, r), tile(scores, r + TILE)], axis=1)
+        pulled = dot(mixing[...], got, ((1,), (0,))) * (1.0 / members)
+        pulled = pulled.astype(jnp.bfloat16)
+        for g in GROUPS:
+            for h in range(2):
+                at = g * SIDE + r + h * TILE
+                lanes = h * D + g * LANES
+                mixed[:, at : at + TILE, :] = pulled[:, lanes : lanes + LANES].reshape(
+                    members, TILE, LANES
+                )
+            store(r, g).start()
+    for r in range(0, SIDE, step):
+        for g in GROUPS:
+            store(r, g).wait()
+
+
+def attract_part(mixing, scores, half_done):
+    members, rows, _ = scores.shape
+    wide = members * TILE
+    vmem = pl.BlockSpec(memory_space=pltpu.VMEM)
+    anywhere = pl.BlockSpec(memory_space=pl.ANY)
+    return pl.pallas_call(
+        attract_kernel,
+        out_shape=pltpu.HBM(half_done.shape, half_done.dtype),
+        in_specs=[vmem, vmem, anywhere],
+        out_specs=anywhere,
+        input_output_aliases={2: 0},
+        scratch_shapes=[
+            pltpu.VMEM(scores.shape, jnp.bfloat16),
+            pltpu.SemaphoreType.DMA((SIDE // (2 * TILE), len(GROUPS))),
+        ],
+        compiler_params=pltpu.CompilerParams(vmem_limit_bytes=24 * 1024 * 1024),
+        cost_estimate=pl.CostEstimate(
+            flops=2 * wide * wide * SIDE // TILE * D,
+            bytes_accessed=4 * members * rows * LANES,
+            transcendentals=0,
+        ),
+        name="attract",
+    )(mixing, scores, half_done)
 
 
 def plain_products(params):
@@ -385,16 +423,16 @@
     tiled = members == BLOCKS
     params = exchange(to_blocks(particles_first, particles_second).reshape(cut))
     scores = particle_scores(
-        particles_first[0],
-        particles_second[0],
-        pool_images,
-        pool_targets,
-        batch_index[0],
-        EXTRA if tiled else 0,
+        particles_first[0], particles_second[0], pool_images, pool_targets, batch_index[0]
     )
     if tiled:
-        scores = exchange(add_distances(params, scores))
-        mixed = exchange(weighted(kernel_scale, scores, params))
+        params, scores = lax.optimization_barrier((params, scores))
+        packed = distances(params)
+        scores = exchange(scores)
+        for bits in ((1,), (2, 4, 6), (8, 16, 24)):
+            packed = add_over(packed, members, bits)
+        spread, mixing = spread_part(kernel_scale, packed, params)
+        mixed = exchange(attract_part(mixing, scores, spread))
     else:
         scores = exchange(scores.reshape(cut))
         gram = lax.psum(plain_products(params), AXES)

time: 245 us -> 245 us (level)
  waiting for transfers between devices: 83.2 us -> 70.2 us
  starting transfers between devices: 11.7 us -> 19.8 us
  local copies, waits for them, and re-layouts: 3.26 us -> 6.35 us
    all_to_all x2, waiting for transfers between devices: 83.2 us -> 28.1 us  [exchange(): return lax.all_to_all(blocks, AXES, split_axis=0, concat_axis=0, tiled=True)]
    ppermute x0 -> x7, waiting for transfers between devices: none -> 42.1 us  [add_over(): lax.ppermute(value, AXES, [(i, i ^ bit) for i in range(members)])]
    ppermute x0 -> x7, starting transfers between devices: none -> 8.02 us  [add_over(): lax.ppermute(value, AXES, [(i, i ^ bit) for i in range(members)])]
    unnamed x10 -> x16, local copies, waits for them, and re-layouts: 3.26 us -> 6.35 us
    pallas_call x2 -> x3, Pallas kernels: 7.71 us -> 8.25 us  [the longest x1 3.63 us: spread_part(): pl.pallas_call(spread_kernel, out_shape=(pltpu.HBM((members, 2 * rows, LA...]
  transfers between devices with their start and end apart: 2 -> 9, of which waited for: 2 -> 6; matrix products, arithmetic and copies ran while one was open for 1% -> 1% of each run, Pallas kernels for 9% -> 12%
where the time goes in v8:
time: 245 us; the launch traced here: 244 us
  blocking collectives  110 us (45%)
  waiting for transfers between devices  70.2 us (29%)
  Pallas kernels  36.6 us (15%)
  starting transfers between devices  19.8 us (8%)
  local copies, waits for them, and re-layouts  6.35 us (3%)
    all_to_all x1, blocking collectives, exchange(): return lax.all_to_all(blocks, AXES, split_axis=0, concat_axis=0, tiled=True)  110 us
    ppermute x7, waiting for transfers between devices, add_over(): lax.ppermute(value, AXES, [(i, i ^ bit) for i in range(members)])  42.1 us
    all_to_all x2, waiting for transfers between devices, exchange(): return lax.all_to_all(blocks, AXES, split_axis=0, concat_axis=0, tiled=True)  28.1 us
    pallas_call x1, Pallas kernels, particle_scores(): pl.pallas_call(functools.partial(score_kernel, DATA / count), out_shape=p...  23.1 us
    all_to_all x2, starting transfers between devices, exchange(): return lax.all_to_all(blocks, AXES, split_axis=0, concat_axis=0, tiled=True)  11.8 us
    ppermute x7, starting transfers between devices, add_over(): lax.ppermute(value, AXES, [(i, i ^ bit) for i in range(members)])  8.02 us
    unnamed x16, local copies, waits for them, and re-layouts  6.35 us
  transfers between devices with their start and end apart: 9, of which 6 were waited for; matrix products, arithmetic and copies ran while one was open for 1% of the time, Pallas kernels for 12%

profile of v8, /device:TPU:0, one launch (start us, length us, event | category | flops | bytes accessed | tf_op | source)
XLA Modules:
  0.0 244.1 jit_solution(11099520640419713913)
XLA Ops:
  0.6 2.8 %pack.1 = bf16[32,288,128]{2,1,0:T(8,128)(2,1)} custom-call(bf16[1,384,1536]{2,1,0:T(8,128)(2,1)} %first.1, bf16[1,1536,384]{2,1,0:T(8,128)(2,1)} %second.1), custom_call_target="tpu_custom_call" | custom-call | bytes 4718592 | tf_op jit(solution)/shard_map/pack/pallas_call | solution.py:348
  3.4 7.3 %all-to-all-start = ((bf16[32,288,128]{2,1,0:T(8,128)(2,1)}), bf16[32,288,128]{2,1,0:T(8,128)(2,1)S(1)}, u32[]{:S(2)}, u32[]{:S(2)}) async-start(bf16[32,288,128]{2,1,0:T(8,128)(2,1)} %pack.1), calls=%async_computation | async-start | bytes 4718592 | tf_op jit(solution)/shard_map/all_to_all | solution.py:415
  10.7 0.0 copy-start.6
  10.7 1.5 copy.11.image
  12.3 0.1 copy-done.6
  12.4 0.0 copy-start.3
  12.4 0.0 copy-start.4
  12.4 0.0 copy-start.5
  12.4 0.2 copy.12.target
  12.5 1.1 copy-done.3
  13.6 0.4 copy-done.4
  14.0 0.0 copy-done.5
  14.0 23.1 %score.1 = bf16[32,288,128]{2,1,0:T(8,128)(2,1)} custom-call(s32[8]{0:T(128)S(1)} %bitcast.5, bf16[8,197,384]{2,1,0:T(8,128)(2,1)S(1)} %copy.11.image, bf16[8,197,384]{2,1,0:T(8,128)(2,1)S(1)} %copy.12.target, bf16[384,1536]{1,0:T(8,128)(2,1)S(1)} %bitcast.3, bf16[1536,384]{1,0:T(8,128)(2,1)S(1)} %bitcast.4), custom_call_target="tpu_custom_call" | custom-call | flops 9814671360 | bytes 7139328 | tf_op jit(solution)/shard_map/score/pallas_call | solution.py:104
  37.1 28.1 %all-to-all-done.params = bf16[32,288,128]{2,1,0:T(8,128)(2,1)S(1)} async-done(((bf16[32,288,128]{2,1,0:T(8,128)(2,1)}), bf16[32,288,128]{2,1,0:T(8,128)(2,1)S(1)}, u32[]{:S(2)}, u32[]{:S(2)}) %all-to-all-start) | async-done | bytes 2359328 | tf_op jit(solution)/shard_map/all_to_all | solution.py:415
  65.1 0.0 copy-start
  65.1 1.4 copy-done
  66.6 4.5 %all-to-all-start.1 = ((bf16[32,288,128]{2,1,0:T(8,128)(2,1)}), bf16[32,288,128]{2,1,0:T(8,128)(2,1)S(1)}, u32[]{:S(2)}, u32[]{:S(2)}) async-start(bf16[32,288,128]{2,1,0:T(8,128)(2,1)} %score.1), calls=%async_computation.1 | async-start | bytes 4718592 | tf_op jit(solution)/shard_map/all_to_all | solution.py:415
  71.0 0.0 copy-start.1
  71.0 1.7 copy-done.1
  72.7 0.0 copy-start.2
  72.7 2.2 gram.1
  74.8 0.1 collective-permute-start
  74.9 1.1 collective-permute-done
  76.0 2.5 %collective-permute-start.3 = (f32[8,128]{1,0:T(8,128)S(1)}, f32[8,128]{1,0:T(8,128)S(1)}, u32[]{:S(2)}, u32[]{:S(2)}) collective-permute-start(f32[8,128]{1,0:T(8,128)S(1)} %add.21), channel_id=1, source_target_pairs={{0,6},{1,7},{2,4},{3,5},{4,2},{5,3},{6,0},{7,1},{8,14},{9,15},{10,... | collective-permute-start | bytes 12296 | tf_op jit(solution)/shard_map/ppermute | solution.py:176
  78.5 0.6 collective-permute-start.2
  79.1 0.4 collective-permute-start.1
  79.5 8.1 %collective-permute-done.3 = f32[8,128]{1,0:T(8,128)S(1)} collective-permute-done((f32[8,128]{1,0:T(8,128)S(1)}, f32[8,128]{1,0:T(8,128)S(1)}, u32[]{:S(2)}, u32[]{:S(2)}) %collective-permute-start.3) | collective-permute-done | bytes 4128 | tf_op jit(solution)/shard_map/ppermute | solution.py:176
  87.6 0.6 collective-permute-done.2
  88.2 0.0 collective-permute-done.1
  88.2 2.3 collective-permute-start.6
  90.5 0.0 collective-permute-start.5
  90.5 2.1 collective-permute-start.4
  93.3 20.6 %collective-permute-done.6 = f32[8,128]{1,0:T(8,128)S(1)} collective-permute-done((f32[8,128]{1,0:T(8,128)S(1)}, f32[8,128]{1,0:T(8,128)S(1)}, u32[]{:S(2)}, u32[]{:S(2)}) %collective-permute-start.6) | collective-permute-done | bytes 4128 | tf_op jit(solution)/shard_map/ppermute | solution.py:176
  113.9 11.8 %collective-permute-done.5 = f32[8,128]{1,0:T(8,128)S(1)} collective-permute-done((f32[8,128]{1,0:T(8,128)S(1)}, f32[8,128]{1,0:T(8,128)S(1)}, u32[]{:S(2)}, u32[]{:S(2)}) %collective-permute-start.5) | collective-permute-done | bytes 4128 | tf_op jit(solution)/shard_map/ppermute | solution.py:176
  125.7 0.0 collective-permute-done.4
  125.7 0.0 copy-done.2
  125.7 3.6 %spread.1 = (bf16[32,576,128]{2,1,0:T(8,128)(2,1)}, bf16[512,512]{1,0:T(8,128)(2,1)S(1)}) custom-call(f32[1]{0:T(128)S(6)} %copy.14.scale, f32[8,128]{1,0:T(8,128)S(1)} %add_add_fusion.packed, bf16[32,288,128]{2,1,0:T(8,128)(2,1)S(1)} %copy-done.2), custom_call_target="tpu_custom_call" | custom-call | flops 1207959552 | bytes 4718592 | tf_op jit(solution)/shard_map/spread/pallas_call | solution.py:224
  129.3 0.0 all-to-all-done.1.scores
  129.3 2.5 %attract.1 = bf16[32,576,128]{2,1,0:T(8,128)(2,1)} custom-call(bf16[512,512]{1,0:T(8,128)(2,1)S(1)} %get-tuple-element.9.mixing, bf16[32,288,128]{2,1,0:T(8,128)(2,1)S(1)} %all-to-all-done.1.scores, bf16[32,576,128]{2,1,0:T(8,128)(2,1)} %get-tuple-element.11.half_done), custom_call_target="tpu_custom_call", output_to_operand_aliasing={{}: (2, {})} | custom-call | flops 1207959552 | bytes 4718592 | tf_op jit(solution)/shard_map/attract/pallas_call | solution.py:275
  131.8 109.6 %all_to_all.15.blocks = bf16[32,576,128]{2,1,0:T(8,128)(2,1)S(1)} all-to-all(bf16[32,576,128]{2,1,0:T(8,128)(2,1)} %attract.1), channel_id=1, replica_groups=mesh['wide'=8,'narrow'=4] {'wide','narrow'}, dimensions={0} | all-to-all | bytes 9437184 | tf_op jit(solution)/shard_map/all_to_all | solution.py:415
  241.4 2.5 %unpack.1 = (bf16[1,384,1536]{2,1,0:T(8,128)(2,1)}, bf16[1,1536,384]{2,1,0:T(8,128)(2,1)}, bf16[1,384,1536]{2,1,0:T(8,128)(2,1)}, bf16[1,1536,384]{2,1,0:T(8,128)(2,1)}) custom-call(bf16[32,576,128]{2,1,0:T(8,128)(2,1)S(1)} %all_to_all.15.blocks), custom_call_target="tpu_custom_call" | custom-call | bytes 9437184 | tf_op jit(solution)/shard_map/unpack/pallas_call | solution.py:398
  (3 shorter events, 0.0 us)
Async XLA Ops:
  3.4 61.7 %all-to-all-start = ((bf16[32,288,128]{2,1,0:T(8,128)(2,1)}), bf16[32,288,128]{2,1,0:T(8,128)(2,1)S(1)}, u32[]{:S(2)}, u32[]{:S(2)}) async-start(bf16[32,288,128]{2,1,0:T(8,128)(2,1)} %pack.1), calls=%async_computation | async-start | bytes 4718592 | tf_op jit(solution)/shard_map/all_to_all | solution.py:415
  10.7 1.6 copy-start.6
  12.4 1.3 copy-start.3
  12.4 1.6 copy-start.4
  12.4 1.6 copy-start.5
  65.1 1.4 copy-start
  66.6 62.8 %all-to-all-start.1 = ((bf16[32,288,128]{2,1,0:T(8,128)(2,1)}), bf16[32,288,128]{2,1,0:T(8,128)(2,1)S(1)}, u32[]{:S(2)}, u32[]{:S(2)}) async-start(bf16[32,288,128]{2,1,0:T(8,128)(2,1)} %score.1), calls=%async_computation.1 | async-start | bytes 4718592 | tf_op jit(solution)/shard_map/all_to_all | solution.py:415
  71.0 1.7 copy-start.1
  72.7 53.0 %copy-start.2 = (bf16[32,288,128]{2,1,0:T(8,128)(2,1)S(1)}, bf16[32,288,128]{2,1,0:T(8,128)(2,1)}, u32[]{:S(2)}) copy-start(bf16[32,288,128]{2,1,0:T(8,128)(2,1)} %copy-done) | copy-start | bytes 7077892
  74.8 1.2 collective-permute-start
  76.0 11.6 %collective-permute-start.3 = (f32[8,128]{1,0:T(8,128)S(1)}, f32[8,128]{1,0:T(8,128)S(1)}, u32[]{:S(2)}, u32[]{:S(2)}) collective-permute-start(f32[8,128]{1,0:T(8,128)S(1)} %add.21), channel_id=1, source_target_pairs={{0,6},{1,7},{2,4},{3,5},{4,2},{5,3},{6,0},{7,1},{8,14},{9,15},{10,... | collective-permute-start | bytes 12296 | tf_op jit(solution)/shard_map/ppermute | solution.py:176
  78.5 9.7 %collective-permute-start.2 = (f32[8,128]{1,0:T(8,128)S(1)}, f32[8,128]{1,0:T(8,128)S(1)}, u32[]{:S(2)}, u32[]{:S(2)}) collective-permute-start(f32[8,128]{1,0:T(8,128)S(1)} %add.21), channel_id=1, source_target_pairs={{0,4},{1,5},{2,6},{3,7},{4,0},{5,1},{6,2},{7,3},{8,12},{9,13},{10,... | collective-permute-start | bytes 12296 | tf_op jit(solution)/shard_map/ppermute | solution.py:176
  79.1 9.1 %collective-permute-start.1 = (f32[8,128]{1,0:T(8,128)S(1)}, f32[8,128]{1,0:T(8,128)S(1)}, u32[]{:S(2)}, u32[]{:S(2)}) collective-permute-start(f32[8,128]{1,0:T(8,128)S(1)} %add.21), channel_id=1, source_target_pairs={{0,2},{1,3},{2,0},{3,1},{4,6},{5,7},{6,4},{7,5},{8,10},{9,11},{10,... | collective-permute-start | bytes 12296 | tf_op jit(solution)/shard_map/ppermute | solution.py:176
  88.2 25.7 %collective-permute-start.6 = (f32[8,128]{1,0:T(8,128)S(1)}, f32[8,128]{1,0:T(8,128)S(1)}, u32[]{:S(2)}, u32[]{:S(2)}) collective-permute-start(f32[8,128]{1,0:T(8,128)S(1)} %add_add_fusion.1), channel_id=1, source_target_pairs={{0,24},{1,25},{2,26},{3,27},{4,28},{5,29},{6,30},{7,31},{8,16},{9,... | collective-permute-start | bytes 12296 | tf_op jit(solution)/shard_map/ppermute | solution.py:176
  90.5 35.1 %collective-permute-start.5 = (f32[8,128]{1,0:T(8,128)S(1)}, f32[8,128]{1,0:T(8,128)S(1)}, u32[]{:S(2)}, u32[]{:S(2)}) collective-permute-start(f32[8,128]{1,0:T(8,128)S(1)} %add_add_fusion.1), channel_id=1, source_target_pairs={{0,16},{1,17},{2,18},{3,19},{4,20},{5,21},{6,22},{7,23},{8,24},{9,... | collective-permute-start | bytes 12296 | tf_op jit(solution)/shard_map/ppermute | solution.py:176
  90.5 35.1 %collective-permute-start.4 = (f32[8,128]{1,0:T(8,128)S(1)}, f32[8,128]{1,0:T(8,128)S(1)}, u32[]{:S(2)}, u32[]{:S(2)}) collective-permute-start(f32[8,128]{1,0:T(8,128)S(1)} %add_add_fusion.1), channel_id=1, source_target_pairs={{0,8},{1,9},{2,10},{3,11},{4,12},{5,13},{6,14},{7,15},{8,0},{9,1},... | collective-permute-start | bytes 12296 | tf_op jit(solution)/shard_map/ppermute | solution.py:176

commit v9 on v7

--- a/solution.py
+++ b/solution.py
@@ -22,7 +22,6 @@
 SIDE = 2 * EDGE
 GROUPS = range(D // LANES)
 ROWS = SIDE * len(GROUPS)
-EXTRA = 8
 
 gelu_c = math.sqrt(2.0 / math.pi)
 isd = 1.0 / math.sqrt(D)
@@ -98,13 +97,13 @@
                 put(out, c * (D // EDGE) + r, EDGE, score[r * EDGE : (r + 1) * EDGE, :])
 
 
-def particle_scores(first, second, images, targets, picks, extra):
+def particle_scores(first, second, images, targets, picks):
     count = picks.shape[0]
     rows = count * PAD
     bf = jnp.bfloat16
     return pl.pallas_call(
         functools.partial(score_kernel, DATA / count),
-        out_shape=pltpu.HBM((BLOCKS, ROWS + extra, LANES), bf),
+        out_shape=pltpu.HBM((BLOCKS, ROWS, LANES), bf),
         grid_spec=pltpu.PrefetchScalarGridSpec(
             num_scalar_prefetch=1,
             grid=(count,),
@@ -135,10 +134,9 @@
     )(picks, images, targets, first, second)
 
 
-def gram_kernel(params, scores, out, total, parts, sem):
+def gram_kernel(params, out, total):
     members, rows, _ = params.shape
     wide = members * TILE
-    half = members // 2
     total[...] = jnp.zeros_like(total)
     for r in range(0, SIDE, TILE):
         part = tile(params, r)
@@ -153,32 +151,16 @@
     col = lax.broadcasted_iota(jnp.int32, gram.shape, 1)
     own = jnp.where(row == col, gram, 0.0)
     dist = jnp.sum(own, axis=1, keepdims=True) + jnp.sum(own, axis=0, keepdims=True) - 2.0 * gram
-    low = jnp.concatenate([dist[half:, half:], dist[half:, :half]], axis=1)
-    once = jnp.where(col[:half] > row[:half], dist[:half], low)
-    high = once.astype(jnp.bfloat16).astype(jnp.float32)
-    rest = once - high
-    both = [x[q : q + EXTRA] for x in (high, rest) for q in range(0, half, EXTRA)]
-    packed = jnp.concatenate(both, axis=1).astype(jnp.bfloat16)
-    parts[...] = jnp.broadcast_to(packed[None], parts.shape)
-    copy = pltpu.make_async_copy(parts, out.at[:, pl.ds(rows, EXTRA), :], sem)
-    copy.start()
-    copy.wait()
-
-
-def add_distances(params, scores):
+    out[...] = jnp.concatenate([dist[q : q + 8] for q in range(0, members, 8)], axis=1)
+
+
+def distances(params):
     members, rows, _ = params.shape
     wide = members * TILE
     return pl.pallas_call(
         gram_kernel,
-        out_shape=pltpu.HBM(scores.shape, scores.dtype),
-        in_specs=[pl.BlockSpec(memory_space=pltpu.VMEM), pl.BlockSpec(memory_space=pl.ANY)],
-        out_specs=pl.BlockSpec(memory_space=pl.ANY),
-        input_output_aliases={1: 0},
-        scratch_shapes=[
-            pltpu.VMEM((wide, wide), jnp.float32),
-            pltpu.VMEM((members, EXTRA, LANES), jnp.bfloat16),
-            pltpu.SemaphoreType.DMA,
-        ],
+        out_shape=jax.ShapeDtypeStruct((8, members * members // 8), jnp.float32),
+        scratch_shapes=[pltpu.VMEM((wide, wide), jnp.float32)],
         compiler_params=pltpu.CompilerParams(vmem_limit_bytes=16 * 1024 * 1024),
         cost_estimate=pl.CostEstimate(
             flops=2 * wide * wide * SIDE // TILE * D,
@@ -186,22 +168,22 @@
             transcendentals=0,
         ),
         name="gram",
-    )(params, scores)
-
-
-def kernel_of(scale, parts):
-    members = parts.shape[0]
-    half = members // 2
-    packed = jnp.sum(parts.astype(jnp.float32), axis=0)
-    both = [packed[:, q : q + members] for q in range(0, LANES, members)]
-    once = jnp.concatenate(both[:2], axis=0) + jnp.concatenate(both[2:], axis=0)
-    row = lax.broadcasted_iota(jnp.int32, once.shape, 0)
-    col = lax.broadcasted_iota(jnp.int32, once.shape, 1)
-    upper = jnp.where(col > row, once, 0.0)
-    lower = jnp.where(col < row, once, 0.0)
-    lower = jnp.concatenate([lower[:, half:], lower[:, :half]], axis=1)
-    dist = jnp.concatenate([upper, lower], axis=0)
-    return jnp.exp(-(dist + dist.T) / scale[0]).astype(jnp.bfloat16)
+    )(params)
+
+
+def add_over(value, members, bits):
+    got = [
+        lax.ppermute(value, AXES, [(i, i ^ bit) for i in range(members)]) for bit in bits
+    ]
+    return sum(got, value)
+
+
+def kernel_of(scale, packed):
+    members = packed.shape[1] // 4
+    dist = jnp.concatenate(
+        [packed[:, members * q : members * (q + 1)] for q in range(members // 8)], axis=0
+    )
+    return jnp.exp(-dist / scale[0]).astype(jnp.bfloat16)
 
 
 def spreading(kernel):
@@ -217,10 +199,10 @@
     return jnp.where(row == col, full, 0.0)
 
 
-def mix_kernel(scale, scores, params, out):
+def mix_kernel(scale, packed, scores, params, out):
     members, rows, _ = params.shape
     wide = members * TILE
-    full = spreading(kernel_of(scale, scores[:, rows : rows + EXTRA, :]))
+    full = spreading(kernel_of(scale, packed[...]))
     ksum = jnp.sum(full, axis=1, keepdims=True)
     mixer = full.astype(jnp.bfloat16)
     for r in range(0, SIDE, TILE):
@@ -236,14 +218,14 @@
             )
 
 
-def weighted(scale, scores, params):
+def weighted(scale, packed, scores, params):
     members, rows, _ = params.shape
     wide = members * TILE
     vmem = pl.BlockSpec(memory_space=pltpu.VMEM)
     return pl.pallas_call(
         mix_kernel,
         out_shape=jax.ShapeDtypeStruct((members, 2 * rows, LANES), jnp.bfloat16),
-        in_specs=[pl.BlockSpec(memory_space=pltpu.SMEM), vmem, vmem],
+        in_specs=[pl.BlockSpec(memory_space=pltpu.SMEM), vmem, vmem, vmem],
         compiler_params=pltpu.CompilerParams(vmem_limit_bytes=24 * 1024 * 1024),
         cost_estimate=pl.CostEstimate(
             flops=4 * wide * wide * SIDE // TILE * D,
@@ -251,7 +233,7 @@
             transcendentals=0,
         ),
         name="mix",
-    )(scale, scores, params)
+    )(scale, packed, scores, params)
 
 
 def plain_products(params):
@@ -385,16 +367,14 @@
     tiled = members == BLOCKS
     params = exchange(to_blocks(particles_first, particles_second).reshape(cut))
     scores = particle_scores(
-        particles_first[0],
-        particles_second[0],
-        pool_images,
-        pool_targets,
-        batch_index[0],
-        EXTRA if tiled else 0,
+        particles_first[0], particles_second[0], pool_images, pool_targets, batch_index[0]
     )
     if tiled:
-        scores = exchange(add_distances(params, scores))
-        mixed = exchange(weighted(kernel_scale, scores, params))
+        packed = distances(params)
+        scores = exchange(scores)
+        for bits in ((1,), (2, 4, 6), (8, 16, 24)):
+            packed = add_over(packed, members, bits)
+        mixed = exchange(weighted(kernel_scale, packed, scores, params))
     else:
         scores = exchange(scores.reshape(cut))
         gram = lax.psum(plain_products(params), AXES)

time: 245 us -> 241 us (0.984)
  waiting for transfers between devices: 83.2 us -> 71.8 us
  starting transfers between devices: 11.7 us -> 19.8 us
    all_to_all x2, waiting for transfers between devices: 83.2 us -> 28.1 us  [exchange(): return lax.all_to_all(blocks, AXES, split_axis=0, concat_axis=0, tiled=True)]
    ppermute x0 -> x7, waiting for transfers between devices: none -> 43.7 us  [add_over(): lax.ppermute(value, AXES, [(i, i ^ bit) for i in range(members)])]
    ppermute x0 -> x7, starting transfers between devices: none -> 8.12 us  [add_over(): lax.ppermute(value, AXES, [(i, i ^ bit) for i in range(members)])]
  transfers between devices with their start and end apart: 2 -> 9, of which waited for: 2 -> 6; matrix products, arithmetic and copies ran while one was open for 1% -> 1% of each run, Pallas kernels for 9% -> 10%
where the time goes in v9:
time: 241 us
  blocking collectives  109 us (45%)
  waiting for transfers between devices  71.8 us (30%)
  Pallas kernels  35.1 us (15%)
  starting transfers between devices  19.8 us (8%)
  local copies, waits for them, and re-layouts  3.26 us (1%)
    all_to_all x1, blocking collectives, exchange(): return lax.all_to_all(blocks, AXES, split_axis=0, concat_axis=0, tiled=True)  109 us
    ppermute x7, waiting for transfers between devices, add_over(): lax.ppermute(value, AXES, [(i, i ^ bit) for i in range(members)])  43.7 us
    all_to_all x2, waiting for transfers between devices, exchange(): return lax.all_to_all(blocks, AXES, split_axis=0, concat_axis=0, tiled=True)  28.1 us
    pallas_call x1, Pallas kernels, particle_scores(): pl.pallas_call(functools.partial(score_kernel, DATA / count), out_shape=p...  23.1 us
    all_to_all x2, starting transfers between devices, exchange(): return lax.all_to_all(blocks, AXES, split_axis=0, concat_axis=0, tiled=True)  11.7 us
    ppermute x7, starting transfers between devices, add_over(): lax.ppermute(value, AXES, [(i, i ^ bit) for i in range(members)])  8.12 us
  transfers between devices with their start and end apart: 9, of which 6 were waited for; matrix products, arithmetic and copies ran while one was open for 1% of the time, Pallas kernels for 10%

profile of v9, /device:TPU:0, one launch (start us, length us, event | category | flops | bytes accessed | tf_op | source)
XLA Modules:
  0.0 240.8 jit_solution(8417860122083481343)
XLA Ops:
  0.6 2.7 %pack.1 = bf16[32,288,128]{2,1,0:T(8,128)(2,1)} custom-call(bf16[1,384,1536]{2,1,0:T(8,128)(2,1)} %first.1, bf16[1,1536,384]{2,1,0:T(8,128)(2,1)} %second.1), custom_call_target="tpu_custom_call" | custom-call | bytes 4718592 | tf_op jit(solution)/shard_map/pack/pallas_call | solution.py:292
  3.4 7.3 %all-to-all-start = ((bf16[32,288,128]{2,1,0:T(8,128)(2,1)}), bf16[32,288,128]{2,1,0:T(8,128)(2,1)S(1)}, u32[]{:S(2)}, u32[]{:S(2)}) async-start(bf16[32,288,128]{2,1,0:T(8,128)(2,1)} %pack.1), calls=%async_computation | async-start | bytes 4718592 | tf_op jit(solution)/shard_map/all_to_all | solution.py:359
  10.7 0.0 copy-start.3
  10.7 1.5 copy.10.image
  12.2 0.1 copy-done.3
  12.3 0.0 copy-start
  12.3 0.0 copy-start.1
  12.3 0.0 copy-start.2
  12.3 0.2 copy.11.target
  12.5 1.1 copy-done
  13.6 0.4 copy-done.1
  13.9 0.0 copy-done.2
  13.9 23.1 %score.1 = bf16[32,288,128]{2,1,0:T(8,128)(2,1)} custom-call(s32[8]{0:T(128)S(1)} %bitcast.5, bf16[8,197,384]{2,1,0:T(8,128)(2,1)S(1)} %copy.10.image, bf16[8,197,384]{2,1,0:T(8,128)(2,1)S(1)} %copy.11.target, bf16[384,1536]{1,0:T(8,128)(2,1)S(1)} %bitcast.3, bf16[1536,384]{1,0:T(8,128)(2,1)S(1)} %bitcast.4), custom_call_target="tpu_custom_call" | custom-call | flops 9814671360 | bytes 7139328 | tf_op jit(solution)/shard_map/score/pallas_call | solution.py:104
  37.0 28.1 %all-to-all-done.params = bf16[32,288,128]{2,1,0:T(8,128)(2,1)S(1)} async-done(((bf16[32,288,128]{2,1,0:T(8,128)(2,1)}), bf16[32,288,128]{2,1,0:T(8,128)(2,1)S(1)}, u32[]{:S(2)}, u32[]{:S(2)}) %all-to-all-start) | async-done | bytes 2359328 | tf_op jit(solution)/shard_map/all_to_all | solution.py:359
  65.1 4.4 %all-to-all-start.1 = ((bf16[32,288,128]{2,1,0:T(8,128)(2,1)}), bf16[32,288,128]{2,1,0:T(8,128)(2,1)}, u32[]{:S(2)}, u32[]{:S(2)}) async-start(bf16[32,288,128]{2,1,0:T(8,128)(2,1)} %score.1), calls=%async_computation.1 | async-start | bytes 4718592 | tf_op jit(solution)/shard_map/all_to_all | solution.py:359
  69.5 2.2 gram.1
  71.6 0.2 collective-permute-start
  71.8 1.0 collective-permute-done
  72.8 2.6 %collective-permute-start.3 = (f32[8,128]{1,0:T(8,128)S(1)}, f32[8,128]{1,0:T(8,128)S(1)}, u32[]{:S(2)}, u32[]{:S(2)}) collective-permute-start(f32[8,128]{1,0:T(8,128)S(1)} %add.21), channel_id=1, source_target_pairs={{0,6},{1,7},{2,4},{3,5},{4,2},{5,3},{6,0},{7,1},{8,14},{9,15},{10,... | collective-permute-start | bytes 12296 | tf_op jit(solution)/shard_map/ppermute | solution.py:176
  75.4 0.6 collective-permute-start.2
  76.0 0.3 collective-permute-start.1
  76.3 9.9 %collective-permute-done.3 = f32[8,128]{1,0:T(8,128)S(1)} collective-permute-done((f32[8,128]{1,0:T(8,128)S(1)}, f32[8,128]{1,0:T(8,128)S(1)}, u32[]{:S(2)}, u32[]{:S(2)}) %collective-permute-start.3) | collective-permute-done | bytes 4128 | tf_op jit(solution)/shard_map/ppermute | solution.py:176
  86.2 0.3 collective-permute-done.2
  86.5 0.0 collective-permute-done.1
  86.5 2.5 %collective-permute-start.6 = (f32[8,128]{1,0:T(8,128)S(1)}, f32[8,128]{1,0:T(8,128)S(1)}, u32[]{:S(2)}, u32[]{:S(2)}) collective-permute-start(f32[8,128]{1,0:T(8,128)S(1)} %add_add_fusion.1), channel_id=1, source_target_pairs={{0,24},{1,25},{2,26},{3,27},{4,28},{5,29},{6,30},{7,31},{8,16},{9,... | collective-permute-start | bytes 12296 | tf_op jit(solution)/shard_map/ppermute | solution.py:176
  89.1 0.0 collective-permute-start.5
  89.1 1.9 collective-permute-start.4
  91.6 20.8 %collective-permute-done.6 = f32[8,128]{1,0:T(8,128)S(1)} collective-permute-done((f32[8,128]{1,0:T(8,128)S(1)}, f32[8,128]{1,0:T(8,128)S(1)}, u32[]{:S(2)}, u32[]{:S(2)}) %collective-permute-start.6) | collective-permute-done | bytes 4128 | tf_op jit(solution)/shard_map/ppermute | solution.py:176
  112.5 11.7 %collective-permute-done.5 = f32[8,128]{1,0:T(8,128)S(1)} collective-permute-done((f32[8,128]{1,0:T(8,128)S(1)}, f32[8,128]{1,0:T(8,128)S(1)}, u32[]{:S(2)}, u32[]{:S(2)}) %collective-permute-start.5) | collective-permute-done | bytes 4128 | tf_op jit(solution)/shard_map/ppermute | solution.py:176
  124.1 0.0 collective-permute-done.4
  124.2 0.0 all-to-all-done.1.scores
  124.2 4.6 %mix.1 = bf16[32,576,128]{2,1,0:T(8,128)(2,1)S(1)} custom-call(f32[1]{0:T(128)S(6)} %copy.12.scale, f32[8,128]{1,0:T(8,128)S(1)} %add_add_fusion.packed, bf16[32,288,128]{2,1,0:T(8,128)(2,1)} %all-to-all-done.1.scores, bf16[32,288,128]{2,1,0:T(8,128)(2,1)S(1)} %all-to-all-done.params), custom_call_target="tpu_custom_call" | custom-call | flops 2415919104 | bytes 9437184 | tf_op jit(solution)/shard_map/mix/pallas_call | solution.py:225
  128.8 109.5 %all_to_all.15.blocks = bf16[32,576,128]{2,1,0:T(8,128)(2,1)S(1)} all-to-all(bf16[32,576,128]{2,1,0:T(8,128)(2,1)S(1)} %mix.1), channel_id=1, replica_groups=mesh['wide'=8,'narrow'=4] {'wide','narrow'}, dimensions={0} | all-to-all | bytes 9437184 | tf_op jit(solution)/shard_map/all_to_all | solution.py:359
  238.3 2.5 %unpack.1 = (bf16[1,384,1536]{2,1,0:T(8,128)(2,1)}, bf16[1,1536,384]{2,1,0:T(8,128)(2,1)}, bf16[1,384,1536]{2,1,0:T(8,128)(2,1)}, bf16[1,1536,384]{2,1,0:T(8,128)(2,1)}) custom-call(bf16[32,576,128]{2,1,0:T(8,128)(2,1)S(1)} %all_to_all.15.blocks), custom_call_target="tpu_custom_call" | custom-call | bytes 9437184 | tf_op jit(solution)/shard_map/unpack/pallas_call | solution.py:342
  (3 shorter events, 0.0 us)
Async XLA Ops:
  3.4 61.7 %all-to-all-start = ((bf16[32,288,128]{2,1,0:T(8,128)(2,1)}), bf16[32,288,128]{2,1,0:T(8,128)(2,1)S(1)}, u32[]{:S(2)}, u32[]{:S(2)}) async-start(bf16[32,288,128]{2,1,0:T(8,128)(2,1)} %pack.1), calls=%async_computation | async-start | bytes 4718592 | tf_op jit(solution)/shard_map/all_to_all | solution.py:359
  10.7 1.6 copy-start.3
  12.3 1.3 copy-start
  12.3 1.6 copy-start.1
  12.3 1.6 copy-start.2
  65.1 59.1 %all-to-all-start.1 = ((bf16[32,288,128]{2,1,0:T(8,128)(2,1)}), bf16[32,288,128]{2,1,0:T(8,128)(2,1)}, u32[]{:S(2)}, u32[]{:S(2)}) async-start(bf16[32,288,128]{2,1,0:T(8,128)(2,1)} %score.1), calls=%async_computation.1 | async-start | bytes 4718592 | tf_op jit(solution)/shard_map/all_to_all | solution.py:359
  71.6 1.2 collective-permute-start
  72.8 13.4 %collective-permute-start.3 = (f32[8,128]{1,0:T(8,128)S(1)}, f32[8,128]{1,0:T(8,128)S(1)}, u32[]{:S(2)}, u32[]{:S(2)}) collective-permute-start(f32[8,128]{1,0:T(8,128)S(1)} %add.21), channel_id=1, source_target_pairs={{0,6},{1,7},{2,4},{3,5},{4,2},{5,3},{6,0},{7,1},{8,14},{9,15},{10,... | collective-permute-start | bytes 12296 | tf_op jit(solution)/shard_map/ppermute | solution.py:176
  75.4 11.1 %collective-permute-start.2 = (f32[8,128]{1,0:T(8,128)S(1)}, f32[8,128]{1,0:T(8,128)S(1)}, u32[]{:S(2)}, u32[]{:S(2)}) collective-permute-start(f32[8,128]{1,0:T(8,128)S(1)} %add.21), channel_id=1, source_target_pairs={{0,4},{1,5},{2,6},{3,7},{4,0},{5,1},{6,2},{7,3},{8,12},{9,13},{10,... | collective-permute-start | bytes 12296 | tf_op jit(solution)/shard_map/ppermute | solution.py:176
  76.0 10.5 %collective-permute-start.1 = (f32[8,128]{1,0:T(8,128)S(1)}, f32[8,128]{1,0:T(8,128)S(1)}, u32[]{:S(2)}, u32[]{:S(2)}) collective-permute-start(f32[8,128]{1,0:T(8,128)S(1)} %add.21), channel_id=1, source_target_pairs={{0,2},{1,3},{2,0},{3,1},{4,6},{5,7},{6,4},{7,5},{8,10},{9,11},{10,... | collective-permute-start | bytes 12296 | tf_op jit(solution)/shard_map/ppermute | solution.py:176
  86.5 25.9 %collective-permute-start.6 = (f32[8,128]{1,0:T(8,128)S(1)}, f32[8,128]{1,0:T(8,128)S(1)}, u32[]{:S(2)}, u32[]{:S(2)}) collective-permute-start(f32[8,128]{1,0:T(8,128)S(1)} %add_add_fusion.1), channel_id=1, source_target_pairs={{0,24},{1,25},{2,26},{3,27},{4,28},{5,29},{6,30},{7,31},{8,16},{9,... | collective-permute-start | bytes 12296 | tf_op jit(solution)/shard_map/ppermute | solution.py:176
  89.1 35.1 %collective-permute-start.5 = (f32[8,128]{1,0:T(8,128)S(1)}, f32[8,128]{1,0:T(8,128)S(1)}, u32[]{:S(2)}, u32[]{:S(2)}) collective-permute-start(f32[8,128]{1,0:T(8,128)S(1)} %add_add_fusion.1), channel_id=1, source_target_pairs={{0,16},{1,17},{2,18},{3,19},{4,20},{5,21},{6,22},{7,23},{8,24},{9,... | collective-permute-start | bytes 12296 | tf_op jit(solution)/shard_map/ppermute | solution.py:176
  89.1 35.1 %collective-permute-start.4 = (f32[8,128]{1,0:T(8,128)S(1)}, f32[8,128]{1,0:T(8,128)S(1)}, u32[]{:S(2)}, u32[]{:S(2)}) collective-permute-start(f32[8,128]{1,0:T(8,128)S(1)} %add_add_fusion.1), channel_id=1, source_target_pairs={{0,8},{1,9},{2,10},{3,11},{4,12},{5,13},{6,14},{7,15},{8,0},{9,1},... | collective-permute-start | bytes 12296 | tf_op jit(solution)/shard_map/ppermute | solution.py:176

commit v10 on v9

--- a/solution.py
+++ b/solution.py
@@ -22,6 +22,9 @@
 SIDE = 2 * EDGE
 GROUPS = range(D // LANES)
 ROWS = SIDE * len(GROUPS)
+MAIN = ROWS - EDGE
+PLANES = 4
+PLANE = BLOCKS // PLANES
 
 gelu_c = math.sqrt(2.0 / math.pi)
 isd = 1.0 / math.sqrt(D)
@@ -32,21 +35,35 @@
     return lax.dot_general(a, b, (dims, ((), ())), preferred_element_type=jnp.float32)
 
 
-def put(out, block, row, value):
+def put(main, side, block, row, value):
     for g in GROUPS:
         at = g * SIDE + row
-        out[block, at : at + EDGE, :] = value[:, g * LANES : (g + 1) * LANES]
-
-
-def tile(ref, r):
-    members = ref.shape[0]
-    parts = [ref[:, g * SIDE + r : g * SIDE + r + TILE, :] for g in GROUPS]
-    return jnp.concatenate([p.reshape(members * TILE, LANES) for p in parts], axis=1)
+        part = value[:, g * LANES : (g + 1) * LANES]
+        if at < MAIN:
+            main[block, at : at + EDGE, :] = part
+        else:
+            side[block, at - MAIN : at - MAIN + EDGE, :] = part
+
+
+def by_plane(me, side, outs):
+    for k in range(BLOCKS):
+        outs[k // PLANE][k % PLANE] = side[k ^ me[0]]
+
+
+def tile(main, side, r):
+    parts = []
+    for g in GROUPS:
+        at = g * SIDE + r
+        ref, at = (main, at) if at < MAIN else (side, at - MAIN)
+        parts.append(ref[:, at : at + TILE, :].reshape(ref.shape[0] * TILE, LANES))
+    return jnp.concatenate(parts, axis=1)
 
 
 def score_kernel(
-    factor, picks, image, target, first, second, out, xs, ts, normed, hidden, deriv, delta, back
+    factor, picks, me, image, target, first, second, *refs
 ):
+    outs, side = refs[1 : 1 + PLANES], refs[1 + PLANES]
+    out, (xs, ts, normed, hidden, deriv, delta, back) = refs[0], refs[2 + PLANES :]
     step = pl.program_id(0)
     images = pl.num_programs(0)
     rows = pl.ds(pl.multiple_of(step * PAD, PAD), PAD)
@@ -90,31 +107,41 @@
             grad = dot(normed[...], back[:, cols], ((0,), (0,))) * (-factor * isd)
             score = (grad - first[:, cols].astype(jnp.float32)).astype(jnp.bfloat16)
             for r in range(D // EDGE):
-                put(out, r * COLS + c, 0, score[r * EDGE : (r + 1) * EDGE, :])
+                put(out, side, r * COLS + c, 0, score[r * EDGE : (r + 1) * EDGE, :])
             grad = dot(hidden[:, cols], delta[...], ((0,), (0,))) * (-factor * isf)
             score = (grad - second[cols, :].astype(jnp.float32)).astype(jnp.bfloat16)
             for r in range(D // EDGE):
-                put(out, c * (D // EDGE) + r, EDGE, score[r * EDGE : (r + 1) * EDGE, :])
-
-
-def particle_scores(first, second, images, targets, picks):
+                at = c * (D // EDGE) + r
+                put(out, side, at, EDGE, score[r * EDGE : (r + 1) * EDGE, :])
+        by_plane(me, side, outs)
+
+
+def side_shapes(rows):
+    return (jax.ShapeDtypeStruct((PLANE, rows, LANES), jnp.bfloat16),) * PLANES
+
+
+def particle_scores(first, second, images, targets, picks, me):
     count = picks.shape[0]
     rows = count * PAD
     bf = jnp.bfloat16
     return pl.pallas_call(
         functools.partial(score_kernel, DATA / count),
-        out_shape=pltpu.HBM((BLOCKS, ROWS, LANES), bf),
+        out_shape=(pltpu.HBM((BLOCKS, MAIN, LANES), bf), *side_shapes(EDGE)),
         grid_spec=pltpu.PrefetchScalarGridSpec(
-            num_scalar_prefetch=1,
+            num_scalar_prefetch=2,
             grid=(count,),
             in_specs=[
-                pl.BlockSpec((1, S, D), lambda b, picks: (picks[b], 0, 0)),
-                pl.BlockSpec((1, S, D), lambda b, picks: (picks[b], 0, 0)),
-                pl.BlockSpec((D, FF), lambda b, picks: (0, 0)),
-                pl.BlockSpec((FF, D), lambda b, picks: (0, 0)),
+                pl.BlockSpec((1, S, D), lambda b, picks, me: (picks[b], 0, 0)),
+                pl.BlockSpec((1, S, D), lambda b, picks, me: (picks[b], 0, 0)),
+                pl.BlockSpec((D, FF), lambda b, picks, me: (0, 0)),
+                pl.BlockSpec((FF, D), lambda b, picks, me: (0, 0)),
             ],
-            out_specs=pl.BlockSpec((BLOCKS, ROWS, LANES), lambda b, picks: (0, 0, 0)),
+            out_specs=(
+                pl.BlockSpec((BLOCKS, MAIN, LANES), lambda b, picks, me: (0, 0, 0)),
+                *[pl.BlockSpec((PLANE, EDGE, LANES), lambda b, picks, me: (0, 0, 0))] * PLANES,
+            ),
             scratch_shapes=[
+                pltpu.VMEM((BLOCKS, EDGE, LANES), bf),
                 pltpu.VMEM((PAD, D), jnp.float32),
                 pltpu.VMEM((PAD, D), jnp.float32),
                 pltpu.VMEM((rows, D), bf),
@@ -131,15 +158,15 @@
             transcendentals=count * PAD * FF,
         ),
         name="score",
-    )(picks, images, targets, first, second)
-
-
-def gram_kernel(params, out, total):
-    members, rows, _ = params.shape
+    )(picks, me, images, targets, first, second)
+
+
+def gram_kernel(main, side, out, total):
+    members = main.shape[0]
     wide = members * TILE
     total[...] = jnp.zeros_like(total)
     for r in range(0, SIDE, TILE):
-        part = tile(params, r)
+        part = tile(main, side, r)
         total[...] += dot(part, part, ((1,), (1,)))
     at = lax.broadcasted_iota(jnp.int32, (wide, wide), 0) % TILE
     to = lax.broadcasted_iota(jnp.int32, (wide, wide), 1) % TILE
@@ -154,8 +181,8 @@
     out[...] = jnp.concatenate([dist[q : q + 8] for q in range(0, members, 8)], axis=1)
 
 
-def distances(params):
-    members, rows, _ = params.shape
+def distances(main, side):
+    members = main.shape[0]
     wide = members * TILE
     return pl.pallas_call(
         gram_kernel,
@@ -164,11 +191,11 @@
         compiler_params=pltpu.CompilerParams(vmem_limit_bytes=16 * 1024 * 1024),
         cost_estimate=pl.CostEstimate(
             flops=2 * wide * wide * SIDE // TILE * D,
-            bytes_accessed=2 * members * rows * LANES,
+            bytes_accessed=2 * members * ROWS * LANES,
             transcendentals=0,
         ),
         name="gram",
-    )(params)
+    )(main, side)
 
 
 def add_over(value, members, bits):
@@ -199,41 +226,106 @@
     return jnp.where(row == col, full, 0.0)
 
 
-def mix_kernel(scale, packed, scores, params, out):
-    members, rows, _ = params.shape
+def mix_kernel(scale, me, packed, scores, side_scores, params, side_params, out, *refs):
+    outs, side = refs[:PLANES], refs[PLANES]
+    members = params.shape[0]
     wide = members * TILE
     full = spreading(kernel_of(scale, packed[...]))
     ksum = jnp.sum(full, axis=1, keepdims=True)
     mixer = full.astype(jnp.bfloat16)
     for r in range(0, SIDE, TILE):
-        own = tile(params, r)
-        both = dot(mixer, jnp.concatenate([tile(scores, r), own], axis=1), ((1,), (0,)))
+        own = tile(params, side_params, r)
+        both = jnp.concatenate([tile(scores, side_scores, r), own], axis=1)
+        both = dot(mixer, both, ((1,), (0,)))
         pushed = ksum * own.astype(jnp.float32) - both[:, D:]
         both = jnp.concatenate([both[:, :D], pushed], axis=1) * (1.0 / members)
         both = both.astype(jnp.bfloat16)
-        for g in range(2 * len(GROUPS)):
-            at = g * SIDE + r
-            out[:, at : at + TILE, :] = both[:, g * LANES : (g + 1) * LANES].reshape(
-                members, TILE, LANES
-            )
-
-
-def weighted(scale, packed, scores, params):
-    members, rows, _ = params.shape
+        for which in range(2):
+            for g in GROUPS:
+                at = g * SIDE + r
+                lanes = which * D + g * LANES
+                part = both[:, lanes : lanes + LANES].reshape(members, TILE, LANES)
+                if at < MAIN:
+                    at += which * MAIN
+                    out[:, at : at + TILE, :] = part
+                else:
+                    at += which * EDGE - MAIN
+                    side[:, at : at + TILE, :] = part
+    by_plane(me, side, outs)
+
+
+def weighted(scale, me, packed, scores, side_scores, params, side_params):
+    members = params.shape[0]
     wide = members * TILE
     vmem = pl.BlockSpec(memory_space=pltpu.VMEM)
+    smem = pl.BlockSpec(memory_space=pltpu.SMEM)
+    main = jax.ShapeDtypeStruct((members, 2 * MAIN, LANES), jnp.bfloat16)
     return pl.pallas_call(
         mix_kernel,
-        out_shape=jax.ShapeDtypeStruct((members, 2 * rows, LANES), jnp.bfloat16),
-        in_specs=[pl.BlockSpec(memory_space=pltpu.SMEM), vmem, vmem, vmem],
+        out_shape=(main, *side_shapes(2 * EDGE)),
+        in_specs=[smem, smem] + [vmem] * 5,
+        scratch_shapes=[pltpu.VMEM((members, 2 * EDGE, LANES), jnp.bfloat16)],
         compiler_params=pltpu.CompilerParams(vmem_limit_bytes=24 * 1024 * 1024),
         cost_estimate=pl.CostEstimate(
             flops=4 * wide * wide * SIDE // TILE * D,
-            bytes_accessed=8 * members * rows * LANES,
+            bytes_accessed=8 * members * ROWS * LANES,
             transcendentals=0,
         ),
         name="mix",
-    )(scale, packed, scores, params)
+    )(scale, me, packed, scores, side_scores, params, side_params)
+
+
+def plane_kernel(*refs):
+    for z in range(PLANES):
+        for q in range(PLANE):
+            refs[PLANES + q // 2][z, q % 2] = refs[z][q]
+
+
+def core_kernel(*refs):
+    for q in range(PLANE // 2):
+        for z in range(PLANES):
+            for c in range(2):
+                refs[PLANE // 2 + c][q, z] = refs[q][z, c]
+
+
+def settle_kernel(me, near, far, out):
+    for c, ref in enumerate((near, far)):
+        for q in range(PLANE // 2):
+            for z in range(PLANES):
+                out[(z * PLANE + 2 * q + c) ^ me[0]] = ref[q, z]
+
+
+def regroup(body, name, shapes, *arrays, me=()):
+    vmem = pl.BlockSpec(memory_space=pltpu.VMEM)
+    size = sum(math.prod(x.shape) for x in arrays)
+    return pl.pallas_call(
+        body,
+        out_shape=shapes,
+        in_specs=[pl.BlockSpec(memory_space=pltpu.SMEM)] * len(me) + [vmem] * len(arrays),
+        compiler_params=pltpu.CompilerParams(vmem_limit_bytes=16 * 1024 * 1024),
+        cost_estimate=pl.CostEstimate(flops=0, bytes_accessed=4 * size, transcendentals=0),
+        name=name,
+    )(*me, *arrays)
+
+
+def swap(value, bits):
+    pairs = [(i, i ^ bits) for i in range(BLOCKS)]
+    return lax.ppermute(value, AXES, pairs)
+
+
+def across_planes(parts):
+    return parts[:1] + [swap(x, z * PLANE) for z, x in enumerate(parts) if z]
+
+
+def within_plane(parts, me):
+    rows = parts[0].shape[1]
+    shape = jax.ShapeDtypeStruct((PLANES, 2, rows, LANES), jnp.bfloat16)
+    parts = regroup(plane_kernel, "plane", (shape,) * (PLANE // 2), *parts)
+    parts = parts[:1] + tuple(swap(x, 2 * q) for q, x in enumerate(parts) if q)
+    shape = jax.ShapeDtypeStruct((PLANE // 2, PLANES, rows, LANES), jnp.bfloat16)
+    near, far = regroup(core_kernel, "core", (shape,) * 2, *parts)
+    shape = jax.ShapeDtypeStruct((BLOCKS, rows, LANES), jnp.bfloat16)
+    return regroup(settle_kernel, "settle", shape, near, swap(far, 1), me=(me,))
 
 
 def plain_products(params):
@@ -258,7 +350,9 @@
 TALL = FF // STEPS
 
 
-def pack_kernel(first, second, out, wide, tall, packed, loads, stores):
+def pack_kernel(me, first, second, out, *refs):
+    outs, (wide, tall, packed, side, loads, stores) = refs[:PLANES], refs[PLANES:]
+
     def load(d):
         return (
             pltpu.make_async_copy(
@@ -280,34 +374,40 @@
         for copy in load(d):
             copy.wait()
         for c in range(COLS):
-            put(packed, d * COLS + c, 0, wide[d, :, c * D : (c + 1) * D])
-            put(packed, d * COLS + c, EDGE, tall[d, c * EDGE : (c + 1) * EDGE, :])
+            put(packed, side, d * COLS + c, 0, wide[d, :, c * D : (c + 1) * D])
+            put(packed, side, d * COLS + c, EDGE, tall[d, c * EDGE : (c + 1) * EDGE, :])
         store(d).start()
+    by_plane(me, side, outs)
     for d in range(STEPS):
         store(d).wait()
 
 
-def to_blocks(first, second):
+def to_blocks(first, second, me):
     bf = jnp.bfloat16
     return pl.pallas_call(
         pack_kernel,
-        out_shape=pltpu.HBM((BLOCKS, ROWS, LANES), bf),
-        in_specs=[pl.BlockSpec(memory_space=pl.ANY)] * 2,
-        out_specs=pl.BlockSpec(memory_space=pl.ANY),
+        out_shape=(pltpu.HBM((BLOCKS, MAIN, LANES), bf), *side_shapes(EDGE)),
+        in_specs=[pl.BlockSpec(memory_space=pltpu.SMEM)]
+        + [pl.BlockSpec(memory_space=pl.ANY)] * 2,
+        out_specs=(
+            pl.BlockSpec(memory_space=pl.ANY),
+            *[pl.BlockSpec(memory_space=pltpu.VMEM)] * PLANES,
+        ),
         scratch_shapes=[
             pltpu.VMEM((STEPS, EDGE, FF), bf),
             pltpu.VMEM((STEPS, TALL, D), bf),
-            pltpu.VMEM((BLOCKS, ROWS, LANES), bf),
+            pltpu.VMEM((BLOCKS, MAIN, LANES), bf),
+            pltpu.VMEM((BLOCKS, EDGE, LANES), bf),
             pltpu.SemaphoreType.DMA((2, STEPS)),
             pltpu.SemaphoreType.DMA((STEPS,)),
         ],
         compiler_params=pltpu.CompilerParams(vmem_limit_bytes=56 * 1024 * 1024),
         cost_estimate=pl.CostEstimate(flops=0, bytes_accessed=8 * D * FF, transcendentals=0),
         name="pack",
-    )(first, second)
-
-
-def unpack_kernel(blocks, first_a, second_a, first_s, second_s, wide, tall, stores):
+    )(me, first, second)
+
+
+def unpack_kernel(main, side, first_a, second_a, first_s, second_s, wide, tall, stores):
     def store(which, d):
         first, second = ((first_a, second_a), (first_s, second_s))[which]
         return (
@@ -323,12 +423,12 @@
         for d in range(STEPS):
             for c in range(COLS):
                 for g in GROUPS:
-                    at = which * ROWS + g * SIDE
+                    b, at = d * COLS + c, which * MAIN + g * SIDE
                     lanes = slice(c * D + g * LANES, c * D + (g + 1) * LANES)
-                    wide[which, d, :, lanes] = blocks[d * COLS + c, at : at + EDGE, :]
-                    tall[which, d, c * EDGE : (c + 1) * EDGE, g * LANES : (g + 1) * LANES] = blocks[
-                        d * COLS + c, at + EDGE : at + SIDE, :
-                    ]
+                    wide[which, d, :, lanes] = main[b, at : at + EDGE, :]
+                    ref, at = (main, at + EDGE) if g * SIDE + EDGE < MAIN else (side, which * EDGE)
+                    lanes = slice(g * LANES, (g + 1) * LANES)
+                    tall[which, d, c * EDGE : (c + 1) * EDGE, lanes] = ref[b, at : at + EDGE, :]
             for copy in store(which, d):
                 copy.start()
     for which in range(2):
@@ -337,12 +437,12 @@
                 copy.wait()
 
 
-def from_blocks(blocks):
+def from_blocks(main, side):
     bf = jnp.bfloat16
     return pl.pallas_call(
         unpack_kernel,
         out_shape=(pltpu.HBM((1, D, FF), bf), pltpu.HBM((1, FF, D), bf)) * 2,
-        in_specs=[pl.BlockSpec(memory_space=pltpu.VMEM)],
+        in_specs=[pl.BlockSpec(memory_space=pltpu.VMEM)] * 2,
         out_specs=(pl.BlockSpec(memory_space=pl.ANY),) * 4,
         scratch_shapes=[
             pltpu.VMEM((2, STEPS, EDGE, FF), bf),
@@ -352,7 +452,7 @@
         compiler_params=pltpu.CompilerParams(vmem_limit_bytes=24 * 1024 * 1024),
         cost_estimate=pl.CostEstimate(flops=0, bytes_accessed=16 * D * FF, transcendentals=0),
         name="unpack",
-    )(blocks)
+    )(main, side)
 
 
 def exchange(blocks):
@@ -363,25 +463,37 @@
     particles_first, particles_second, pool_images, pool_targets, batch_index, kernel_scale
 ):
     members = math.prod(lax.axis_size(name) for name in AXES)
-    cut = (members, BLOCKS * ROWS // members, LANES)
     tiled = members == BLOCKS
-    params = exchange(to_blocks(particles_first, particles_second).reshape(cut))
-    scores = particle_scores(
-        particles_first[0], particles_second[0], pool_images, pool_targets, batch_index[0]
+    me = lax.axis_index(AXES) if tiled else 0
+    me = jnp.full((1,), me, jnp.int32)
+    params, *side_params = to_blocks(particles_first, particles_second, me)
+    scores, *side_scores = particle_scores(
+        particles_first[0], particles_second[0], pool_images, pool_targets, batch_index[0], me
     )
     if tiled:
-        packed = distances(params)
-        scores = exchange(scores)
+        params, scores = exchange(params), exchange(scores)
+        side_params, side_scores = across_planes(side_params), across_planes(side_scores)
+        params, side_params, side_scores = lax.optimization_barrier(
+            (params, side_params, side_scores)
+        )
+        side_params = within_plane(side_params, me)
+        side_scores = within_plane(side_scores, me)
+        packed = distances(params, side_params)
         for bits in ((1,), (2, 4, 6), (8, 16, 24)):
             packed = add_over(packed, members, bits)
-        mixed = exchange(weighted(kernel_scale, packed, scores, params))
-    else:
-        scores = exchange(scores.reshape(cut))
-        gram = lax.psum(plain_products(params), AXES)
-        parts = plain_weighted(gram, kernel_scale, params, scores)
-        mixed = [exchange(x).reshape(BLOCKS, ROWS, LANES) for x in parts]
-        mixed = jnp.concatenate(mixed, axis=1)
-    return from_blocks(mixed)
+        main, *side = weighted(
+            kernel_scale, me, packed, scores, side_scores, params, side_params
+        )
+        return from_blocks(exchange(main), within_plane(across_planes(side), me))
+    cut = (members, BLOCKS * ROWS // members, LANES)
+    params = jnp.concatenate([params, jnp.concatenate(side_params)], axis=1)
+    scores = jnp.concatenate([scores, jnp.concatenate(side_scores)], axis=1)
+    params, scores = exchange(params.reshape(cut)), exchange(scores.reshape(cut))
+    gram = lax.psum(plain_products(params), AXES)
+    parts = plain_weighted(gram, kernel_scale, params, scores)
+    parts = [exchange(x).reshape(BLOCKS, ROWS, LANES) for x in parts]
+    main = jnp.concatenate([x[:, :MAIN] for x in parts], axis=1)
+    return from_blocks(main, jnp.concatenate([x[:, MAIN:] for x in parts], axis=1))
 
 
 def solution(mesh):

time: 241 us -> 284 us (1.18)
  waiting for transfers between devices: 71.8 us -> 186 us
  blocking collectives: 109 us -> 0 us
  starting transfers between devices: 19.8 us -> 50.2 us
  Pallas kernels: 35.1 us -> 38.1 us
    ppermute x0 -> x21, waiting for transfers between devices: none -> 161 us  [swap(): return lax.ppermute(value, AXES, pairs)]
    all_to_all x1 -> x0, blocking collectives: 109 us -> none  [exchange(): return lax.all_to_all(blocks, AXES, split_axis=0, concat_axis=0, tiled=True)]
    ppermute x7, waiting for transfers between devices: 43.7 us -> 5.5 us  [add_over(): lax.ppermute(value, AXES, [(i, i ^ bit) for i in range(members)])]
    ppermute x0 -> x21, starting transfers between devices: none -> 27.2 us  [swap(): return lax.ppermute(value, AXES, pairs)]
    all_to_all x2 -> x3, waiting for transfers between devices: 28.1 us -> 20 us  [exchange(): return lax.all_to_all(blocks, AXES, split_axis=0, concat_axis=0, tiled=True)]
    all_to_all x2 -> x3, starting transfers between devices: 11.7 us -> 15.1 us  [exchange(): return lax.all_to_all(blocks, AXES, split_axis=0, concat_axis=0, tiled=True)]
    pallas_call x3 -> x12, Pallas kernels: 30.4 us -> 31.3 us  [the longest x1 23 us: particle_scores(): pl.pallas_call(functools.partial(score_kernel, DATA / count), out_shape=(...]
  transfers between devices with their start and end apart: 9 -> 31, of which waited for: 6 -> 20; matrix products, arithmetic and copies ran while one was open for 1% -> 0% of each run, Pallas kernels for 10% -> 9%
where the time goes in v10:
time: 284 us; the launch traced here: 281 us
  waiting for transfers between devices  186 us (65%)
  starting transfers between devices  50.2 us (18%)
  Pallas kernels  38.1 us (13%)
  local copies, waits for them, and re-layouts  4.81 us (2%)
    ppermute x21, waiting for transfers between devices, swap(): return lax.ppermute(value, AXES, pairs)  161 us
    ppermute x21, starting transfers between devices, swap(): return lax.ppermute(value, AXES, pairs)  27.2 us
    pallas_call x1, Pallas kernels, particle_scores(): pl.pallas_call(functools.partial(score_kernel, DATA / count), out_shape=(...  23 us
    all_to_all x3, waiting for transfers between devices, exchange(): return lax.all_to_all(blocks, AXES, split_axis=0, concat_axis=0, tiled=True)  20 us
    all_to_all x3, starting transfers between devices, exchange(): return lax.all_to_all(blocks, AXES, split_axis=0, concat_axis=0, tiled=True)  15.1 us
    ppermute x7, starting transfers between devices, add_over(): lax.ppermute(value, AXES, [(i, i ^ bit) for i in range(members)])  7.88 us
  transfers between devices with their start and end apart: 31, of which 20 were waited for; matrix products, arithmetic and copies ran while one was open for 0% of the time, Pallas kernels for 9%

profile of v10, /device:TPU:0, one launch (start us, length us, event | category | flops | bytes accessed | tf_op | source)
XLA Modules:
  0.0 281.1 jit_solution(3116452728272426002)
XLA Ops:
  0.6 3.4 %pack.1 = (bf16[32,240,128]{2,1,0:T(8,128)(2,1)}, bf16[8,48,128]{2,1,0:T(8,128)(2,1)}, bf16[8,48,128]{2,1,0:T(8,128)(2,1)}, bf16[8,48,128]{2,1,0:T(8,128)(2,1)}, bf16[8,48,128]{2,1,0:T(8,128)(2,1)}) custom-call(s32[1]{0:T(128)} %bitcast.me, bf16[1,384,1536]{2,1,0:T(8,128)(2,1)} %first.1, bf16[1,1536,384]{2,1,0:T(8,128)(2,1)} %second.1), custom_call_target="tpu_custom_call" | custom-call | bytes 4718592 | tf_op jit(solution)/shard_map/pack/pallas_call | solution.py:387
  4.1 7.3 %all-to-all-start = ((bf16[32,240,128]{2,1,0:T(8,128)(2,1)}), bf16[32,240,128]{2,1,0:T(8,128)(2,1)S(1)}, u32[]{:S(2)}, u32[]{:S(2)}) async-start(bf16[32,240,128]{2,1,0:T(8,128)(2,1)} %get-tuple-element.46), calls=%async_computation | async-start | bytes 3932160 | tf_op jit(solution)/shard_map/all_to_all | solution.py:459
  11.6 1.1 copy-done.6
  12.8 1.1 copy-done.1
  14.3 23.0 %score.1 = (bf16[32,240,128]{2,1,0:T(8,128)(2,1)}, bf16[8,48,128]{2,1,0:T(8,128)(2,1)S(1)}, bf16[8,48,128]{2,1,0:T(8,128)(2,1)S(1)}, bf16[8,48,128]{2,1,0:T(8,128)(2,1)S(1)}, bf16[8,48,128]{2,1,0:T(8,128)(2,1)S(1)}) custom-call(s32[8]{0:T(128)S(1)} %bitcast.6, s32[1]{0:T(128)} %bitcast.me, bf16[8,197,384]{2,1,0:T(8,128)(2,1)S(1)} %copy.10.image, ...), custom_call_target="tpu_custom_call" | custom-call | flops 9814671360 | bytes 7139328 | tf_op jit(solution)/shard_map/score/pallas_call | solution.py:127
  37.3 20.0 %all-to-all-done.main.params = bf16[32,240,128]{2,1,0:T(8,128)(2,1)S(1)} async-done(((bf16[32,240,128]{2,1,0:T(8,128)(2,1)}), bf16[32,240,128]{2,1,0:T(8,128)(2,1)S(1)}, u32[]{:S(2)}, u32[]{:S(2)}) %all-to-all-start) | async-done | bytes 1966112 | tf_op jit(solution)/shard_map/all_to_all | solution.py:459
  57.3 4.3 %all-to-all-start.1 = ((bf16[32,240,128]{2,1,0:T(8,128)(2,1)}), bf16[32,240,128]{2,1,0:T(8,128)(2,1)}, u32[]{:S(2)}, u32[]{:S(2)}) async-start(bf16[32,240,128]{2,1,0:T(8,128)(2,1)} %get-tuple-element.66), calls=%async_computation.1 | async-start | bytes 3932160 | tf_op jit(solution)/shard_map/all_to_all | solution.py:459
  61.6 1.6 collective-permute-start.3
  63.2 2.4 collective-permute-start.4
  66.1 0.6 collective-permute-start
  66.7 3.3 %collective-permute-start.1 = (bf16[8,48,128]{2,1,0:T(8,128)(2,1)S(1)}, bf16[8,48,128]{2,1,0:T(8,128)(2,1)S(1)}, u32[]{:S(2)}, u32[]{:S(2)}) collective-permute-start(bf16[8,48,128]{2,1,0:T(8,128)(2,1)S(1)} %copy-done.8), channel_id=1, source_target_pairs={{0,16},{1,17},{2,18},{3,19},{4,20},{5,21},{6,22},{7,23},{8,24},{9,... | collective-permute-start | bytes 294920 | tf_op jit(solution)/shard_map/ppermute | solution.py:313
  70.0 26.3 %collective-permute-done.3.refs_1_ = bf16[8,48,128]{2,1,0:T(8,128)(2,1)S(1)} collective-permute-done((bf16[8,48,128]{2,1,0:T(8,128)(2,1)S(1)}, bf16[8,48,128]{2,1,0:T(8,128)(2,1)S(1)}, u32[]{:S(2)}, u32[]{:S(2)}) %collective-permute-start.3) | collective-permute-done | bytes 98336 | tf_op jit(solution)/shard_map/ppermute | solution.py:313
  96.3 3.5 %collective-permute-start.2 = (bf16[8,48,128]{2,1,0:T(8,128)(2,1)S(1)}, bf16[8,48,128]{2,1,0:T(8,128)(2,1)S(1)}, u32[]{:S(2)}, u32[]{:S(2)}) collective-permute-start(bf16[8,48,128]{2,1,0:T(8,128)(2,1)S(1)} %copy-done.7), channel_id=1, source_target_pairs={{0,24},{1,25},{2,26},{3,27},{4,28},{5,29},{6,30},{7,31},{8,16},{9,... | collective-permute-start | bytes 294920 | tf_op jit(solution)/shard_map/ppermute | solution.py:313
  99.8 18.5 %collective-permute-done.4.refs_2_ = bf16[8,48,128]{2,1,0:T(8,128)(2,1)S(1)} collective-permute-done((bf16[8,48,128]{2,1,0:T(8,128)(2,1)S(1)}, bf16[8,48,128]{2,1,0:T(8,128)(2,1)S(1)}, u32[]{:S(2)}, u32[]{:S(2)}) %collective-permute-start.4) | collective-permute-done | bytes 98336 | tf_op jit(solution)/shard_map/ppermute | solution.py:313
  118.3 4.2 %collective-permute-done.1.refs_2_ = bf16[8,48,128]{2,1,0:T(8,128)(2,1)S(1)} collective-permute-done((bf16[8,48,128]{2,1,0:T(8,128)(2,1)S(1)}, bf16[8,48,128]{2,1,0:T(8,128)(2,1)S(1)}, u32[]{:S(2)}, u32[]{:S(2)}) %collective-permute-start.1) | collective-permute-done | bytes 98336 | tf_op jit(solution)/shard_map/ppermute | solution.py:313
  122.5 1.5 collective-permute-start.6
  124.1 1.5 collective-permute-start.7
  126.1 1.2 collective-permute-done.6.refs_1_
  127.3 1.5 collective-permute-done.7.refs_2_
  128.8 2.3 collective-permute-done.8.refs_3_
  131.8 1.2 collective-permute-start.18
  133.0 1.8 collective-permute-start.19
  134.8 2.2 gram.1
  137.0 1.2 collective-permute-done.10
  138.1 1.1 collective-permute-start.13
  139.3 0.8 collective-permute-start.12
  140.1 1.5 collective-permute-start.11
  141.8 0.9 collective-permute-done.13
  142.9 0.8 collective-permute-done.11
  143.7 1.8 collective-permute-start.16
  145.5 2.0 collective-permute-start.15
  149.1 0.9 collective-permute-done.15
  150.0 1.1 collective-permute-done.14
  151.2 4.5 %mix.1 = (bf16[32,480,128]{2,1,0:T(8,128)(2,1)S(1)}, bf16[8,96,128]{2,1,0:T(8,128)(2,1)S(1)}, bf16[8,96,128]{2,1,0:T(8,128)(2,1)S(1)}, bf16[8,96,128]{2,1,0:T(8,128)(2,1)S(1)}, bf16[8,96,128]{2,1,0:T(8,128)(2,1)S(1)}) custom-call(f32[1]{0:T(128)S(6)} %copy.12.scale, s32[1]{0:T(128)} %bitcast.me, f32[8,128]{1,0:T(8,128)S(1)} %add_add_fusion.packed, ...), custom_call_target="tpu_custom_call" | custom-call | flops 2415919104 | bytes 9437184 | tf_op jit(solution)/shard_map/mix/pallas_call | solution.py:263
  155.8 1.9 copy-done
  157.7 3.6 %all-to-all-start.2 = ((bf16[32,480,128]{2,1,0:T(8,128)(2,1)}), bf16[32,480,128]{2,1,0:T(8,128)(2,1)}, u32[]{:S(2)}, u32[]{:S(2)}) async-start(bf16[32,480,128]{2,1,0:T(8,128)(2,1)} %copy-done), calls=%async_computation.2 | async-start | bytes 7864320 | tf_op jit(solution)/shard_map/all_to_all | solution.py:459
  161.2 1.7 collective-permute-start.21
  163.0 2.4 collective-permute-start.22
  165.7 65.1 %collective-permute-done.21.refs_1_ = bf16[8,96,128]{2,1,0:T(8,128)(2,1)S(1)} collective-permute-done((bf16[8,96,128]{2,1,0:T(8,128)(2,1)S(1)}, bf16[8,96,128]{2,1,0:T(8,128)(2,1)S(1)}, u32[]{:S(2)}, u32[]{:S(2)}) %collective-permute-start.21) | collective-permute-done | bytes 196640 | tf_op jit(solution)/shard_map/ppermute | solution.py:313
  230.8 32.1 %collective-permute-done.22.refs_2_ = bf16[8,96,128]{2,1,0:T(8,128)(2,1)S(1)} collective-permute-done((bf16[8,96,128]{2,1,0:T(8,128)(2,1)S(1)}, bf16[8,96,128]{2,1,0:T(8,128)(2,1)S(1)}, u32[]{:S(2)}, u32[]{:S(2)}) %collective-permute-start.22) | collective-permute-done | bytes 196640 | tf_op jit(solution)/shard_map/ppermute | solution.py:313
  263.0 1.0 collective-permute-start.24
  263.9 1.5 collective-permute-start.25
  265.4 1.1 collective-permute-start.26
  266.5 3.4 %collective-permute-done.24.refs_1_ = bf16[4,2,96,128]{3,2,1,0:T(8,128)(2,1)S(1)} collective-permute-done((bf16[4,2,96,128]{3,2,1,0:T(8,128)(2,1)S(1)}, bf16[4,2,96,128]{3,2,1,0:T(8,128)(2,1)S(1)}, u32[]{:S(2)}, u32[]{:S(2)}) %collective-permute-start.24) | collective-permute-done | bytes 196640 | tf_op jit(solution)/shard_map/ppermute | solution.py:313
  270.0 1.8 collective-permute-done.25.refs_2_
  271.7 2.7 collective-permute-done.26.refs_3_
  274.5 1.7 collective-permute-done.27.far
  276.3 4.6 %unpack.1 = (bf16[1,384,1536]{2,1,0:T(8,128)(2,1)}, bf16[1,1536,384]{2,1,0:T(8,128)(2,1)}, bf16[1,384,1536]{2,1,0:T(8,128)(2,1)}, bf16[1,1536,384]{2,1,0:T(8,128)(2,1)}) custom-call(bf16[32,480,128]{2,1,0:T(8,128)(2,1)} %all-to-all-done.2.main, bf16[32,96,128]{2,1,0:T(8,128)(2,1)S(1)} %settle.5.side), custom_call_target="tpu_custom_call" | custom-call | bytes 9437184 | tf_op jit(solution)/shard_map/unpack/pallas_call | solution.py:442
  (53 shorter events, 4.1 us)
Async XLA Ops:
  4.1 7.3 %copy-start.5 = (bf16[8,197,384]{2,0,1:T(8,128)(2,1)S(1)}, bf16[8,197,384]{2,0,1:T(8,128)(2,1)}, u32[]{:S(2)}) copy-start(bf16[8,197,384]{2,0,1:T(8,128)(2,1)} %param.8) | copy-start | bytes 3631108
  4.1 53.3 %all-to-all-start = ((bf16[32,240,128]{2,1,0:T(8,128)(2,1)}), bf16[32,240,128]{2,1,0:T(8,128)(2,1)S(1)}, u32[]{:S(2)}, u32[]{:S(2)}) async-start(bf16[32,240,128]{2,1,0:T(8,128)(2,1)} %get-tuple-element.46), calls=%async_computation | async-start | bytes 3932160 | tf_op jit(solution)/shard_map/all_to_all | solution.py:459
  11.4 1.3 copy-start.6
  12.7 1.3 copy-start.1
  12.7 1.6 copy-start.2
  12.7 1.6 copy-start.4
  57.3 8.8 %copy-start.9 = (bf16[8,48,128]{2,1,0:T(8,128)(2,1)S(1)}, bf16[8,48,128]{2,1,0:T(8,128)(2,1)}, u32[]{:S(2)}) copy-start(bf16[8,48,128]{2,1,0:T(8,128)(2,1)} %get-tuple-element.48) | copy-start | bytes 294916
  57.3 9.4 %copy-start.8 = (bf16[8,48,128]{2,1,0:T(8,128)(2,1)S(1)}, bf16[8,48,128]{2,1,0:T(8,128)(2,1)}, u32[]{:S(2)}) copy-start(bf16[8,48,128]{2,1,0:T(8,128)(2,1)} %get-tuple-element.49) | copy-start | bytes 294916
  57.3 39.0 %copy-start.7 = (bf16[8,48,128]{2,1,0:T(8,128)(2,1)S(1)}, bf16[8,48,128]{2,1,0:T(8,128)(2,1)}, u32[]{:S(2)}) copy-start(bf16[8,48,128]{2,1,0:T(8,128)(2,1)} %get-tuple-element.50) | copy-start | bytes 294916
  57.3 65.2 %copy-start.3 = (bf16[8,48,128]{2,1,0:T(8,128)(2,1)S(1)}, bf16[8,48,128]{2,1,0:T(8,128)(2,1)}, u32[]{:S(2)}) copy-start(bf16[8,48,128]{2,1,0:T(8,128)(2,1)} %get-tuple-element.56.refs_0_) | copy-start | bytes 294916
  57.3 93.9 %all-to-all-start.1 = ((bf16[32,240,128]{2,1,0:T(8,128)(2,1)}), bf16[32,240,128]{2,1,0:T(8,128)(2,1)}, u32[]{:S(2)}, u32[]{:S(2)}) async-start(bf16[32,240,128]{2,1,0:T(8,128)(2,1)} %get-tuple-element.66), calls=%async_computation.1 | async-start | bytes 3932160 | tf_op jit(solution)/shard_map/all_to_all | solution.py:459
  61.6 34.7 %collective-permute-start.3 = (bf16[8,48,128]{2,1,0:T(8,128)(2,1)S(1)}, bf16[8,48,128]{2,1,0:T(8,128)(2,1)S(1)}, u32[]{:S(2)}, u32[]{:S(2)}) collective-permute-start(bf16[8,48,128]{2,1,0:T(8,128)(2,1)S(1)} %get-tuple-element.52), channel_id=1, source_target_pairs={{0,8},{1,9},{2,10},{3,11},{4,12},{5,13},{6,14},{7,15},{8,0},{9,1},... | collective-permute-start | bytes 294920 | tf_op jit(solution)/shard_map/ppermute | solution.py:313
  63.2 55.1 %collective-permute-start.4 = (bf16[8,48,128]{2,1,0:T(8,128)(2,1)S(1)}, bf16[8,48,128]{2,1,0:T(8,128)(2,1)S(1)}, u32[]{:S(2)}, u32[]{:S(2)}) collective-permute-start(bf16[8,48,128]{2,1,0:T(8,128)(2,1)S(1)} %get-tuple-element.53), channel_id=1, source_target_pairs={{0,16},{1,17},{2,18},{3,19},{4,20},{5,21},{6,22},{7,23},{8,24},{9,... | collective-permute-start | bytes 294920 | tf_op jit(solution)/shard_map/ppermute | solution.py:313
  65.6 52.6 %collective-permute-start.5 = (bf16[8,48,128]{2,1,0:T(8,128)(2,1)S(1)}, bf16[8,48,128]{2,1,0:T(8,128)(2,1)S(1)}, u32[]{:S(2)}, u32[]{:S(2)}) collective-permute-start(bf16[8,48,128]{2,1,0:T(8,128)(2,1)S(1)} %get-tuple-element.54), channel_id=1, source_target_pairs={{0,24},{1,25},{2,26},{3,27},{4,28},{5,29},{6,30},{7,31},{8,16},{9,... | collective-permute-start | bytes 294920 | tf_op jit(solution)/shard_map/ppermute | solution.py:313
  66.1 52.2 %collective-permute-start = (bf16[8,48,128]{2,1,0:T(8,128)(2,1)S(1)}, bf16[8,48,128]{2,1,0:T(8,128)(2,1)S(1)}, u32[]{:S(2)}, u32[]{:S(2)}) collective-permute-start(bf16[8,48,128]{2,1,0:T(8,128)(2,1)S(1)} %copy-done.9), channel_id=1, source_target_pairs={{0,8},{1,9},{2,10},{3,11},{4,12},{5,13},{6,14},{7,15},{8,0},{9,1},... | collective-permute-start | bytes 294920 | tf_op jit(solution)/shard_map/ppermute | solution.py:313
  66.7 55.8 %collective-permute-start.1 = (bf16[8,48,128]{2,1,0:T(8,128)(2,1)S(1)}, bf16[8,48,128]{2,1,0:T(8,128)(2,1)S(1)}, u32[]{:S(2)}, u32[]{:S(2)}) collective-permute-start(bf16[8,48,128]{2,1,0:T(8,128)(2,1)S(1)} %copy-done.8), channel_id=1, source_target_pairs={{0,16},{1,17},{2,18},{3,19},{4,20},{5,21},{6,22},{7,23},{8,24},{9,... | collective-permute-start | bytes 294920 | tf_op jit(solution)/shard_map/ppermute | solution.py:313
  96.3 26.2 %collective-permute-start.2 = (bf16[8,48,128]{2,1,0:T(8,128)(2,1)S(1)}, bf16[8,48,128]{2,1,0:T(8,128)(2,1)S(1)}, u32[]{:S(2)}, u32[]{:S(2)}) collective-permute-start(bf16[8,48,128]{2,1,0:T(8,128)(2,1)S(1)} %copy-done.7), channel_id=1, source_target_pairs={{0,24},{1,25},{2,26},{3,27},{4,28},{5,29},{6,30},{7,31},{8,16},{9,... | collective-permute-start | bytes 294920 | tf_op jit(solution)/shard_map/ppermute | solution.py:313
  122.5 4.8 %collective-permute-start.6 = (bf16[4,2,48,128]{3,2,1,0:T(8,128)(2,1)S(1)}, bf16[4,2,48,128]{3,2,1,0:T(8,128)(2,1)S(1)}, u32[]{:S(2)}, u32[]{:S(2)}) collective-permute-start(bf16[4,2,48,128]{3,2,1,0:T(8,128)(2,1)S(1)} %get-tuple-element.61), channel_id=1, source_target_pairs={{0,2},{1,3},{2,0},{3,1},{4,6},{5,7},{6,4},{7,5},{8,10},{9,11},{10,... | collective-permute-start | bytes 294920 | tf_op jit(solution)/shard_map/ppermute | solution.py:313
  124.1 4.7 %collective-permute-start.7 = (bf16[4,2,48,128]{3,2,1,0:T(8,128)(2,1)S(1)}, bf16[4,2,48,128]{3,2,1,0:T(8,128)(2,1)S(1)}, u32[]{:S(2)}, u32[]{:S(2)}) collective-permute-start(bf16[4,2,48,128]{3,2,1,0:T(8,128)(2,1)S(1)} %get-tuple-element.62), channel_id=1, source_target_pairs={{0,4},{1,5},{2,6},{3,7},{4,0},{5,1},{6,2},{7,3},{8,12},{9,13},{10,... | collective-permute-start | bytes 294920 | tf_op jit(solution)/shard_map/ppermute | solution.py:313
  125.5 5.5 %collective-permute-start.8 = (bf16[4,2,48,128]{3,2,1,0:T(8,128)(2,1)S(1)}, bf16[4,2,48,128]{3,2,1,0:T(8,128)(2,1)S(1)}, u32[]{:S(2)}, u32[]{:S(2)}) collective-permute-start(bf16[4,2,48,128]{3,2,1,0:T(8,128)(2,1)S(1)} %get-tuple-element.63), channel_id=1, source_target_pairs={{0,6},{1,7},{2,4},{3,5},{4,2},{5,3},{6,0},{7,1},{8,14},{9,15},{10,... | collective-permute-start | bytes 294920 | tf_op jit(solution)/shard_map/ppermute | solution.py:313
  131.1 3.7 %collective-permute-start.9 = (bf16[4,4,48,128]{3,2,1,0:T(8,128)(2,1)S(1)}, bf16[4,4,48,128]{3,2,1,0:T(8,128)(2,1)S(1)}, u32[]{:S(2)}, u32[]{:S(2)}) collective-permute-start(bf16[4,4,48,128]{3,2,1,0:T(8,128)(2,1)S(1)} %get-tuple-element.65), channel_id=1, source_target_pairs={{0,1},{1,0},{2,3},{3,2},{4,5},{5,4},{6,7},{7,6},{8,9},{9,8},{10,11... | collective-permute-start | bytes 589832 | tf_op jit(solution)/shard_map/ppermute | solution.py:313
  131.2 8.9 %collective-permute-start.17 = (bf16[4,2,48,128]{3,2,1,0:T(8,128)(2,1)S(1)}, bf16[4,2,48,128]{3,2,1,0:T(8,128)(2,1)S(1)}, u32[]{:S(2)}, u32[]{:S(2)}) collective-permute-start(bf16[4,2,48,128]{3,2,1,0:T(8,128)(2,1)S(1)} %get-tuple-element.72), channel_id=1, source_target_pairs={{0,2},{1,3},{2,0},{3,1},{4,6},{5,7},{6,4},{7,5},{8,10},{9,11},{10,... | collective-permute-start | bytes 294920 | tf_op jit(solution)/shard_map/ppermute | solution.py:313
  131.8 9.9 %collective-permute-start.18 = (bf16[4,2,48,128]{3,2,1,0:T(8,128)(2,1)S(1)}, bf16[4,2,48,128]{3,2,1,0:T(8,128)(2,1)S(1)}, u32[]{:S(2)}, u32[]{:S(2)}) collective-permute-start(bf16[4,2,48,128]{3,2,1,0:T(8,128)(2,1)S(1)} %get-tuple-element.73), channel_id=1, source_target_pairs={{0,4},{1,5},{2,6},{3,7},{4,0},{5,1},{6,2},{7,3},{8,12},{9,13},{10,... | collective-permute-start | bytes 294920 | tf_op jit(solution)/shard_map/ppermute | solution.py:313
  133.0 8.7 %collective-permute-start.19 = (bf16[4,2,48,128]{3,2,1,0:T(8,128)(2,1)S(1)}, bf16[4,2,48,128]{3,2,1,0:T(8,128)(2,1)S(1)}, u32[]{:S(2)}, u32[]{:S(2)}) collective-permute-start(bf16[4,2,48,128]{3,2,1,0:T(8,128)(2,1)S(1)} %get-tuple-element.74), channel_id=1, source_target_pairs={{0,6},{1,7},{2,4},{3,5},{4,2},{5,3},{6,0},{7,1},{8,14},{9,15},{10,... | collective-permute-start | bytes 294920 | tf_op jit(solution)/shard_map/ppermute | solution.py:313
  137.0 1.2 collective-permute-start.10
  138.1 4.5 %collective-permute-start.13 = (f32[8,128]{1,0:T(8,128)S(1)}, f32[8,128]{1,0:T(8,128)S(1)}, u32[]{:S(2)}, u32[]{:S(2)}) collective-permute-start(f32[8,128]{1,0:T(8,128)S(1)} %add.25), channel_id=1, source_target_pairs={{0,6},{1,7},{2,4},{3,5},{4,2},{5,3},{6,0},{7,1},{8,14},{9,15},{10,... | collective-permute-start | bytes 12296 | tf_op jit(solution)/shard_map/ppermute | solution.py:203
  139.3 3.6 %collective-permute-start.12 = (f32[8,128]{1,0:T(8,128)S(1)}, f32[8,128]{1,0:T(8,128)S(1)}, u32[]{:S(2)}, u32[]{:S(2)}) collective-permute-start(f32[8,128]{1,0:T(8,128)S(1)} %add.25), channel_id=1, source_target_pairs={{0,4},{1,5},{2,6},{3,7},{4,0},{5,1},{6,2},{7,3},{8,12},{9,13},{10,... | collective-permute-start | bytes 12296 | tf_op jit(solution)/shard_map/ppermute | solution.py:203
  140.1 3.6 %collective-permute-start.11 = (f32[8,128]{1,0:T(8,128)S(1)}, f32[8,128]{1,0:T(8,128)S(1)}, u32[]{:S(2)}, u32[]{:S(2)}) collective-permute-start(f32[8,128]{1,0:T(8,128)S(1)} %add.25), channel_id=1, source_target_pairs={{0,2},{1,3},{2,0},{3,1},{4,6},{5,7},{6,4},{7,5},{8,10},{9,11},{10,... | collective-permute-start | bytes 12296 | tf_op jit(solution)/shard_map/ppermute | solution.py:203
  141.7 7.1 %collective-permute-start.20 = (bf16[4,4,48,128]{3,2,1,0:T(8,128)(2,1)S(1)}, bf16[4,4,48,128]{3,2,1,0:T(8,128)(2,1)S(1)}, u32[]{:S(2)}, u32[]{:S(2)}) collective-permute-start(bf16[4,4,48,128]{3,2,1,0:T(8,128)(2,1)S(1)} %get-tuple-element.76), channel_id=1, source_target_pairs={{0,1},{1,0},{2,3},{3,2},{4,5},{5,4},{6,7},{7,6},{8,9},{9,8},{10,11... | collective-permute-start | bytes 589832 | tf_op jit(solution)/shard_map/ppermute | solution.py:313
  143.7 5.4 %collective-permute-start.16 = (f32[8,128]{1,0:T(8,128)S(1)}, f32[8,128]{1,0:T(8,128)S(1)}, u32[]{:S(2)}, u32[]{:S(2)}) collective-permute-start(f32[8,128]{1,0:T(8,128)S(1)} %add_add_fusion.1), channel_id=1, source_target_pairs={{0,24},{1,25},{2,26},{3,27},{4,28},{5,29},{6,30},{7,31},{8,16},{9,... | collective-permute-start | bytes 12296 | tf_op jit(solution)/shard_map/ppermute | solution.py:203
  145.5 4.5 %collective-permute-start.15 = (f32[8,128]{1,0:T(8,128)S(1)}, f32[8,128]{1,0:T(8,128)S(1)}, u32[]{:S(2)}, u32[]{:S(2)}) collective-permute-start(f32[8,128]{1,0:T(8,128)S(1)} %add_add_fusion.1), channel_id=1, source_target_pairs={{0,16},{1,17},{2,18},{3,19},{4,20},{5,21},{6,22},{7,23},{8,24},{9,... | collective-permute-start | bytes 12296 | tf_op jit(solution)/shard_map/ppermute | solution.py:203
  147.6 3.6 %collective-permute-start.14 = (f32[8,128]{1,0:T(8,128)S(1)}, f32[8,128]{1,0:T(8,128)S(1)}, u32[]{:S(2)}, u32[]{:S(2)}) collective-permute-start(f32[8,128]{1,0:T(8,128)S(1)} %add_add_fusion.1), channel_id=1, source_target_pairs={{0,8},{1,9},{2,10},{3,11},{4,12},{5,13},{6,14},{7,15},{8,0},{9,1},... | collective-permute-start | bytes 12296 | tf_op jit(solution)/shard_map/ppermute | solution.py:203
  155.8 1.9 copy-start
  157.7 118.6 %all-to-all-start.2 = ((bf16[32,480,128]{2,1,0:T(8,128)(2,1)}), bf16[32,480,128]{2,1,0:T(8,128)(2,1)}, u32[]{:S(2)}, u32[]{:S(2)}) async-start(bf16[32,480,128]{2,1,0:T(8,128)(2,1)} %copy-done), calls=%async_computation.2 | async-start | bytes 7864320 | tf_op jit(solution)/shard_map/all_to_all | solution.py:459
  161.2 69.5 %collective-permute-start.21 = (bf16[8,96,128]{2,1,0:T(8,128)(2,1)S(1)}, bf16[8,96,128]{2,1,0:T(8,128)(2,1)S(1)}, u32[]{:S(2)}, u32[]{:S(2)}) collective-permute-start(bf16[8,96,128]{2,1,0:T(8,128)(2,1)S(1)} %get-tuple-element.79), channel_id=1, source_target_pairs={{0,8},{1,9},{2,10},{3,11},{4,12},{5,13},{6,14},{7,15},{8,0},{9,1},... | collective-permute-start | bytes 589832 | tf_op jit(solution)/shard_map/ppermute | solution.py:313
  163.0 99.9 %collective-permute-start.22 = (bf16[8,96,128]{2,1,0:T(8,128)(2,1)S(1)}, bf16[8,96,128]{2,1,0:T(8,128)(2,1)S(1)}, u32[]{:S(2)}, u32[]{:S(2)}) collective-permute-start(bf16[8,96,128]{2,1,0:T(8,128)(2,1)S(1)} %get-tuple-element.80), channel_id=1, source_target_pairs={{0,16},{1,17},{2,18},{3,19},{4,20},{5,21},{6,22},{7,23},{8,24},{9,... | collective-permute-start | bytes 589832 | tf_op jit(solution)/shard_map/ppermute | solution.py:313
  165.4 97.5 %collective-permute-start.23 = (bf16[8,96,128]{2,1,0:T(8,128)(2,1)S(1)}, bf16[8,96,128]{2,1,0:T(8,128)(2,1)S(1)}, u32[]{:S(2)}, u32[]{:S(2)}) collective-permute-start(bf16[8,96,128]{2,1,0:T(8,128)(2,1)S(1)} %get-tuple-element.81), channel_id=1, source_target_pairs={{0,24},{1,25},{2,26},{3,27},{4,28},{5,29},{6,30},{7,31},{8,16},{9,... | collective-permute-start | bytes 589832 | tf_op jit(solution)/shard_map/ppermute | solution.py:313
  263.0 7.0 %collective-permute-start.24 = (bf16[4,2,96,128]{3,2,1,0:T(8,128)(2,1)S(1)}, bf16[4,2,96,128]{3,2,1,0:T(8,128)(2,1)S(1)}, u32[]{:S(2)}, u32[]{:S(2)}) collective-permute-start(bf16[4,2,96,128]{3,2,1,0:T(8,128)(2,1)S(1)} %get-tuple-element.83), channel_id=1, source_target_pairs={{0,2},{1,3},{2,0},{3,1},{4,6},{5,7},{6,4},{7,5},{8,10},{9,11},{10,... | collective-permute-start | bytes 589832 | tf_op jit(solution)/shard_map/ppermute | solution.py:313
  263.9 7.8 %collective-permute-start.25 = (bf16[4,2,96,128]{3,2,1,0:T(8,128)(2,1)S(1)}, bf16[4,2,96,128]{3,2,1,0:T(8,128)(2,1)S(1)}, u32[]{:S(2)}, u32[]{:S(2)}) collective-permute-start(bf16[4,2,96,128]{3,2,1,0:T(8,128)(2,1)S(1)} %get-tuple-element.84), channel_id=1, source_target_pairs={{0,4},{1,5},{2,6},{3,7},{4,0},{5,1},{6,2},{7,3},{8,12},{9,13},{10,... | collective-permute-start | bytes 589832 | tf_op jit(solution)/shard_map/ppermute | solution.py:313
  265.4 9.0 %collective-permute-start.26 = (bf16[4,2,96,128]{3,2,1,0:T(8,128)(2,1)S(1)}, bf16[4,2,96,128]{3,2,1,0:T(8,128)(2,1)S(1)}, u32[]{:S(2)}, u32[]{:S(2)}) collective-permute-start(bf16[4,2,96,128]{3,2,1,0:T(8,128)(2,1)S(1)} %get-tuple-element.85), channel_id=1, source_target_pairs={{0,6},{1,7},{2,4},{3,5},{4,2},{5,3},{6,0},{7,1},{8,14},{9,15},{10,... | collective-permute-start | bytes 589832 | tf_op jit(solution)/shard_map/ppermute | solution.py:313
  274.4 1.8 collective-permute-start.27

commit v11 on v10

--- a/solution.py
+++ b/solution.py
@@ -25,6 +25,7 @@
 MAIN = ROWS - EDGE
 PLANES = 4
 PLANE = BLOCKS // PLANES
+LONG = 10**11
 
 gelu_c = math.sqrt(2.0 / math.pi)
 isd = 1.0 / math.sqrt(D)
@@ -39,7 +40,7 @@
     for g in GROUPS:
         at = g * SIDE + row
         part = value[:, g * LANES : (g + 1) * LANES]
-        if at < MAIN:
+        if side is None or at < MAIN:
             main[block, at : at + EDGE, :] = part
         else:
             side[block, at - MAIN : at - MAIN + EDGE, :] = part
@@ -54,7 +55,7 @@
     parts = []
     for g in GROUPS:
         at = g * SIDE + r
-        ref, at = (main, at) if at < MAIN else (side, at - MAIN)
+        ref, at = (main, at) if side is None or at < MAIN else (side, at - MAIN)
         parts.append(ref[:, at : at + TILE, :].reshape(ref.shape[0] * TILE, LANES))
     return jnp.concatenate(parts, axis=1)
 
@@ -161,12 +162,12 @@
     )(picks, me, images, targets, first, second)
 
 
-def gram_kernel(main, side, out, total):
-    members = main.shape[0]
+def gram_kernel(params, out, total):
+    members, rows, _ = params.shape
     wide = members * TILE
     total[...] = jnp.zeros_like(total)
     for r in range(0, SIDE, TILE):
-        part = tile(main, side, r)
+        part = tile(params, None, r)
         total[...] += dot(part, part, ((1,), (1,)))
     at = lax.broadcasted_iota(jnp.int32, (wide, wide), 0) % TILE
     to = lax.broadcasted_iota(jnp.int32, (wide, wide), 1) % TILE
@@ -181,8 +182,8 @@
     out[...] = jnp.concatenate([dist[q : q + 8] for q in range(0, members, 8)], axis=1)
 
 
-def distances(main, side):
-    members = main.shape[0]
+def distances(params):
+    members, rows, _ = params.shape
     wide = members * TILE
     return pl.pallas_call(
         gram_kernel,
@@ -191,11 +192,11 @@
         compiler_params=pltpu.CompilerParams(vmem_limit_bytes=16 * 1024 * 1024),
         cost_estimate=pl.CostEstimate(
             flops=2 * wide * wide * SIDE // TILE * D,
-            bytes_accessed=2 * members * ROWS * LANES,
+            bytes_accessed=2 * members * rows * LANES,
             transcendentals=0,
         ),
         name="gram",
-    )(main, side)
+    )(params)
 
 
 def add_over(value, members, bits):
@@ -226,7 +227,7 @@
     return jnp.where(row == col, full, 0.0)
 
 
-def mix_kernel(scale, me, packed, scores, side_scores, params, side_params, out, *refs):
+def mix_kernel(scale, me, packed, scores, side_scores, params, out, *refs):
     outs, side = refs[:PLANES], refs[PLANES]
     members = params.shape[0]
     wide = members * TILE
@@ -234,7 +235,7 @@
     ksum = jnp.sum(full, axis=1, keepdims=True)
     mixer = full.astype(jnp.bfloat16)
     for r in range(0, SIDE, TILE):
-        own = tile(params, side_params, r)
+        own = tile(params, None, r)
         both = jnp.concatenate([tile(scores, side_scores, r), own], axis=1)
         both = dot(mixer, both, ((1,), (0,)))
         pushed = ksum * own.astype(jnp.float32) - both[:, D:]
@@ -254,7 +255,7 @@
     by_plane(me, side, outs)
 
 
-def weighted(scale, me, packed, scores, side_scores, params, side_params):
+def weighted(scale, me, packed, scores, side_scores, params):
     members = params.shape[0]
     wide = members * TILE
     vmem = pl.BlockSpec(memory_space=pltpu.VMEM)
@@ -263,7 +264,7 @@
     return pl.pallas_call(
         mix_kernel,
         out_shape=(main, *side_shapes(2 * EDGE)),
-        in_specs=[smem, smem] + [vmem] * 5,
+        in_specs=[smem, smem] + [vmem] * 4,
         scratch_shapes=[pltpu.VMEM((members, 2 * EDGE, LANES), jnp.bfloat16)],
         compiler_params=pltpu.CompilerParams(vmem_limit_bytes=24 * 1024 * 1024),
         cost_estimate=pl.CostEstimate(
@@ -272,7 +273,7 @@
             transcendentals=0,
         ),
         name="mix",
-    )(scale, me, packed, scores, side_scores, params, side_params)
+    )(scale, me, packed, scores, side_scores, params)
 
 
 def plane_kernel(*refs):
@@ -295,7 +296,7 @@
                 out[(z * PLANE + 2 * q + c) ^ me[0]] = ref[q, z]
 
 
-def regroup(body, name, shapes, *arrays, me=()):
+def regroup(body, name, shapes, *arrays, me=(), flops=0):
     vmem = pl.BlockSpec(memory_space=pltpu.VMEM)
     size = sum(math.prod(x.shape) for x in arrays)
     return pl.pallas_call(
@@ -303,7 +304,7 @@
         out_shape=shapes,
         in_specs=[pl.BlockSpec(memory_space=pltpu.SMEM)] * len(me) + [vmem] * len(arrays),
         compiler_params=pltpu.CompilerParams(vmem_limit_bytes=16 * 1024 * 1024),
-        cost_estimate=pl.CostEstimate(flops=0, bytes_accessed=4 * size, transcendentals=0),
+        cost_estimate=pl.CostEstimate(flops=flops, bytes_accessed=4 * size, transcendentals=0),
         name=name,
     )(*me, *arrays)
 
@@ -320,7 +321,7 @@
 def within_plane(parts, me):
     rows = parts[0].shape[1]
     shape = jax.ShapeDtypeStruct((PLANES, 2, rows, LANES), jnp.bfloat16)
-    parts = regroup(plane_kernel, "plane", (shape,) * (PLANE // 2), *parts)
+    parts = regroup(plane_kernel, "plane", (shape,) * (PLANE // 2), *parts, flops=LONG)
     parts = parts[:1] + tuple(swap(x, 2 * q) for q, x in enumerate(parts) if q)
     shape = jax.ShapeDtypeStruct((PLANE // 2, PLANES, rows, LANES), jnp.bfloat16)
     near, far = regroup(core_kernel, "core", (shape,) * 2, *parts)
@@ -350,9 +351,7 @@
 TALL = FF // STEPS
 
 
-def pack_kernel(me, first, second, out, *refs):
-    outs, (wide, tall, packed, side, loads, stores) = refs[:PLANES], refs[PLANES:]
-
+def pack_kernel(first, second, out, wide, tall, packed, loads, stores):
     def load(d):
         return (
             pltpu.make_async_copy(
@@ -374,37 +373,31 @@
         for copy in load(d):
             copy.wait()
         for c in range(COLS):
-            put(packed, side, d * COLS + c, 0, wide[d, :, c * D : (c + 1) * D])
-            put(packed, side, d * COLS + c, EDGE, tall[d, c * EDGE : (c + 1) * EDGE, :])
+            put(packed, None, d * COLS + c, 0, wide[d, :, c * D : (c + 1) * D])
+            put(packed, None, d * COLS + c, EDGE, tall[d, c * EDGE : (c + 1) * EDGE, :])
         store(d).start()
-    by_plane(me, side, outs)
     for d in range(STEPS):
         store(d).wait()
 
 
-def to_blocks(first, second, me):
+def to_blocks(first, second):
     bf = jnp.bfloat16
     return pl.pallas_call(
         pack_kernel,
-        out_shape=(pltpu.HBM((BLOCKS, MAIN, LANES), bf), *side_shapes(EDGE)),
-        in_specs=[pl.BlockSpec(memory_space=pltpu.SMEM)]
-        + [pl.BlockSpec(memory_space=pl.ANY)] * 2,
-        out_specs=(
-            pl.BlockSpec(memory_space=pl.ANY),
-            *[pl.BlockSpec(memory_space=pltpu.VMEM)] * PLANES,
-        ),
+        out_shape=pltpu.HBM((BLOCKS, ROWS, LANES), bf),
+        in_specs=[pl.BlockSpec(memory_space=pl.ANY)] * 2,
+        out_specs=pl.BlockSpec(memory_space=pl.ANY),
         scratch_shapes=[
             pltpu.VMEM((STEPS, EDGE, FF), bf),
             pltpu.VMEM((STEPS, TALL, D), bf),
-            pltpu.VMEM((BLOCKS, MAIN, LANES), bf),
-            pltpu.VMEM((BLOCKS, EDGE, LANES), bf),
+            pltpu.VMEM((BLOCKS, ROWS, LANES), bf),
             pltpu.SemaphoreType.DMA((2, STEPS)),
             pltpu.SemaphoreType.DMA((STEPS,)),
         ],
         compiler_params=pltpu.CompilerParams(vmem_limit_bytes=56 * 1024 * 1024),
         cost_estimate=pl.CostEstimate(flops=0, bytes_accessed=8 * D * FF, transcendentals=0),
         name="pack",
-    )(me, first, second)
+    )(first, second)
 
 
 def unpack_kernel(main, side, first_a, second_a, first_s, second_s, wide, tall, stores):
@@ -466,27 +459,20 @@
     tiled = members == BLOCKS
     me = lax.axis_index(AXES) if tiled else 0
     me = jnp.full((1,), me, jnp.int32)
-    params, *side_params = to_blocks(particles_first, particles_second, me)
+    params = to_blocks(particles_first, particles_second)
     scores, *side_scores = particle_scores(
         particles_first[0], particles_second[0], pool_images, pool_targets, batch_index[0], me
     )
     if tiled:
         params, scores = exchange(params), exchange(scores)
-        side_params, side_scores = across_planes(side_params), across_planes(side_scores)
-        params, side_params, side_scores = lax.optimization_barrier(
-            (params, side_params, side_scores)
-        )
-        side_params = within_plane(side_params, me)
+        params, side_scores = lax.optimization_barrier((params, across_planes(side_scores)))
         side_scores = within_plane(side_scores, me)
-        packed = distances(params, side_params)
+        packed = distances(params)
         for bits in ((1,), (2, 4, 6), (8, 16, 24)):
             packed = add_over(packed, members, bits)
-        main, *side = weighted(
-            kernel_scale, me, packed, scores, side_scores, params, side_params
-        )
+        main, *side = weighted(kernel_scale, me, packed, scores, side_scores, params)
         return from_blocks(exchange(main), within_plane(across_planes(side), me))
     cut = (members, BLOCKS * ROWS // members, LANES)
-    params = jnp.concatenate([params, jnp.concatenate(side_params)], axis=1)
     scores = jnp.concatenate([scores, jnp.concatenate(side_scores)], axis=1)
     params, scores = exchange(params.reshape(cut)), exchange(scores.reshape(cut))
     gram = lax.psum(plain_products(params), AXES)

time: 284 us -> 242 us (0.85)
  waiting for transfers between devices: 186 us -> 147 us
  local copies, waits for them, and re-layouts: 4.81 us -> 10.7 us
  starting transfers between devices: 50.2 us -> 45 us
    ppermute x21 -> x14, waiting for transfers between devices: 161 us -> 61.1 us  [swap(): return lax.ppermute(value, AXES, pairs)]
    all_to_all x3, waiting for transfers between devices: 20 us -> 55.5 us  [exchange(): return lax.all_to_all(blocks, AXES, split_axis=0, concat_axis=0, tiled=True)]
    ppermute x7, waiting for transfers between devices: 5.5 us -> 30.5 us  [add_over(): lax.ppermute(value, AXES, [(i, i ^ bit) for i in range(members)])]
    ppermute x21 -> x14, starting transfers between devices: 27.2 us -> 20.1 us  [swap(): return lax.ppermute(value, AXES, pairs)]
    unnamed x22 -> x20, local copies, waits for them, and re-layouts: 4.81 us -> 10.7 us
  transfers between devices with their start and end apart: 31 -> 24, of which waited for: 20 -> 12; matrix products, arithmetic and copies ran while one was open for 0% -> 2% of each run, Pallas kernels for 9% -> 10%
where the time goes in v11:
time: 242 us
  waiting for transfers between devices  147 us (61%)
  starting transfers between devices  45 us (19%)
  Pallas kernels  37.3 us (15%)
  local copies, waits for them, and re-layouts  10.7 us (4%)
    ppermute x14, waiting for transfers between devices, swap(): return lax.ppermute(value, AXES, pairs)  61.1 us
    all_to_all x3, waiting for transfers between devices, exchange(): return lax.all_to_all(blocks, AXES, split_axis=0, concat_axis=0, tiled=True)  55.5 us
    ppermute x7, waiting for transfers between devices, add_over(): lax.ppermute(value, AXES, [(i, i ^ bit) for i in range(members)])  30.5 us
    pallas_call x1, Pallas kernels, particle_scores(): pl.pallas_call(functools.partial(score_kernel, DATA / count), out_shape=(...  23 us
    ppermute x14, starting transfers between devices, swap(): return lax.ppermute(value, AXES, pairs)  20.1 us
    all_to_all x3, starting transfers between devices, exchange(): return lax.all_to_all(blocks, AXES, split_axis=0, concat_axis=0, tiled=True)  16.9 us
    unnamed x20, local copies, waits for them, and re-layouts  10.7 us
    ppermute x7, starting transfers between devices, add_over(): lax.ppermute(value, AXES, [(i, i ^ bit) for i in range(members)])  8.01 us
  transfers between devices with their start and end apart: 24, of which 12 were waited for; matrix products, arithmetic and copies ran while one was open for 2% of the time, Pallas kernels for 10%

profile of v11, /device:TPU:0, one launch (start us, length us, event | category | flops | bytes accessed | tf_op | source)
XLA Modules:
  0.0 241.7 jit_solution(4112000009483760685)
XLA Ops:
  0.6 2.7 %pack.1 = bf16[32,288,128]{2,1,0:T(8,128)(2,1)} custom-call(bf16[1,384,1536]{2,1,0:T(8,128)(2,1)} %first.1, bf16[1,1536,384]{2,1,0:T(8,128)(2,1)} %second.1), custom_call_target="tpu_custom_call" | custom-call | bytes 4718592 | tf_op jit(solution)/shard_map/pack/pallas_call | solution.py:385
  3.4 7.3 %all-to-all-start = ((bf16[32,288,128]{2,1,0:T(8,128)(2,1)}), bf16[32,288,128]{2,1,0:T(8,128)(2,1)S(1)}, u32[]{:S(2)}, u32[]{:S(2)}) async-start(bf16[32,288,128]{2,1,0:T(8,128)(2,1)} %pack.1), calls=%async_computation | async-start | bytes 4718592 | tf_op jit(solution)/shard_map/all_to_all | solution.py:452
  10.7 2.6 %copy.10.image = bf16[8,197,384]{2,1,0:T(8,128)(2,1)} copy(bf16[8,197,384]{2,0,1:T(8,128)(2,1)} %param.8) | data formatting | bytes 2420736 | tf_op args[2]
  13.3 1.2 copy.11.target
  14.5 0.5 copy-done.3
  15.0 1.3 copy-done.1
  16.3 1.3 copy-done.2
  17.6 1.3 copy-done.4
  18.9 23.0 %score.1 = (bf16[32,240,128]{2,1,0:T(8,128)(2,1)}, bf16[8,48,128]{2,1,0:T(8,128)(2,1)S(1)}, bf16[8,48,128]{2,1,0:T(8,128)(2,1)S(1)}, bf16[8,48,128]{2,1,0:T(8,128)(2,1)S(1)}, bf16[8,48,128]{2,1,0:T(8,128)(2,1)S(1)}) custom-call(s32[8]{0:T(128)S(1)} %bitcast.6, s32[1]{0:T(128)} %bitcast.me, bf16[8,197,384]{2,1,0:T(8,128)(2,1)S(1)} %copy-done.1, ...), custom_call_target="tpu_custom_call" | custom-call | flops 9814671360 | bytes 7139328 | tf_op jit(solution)/shard_map/score/pallas_call | solution.py:128
  41.9 0.6 copy-done.6
  42.5 1.8 collective-permute-start
  44.3 2.4 collective-permute-start.1
  46.7 0.2 collective-permute-start.2
  46.9 5.1 %collective-permute-done.refs_1_ = bf16[8,48,128]{2,1,0:T(8,128)(2,1)S(1)} collective-permute-done((bf16[8,48,128]{2,1,0:T(8,128)(2,1)S(1)}, bf16[8,48,128]{2,1,0:T(8,128)(2,1)S(1)}, u32[]{:S(2)}, u32[]{:S(2)}) %collective-permute-start) | collective-permute-done | bytes 98336 | tf_op jit(solution)/shard_map/ppermute | solution.py:314
  52.0 19.9 %collective-permute-done.1.refs_2_ = bf16[8,48,128]{2,1,0:T(8,128)(2,1)S(1)} collective-permute-done((bf16[8,48,128]{2,1,0:T(8,128)(2,1)S(1)}, bf16[8,48,128]{2,1,0:T(8,128)(2,1)S(1)}, u32[]{:S(2)}, u32[]{:S(2)}) %collective-permute-start.1) | collective-permute-done | bytes 98336 | tf_op jit(solution)/shard_map/ppermute | solution.py:314
  71.9 2.2 gram.1
  74.1 5.5 %all-to-all-start.1 = ((bf16[32,240,128]{2,1,0:T(8,128)(2,1)}), bf16[32,240,128]{2,1,0:T(8,128)(2,1)}, u32[]{:S(2)}, u32[]{:S(2)}) async-start(bf16[32,240,128]{2,1,0:T(8,128)(2,1)} %get-tuple-element.36), calls=%async_computation.1 | async-start | bytes 3932160 | tf_op jit(solution)/shard_map/all_to_all | solution.py:452
  79.6 2.5 %collective-permute-start.6 = (f32[8,128]{1,0:T(8,128)S(1)}, f32[8,128]{1,0:T(8,128)S(1)}, u32[]{:S(2)}, u32[]{:S(2)}) collective-permute-start(f32[8,128]{1,0:T(8,128)S(1)} %add.25), channel_id=1, source_target_pairs={{0,6},{1,7},{2,4},{3,5},{4,2},{5,3},{6,0},{7,1},{8,14},{9,15},{10,... | collective-permute-start | bytes 12296 | tf_op jit(solution)/shard_map/ppermute | solution.py:204
  82.1 0.6 collective-permute-start.5
  82.6 0.5 collective-permute-start.4
  83.2 1.6 collective-permute-start.10
  84.8 1.5 collective-permute-start.11
  86.2 8.0 %collective-permute-done.6 = f32[8,128]{1,0:T(8,128)S(1)} collective-permute-done((f32[8,128]{1,0:T(8,128)S(1)}, f32[8,128]{1,0:T(8,128)S(1)}, u32[]{:S(2)}, u32[]{:S(2)}) %collective-permute-start.6) | collective-permute-done | bytes 4128 | tf_op jit(solution)/shard_map/ppermute | solution.py:204
  94.2 1.4 collective-permute-start.12
  95.6 3.7 %collective-permute-start.9 = (f32[8,128]{1,0:T(8,128)S(1)}, f32[8,128]{1,0:T(8,128)S(1)}, u32[]{:S(2)}, u32[]{:S(2)}) collective-permute-start(f32[8,128]{1,0:T(8,128)S(1)} %add_add_fusion.1), channel_id=1, source_target_pairs={{0,24},{1,25},{2,26},{3,27},{4,28},{5,29},{6,30},{7,31},{8,16},{9,... | collective-permute-start | bytes 12296 | tf_op jit(solution)/shard_map/ppermute | solution.py:204
  99.3 0.8 collective-permute-start.7
  100.7 2.1 collective-permute-done.12.refs_3_
  102.9 0.1 collective-permute-start.13
  103.0 12.8 %collective-permute-done.9 = f32[8,128]{1,0:T(8,128)S(1)} collective-permute-done((f32[8,128]{1,0:T(8,128)S(1)}, f32[8,128]{1,0:T(8,128)S(1)}, u32[]{:S(2)}, u32[]{:S(2)}) %collective-permute-start.9) | collective-permute-done | bytes 4128 | tf_op jit(solution)/shard_map/ppermute | solution.py:204
  115.8 9.8 %collective-permute-done.8 = f32[8,128]{1,0:T(8,128)S(1)} collective-permute-done((f32[8,128]{1,0:T(8,128)S(1)}, f32[8,128]{1,0:T(8,128)S(1)}, u32[]{:S(2)}, u32[]{:S(2)}) %collective-permute-start.8) | collective-permute-done | bytes 4128 | tf_op jit(solution)/shard_map/ppermute | solution.py:204
  125.6 4.6 %mix.1 = (bf16[32,480,128]{2,1,0:T(8,128)(2,1)S(1)}, bf16[8,96,128]{2,1,0:T(8,128)(2,1)S(1)}, bf16[8,96,128]{2,1,0:T(8,128)(2,1)S(1)}, bf16[8,96,128]{2,1,0:T(8,128)(2,1)S(1)}, bf16[8,96,128]{2,1,0:T(8,128)(2,1)S(1)}) custom-call(f32[1]{0:T(128)S(6)} %copy.12.scale, s32[1]{0:T(128)} %bitcast.me, f32[8,128]{1,0:T(8,128)S(1)} %add_add_fusion.packed, ...), custom_call_target="tpu_custom_call" | custom-call | flops 2415919104 | bytes 9437184 | tf_op jit(solution)/shard_map/mix/pallas_call | solution.py:264
  130.2 1.9 copy-done
  132.1 0.5 collective-permute-start.14
  132.6 1.5 collective-permute-start.15
  134.1 2.4 collective-permute-start.16
  136.5 4.1 %all-to-all-start.2 = ((bf16[32,480,128]{2,1,0:T(8,128)(2,1)}), bf16[32,480,128]{2,1,0:T(8,128)(2,1)}, u32[]{:S(2)}, u32[]{:S(2)}) async-start(bf16[32,480,128]{2,1,0:T(8,128)(2,1)} %copy-done), calls=%async_computation.2 | async-start | bytes 7864320 | tf_op jit(solution)/shard_map/all_to_all | solution.py:452
  140.6 1.3 collective-permute-done.14.refs_1_
  142.0 7.9 %collective-permute-done.15.refs_2_ = bf16[8,96,128]{2,1,0:T(8,128)(2,1)S(1)} collective-permute-done((bf16[8,96,128]{2,1,0:T(8,128)(2,1)S(1)}, bf16[8,96,128]{2,1,0:T(8,128)(2,1)S(1)}, u32[]{:S(2)}, u32[]{:S(2)}) %collective-permute-start.15) | collective-permute-done | bytes 196640 | tf_op jit(solution)/shard_map/ppermute | solution.py:314
  149.9 2.8 %collective-permute-start.17 = (bf16[4,2,96,128]{3,2,1,0:T(8,128)(2,1)S(1)}, bf16[4,2,96,128]{3,2,1,0:T(8,128)(2,1)S(1)}, u32[]{:S(2)}, u32[]{:S(2)}) collective-permute-start(bf16[4,2,96,128]{3,2,1,0:T(8,128)(2,1)S(1)} %get-tuple-element.53), channel_id=1, source_target_pairs={{0,2},{1,3},{2,0},{3,1},{4,6},{5,7},{6,4},{7,5},{8,10},{9,11},{10,... | collective-permute-start | bytes 589832 | tf_op jit(solution)/shard_map/ppermute | solution.py:314
  152.7 3.6 %collective-permute-start.18 = (bf16[4,2,96,128]{3,2,1,0:T(8,128)(2,1)S(1)}, bf16[4,2,96,128]{3,2,1,0:T(8,128)(2,1)S(1)}, u32[]{:S(2)}, u32[]{:S(2)}) collective-permute-start(bf16[4,2,96,128]{3,2,1,0:T(8,128)(2,1)S(1)} %get-tuple-element.54), channel_id=1, source_target_pairs={{0,4},{1,5},{2,6},{3,7},{4,0},{5,1},{6,2},{7,3},{8,12},{9,13},{10,... | collective-permute-start | bytes 589832 | tf_op jit(solution)/shard_map/ppermute | solution.py:314
  156.3 0.3 collective-permute-start.19
  156.6 13.3 %collective-permute-done.17.refs_1_ = bf16[4,2,96,128]{3,2,1,0:T(8,128)(2,1)S(1)} collective-permute-done((bf16[4,2,96,128]{3,2,1,0:T(8,128)(2,1)S(1)}, bf16[4,2,96,128]{3,2,1,0:T(8,128)(2,1)S(1)}, u32[]{:S(2)}, u32[]{:S(2)}) %collective-permute-start.17) | collective-permute-done | bytes 196640 | tf_op jit(solution)/shard_map/ppermute | solution.py:314
  169.9 9.7 %collective-permute-done.19.refs_3_ = bf16[4,2,96,128]{3,2,1,0:T(8,128)(2,1)S(1)} collective-permute-done((bf16[4,2,96,128]{3,2,1,0:T(8,128)(2,1)S(1)}, bf16[4,2,96,128]{3,2,1,0:T(8,128)(2,1)S(1)}, u32[]{:S(2)}, u32[]{:S(2)}) %collective-permute-start.19) | collective-permute-done | bytes 196640 | tf_op jit(solution)/shard_map/ppermute | solution.py:314
  179.6 0.1 collective-permute-start.20
  179.7 1.7 collective-permute-done.20.far
  181.4 0.1 settle.3.side
  181.4 55.5 %all-to-all-done.2.main = bf16[32,480,128]{2,1,0:T(8,128)(2,1)} async-done(((bf16[32,480,128]{2,1,0:T(8,128)(2,1)}), bf16[32,480,128]{2,1,0:T(8,128)(2,1)}, u32[]{:S(2)}, u32[]{:S(2)}) %all-to-all-start.2) | async-done | bytes 3932192 | tf_op jit(solution)/shard_map/all_to_all | solution.py:452
  236.9 4.6 %unpack.1 = (bf16[1,384,1536]{2,1,0:T(8,128)(2,1)}, bf16[1,1536,384]{2,1,0:T(8,128)(2,1)}, bf16[1,384,1536]{2,1,0:T(8,128)(2,1)}, bf16[1,1536,384]{2,1,0:T(8,128)(2,1)}) custom-call(bf16[32,480,128]{2,1,0:T(8,128)(2,1)} %all-to-all-done.2.main, bf16[32,96,128]{2,1,0:T(8,128)(2,1)S(1)} %settle.3.side), custom_call_target="tpu_custom_call" | custom-call | bytes 9437184 | tf_op jit(solution)/shard_map/unpack/pallas_call | solution.py:435
  (34 shorter events, 0.3 us)
Async XLA Ops:
  3.4 68.5 %all-to-all-start = ((bf16[32,288,128]{2,1,0:T(8,128)(2,1)}), bf16[32,288,128]{2,1,0:T(8,128)(2,1)S(1)}, u32[]{:S(2)}, u32[]{:S(2)}) async-start(bf16[32,288,128]{2,1,0:T(8,128)(2,1)} %pack.1), calls=%async_computation | async-start | bytes 4718592 | tf_op jit(solution)/shard_map/all_to_all | solution.py:452
  10.7 2.6 %copy-start.8 = (bf16[8,197,384]{2,0,1:T(8,128)(2,1)S(1)}, bf16[8,197,384]{2,0,1:T(8,128)(2,1)}, u32[]{:S(2)}) copy-start(bf16[8,197,384]{2,0,1:T(8,128)(2,1)} %param.9) | copy-start | bytes 3631108
  13.3 1.7 copy-start.3
  13.3 1.7 copy-start.5
  15.0 1.3 copy-start.1
  16.3 1.3 copy-start.2
  17.6 1.3 copy-start.4
  41.9 0.6 copy-start.6
  42.5 9.5 %collective-permute-start = (bf16[8,48,128]{2,1,0:T(8,128)(2,1)S(1)}, bf16[8,48,128]{2,1,0:T(8,128)(2,1)S(1)}, u32[]{:S(2)}, u32[]{:S(2)}) collective-permute-start(bf16[8,48,128]{2,1,0:T(8,128)(2,1)S(1)} %get-tuple-element.32), channel_id=1, source_target_pairs={{0,8},{1,9},{2,10},{3,11},{4,12},{5,13},{6,14},{7,15},{8,0},{9,1},... | collective-permute-start | bytes 294920 | tf_op jit(solution)/shard_map/ppermute | solution.py:314
  44.3 27.6 %collective-permute-start.1 = (bf16[8,48,128]{2,1,0:T(8,128)(2,1)S(1)}, bf16[8,48,128]{2,1,0:T(8,128)(2,1)S(1)}, u32[]{:S(2)}, u32[]{:S(2)}) collective-permute-start(bf16[8,48,128]{2,1,0:T(8,128)(2,1)S(1)} %get-tuple-element.33), channel_id=1, source_target_pairs={{0,16},{1,17},{2,18},{3,19},{4,20},{5,21},{6,22},{7,23},{8,24},{9,... | collective-permute-start | bytes 294920 | tf_op jit(solution)/shard_map/ppermute | solution.py:314
  46.7 25.2 %collective-permute-start.2 = (bf16[8,48,128]{2,1,0:T(8,128)(2,1)S(1)}, bf16[8,48,128]{2,1,0:T(8,128)(2,1)S(1)}, u32[]{:S(2)}, u32[]{:S(2)}) collective-permute-start(bf16[8,48,128]{2,1,0:T(8,128)(2,1)S(1)} %get-tuple-element.34), channel_id=1, source_target_pairs={{0,24},{1,25},{2,26},{3,27},{4,28},{5,29},{6,30},{7,31},{8,16},{9,... | collective-permute-start | bytes 294920 | tf_op jit(solution)/shard_map/ppermute | solution.py:314
  74.1 5.5 %collective-permute-start.3 = (f32[8,128]{1,0:T(8,128)S(1)}, f32[8,128]{1,0:T(8,128)S(1)}, u32[]{:S(2)}, u32[]{:S(2)}) collective-permute-start(f32[8,128]{1,0:T(8,128)S(1)} %gram.1), channel_id=1, source_target_pairs={{0,1},{1,0},{2,3},{3,2},{4,5},{5,4},{6,7},{7,6},{8,9},{9,8},{10,11... | collective-permute-start | bytes 12296 | tf_op jit(solution)/shard_map/ppermute | solution.py:204
  74.1 9.1 %copy-start.7 = (bf16[8,48,128]{2,1,0:T(8,128)(2,1)S(1)}, bf16[8,48,128]{2,1,0:T(8,128)(2,1)}, u32[]{:S(2)}) copy-start(bf16[8,48,128]{2,1,0:T(8,128)(2,1)} %copy-done.6) | copy-start | bytes 294916
  74.1 51.6 %all-to-all-start.1 = ((bf16[32,240,128]{2,1,0:T(8,128)(2,1)}), bf16[32,240,128]{2,1,0:T(8,128)(2,1)}, u32[]{:S(2)}, u32[]{:S(2)}) async-start(bf16[32,240,128]{2,1,0:T(8,128)(2,1)} %get-tuple-element.36), calls=%async_computation.1 | async-start | bytes 3932160 | tf_op jit(solution)/shard_map/all_to_all | solution.py:452
  79.6 14.6 %collective-permute-start.6 = (f32[8,128]{1,0:T(8,128)S(1)}, f32[8,128]{1,0:T(8,128)S(1)}, u32[]{:S(2)}, u32[]{:S(2)}) collective-permute-start(f32[8,128]{1,0:T(8,128)S(1)} %add.25), channel_id=1, source_target_pairs={{0,6},{1,7},{2,4},{3,5},{4,2},{5,3},{6,0},{7,1},{8,14},{9,15},{10,... | collective-permute-start | bytes 12296 | tf_op jit(solution)/shard_map/ppermute | solution.py:204
  82.1 13.5 %collective-permute-start.5 = (f32[8,128]{1,0:T(8,128)S(1)}, f32[8,128]{1,0:T(8,128)S(1)}, u32[]{:S(2)}, u32[]{:S(2)}) collective-permute-start(f32[8,128]{1,0:T(8,128)S(1)} %add.25), channel_id=1, source_target_pairs={{0,4},{1,5},{2,6},{3,7},{4,0},{5,1},{6,2},{7,3},{8,12},{9,13},{10,... | collective-permute-start | bytes 12296 | tf_op jit(solution)/shard_map/ppermute | solution.py:204
  82.6 13.0 %collective-permute-start.4 = (f32[8,128]{1,0:T(8,128)S(1)}, f32[8,128]{1,0:T(8,128)S(1)}, u32[]{:S(2)}, u32[]{:S(2)}) collective-permute-start(f32[8,128]{1,0:T(8,128)S(1)} %add.25), channel_id=1, source_target_pairs={{0,2},{1,3},{2,0},{3,1},{4,6},{5,7},{6,4},{7,5},{8,10},{9,11},{10,... | collective-permute-start | bytes 12296 | tf_op jit(solution)/shard_map/ppermute | solution.py:204
  83.2 16.2 %collective-permute-start.10 = (bf16[4,2,48,128]{3,2,1,0:T(8,128)(2,1)S(1)}, bf16[4,2,48,128]{3,2,1,0:T(8,128)(2,1)S(1)}, u32[]{:S(2)}, u32[]{:S(2)}) collective-permute-start(bf16[4,2,48,128]{3,2,1,0:T(8,128)(2,1)S(1)} %get-tuple-element.42), channel_id=1, source_target_pairs={{0,2},{1,3},{2,0},{3,1},{4,6},{5,7},{6,4},{7,5},{8,10},{9,11},{10,... | collective-permute-start | bytes 294920 | tf_op jit(solution)/shard_map/ppermute | solution.py:314
  84.8 16.0 %collective-permute-start.11 = (bf16[4,2,48,128]{3,2,1,0:T(8,128)(2,1)S(1)}, bf16[4,2,48,128]{3,2,1,0:T(8,128)(2,1)S(1)}, u32[]{:S(2)}, u32[]{:S(2)}) collective-permute-start(bf16[4,2,48,128]{3,2,1,0:T(8,128)(2,1)S(1)} %get-tuple-element.43), channel_id=1, source_target_pairs={{0,4},{1,5},{2,6},{3,7},{4,0},{5,1},{6,2},{7,3},{8,12},{9,13},{10,... | collective-permute-start | bytes 294920 | tf_op jit(solution)/shard_map/ppermute | solution.py:314
  94.2 8.7 %collective-permute-start.12 = (bf16[4,2,48,128]{3,2,1,0:T(8,128)(2,1)S(1)}, bf16[4,2,48,128]{3,2,1,0:T(8,128)(2,1)S(1)}, u32[]{:S(2)}, u32[]{:S(2)}) collective-permute-start(bf16[4,2,48,128]{3,2,1,0:T(8,128)(2,1)S(1)} %get-tuple-element.44), channel_id=1, source_target_pairs={{0,6},{1,7},{2,4},{3,5},{4,2},{5,3},{6,0},{7,1},{8,14},{9,15},{10,... | collective-permute-start | bytes 294920 | tf_op jit(solution)/shard_map/ppermute | solution.py:314
  95.6 20.2 %collective-permute-start.9 = (f32[8,128]{1,0:T(8,128)S(1)}, f32[8,128]{1,0:T(8,128)S(1)}, u32[]{:S(2)}, u32[]{:S(2)}) collective-permute-start(f32[8,128]{1,0:T(8,128)S(1)} %add_add_fusion.1), channel_id=1, source_target_pairs={{0,24},{1,25},{2,26},{3,27},{4,28},{5,29},{6,30},{7,31},{8,16},{9,... | collective-permute-start | bytes 12296 | tf_op jit(solution)/shard_map/ppermute | solution.py:204
  99.3 26.2 %collective-permute-start.8 = (f32[8,128]{1,0:T(8,128)S(1)}, f32[8,128]{1,0:T(8,128)S(1)}, u32[]{:S(2)}, u32[]{:S(2)}) collective-permute-start(f32[8,128]{1,0:T(8,128)S(1)} %add_add_fusion.1), channel_id=1, source_target_pairs={{0,16},{1,17},{2,18},{3,19},{4,20},{5,21},{6,22},{7,23},{8,24},{9,... | collective-permute-start | bytes 12296 | tf_op jit(solution)/shard_map/ppermute | solution.py:204
  99.3 26.2 %collective-permute-start.7 = (f32[8,128]{1,0:T(8,128)S(1)}, f32[8,128]{1,0:T(8,128)S(1)}, u32[]{:S(2)}, u32[]{:S(2)}) collective-permute-start(f32[8,128]{1,0:T(8,128)S(1)} %add_add_fusion.1), channel_id=1, source_target_pairs={{0,8},{1,9},{2,10},{3,11},{4,12},{5,13},{6,14},{7,15},{8,0},{9,1},... | collective-permute-start | bytes 12296 | tf_op jit(solution)/shard_map/ppermute | solution.py:204
  102.9 22.7 %collective-permute-start.13 = (bf16[4,4,48,128]{3,2,1,0:T(8,128)(2,1)S(1)}, bf16[4,4,48,128]{3,2,1,0:T(8,128)(2,1)S(1)}, u32[]{:S(2)}, u32[]{:S(2)}) collective-permute-start(bf16[4,4,48,128]{3,2,1,0:T(8,128)(2,1)S(1)} %get-tuple-element.46), channel_id=1, source_target_pairs={{0,1},{1,0},{2,3},{3,2},{4,5},{5,4},{6,7},{7,6},{8,9},{9,8},{10,11... | collective-permute-start | bytes 589832 | tf_op jit(solution)/shard_map/ppermute | solution.py:314
  130.2 1.9 copy-start
  132.1 9.9 %collective-permute-start.14 = (bf16[8,96,128]{2,1,0:T(8,128)(2,1)S(1)}, bf16[8,96,128]{2,1,0:T(8,128)(2,1)S(1)}, u32[]{:S(2)}, u32[]{:S(2)}) collective-permute-start(bf16[8,96,128]{2,1,0:T(8,128)(2,1)S(1)} %get-tuple-element.49), channel_id=1, source_target_pairs={{0,8},{1,9},{2,10},{3,11},{4,12},{5,13},{6,14},{7,15},{8,0},{9,1},... | collective-permute-start | bytes 589832 | tf_op jit(solution)/shard_map/ppermute | solution.py:314
  132.6 17.2 %collective-permute-start.15 = (bf16[8,96,128]{2,1,0:T(8,128)(2,1)S(1)}, bf16[8,96,128]{2,1,0:T(8,128)(2,1)S(1)}, u32[]{:S(2)}, u32[]{:S(2)}) collective-permute-start(bf16[8,96,128]{2,1,0:T(8,128)(2,1)S(1)} %get-tuple-element.50), channel_id=1, source_target_pairs={{0,16},{1,17},{2,18},{3,19},{4,20},{5,21},{6,22},{7,23},{8,24},{9,... | collective-permute-start | bytes 589832 | tf_op jit(solution)/shard_map/ppermute | solution.py:314
  134.1 15.7 %collective-permute-start.16 = (bf16[8,96,128]{2,1,0:T(8,128)(2,1)S(1)}, bf16[8,96,128]{2,1,0:T(8,128)(2,1)S(1)}, u32[]{:S(2)}, u32[]{:S(2)}) collective-permute-start(bf16[8,96,128]{2,1,0:T(8,128)(2,1)S(1)} %get-tuple-element.51), channel_id=1, source_target_pairs={{0,24},{1,25},{2,26},{3,27},{4,28},{5,29},{6,30},{7,31},{8,16},{9,... | collective-permute-start | bytes 589832 | tf_op jit(solution)/shard_map/ppermute | solution.py:314
  136.5 100.4 %all-to-all-start.2 = ((bf16[32,480,128]{2,1,0:T(8,128)(2,1)}), bf16[32,480,128]{2,1,0:T(8,128)(2,1)}, u32[]{:S(2)}, u32[]{:S(2)}) async-start(bf16[32,480,128]{2,1,0:T(8,128)(2,1)} %copy-done), calls=%async_computation.2 | async-start | bytes 7864320 | tf_op jit(solution)/shard_map/all_to_all | solution.py:452
  149.9 20.0 %collective-permute-start.17 = (bf16[4,2,96,128]{3,2,1,0:T(8,128)(2,1)S(1)}, bf16[4,2,96,128]{3,2,1,0:T(8,128)(2,1)S(1)}, u32[]{:S(2)}, u32[]{:S(2)}) collective-permute-start(bf16[4,2,96,128]{3,2,1,0:T(8,128)(2,1)S(1)} %get-tuple-element.53), channel_id=1, source_target_pairs={{0,2},{1,3},{2,0},{3,1},{4,6},{5,7},{6,4},{7,5},{8,10},{9,11},{10,... | collective-permute-start | bytes 589832 | tf_op jit(solution)/shard_map/ppermute | solution.py:314
  152.7 17.2 %collective-permute-start.18 = (bf16[4,2,96,128]{3,2,1,0:T(8,128)(2,1)S(1)}, bf16[4,2,96,128]{3,2,1,0:T(8,128)(2,1)S(1)}, u32[]{:S(2)}, u32[]{:S(2)}) collective-permute-start(bf16[4,2,96,128]{3,2,1,0:T(8,128)(2,1)S(1)} %get-tuple-element.54), channel_id=1, source_target_pairs={{0,4},{1,5},{2,6},{3,7},{4,0},{5,1},{6,2},{7,3},{8,12},{9,13},{10,... | collective-permute-start | bytes 589832 | tf_op jit(solution)/shard_map/ppermute | solution.py:314
  156.3 23.3 %collective-permute-start.19 = (bf16[4,2,96,128]{3,2,1,0:T(8,128)(2,1)S(1)}, bf16[4,2,96,128]{3,2,1,0:T(8,128)(2,1)S(1)}, u32[]{:S(2)}, u32[]{:S(2)}) collective-permute-start(bf16[4,2,96,128]{3,2,1,0:T(8,128)(2,1)S(1)} %get-tuple-element.55), channel_id=1, source_target_pairs={{0,6},{1,7},{2,4},{3,5},{4,2},{5,3},{6,0},{7,1},{8,14},{9,15},{10,... | collective-permute-start | bytes 589832 | tf_op jit(solution)/shard_map/ppermute | solution.py:314
  179.6 1.8 collective-permute-start.20

commit v12 on v10

--- a/solution.py
+++ b/solution.py
@@ -25,6 +25,7 @@
 MAIN = ROWS - EDGE
 PLANES = 4
 PLANE = BLOCKS // PLANES
+LONG = 10**11
 
 gelu_c = math.sqrt(2.0 / math.pi)
 isd = 1.0 / math.sqrt(D)
@@ -227,12 +228,13 @@
 
 
 def mix_kernel(scale, me, packed, scores, side_scores, params, side_params, out, *refs):
-    outs, side = refs[:PLANES], refs[PLANES]
+    outs, (side, mixed, stores) = refs[:PLANES], refs[PLANES:]
     members = params.shape[0]
     wide = members * TILE
     full = spreading(kernel_of(scale, packed[...]))
     ksum = jnp.sum(full, axis=1, keepdims=True)
     mixer = full.astype(jnp.bfloat16)
+    copies = []
     for r in range(0, SIDE, TILE):
         own = tile(params, side_params, r)
         both = jnp.concatenate([tile(scores, side_scores, r), own], axis=1)
@@ -247,11 +249,20 @@
                 part = both[:, lanes : lanes + LANES].reshape(members, TILE, LANES)
                 if at < MAIN:
                     at += which * MAIN
-                    out[:, at : at + TILE, :] = part
+                    mixed[:, at : at + TILE, :] = part
+                    here = pl.ds(at, TILE)
+                    copies.append(
+                        pltpu.make_async_copy(
+                            mixed.at[:, here, :], out.at[:, here, :], stores.at[at // TILE]
+                        )
+                    )
+                    copies[-1].start()
                 else:
                     at += which * EDGE - MAIN
                     side[:, at : at + TILE, :] = part
     by_plane(me, side, outs)
+    for copy in copies:
+        copy.wait()
 
 
 def weighted(scale, me, packed, scores, side_scores, params, side_params):
@@ -259,12 +270,16 @@
     wide = members * TILE
     vmem = pl.BlockSpec(memory_space=pltpu.VMEM)
     smem = pl.BlockSpec(memory_space=pltpu.SMEM)
-    main = jax.ShapeDtypeStruct((members, 2 * MAIN, LANES), jnp.bfloat16)
     return pl.pallas_call(
         mix_kernel,
-        out_shape=(main, *side_shapes(2 * EDGE)),
+        out_shape=(pltpu.HBM((members, 2 * MAIN, LANES), jnp.bfloat16), *side_shapes(2 * EDGE)),
         in_specs=[smem, smem] + [vmem] * 5,
-        scratch_shapes=[pltpu.VMEM((members, 2 * EDGE, LANES), jnp.bfloat16)],
+        out_specs=(pl.BlockSpec(memory_space=pl.ANY), *[vmem] * PLANES),
+        scratch_shapes=[
+            pltpu.VMEM((members, 2 * EDGE, LANES), jnp.bfloat16),
+            pltpu.VMEM((members, 2 * MAIN, LANES), jnp.bfloat16),
+            pltpu.SemaphoreType.DMA((2 * MAIN // TILE,)),
+        ],
         compiler_params=pltpu.CompilerParams(vmem_limit_bytes=24 * 1024 * 1024),
         cost_estimate=pl.CostEstimate(
             flops=4 * wide * wide * SIDE // TILE * D,
@@ -295,7 +310,7 @@
                 out[(z * PLANE + 2 * q + c) ^ me[0]] = ref[q, z]
 
 
-def regroup(body, name, shapes, *arrays, me=()):
+def regroup(body, name, shapes, *arrays, me=(), flops=0):
     vmem = pl.BlockSpec(memory_space=pltpu.VMEM)
     size = sum(math.prod(x.shape) for x in arrays)
     return pl.pallas_call(
@@ -303,7 +318,7 @@
         out_shape=shapes,
         in_specs=[pl.BlockSpec(memory_space=pltpu.SMEM)] * len(me) + [vmem] * len(arrays),
         compiler_params=pltpu.CompilerParams(vmem_limit_bytes=16 * 1024 * 1024),
-        cost_estimate=pl.CostEstimate(flops=0, bytes_accessed=4 * size, transcendentals=0),
+        cost_estimate=pl.CostEstimate(flops=flops, bytes_accessed=4 * size, transcendentals=0),
         name=name,
     )(*me, *arrays)
 
@@ -317,15 +332,26 @@
     return parts[:1] + [swap(x, z * PLANE) for z, x in enumerate(parts) if z]
 
 
-def within_plane(parts, me):
+def in_plane(parts):
     rows = parts[0].shape[1]
     shape = jax.ShapeDtypeStruct((PLANES, 2, rows, LANES), jnp.bfloat16)
-    parts = regroup(plane_kernel, "plane", (shape,) * (PLANE // 2), *parts)
-    parts = parts[:1] + tuple(swap(x, 2 * q) for q, x in enumerate(parts) if q)
+    return regroup(plane_kernel, "plane", (shape,) * (PLANE // 2), *parts, flops=LONG)
+
+
+def across_chips(parts):
+    return parts[:1] + tuple(swap(x, 2 * q) for q, x in enumerate(parts) if q)
+
+
+def in_order(parts, me):
+    rows = parts[0].shape[2]
     shape = jax.ShapeDtypeStruct((PLANE // 2, PLANES, rows, LANES), jnp.bfloat16)
     near, far = regroup(core_kernel, "core", (shape,) * 2, *parts)
     shape = jax.ShapeDtypeStruct((BLOCKS, rows, LANES), jnp.bfloat16)
     return regroup(settle_kernel, "settle", shape, near, swap(far, 1), me=(me,))
+
+
+def after(values, *others):
+    return lax.optimization_barrier((values, *others))[0]
 
 
 def plain_products(params):
@@ -467,24 +493,29 @@
     me = lax.axis_index(AXES) if tiled else 0
     me = jnp.full((1,), me, jnp.int32)
     params, *side_params = to_blocks(particles_first, particles_second, me)
+    first, second = particles_first[0], particles_second[0]
+    if tiled:
+        params = exchange(params)
+        side_params = in_plane(across_planes(side_params))
+        first, second = after((first, second), side_params[0])
+        side_params = across_chips(side_params)
     scores, *side_scores = particle_scores(
-        particles_first[0], particles_second[0], pool_images, pool_targets, batch_index[0], me
+        first, second, pool_images, pool_targets, batch_index[0], me
     )
     if tiled:
-        params, scores = exchange(params), exchange(scores)
-        side_params, side_scores = across_planes(side_params), across_planes(side_scores)
-        params, side_params, side_scores = lax.optimization_barrier(
-            (params, side_params, side_scores)
-        )
-        side_params = within_plane(side_params, me)
-        side_scores = within_plane(side_scores, me)
-        packed = distances(params, side_params)
+        side_params = in_order(after(side_params, side_scores[0]), me)
+        scores = exchange(scores)
+        side_scores = in_plane(across_planes(after(side_scores, params)))
+        packed = distances(*after((params, side_params), side_scores[0]))
+        side_scores = in_order(across_chips(side_scores), me)
         for bits in ((1,), (2, 4, 6), (8, 16, 24)):
             packed = add_over(packed, members, bits)
         main, *side = weighted(
             kernel_scale, me, packed, scores, side_scores, params, side_params
         )
-        return from_blocks(exchange(main), within_plane(across_planes(side), me))
+        side = in_order(across_chips(in_plane(across_planes(side))), me)
+        main = pltpu.with_memory_space_constraint(exchange(main), pltpu.VMEM)
+        return from_blocks(main, side)
     cut = (members, BLOCKS * ROWS // members, LANES)
     params = jnp.concatenate([params, jnp.concatenate(side_params)], axis=1)
     scores = jnp.concatenate([scores, jnp.concatenate(side_scores)], axis=1)

time: 284 us -> 233 us (0.82)
  waiting for transfers between devices: 186 us -> 135 us
    ppermute x21, waiting for transfers between devices: 161 us -> 38.4 us  [swap(): return lax.ppermute(value, AXES, pairs)]
    all_to_all x3, waiting for transfers between devices: 20 us -> 71.3 us  [exchange(): return lax.all_to_all(blocks, AXES, split_axis=0, concat_axis=0, tiled=True)]
    ppermute x7, waiting for transfers between devices: 5.5 us -> 25.5 us  [add_over(): lax.ppermute(value, AXES, [(i, i ^ bit) for i in range(members)])]
  transfers between devices with their start and end apart: 31 -> 31, of which waited for: 20 -> 14; matrix products, arithmetic and copies ran while one was open for 0% -> 1% of each run, Pallas kernels for 9% -> 11%
where the time goes in v12:
time: 233 us; the launch traced here: 232 us
  waiting for transfers between devices  135 us (58%)
  starting transfers between devices  52.2 us (22%)
  Pallas kernels  39.2 us (17%)
  local copies, waits for them, and re-layouts  3.86 us (2%)
    all_to_all x3, waiting for transfers between devices, exchange(): return lax.all_to_all(blocks, AXES, split_axis=0, concat_axis=0, tiled=True)  71.3 us
    ppermute x21, waiting for transfers between devices, swap(): return lax.ppermute(value, AXES, pairs)  38.4 us
    ppermute x21, starting transfers between devices, swap(): return lax.ppermute(value, AXES, pairs)  29.4 us
    ppermute x7, waiting for transfers between devices, add_over(): lax.ppermute(value, AXES, [(i, i ^ bit) for i in range(members)])  25.5 us
    pallas_call x1, Pallas kernels, particle_scores(): pl.pallas_call(functools.partial(score_kernel, DATA / count), out_shape=(...  23 us
    all_to_all x3, starting transfers between devices, exchange(): return lax.all_to_all(blocks, AXES, split_axis=0, concat_axis=0, tiled=True)  14.8 us
    ppermute x7, starting transfers between devices, add_over(): lax.ppermute(value, AXES, [(i, i ^ bit) for i in range(members)])  7.94 us
    pallas_call x1, Pallas kernels, weighted(): pl.pallas_call(mix_kernel, out_shape=(pltpu.HBM((members, 2 * MAIN, LANES...  5.71 us
  transfers between devices with their start and end apart: 31, of which 14 were waited for; matrix products, arithmetic and copies ran while one was open for 1% of the time, Pallas kernels for 11%

profile of v12, /device:TPU:0, one launch (start us, length us, event | category | flops | bytes accessed | tf_op | source)
XLA Modules:
  0.0 232.2 jit_solution(10627682304196550425)
XLA Ops:
  0.6 3.4 %pack.1 = (bf16[32,240,128]{2,1,0:T(8,128)(2,1)}, bf16[8,48,128]{2,1,0:T(8,128)(2,1)}, bf16[8,48,128]{2,1,0:T(8,128)(2,1)}, bf16[8,48,128]{2,1,0:T(8,128)(2,1)}, bf16[8,48,128]{2,1,0:T(8,128)(2,1)}) custom-call(s32[1]{0:T(128)} %bitcast.me, bf16[1,384,1536]{2,1,0:T(8,128)(2,1)} %first.1, bf16[1,1536,384]{2,1,0:T(8,128)(2,1)} %second.1), custom_call_target="tpu_custom_call" | custom-call | bytes 4718592 | tf_op jit(solution)/shard_map/pack/pallas_call | solution.py:413
  4.0 3.1 %collective-permute-start = (bf16[8,48,128]{2,1,0:T(8,128)(2,1)}, bf16[8,48,128]{2,1,0:T(8,128)(2,1)S(1)}, u32[]{:S(2)}, u32[]{:S(2)}) collective-permute-start(bf16[8,48,128]{2,1,0:T(8,128)(2,1)} %get-tuple-element.51), channel_id=1, source_target_pairs={{0,8},{1,9},{2,10},{3,11},{4,12},{5,13},{6,14},{7,15},{8,0},{9,1},... | collective-permute-start | bytes 294920 | tf_op jit(solution)/shard_map/ppermute | solution.py:328
  7.1 2.6 %collective-permute-start.1 = (bf16[8,48,128]{2,1,0:T(8,128)(2,1)}, bf16[8,48,128]{2,1,0:T(8,128)(2,1)S(1)}, u32[]{:S(2)}, u32[]{:S(2)}) collective-permute-start(bf16[8,48,128]{2,1,0:T(8,128)(2,1)} %get-tuple-element.52), channel_id=1, source_target_pairs={{0,16},{1,17},{2,18},{3,19},{4,20},{5,21},{6,22},{7,23},{8,24},{9,... | collective-permute-start | bytes 294920 | tf_op jit(solution)/shard_map/ppermute | solution.py:328
  9.7 6.1 %all-to-all-start = ((bf16[32,240,128]{2,1,0:T(8,128)(2,1)}), bf16[32,240,128]{2,1,0:T(8,128)(2,1)S(1)}, u32[]{:S(2)}, u32[]{:S(2)}) async-start(bf16[32,240,128]{2,1,0:T(8,128)(2,1)} %get-tuple-element.49), calls=%async_computation | async-start | bytes 3932160 | tf_op jit(solution)/shard_map/all_to_all | solution.py:485
  15.8 1.5 copy.10.image
  17.4 0.2 copy.11.target
  17.6 0.1 collective-permute-done.1.refs_2_
  17.8 0.6 copy-done.2
  18.4 1.8 collective-permute-start.3
  20.2 1.5 collective-permute-start.4
  21.7 0.3 collective-permute-start.5
  21.9 23.0 %score.1 = (bf16[32,240,128]{2,1,0:T(8,128)(2,1)}, bf16[8,48,128]{2,1,0:T(8,128)(2,1)S(1)}, bf16[8,48,128]{2,1,0:T(8,128)(2,1)S(1)}, bf16[8,48,128]{2,1,0:T(8,128)(2,1)S(1)}, bf16[8,48,128]{2,1,0:T(8,128)(2,1)S(1)}) custom-call(s32[8]{0:T(128)S(1)} %bitcast.6, s32[1]{0:T(128)} %bitcast.me, bf16[8,197,384]{2,1,0:T(8,128)(2,1)S(1)} %copy.10.image, ...), custom_call_target="tpu_custom_call" | custom-call | flops 9814671360 | bytes 7139328 | tf_op jit(solution)/shard_map/score/pallas_call | solution.py:128
  45.0 0.6 copy-done.4
  45.6 16.1 %all-to-all-done.main.params = bf16[32,240,128]{2,1,0:T(8,128)(2,1)S(1)} async-done(((bf16[32,240,128]{2,1,0:T(8,128)(2,1)}), bf16[32,240,128]{2,1,0:T(8,128)(2,1)S(1)}, u32[]{:S(2)}, u32[]{:S(2)}) %all-to-all-start) | async-done | bytes 1966112 | tf_op jit(solution)/shard_map/all_to_all | solution.py:485
  61.7 2.4 %collective-permute-start.8 = (bf16[8,48,128]{2,1,0:T(8,128)(2,1)S(1)}, bf16[8,48,128]{2,1,0:T(8,128)(2,1)S(1)}, u32[]{:S(2)}, u32[]{:S(2)}) collective-permute-start(bf16[8,48,128]{2,1,0:T(8,128)(2,1)S(1)} %get-tuple-element.72), channel_id=1, source_target_pairs={{0,16},{1,17},{2,18},{3,19},{4,20},{5,21},{6,22},{7,23},{8,24},{9,... | collective-permute-start | bytes 294920 | tf_op jit(solution)/shard_map/ppermute | solution.py:328
  64.1 2.0 collective-permute-start.9
  66.1 4.7 %all-to-all-start.1 = ((bf16[32,240,128]{2,1,0:T(8,128)(2,1)}), bf16[32,240,128]{2,1,0:T(8,128)(2,1)}, u32[]{:S(2)}, u32[]{:S(2)}) async-start(bf16[32,240,128]{2,1,0:T(8,128)(2,1)} %get-tuple-element.77), calls=%async_computation.1 | async-start | bytes 3932160 | tf_op jit(solution)/shard_map/all_to_all | solution.py:485
  70.9 1.2 collective-permute-done.8.refs_2_
  72.1 0.9 copy-done.5
  73.0 2.2 gram.1
  75.2 1.2 collective-permute-done.10
  76.4 2.6 %collective-permute-start.13 = (f32[8,128]{1,0:T(8,128)S(1)}, f32[8,128]{1,0:T(8,128)S(1)}, u32[]{:S(2)}, u32[]{:S(2)}) collective-permute-start(f32[8,128]{1,0:T(8,128)S(1)} %add.25), channel_id=1, source_target_pairs={{0,6},{1,7},{2,4},{3,5},{4,2},{5,3},{6,0},{7,1},{8,14},{9,15},{10,... | collective-permute-start | bytes 12296 | tf_op jit(solution)/shard_map/ppermute | solution.py:204
  79.0 0.6 collective-permute-start.12
  79.6 0.3 collective-permute-start.11
  79.9 1.8 collective-permute-start.17
  81.6 1.4 collective-permute-start.18
  83.0 2.5 %collective-permute-done.13 = f32[8,128]{1,0:T(8,128)S(1)} collective-permute-done((f32[8,128]{1,0:T(8,128)S(1)}, f32[8,128]{1,0:T(8,128)S(1)}, u32[]{:S(2)}, u32[]{:S(2)}) %collective-permute-start.13) | collective-permute-done | bytes 4128 | tf_op jit(solution)/shard_map/ppermute | solution.py:204
  85.5 1.4 collective-permute-start.19
  86.9 3.8 %collective-permute-start.16 = (f32[8,128]{1,0:T(8,128)S(1)}, f32[8,128]{1,0:T(8,128)S(1)}, u32[]{:S(2)}, u32[]{:S(2)}) collective-permute-start(f32[8,128]{1,0:T(8,128)S(1)} %add_add_fusion.1), channel_id=1, source_target_pairs={{0,24},{1,25},{2,26},{3,27},{4,28},{5,29},{6,30},{7,31},{8,16},{9,... | collective-permute-start | bytes 12296 | tf_op jit(solution)/shard_map/ppermute | solution.py:204
  90.6 0.7 collective-permute-start.14
  92.0 2.8 %collective-permute-done.19.refs_3_ = bf16[4,2,48,128]{3,2,1,0:T(8,128)(2,1)S(1)} collective-permute-done((bf16[4,2,48,128]{3,2,1,0:T(8,128)(2,1)S(1)}, bf16[4,2,48,128]{3,2,1,0:T(8,128)(2,1)S(1)}, u32[]{:S(2)}, u32[]{:S(2)}) %collective-permute-start.19) | collective-permute-done | bytes 98336 | tf_op jit(solution)/shard_map/ppermute | solution.py:328
  94.9 12.1 %collective-permute-done.16 = f32[8,128]{1,0:T(8,128)S(1)} collective-permute-done((f32[8,128]{1,0:T(8,128)S(1)}, f32[8,128]{1,0:T(8,128)S(1)}, u32[]{:S(2)}, u32[]{:S(2)}) %collective-permute-start.16) | collective-permute-done | bytes 4128 | tf_op jit(solution)/shard_map/ppermute | solution.py:204
  107.0 9.8 %collective-permute-done.15 = f32[8,128]{1,0:T(8,128)S(1)} collective-permute-done((f32[8,128]{1,0:T(8,128)S(1)}, f32[8,128]{1,0:T(8,128)S(1)}, u32[]{:S(2)}, u32[]{:S(2)}) %collective-permute-start.15) | collective-permute-done | bytes 4128 | tf_op jit(solution)/shard_map/ppermute | solution.py:204
  116.9 5.7 %mix.1 = (bf16[32,480,128]{2,1,0:T(8,128)(2,1)}, bf16[8,96,128]{2,1,0:T(8,128)(2,1)S(1)}, bf16[8,96,128]{2,1,0:T(8,128)(2,1)S(1)}, bf16[8,96,128]{2,1,0:T(8,128)(2,1)S(1)}, bf16[8,96,128]{2,1,0:T(8,128)(2,1)S(1)}) custom-call(f32[1]{0:T(128)S(6)} %copy.12.scale, s32[1]{0:T(128)} %bitcast.me, f32[8,128]{1,0:T(8,128)S(1)} %add_add_fusion.packed, ...), custom_call_target="tpu_custom_call" | custom-call | flops 2415919104 | bytes 9437184 | tf_op jit(solution)/shard_map/mix/pallas_call | solution.py:273
  122.6 0.6 collective-permute-start.21
  123.2 2.1 collective-permute-start.22
  125.2 1.8 collective-permute-start.23
  127.1 4.1 %all-to-all-start.2 = ((bf16[32,480,128]{2,1,0:T(8,128)(2,1)}), bf16[32,480,128]{2,1,0:T(8,128)(2,1)}, u32[]{:S(2)}, u32[]{:S(2)}) async-start(bf16[32,480,128]{2,1,0:T(8,128)(2,1)} %get-tuple-element.83), calls=%async_computation.2 | async-start | bytes 7864320 | tf_op jit(solution)/shard_map/all_to_all | solution.py:485
  131.2 1.4 collective-permute-done.21.refs_1_
  132.5 7.8 %collective-permute-done.22.refs_2_ = bf16[8,96,128]{2,1,0:T(8,128)(2,1)S(1)} collective-permute-done((bf16[8,96,128]{2,1,0:T(8,128)(2,1)S(1)}, bf16[8,96,128]{2,1,0:T(8,128)(2,1)S(1)}, u32[]{:S(2)}, u32[]{:S(2)}) %collective-permute-start.22) | collective-permute-done | bytes 196640 | tf_op jit(solution)/shard_map/ppermute | solution.py:328
  140.4 2.8 %collective-permute-start.24 = (bf16[4,2,96,128]{3,2,1,0:T(8,128)(2,1)S(1)}, bf16[4,2,96,128]{3,2,1,0:T(8,128)(2,1)S(1)}, u32[]{:S(2)}, u32[]{:S(2)}) collective-permute-start(bf16[4,2,96,128]{3,2,1,0:T(8,128)(2,1)S(1)} %get-tuple-element.89), channel_id=1, source_target_pairs={{0,2},{1,3},{2,0},{3,1},{4,6},{5,7},{6,4},{7,5},{8,10},{9,11},{10,... | collective-permute-start | bytes 589832 | tf_op jit(solution)/shard_map/ppermute | solution.py:328
  143.3 3.6 %collective-permute-start.25 = (bf16[4,2,96,128]{3,2,1,0:T(8,128)(2,1)S(1)}, bf16[4,2,96,128]{3,2,1,0:T(8,128)(2,1)S(1)}, u32[]{:S(2)}, u32[]{:S(2)}) collective-permute-start(bf16[4,2,96,128]{3,2,1,0:T(8,128)(2,1)S(1)} %get-tuple-element.90), channel_id=1, source_target_pairs={{0,4},{1,5},{2,6},{3,7},{4,0},{5,1},{6,2},{7,3},{8,12},{9,13},{10,... | collective-permute-start | bytes 589832 | tf_op jit(solution)/shard_map/ppermute | solution.py:328
  146.8 0.3 collective-permute-start.26
  147.1 13.2 %collective-permute-done.24.refs_1_ = bf16[4,2,96,128]{3,2,1,0:T(8,128)(2,1)S(1)} collective-permute-done((bf16[4,2,96,128]{3,2,1,0:T(8,128)(2,1)S(1)}, bf16[4,2,96,128]{3,2,1,0:T(8,128)(2,1)S(1)}, u32[]{:S(2)}, u32[]{:S(2)}) %collective-permute-start.24) | collective-permute-done | bytes 196640 | tf_op jit(solution)/shard_map/ppermute | solution.py:328
  160.4 10.0 %collective-permute-done.26.refs_3_ = bf16[4,2,96,128]{3,2,1,0:T(8,128)(2,1)S(1)} collective-permute-done((bf16[4,2,96,128]{3,2,1,0:T(8,128)(2,1)S(1)}, bf16[4,2,96,128]{3,2,1,0:T(8,128)(2,1)S(1)}, u32[]{:S(2)}, u32[]{:S(2)}) %collective-permute-start.26) | collective-permute-done | bytes 196640 | tf_op jit(solution)/shard_map/ppermute | solution.py:328
  170.5 1.7 collective-permute-done.27.far
  172.3 55.2 %all-to-all-done.2.main = bf16[32,480,128]{2,1,0:T(8,128)(2,1)} async-done(((bf16[32,480,128]{2,1,0:T(8,128)(2,1)}), bf16[32,480,128]{2,1,0:T(8,128)(2,1)}, u32[]{:S(2)}, u32[]{:S(2)}) %all-to-all-start.2) | async-done | bytes 3932192 | tf_op jit(solution)/shard_map/all_to_all | solution.py:485
  227.5 4.6 %unpack.1 = (bf16[1,384,1536]{2,1,0:T(8,128)(2,1)}, bf16[1,1536,384]{2,1,0:T(8,128)(2,1)}, bf16[1,384,1536]{2,1,0:T(8,128)(2,1)}, bf16[1,1536,384]{2,1,0:T(8,128)(2,1)}) custom-call(bf16[32,480,128]{2,1,0:T(8,128)(2,1)} %all-to-all-done.2.main, bf16[32,96,128]{2,1,0:T(8,128)(2,1)S(1)} %settle.5.side), custom_call_target="tpu_custom_call" | custom-call | bytes 9437184 | tf_op jit(solution)/shard_map/unpack/pallas_call | solution.py:468
  (47 shorter events, 0.7 us)
Async XLA Ops:
  4.0 13.6 %collective-permute-start = (bf16[8,48,128]{2,1,0:T(8,128)(2,1)}, bf16[8,48,128]{2,1,0:T(8,128)(2,1)S(1)}, u32[]{:S(2)}, u32[]{:S(2)}) collective-permute-start(bf16[8,48,128]{2,1,0:T(8,128)(2,1)} %get-tuple-element.51), channel_id=1, source_target_pairs={{0,8},{1,9},{2,10},{3,11},{4,12},{5,13},{6,14},{7,15},{8,0},{9,1},... | collective-permute-start | bytes 294920 | tf_op jit(solution)/shard_map/ppermute | solution.py:328
  7.1 10.6 %collective-permute-start.1 = (bf16[8,48,128]{2,1,0:T(8,128)(2,1)}, bf16[8,48,128]{2,1,0:T(8,128)(2,1)S(1)}, u32[]{:S(2)}, u32[]{:S(2)}) collective-permute-start(bf16[8,48,128]{2,1,0:T(8,128)(2,1)} %get-tuple-element.52), channel_id=1, source_target_pairs={{0,16},{1,17},{2,18},{3,19},{4,20},{5,21},{6,22},{7,23},{8,24},{9,... | collective-permute-start | bytes 294920 | tf_op jit(solution)/shard_map/ppermute | solution.py:328
  9.7 8.0 %collective-permute-start.2 = (bf16[8,48,128]{2,1,0:T(8,128)(2,1)}, bf16[8,48,128]{2,1,0:T(8,128)(2,1)S(1)}, u32[]{:S(2)}, u32[]{:S(2)}) collective-permute-start(bf16[8,48,128]{2,1,0:T(8,128)(2,1)} %get-tuple-element.53), channel_id=1, source_target_pairs={{0,24},{1,25},{2,26},{3,27},{4,28},{5,29},{6,30},{7,31},{8,16},{9,... | collective-permute-start | bytes 294920 | tf_op jit(solution)/shard_map/ppermute | solution.py:328
  9.7 52.0 %all-to-all-start = ((bf16[32,240,128]{2,1,0:T(8,128)(2,1)}), bf16[32,240,128]{2,1,0:T(8,128)(2,1)S(1)}, u32[]{:S(2)}, u32[]{:S(2)}) async-start(bf16[32,240,128]{2,1,0:T(8,128)(2,1)} %get-tuple-element.49), calls=%async_computation | async-start | bytes 3932160 | tf_op jit(solution)/shard_map/all_to_all | solution.py:485
  15.8 1.6 copy-start.6
  17.4 0.9 copy-start.2
  18.3 3.6 %copy-start = (bf16[1,384,1536]{2,1,0:T(8,128)(2,1)S(1)}, bf16[1,384,1536]{2,1,0:T(8,128)(2,1)}, u32[]{:S(2)}) copy-start(bf16[1,384,1536]{2,1,0:T(8,128)(2,1)} %first.1) | copy-start | bytes 3538948
  18.3 3.6 %copy-start.1 = (bf16[1,1536,384]{2,1,0:T(8,128)(2,1)S(1)}, bf16[1,1536,384]{2,1,0:T(8,128)(2,1)}, u32[]{:S(2)}) copy-start(bf16[1,1536,384]{2,1,0:T(8,128)(2,1)} %second.1) | copy-start | bytes 3538948
  18.3 3.6 %copy-start.3 = (s32[1,8]{1,0:T(1,128)S(1)}, s32[1,8]{1,0:T(1,128)}, u32[]{:S(2)}) copy-start(s32[1,8]{1,0:T(1,128)} %param.10) | copy-start | bytes 100
  18.4 26.6 %collective-permute-start.3 = (bf16[4,2,48,128]{3,2,1,0:T(8,128)(2,1)S(1)}, bf16[4,2,48,128]{3,2,1,0:T(8,128)(2,1)S(1)}, u32[]{:S(2)}, u32[]{:S(2)}) collective-permute-start(bf16[4,2,48,128]{3,2,1,0:T(8,128)(2,1)S(1)} %get-tuple-element.55), channel_id=1, source_target_pairs={{0,2},{1,3},{2,0},{3,1},{4,6},{5,7},{6,4},{7,5},{8,10},{9,11},{10,... | collective-permute-start | bytes 294920 | tf_op jit(solution)/shard_map/ppermute | solution.py:328
  20.2 24.8 %collective-permute-start.4 = (bf16[4,2,48,128]{3,2,1,0:T(8,128)(2,1)S(1)}, bf16[4,2,48,128]{3,2,1,0:T(8,128)(2,1)S(1)}, u32[]{:S(2)}, u32[]{:S(2)}) collective-permute-start(bf16[4,2,48,128]{3,2,1,0:T(8,128)(2,1)S(1)} %get-tuple-element.56), channel_id=1, source_target_pairs={{0,4},{1,5},{2,6},{3,7},{4,0},{5,1},{6,2},{7,3},{8,12},{9,13},{10,... | collective-permute-start | bytes 294920 | tf_op jit(solution)/shard_map/ppermute | solution.py:328
  21.7 23.3 %collective-permute-start.5 = (bf16[4,2,48,128]{3,2,1,0:T(8,128)(2,1)S(1)}, bf16[4,2,48,128]{3,2,1,0:T(8,128)(2,1)S(1)}, u32[]{:S(2)}, u32[]{:S(2)}) collective-permute-start(bf16[4,2,48,128]{3,2,1,0:T(8,128)(2,1)S(1)} %get-tuple-element.57), channel_id=1, source_target_pairs={{0,6},{1,7},{2,4},{3,5},{4,2},{5,3},{6,0},{7,1},{8,14},{9,15},{10,... | collective-permute-start | bytes 294920 | tf_op jit(solution)/shard_map/ppermute | solution.py:328
  44.9 0.6 copy-start.4
  45.6 25.2 %collective-permute-start.6 = (bf16[4,4,48,128]{3,2,1,0:T(8,128)(2,1)S(1)}, bf16[4,4,48,128]{3,2,1,0:T(8,128)(2,1)S(1)}, u32[]{:S(2)}, u32[]{:S(2)}) collective-permute-start(bf16[4,4,48,128]{3,2,1,0:T(8,128)(2,1)S(1)} %get-tuple-element.66), channel_id=1, source_target_pairs={{0,1},{1,0},{2,3},{3,2},{4,5},{5,4},{6,7},{7,6},{8,9},{9,8},{10,11... | collective-permute-start | bytes 589832 | tf_op jit(solution)/shard_map/ppermute | solution.py:328
  61.7 9.1 %collective-permute-start.7 = (bf16[8,48,128]{2,1,0:T(8,128)(2,1)S(1)}, bf16[8,48,128]{2,1,0:T(8,128)(2,1)S(1)}, u32[]{:S(2)}, u32[]{:S(2)}) collective-permute-start(bf16[8,48,128]{2,1,0:T(8,128)(2,1)S(1)} %get-tuple-element.71), channel_id=1, source_target_pairs={{0,8},{1,9},{2,10},{3,11},{4,12},{5,13},{6,14},{7,15},{8,0},{9,1},... | collective-permute-start | bytes 294920 | tf_op jit(solution)/shard_map/ppermute | solution.py:328
  61.7 10.4 %collective-permute-start.8 = (bf16[8,48,128]{2,1,0:T(8,128)(2,1)S(1)}, bf16[8,48,128]{2,1,0:T(8,128)(2,1)S(1)}, u32[]{:S(2)}, u32[]{:S(2)}) collective-permute-start(bf16[8,48,128]{2,1,0:T(8,128)(2,1)S(1)} %get-tuple-element.72), channel_id=1, source_target_pairs={{0,16},{1,17},{2,18},{3,19},{4,20},{5,21},{6,22},{7,23},{8,24},{9,... | collective-permute-start | bytes 294920 | tf_op jit(solution)/shard_map/ppermute | solution.py:328
  64.1 8.0 %collective-permute-start.9 = (bf16[8,48,128]{2,1,0:T(8,128)(2,1)S(1)}, bf16[8,48,128]{2,1,0:T(8,128)(2,1)S(1)}, u32[]{:S(2)}, u32[]{:S(2)}) collective-permute-start(bf16[8,48,128]{2,1,0:T(8,128)(2,1)S(1)} %get-tuple-element.73), channel_id=1, source_target_pairs={{0,24},{1,25},{2,26},{3,27},{4,28},{5,29},{6,30},{7,31},{8,16},{9,... | collective-permute-start | bytes 294920 | tf_op jit(solution)/shard_map/ppermute | solution.py:328
  66.1 50.8 %all-to-all-start.1 = ((bf16[32,240,128]{2,1,0:T(8,128)(2,1)}), bf16[32,240,128]{2,1,0:T(8,128)(2,1)}, u32[]{:S(2)}, u32[]{:S(2)}) async-start(bf16[32,240,128]{2,1,0:T(8,128)(2,1)} %get-tuple-element.77), calls=%async_computation.1 | async-start | bytes 3932160 | tf_op jit(solution)/shard_map/all_to_all | solution.py:485
  72.1 0.9 copy-start.5
  75.2 1.2 collective-permute-start.10
  76.4 9.1 %collective-permute-start.13 = (f32[8,128]{1,0:T(8,128)S(1)}, f32[8,128]{1,0:T(8,128)S(1)}, u32[]{:S(2)}, u32[]{:S(2)}) collective-permute-start(f32[8,128]{1,0:T(8,128)S(1)} %add.25), channel_id=1, source_target_pairs={{0,6},{1,7},{2,4},{3,5},{4,2},{5,3},{6,0},{7,1},{8,14},{9,15},{10,... | collective-permute-start | bytes 12296 | tf_op jit(solution)/shard_map/ppermute | solution.py:204
  79.0 7.9 %collective-permute-start.12 = (f32[8,128]{1,0:T(8,128)S(1)}, f32[8,128]{1,0:T(8,128)S(1)}, u32[]{:S(2)}, u32[]{:S(2)}) collective-permute-start(f32[8,128]{1,0:T(8,128)S(1)} %add.25), channel_id=1, source_target_pairs={{0,4},{1,5},{2,6},{3,7},{4,0},{5,1},{6,2},{7,3},{8,12},{9,13},{10,... | collective-permute-start | bytes 12296 | tf_op jit(solution)/shard_map/ppermute | solution.py:204
  79.6 7.3 %collective-permute-start.11 = (f32[8,128]{1,0:T(8,128)S(1)}, f32[8,128]{1,0:T(8,128)S(1)}, u32[]{:S(2)}, u32[]{:S(2)}) collective-permute-start(f32[8,128]{1,0:T(8,128)S(1)} %add.25), channel_id=1, source_target_pairs={{0,2},{1,3},{2,0},{3,1},{4,6},{5,7},{6,4},{7,5},{8,10},{9,11},{10,... | collective-permute-start | bytes 12296 | tf_op jit(solution)/shard_map/ppermute | solution.py:204
  79.9 10.8 %collective-permute-start.17 = (bf16[4,2,48,128]{3,2,1,0:T(8,128)(2,1)S(1)}, bf16[4,2,48,128]{3,2,1,0:T(8,128)(2,1)S(1)}, u32[]{:S(2)}, u32[]{:S(2)}) collective-permute-start(bf16[4,2,48,128]{3,2,1,0:T(8,128)(2,1)S(1)} %get-tuple-element.78), channel_id=1, source_target_pairs={{0,2},{1,3},{2,0},{3,1},{4,6},{5,7},{6,4},{7,5},{8,10},{9,11},{10,... | collective-permute-start | bytes 294920 | tf_op jit(solution)/shard_map/ppermute | solution.py:328
  81.6 10.4 %collective-permute-start.18 = (bf16[4,2,48,128]{3,2,1,0:T(8,128)(2,1)S(1)}, bf16[4,2,48,128]{3,2,1,0:T(8,128)(2,1)S(1)}, u32[]{:S(2)}, u32[]{:S(2)}) collective-permute-start(bf16[4,2,48,128]{3,2,1,0:T(8,128)(2,1)S(1)} %get-tuple-element.79), channel_id=1, source_target_pairs={{0,4},{1,5},{2,6},{3,7},{4,0},{5,1},{6,2},{7,3},{8,12},{9,13},{10,... | collective-permute-start | bytes 294920 | tf_op jit(solution)/shard_map/ppermute | solution.py:328
  85.5 9.3 %collective-permute-start.19 = (bf16[4,2,48,128]{3,2,1,0:T(8,128)(2,1)S(1)}, bf16[4,2,48,128]{3,2,1,0:T(8,128)(2,1)S(1)}, u32[]{:S(2)}, u32[]{:S(2)}) collective-permute-start(bf16[4,2,48,128]{3,2,1,0:T(8,128)(2,1)S(1)} %get-tuple-element.80), channel_id=1, source_target_pairs={{0,6},{1,7},{2,4},{3,5},{4,2},{5,3},{6,0},{7,1},{8,14},{9,15},{10,... | collective-permute-start | bytes 294920 | tf_op jit(solution)/shard_map/ppermute | solution.py:328
  86.9 20.2 %collective-permute-start.16 = (f32[8,128]{1,0:T(8,128)S(1)}, f32[8,128]{1,0:T(8,128)S(1)}, u32[]{:S(2)}, u32[]{:S(2)}) collective-permute-start(f32[8,128]{1,0:T(8,128)S(1)} %add_add_fusion.1), channel_id=1, source_target_pairs={{0,24},{1,25},{2,26},{3,27},{4,28},{5,29},{6,30},{7,31},{8,16},{9,... | collective-permute-start | bytes 12296 | tf_op jit(solution)/shard_map/ppermute | solution.py:204
  90.6 26.2 %collective-permute-start.15 = (f32[8,128]{1,0:T(8,128)S(1)}, f32[8,128]{1,0:T(8,128)S(1)}, u32[]{:S(2)}, u32[]{:S(2)}) collective-permute-start(f32[8,128]{1,0:T(8,128)S(1)} %add_add_fusion.1), channel_id=1, source_target_pairs={{0,16},{1,17},{2,18},{3,19},{4,20},{5,21},{6,22},{7,23},{8,24},{9,... | collective-permute-start | bytes 12296 | tf_op jit(solution)/shard_map/ppermute | solution.py:204
  90.6 26.2 %collective-permute-start.14 = (f32[8,128]{1,0:T(8,128)S(1)}, f32[8,128]{1,0:T(8,128)S(1)}, u32[]{:S(2)}, u32[]{:S(2)}) collective-permute-start(f32[8,128]{1,0:T(8,128)S(1)} %add_add_fusion.1), channel_id=1, source_target_pairs={{0,8},{1,9},{2,10},{3,11},{4,12},{5,13},{6,14},{7,15},{8,0},{9,1},... | collective-permute-start | bytes 12296 | tf_op jit(solution)/shard_map/ppermute | solution.py:204
  94.9 22.0 %collective-permute-start.20 = (bf16[4,4,48,128]{3,2,1,0:T(8,128)(2,1)S(1)}, bf16[4,4,48,128]{3,2,1,0:T(8,128)(2,1)S(1)}, u32[]{:S(2)}, u32[]{:S(2)}) collective-permute-start(bf16[4,4,48,128]{3,2,1,0:T(8,128)(2,1)S(1)} %get-tuple-element.82), channel_id=1, source_target_pairs={{0,1},{1,0},{2,3},{3,2},{4,5},{5,4},{6,7},{7,6},{8,9},{9,8},{10,11... | collective-permute-start | bytes 589832 | tf_op jit(solution)/shard_map/ppermute | solution.py:328
  122.6 9.9 %collective-permute-start.21 = (bf16[8,96,128]{2,1,0:T(8,128)(2,1)S(1)}, bf16[8,96,128]{2,1,0:T(8,128)(2,1)S(1)}, u32[]{:S(2)}, u32[]{:S(2)}) collective-permute-start(bf16[8,96,128]{2,1,0:T(8,128)(2,1)S(1)} %get-tuple-element.85), channel_id=1, source_target_pairs={{0,8},{1,9},{2,10},{3,11},{4,12},{5,13},{6,14},{7,15},{8,0},{9,1},... | collective-permute-start | bytes 589832 | tf_op jit(solution)/shard_map/ppermute | solution.py:328
  123.2 17.2 %collective-permute-start.22 = (bf16[8,96,128]{2,1,0:T(8,128)(2,1)S(1)}, bf16[8,96,128]{2,1,0:T(8,128)(2,1)S(1)}, u32[]{:S(2)}, u32[]{:S(2)}) collective-permute-start(bf16[8,96,128]{2,1,0:T(8,128)(2,1)S(1)} %get-tuple-element.86), channel_id=1, source_target_pairs={{0,16},{1,17},{2,18},{3,19},{4,20},{5,21},{6,22},{7,23},{8,24},{9,... | collective-permute-start | bytes 589832 | tf_op jit(solution)/shard_map/ppermute | solution.py:328
  125.2 15.1 %collective-permute-start.23 = (bf16[8,96,128]{2,1,0:T(8,128)(2,1)S(1)}, bf16[8,96,128]{2,1,0:T(8,128)(2,1)S(1)}, u32[]{:S(2)}, u32[]{:S(2)}) collective-permute-start(bf16[8,96,128]{2,1,0:T(8,128)(2,1)S(1)} %get-tuple-element.87), channel_id=1, source_target_pairs={{0,24},{1,25},{2,26},{3,27},{4,28},{5,29},{6,30},{7,31},{8,16},{9,... | collective-permute-start | bytes 589832 | tf_op jit(solution)/shard_map/ppermute | solution.py:328
  127.1 100.4 %all-to-all-start.2 = ((bf16[32,480,128]{2,1,0:T(8,128)(2,1)}), bf16[32,480,128]{2,1,0:T(8,128)(2,1)}, u32[]{:S(2)}, u32[]{:S(2)}) async-start(bf16[32,480,128]{2,1,0:T(8,128)(2,1)} %get-tuple-element.83), calls=%async_computation.2 | async-start | bytes 7864320 | tf_op jit(solution)/shard_map/all_to_all | solution.py:485
  140.4 19.9 %collective-permute-start.24 = (bf16[4,2,96,128]{3,2,1,0:T(8,128)(2,1)S(1)}, bf16[4,2,96,128]{3,2,1,0:T(8,128)(2,1)S(1)}, u32[]{:S(2)}, u32[]{:S(2)}) collective-permute-start(bf16[4,2,96,128]{3,2,1,0:T(8,128)(2,1)S(1)} %get-tuple-element.89), channel_id=1, source_target_pairs={{0,2},{1,3},{2,0},{3,1},{4,6},{5,7},{6,4},{7,5},{8,10},{9,11},{10,... | collective-permute-start | bytes 589832 | tf_op jit(solution)/shard_map/ppermute | solution.py:328
  143.3 17.1 %collective-permute-start.25 = (bf16[4,2,96,128]{3,2,1,0:T(8,128)(2,1)S(1)}, bf16[4,2,96,128]{3,2,1,0:T(8,128)(2,1)S(1)}, u32[]{:S(2)}, u32[]{:S(2)}) collective-permute-start(bf16[4,2,96,128]{3,2,1,0:T(8,128)(2,1)S(1)} %get-tuple-element.90), channel_id=1, source_target_pairs={{0,4},{1,5},{2,6},{3,7},{4,0},{5,1},{6,2},{7,3},{8,12},{9,13},{10,... | collective-permute-start | bytes 589832 | tf_op jit(solution)/shard_map/ppermute | solution.py:328
  146.8 23.6 %collective-permute-start.26 = (bf16[4,2,96,128]{3,2,1,0:T(8,128)(2,1)S(1)}, bf16[4,2,96,128]{3,2,1,0:T(8,128)(2,1)S(1)}, u32[]{:S(2)}, u32[]{:S(2)}) collective-permute-start(bf16[4,2,96,128]{3,2,1,0:T(8,128)(2,1)S(1)} %get-tuple-element.91), channel_id=1, source_target_pairs={{0,6},{1,7},{2,4},{3,5},{4,2},{5,3},{6,0},{7,1},{8,14},{9,15},{10,... | collective-permute-start | bytes 589832 | tf_op jit(solution)/shard_map/ppermute | solution.py:328
  170.4 1.8 collective-permute-start.27

commit v13 on v12

--- a/solution.py
+++ b/solution.py
@@ -22,7 +22,8 @@
 SIDE = 2 * EDGE
 GROUPS = range(D // LANES)
 ROWS = SIDE * len(GROUPS)
-MAIN = ROWS - EDGE
+MAIN = 2 * SIDE
+REST = ROWS - MAIN
 PLANES = 4
 PLANE = BLOCKS // PLANES
 LONG = 10**11
@@ -40,10 +41,10 @@
     for g in GROUPS:
         at = g * SIDE + row
         part = value[:, g * LANES : (g + 1) * LANES]
-        if at < MAIN:
+        if at >= MAIN:
+            side[block, at - MAIN : at - MAIN + EDGE, :] = part
+        else:
             main[block, at : at + EDGE, :] = part
-        else:
-            side[block, at - MAIN : at - MAIN + EDGE, :] = part
 
 
 def by_plane(me, side, outs):
@@ -127,7 +128,7 @@
     bf = jnp.bfloat16
     return pl.pallas_call(
         functools.partial(score_kernel, DATA / count),
-        out_shape=(pltpu.HBM((BLOCKS, MAIN, LANES), bf), *side_shapes(EDGE)),
+        out_shape=(pltpu.HBM((BLOCKS, MAIN, LANES), bf), *side_shapes(REST)),
         grid_spec=pltpu.PrefetchScalarGridSpec(
             num_scalar_prefetch=2,
             grid=(count,),
@@ -139,10 +140,10 @@
             ],
             out_specs=(
                 pl.BlockSpec((BLOCKS, MAIN, LANES), lambda b, picks, me: (0, 0, 0)),
-                *[pl.BlockSpec((PLANE, EDGE, LANES), lambda b, picks, me: (0, 0, 0))] * PLANES,
+                *[pl.BlockSpec((PLANE, REST, LANES), lambda b, picks, me: (0, 0, 0))] * PLANES,
             ),
             scratch_shapes=[
-                pltpu.VMEM((BLOCKS, EDGE, LANES), bf),
+                pltpu.VMEM((BLOCKS, REST, LANES), bf),
                 pltpu.VMEM((PAD, D), jnp.float32),
                 pltpu.VMEM((PAD, D), jnp.float32),
                 pltpu.VMEM((rows, D), bf),
@@ -227,67 +228,107 @@
     return jnp.where(row == col, full, 0.0)
 
 
-def mix_kernel(scale, me, packed, scores, side_scores, params, side_params, out, *refs):
-    outs, (side, mixed, stores) = refs[:PLANES], refs[PLANES:]
+def mix(mixer, ksum, scores, own):
+    members = mixer.shape[0] // TILE
+    wide = own.shape[1]
+    both = dot(mixer, jnp.concatenate([scores, own], axis=1), ((1,), (0,)))
+    pushed = ksum * own.astype(jnp.float32) - both[:, wide:]
+    both = jnp.concatenate([both[:, :wide], pushed], axis=1) * (1.0 / members)
+    return both.astype(jnp.bfloat16)
+
+
+def rows_of(ref, at):
+    return ref[:, at : at + TILE, :].reshape(ref.shape[0] * TILE, LANES)
+
+
+def mix_side_kernel(scale, me, packed, scores, params, mixing, *refs):
+    outs, side = refs[:PLANES], refs[PLANES]
     members = params.shape[0]
-    wide = members * TILE
     full = spreading(kernel_of(scale, packed[...]))
     ksum = jnp.sum(full, axis=1, keepdims=True)
     mixer = full.astype(jnp.bfloat16)
-    copies = []
-    for r in range(0, SIDE, TILE):
-        own = tile(params, side_params, r)
-        both = jnp.concatenate([tile(scores, side_scores, r), own], axis=1)
-        both = dot(mixer, both, ((1,), (0,)))
-        pushed = ksum * own.astype(jnp.float32) - both[:, D:]
-        both = jnp.concatenate([both[:, :D], pushed], axis=1) * (1.0 / members)
-        both = both.astype(jnp.bfloat16)
-        for which in range(2):
-            for g in GROUPS:
-                at = g * SIDE + r
-                lanes = which * D + g * LANES
-                part = both[:, lanes : lanes + LANES].reshape(members, TILE, LANES)
-                if at < MAIN:
-                    at += which * MAIN
-                    mixed[:, at : at + TILE, :] = part
-                    here = pl.ds(at, TILE)
-                    copies.append(
-                        pltpu.make_async_copy(
-                            mixed.at[:, here, :], out.at[:, here, :], stores.at[at // TILE]
-                        )
-                    )
-                    copies[-1].start()
-                else:
-                    at += which * EDGE - MAIN
-                    side[:, at : at + TILE, :] = part
+    mixing[...] = mixer
+    count = SIDE // TILE // 2
+    for start in range(0, SIDE, count * TILE):
+        at = [start + q * TILE for q in range(count)]
+        got = jnp.concatenate([rows_of(scores, r) for r in at], axis=1)
+        own = jnp.concatenate([rows_of(params, r) for r in at], axis=1)
+        both = mix(mixer, ksum, got, own)
+        for q in range(2 * count):
+            part = both[:, q * LANES : (q + 1) * LANES].reshape(members, TILE, LANES)
+            r = q // count * REST + at[q % count]
+            side[:, r : r + TILE, :] = part
     by_plane(me, side, outs)
-    for copy in copies:
-        copy.wait()
-
-
-def weighted(scale, me, packed, scores, side_scores, params, side_params):
+
+
+def mix_side(scale, me, packed, scores, params):
     members = params.shape[0]
     wide = members * TILE
     vmem = pl.BlockSpec(memory_space=pltpu.VMEM)
     smem = pl.BlockSpec(memory_space=pltpu.SMEM)
+    mixing = jax.ShapeDtypeStruct((wide, wide), jnp.bfloat16)
     return pl.pallas_call(
-        mix_kernel,
-        out_shape=(pltpu.HBM((members, 2 * MAIN, LANES), jnp.bfloat16), *side_shapes(2 * EDGE)),
-        in_specs=[smem, smem] + [vmem] * 5,
-        out_specs=(pl.BlockSpec(memory_space=pl.ANY), *[vmem] * PLANES),
+        mix_side_kernel,
+        out_shape=(mixing, *side_shapes(2 * REST)),
+        in_specs=[smem, smem] + [vmem] * 3,
+        scratch_shapes=[pltpu.VMEM((members, 2 * REST, LANES), jnp.bfloat16)],
+        compiler_params=pltpu.CompilerParams(vmem_limit_bytes=24 * 1024 * 1024),
+        cost_estimate=pl.CostEstimate(
+            flops=4 * wide * wide * REST // TILE * LANES,
+            bytes_accessed=8 * members * REST * LANES,
+            transcendentals=0,
+        ),
+        name="mix_side",
+    )(scale, me, packed, scores, params)
+
+
+def mix_main_kernel(mixing, scores, params, out, mixed, stores):
+    members = params.shape[0]
+    mixer = mixing[...]
+    ksum = jnp.sum(mixer.astype(jnp.float32), axis=1, keepdims=True)
+    groups = MAIN // SIDE
+    copies = []
+    for r in range(0, SIDE, TILE):
+        at = [g * SIDE + r for g in range(groups)]
+        got = jnp.concatenate([rows_of(scores, x) for x in at], axis=1)
+        own = jnp.concatenate([rows_of(params, x) for x in at], axis=1)
+        both = mix(mixer, ksum, got, own)
+        for q in range(2 * groups):
+            part = both[:, q * LANES : (q + 1) * LANES].reshape(members, TILE, LANES)
+            x = q // groups * MAIN + at[q % groups]
+            mixed[:, x : x + TILE, :] = part
+            here = pl.ds(x, TILE)
+            copies.append(
+                pltpu.make_async_copy(
+                    mixed.at[:, here, :], out.at[:, here, :], stores.at[x // TILE]
+                )
+            )
+            copies[-1].start()
+    for copy in copies:
+        copy.wait()
+
+
+def mix_main(mixing, scores, params):
+    members = params.shape[0]
+    wide = members * TILE
+    vmem = pl.BlockSpec(memory_space=pltpu.VMEM)
+    return pl.pallas_call(
+        mix_main_kernel,
+        out_shape=pltpu.HBM((members, 2 * MAIN, LANES), jnp.bfloat16),
+        in_specs=[vmem] * 3,
+        out_specs=pl.BlockSpec(memory_space=pl.ANY),
         scratch_shapes=[
-            pltpu.VMEM((members, 2 * EDGE, LANES), jnp.bfloat16),
             pltpu.VMEM((members, 2 * MAIN, LANES), jnp.bfloat16),
             pltpu.SemaphoreType.DMA((2 * MAIN // TILE,)),
         ],
         compiler_params=pltpu.CompilerParams(vmem_limit_bytes=24 * 1024 * 1024),
         cost_estimate=pl.CostEstimate(
-            flops=4 * wide * wide * SIDE // TILE * D,
-            bytes_accessed=8 * members * ROWS * LANES,
+            flops=4 * wide * wide * MAIN // TILE * LANES,
+            bytes_accessed=8 * members * MAIN * LANES,
             transcendentals=0,
         ),
-        name="mix",
-    )(scale, me, packed, scores, side_scores, params, side_params)
+        name="mix_main",
+    )(mixing, scores, params)
 
 
 def plane_kernel(*refs):
@@ -376,9 +417,24 @@
 TALL = FF // STEPS
 
 
-def pack_kernel(me, first, second, out, *refs):
-    outs, (wide, tall, packed, side, loads, stores) = refs[:PLANES], refs[PLANES:]
-
+def pack_side_kernel(me, first, second, *refs):
+    outs, (wide, tall, side, loads) = refs[:PLANES], refs[PLANES:]
+    copies = [pltpu.make_async_copy(second.at[0, :, pl.ds(D - LANES, LANES)], tall, loads.at[COLS])]
+    for c in range(COLS):
+        here = first.at[0, :, pl.ds((c + 1) * D - LANES, LANES)]
+        copies.append(pltpu.make_async_copy(here, wide.at[c], loads.at[c]))
+    for copy in copies:
+        copy.start()
+    for copy in copies:
+        copy.wait()
+    for b in range(BLOCKS):
+        r = b // COLS * EDGE
+        side[b, 0:EDGE, :] = wide[b % COLS, r : r + EDGE, :]
+        side[b, EDGE:REST, :] = tall[b * EDGE : (b + 1) * EDGE, :]
+    by_plane(me, side, outs)
+
+
+def pack_main_kernel(first, second, out, wide, tall, packed, loads, stores):
     def load(d):
         return (
             pltpu.make_async_copy(
@@ -400,40 +456,63 @@
         for copy in load(d):
             copy.wait()
         for c in range(COLS):
-            put(packed, side, d * COLS + c, 0, wide[d, :, c * D : (c + 1) * D])
-            put(packed, side, d * COLS + c, EDGE, tall[d, c * EDGE : (c + 1) * EDGE, :])
+            for g in range(MAIN // SIDE):
+                b, at = d * COLS + c, g * SIDE
+                lanes = g * LANES
+                packed[b, at : at + EDGE, :] = wide[d, :, c * D + lanes : c * D + lanes + LANES]
+                packed[b, at + EDGE : at + SIDE, :] = tall[
+                    d, c * EDGE : (c + 1) * EDGE, lanes : lanes + LANES
+                ]
         store(d).start()
-    by_plane(me, side, outs)
     for d in range(STEPS):
         store(d).wait()
 
 
 def to_blocks(first, second, me):
     bf = jnp.bfloat16
-    return pl.pallas_call(
-        pack_kernel,
-        out_shape=(pltpu.HBM((BLOCKS, MAIN, LANES), bf), *side_shapes(EDGE)),
-        in_specs=[pl.BlockSpec(memory_space=pltpu.SMEM)]
-        + [pl.BlockSpec(memory_space=pl.ANY)] * 2,
-        out_specs=(
-            pl.BlockSpec(memory_space=pl.ANY),
-            *[pl.BlockSpec(memory_space=pltpu.VMEM)] * PLANES,
-        ),
+    anywhere = [pl.BlockSpec(memory_space=pl.ANY)]
+    params = pltpu.CompilerParams(vmem_limit_bytes=56 * 1024 * 1024)
+    cost = pl.CostEstimate(flops=0, bytes_accessed=4 * D * FF, transcendentals=0)
+    side = pl.pallas_call(
+        pack_side_kernel,
+        out_shape=side_shapes(REST),
+        in_specs=[pl.BlockSpec(memory_space=pltpu.SMEM)] + anywhere * 2,
+        scratch_shapes=[
+            pltpu.VMEM((COLS, D, LANES), bf),
+            pltpu.VMEM((FF, LANES), bf),
+            pltpu.VMEM((BLOCKS, REST, LANES), bf),
+            pltpu.SemaphoreType.DMA((COLS + 1,)),
+        ],
+        compiler_params=params,
+        cost_estimate=cost,
+        name="pack_side",
+    )(me, first, second)
+    main = pl.pallas_call(
+        pack_main_kernel,
+        out_shape=pltpu.HBM((BLOCKS, MAIN, LANES), bf),
+        in_specs=anywhere * 2,
+        out_specs=anywhere[0],
         scratch_shapes=[
             pltpu.VMEM((STEPS, EDGE, FF), bf),
             pltpu.VMEM((STEPS, TALL, D), bf),
             pltpu.VMEM((BLOCKS, MAIN, LANES), bf),
-            pltpu.VMEM((BLOCKS, EDGE, LANES), bf),
             pltpu.SemaphoreType.DMA((2, STEPS)),
             pltpu.SemaphoreType.DMA((STEPS,)),
         ],
-        compiler_params=pltpu.CompilerParams(vmem_limit_bytes=56 * 1024 * 1024),
-        cost_estimate=pl.CostEstimate(flops=0, bytes_accessed=8 * D * FF, transcendentals=0),
-        name="pack",
-    )(me, first, second)
-
-
-def unpack_kernel(main, side, first_a, second_a, first_s, second_s, wide, tall, stores):
+        compiler_params=params,
+        cost_estimate=cost,
+        name="pack_main",
+    )(first, second)
+    return main, side
+
+
+def unpack_kernel(source, side, first_a, second_a, first_s, second_s, *refs):
+    main, wide, tall, loads, stores = refs
+
+    def load(d):
+        here = pl.ds(d * COLS, COLS)
+        return pltpu.make_async_copy(source.at[here], main.at[here], loads.at[d])
+
     def store(which, d):
         first, second = ((first_a, second_a), (first_s, second_s))[which]
         return (
@@ -445,16 +524,23 @@
             ),
         )
 
-    for which in range(2):
-        for d in range(STEPS):
+    for d in range(STEPS):
+        load(d).start()
+    for d in range(STEPS):
+        load(d).wait()
+        for which in range(2):
             for c in range(COLS):
                 for g in GROUPS:
-                    b, at = d * COLS + c, which * MAIN + g * SIDE
+                    b, at = d * COLS + c, g * SIDE
+                    if at < MAIN:
+                        ref, at = main, which * MAIN + at
+                    else:
+                        ref, at = side, which * REST + at - MAIN
                     lanes = slice(c * D + g * LANES, c * D + (g + 1) * LANES)
-                    wide[which, d, :, lanes] = main[b, at : at + EDGE, :]
-                    ref, at = (main, at + EDGE) if g * SIDE + EDGE < MAIN else (side, which * EDGE)
+                    wide[which, d, :, lanes] = ref[b, at : at + EDGE, :]
                     lanes = slice(g * LANES, (g + 1) * LANES)
-                    tall[which, d, c * EDGE : (c + 1) * EDGE, lanes] = ref[b, at : at + EDGE, :]
+                    here = slice(c * EDGE, (c + 1) * EDGE)
+                    tall[which, d, here, lanes] = ref[b, at + EDGE : at + SIDE, :]
             for copy in store(which, d):
                 copy.start()
     for which in range(2):
@@ -468,14 +554,16 @@
     return pl.pallas_call(
         unpack_kernel,
         out_shape=(pltpu.HBM((1, D, FF), bf), pltpu.HBM((1, FF, D), bf)) * 2,
-        in_specs=[pl.BlockSpec(memory_space=pltpu.VMEM)] * 2,
+        in_specs=[pl.BlockSpec(memory_space=pl.ANY), pl.BlockSpec(memory_space=pltpu.VMEM)],
         out_specs=(pl.BlockSpec(memory_space=pl.ANY),) * 4,
         scratch_shapes=[
+            pltpu.VMEM((BLOCKS, 2 * MAIN, LANES), bf),
             pltpu.VMEM((2, STEPS, EDGE, FF), bf),
             pltpu.VMEM((2, STEPS, TALL, D), bf),
+            pltpu.SemaphoreType.DMA((STEPS,)),
             pltpu.SemaphoreType.DMA((2, 2, STEPS)),
         ],
-        compiler_params=pltpu.CompilerParams(vmem_limit_bytes=24 * 1024 * 1024),
+        compiler_params=pltpu.CompilerParams(vmem_limit_bytes=57 * 1024 * 1024),
         cost_estimate=pl.CostEstimate(flops=0, bytes_accessed=16 * D * FF, transcendentals=0),
         name="unpack",
     )(main, side)
@@ -492,11 +580,11 @@
     tiled = members == BLOCKS
     me = lax.axis_index(AXES) if tiled else 0
     me = jnp.full((1,), me, jnp.int32)
-    params, *side_params = to_blocks(particles_first, particles_second, me)
+    params, side_params = to_blocks(particles_first, particles_second, me)
     first, second = particles_first[0], particles_second[0]
     if tiled:
         params = exchange(params)
-        side_params = in_plane(across_planes(side_params))
+        side_params = in_plane(across_planes(list(side_params)))
         first, second = after((first, second), side_params[0])
         side_params = across_chips(side_params)
     scores, *side_scores = particle_scores(
@@ -510,12 +598,10 @@
         side_scores = in_order(across_chips(side_scores), me)
         for bits in ((1,), (2, 4, 6), (8, 16, 24)):
             packed = add_over(packed, members, bits)
-        main, *side = weighted(
-            kernel_scale, me, packed, scores, side_scores, params, side_params
-        )
+        mixing, *side = mix_side(kernel_scale, me, packed, side_scores, side_params)
+        main = mix_main(mixing, scores, params)
         side = in_order(across_chips(in_plane(across_planes(side))), me)
-        main = pltpu.with_memory_space_constraint(exchange(main), pltpu.VMEM)
-        return from_blocks(main, side)
+        return from_blocks(exchange(main), side)
     cut = (members, BLOCKS * ROWS // members, LANES)
     params = jnp.concatenate([params, jnp.concatenate(side_params)], axis=1)
     scores = jnp.concatenate([scores, jnp.concatenate(side_scores)], axis=1)

time: 233 us -> 233 us (level)
  waiting for transfers between devices: 135 us -> 110 us
  starting transfers between devices: 52.2 us -> 68.2 us
  Pallas kernels: 39.2 us -> 45.2 us
  local copies, waits for them, and re-layouts: 3.86 us -> 7.22 us
    all_to_all x3, waiting for transfers between devices: 71.3 us -> 43.2 us  [exchange(): return lax.all_to_all(blocks, AXES, split_axis=0, concat_axis=0, tiled=True)]
    ppermute x21, waiting for transfers between devices: 38.4 us -> 59.7 us  [swap(): return lax.ppermute(value, AXES, pairs)]
    ppermute x7, waiting for transfers between devices: 25.5 us -> 7.07 us  [add_over(): lax.ppermute(value, AXES, [(i, i ^ bit) for i in range(members)])]
    ppermute x21, starting transfers between devices: 29.4 us -> 41.1 us  [swap(): return lax.ppermute(value, AXES, pairs)]
    pallas_call x9, Pallas kernels: 0.34 us -> 4.62 us  [regroup(): pl.pallas_call(body, out_shape=shapes, in_specs=[pl.BlockSpec(memory_spac...]
    unnamed x16 -> x26, local copies, waits for them, and re-layouts: 3.86 us -> 7.22 us
    ppermute x7, starting transfers between devices: 7.94 us -> 11 us  [add_over(): lax.ppermute(value, AXES, [(i, i ^ bit) for i in range(members)])]
    pallas_call x2 -> x4, Pallas kernels: 9.09 us -> 10.3 us  [the longest x1 3.24 us: mix_main(): pl.pallas_call(mix_main_kernel, out_shape=pltpu.HBM((members, 2 * MAIN, L...]
  transfers between devices with their start and end apart: 31 -> 31, of which waited for: 14 -> 15; matrix products, arithmetic and copies ran while one was open for 1% -> 1% of each run, Pallas kernels for 11% -> 16%
where the time goes in v13:
time: 233 us; the launch traced here: 232 us
  waiting for transfers between devices  110 us (47%)
  starting transfers between devices  68.2 us (29%)
  Pallas kernels  45.2 us (19%)
  local copies, waits for them, and re-layouts  7.22 us (3%)
    ppermute x21, waiting for transfers between devices, swap(): return lax.ppermute(value, AXES, pairs)  59.7 us
    all_to_all x3, waiting for transfers between devices, exchange(): return lax.all_to_all(blocks, AXES, split_axis=0, concat_axis=0, tiled=True)  43.2 us
    ppermute x21, starting transfers between devices, swap(): return lax.ppermute(value, AXES, pairs)  41.1 us
    pallas_call x1, Pallas kernels, particle_scores(): pl.pallas_call(functools.partial(score_kernel, DATA / count), out_shape=(...  23.1 us
    all_to_all x3, starting transfers between devices, exchange(): return lax.all_to_all(blocks, AXES, split_axis=0, concat_axis=0, tiled=True)  16.1 us
    ppermute x7, starting transfers between devices, add_over(): lax.ppermute(value, AXES, [(i, i ^ bit) for i in range(members)])  11 us
    unnamed x26, local copies, waits for them, and re-layouts  7.22 us
    ppermute x7, waiting for transfers between devices, add_over(): lax.ppermute(value, AXES, [(i, i ^ bit) for i in range(members)])  7.07 us
  transfers between devices with their start and end apart: 31, of which 15 were waited for; matrix products, arithmetic and copies ran while one was open for 1% of the time, Pallas kernels for 16%

profile of v13, /device:TPU:0, one launch (start us, length us, event | category | flops | bytes accessed | tf_op | source)
XLA Modules:
  0.0 232.3 jit_solution(13748170304735990052)
XLA Ops:
  0.6 2.1 pack_side.1
  2.8 3.1 %collective-permute-start = (bf16[8,96,128]{2,1,0:T(8,128)(2,1)}, bf16[8,96,128]{2,1,0:T(8,128)(2,1)S(1)}, u32[]{:S(2)}, u32[]{:S(2)}) collective-permute-start(bf16[8,96,128]{2,1,0:T(8,128)(2,1)} %get-tuple-element.49), channel_id=1, source_target_pairs={{0,8},{1,9},{2,10},{3,11},{4,12},{5,13},{6,14},{7,15},{8,0},{9,1},... | collective-permute-start | bytes 589832 | tf_op jit(solution)/shard_map/ppermute | solution.py:369
  5.9 2.6 %collective-permute-start.1 = (bf16[8,96,128]{2,1,0:T(8,128)(2,1)}, bf16[8,96,128]{2,1,0:T(8,128)(2,1)S(1)}, u32[]{:S(2)}, u32[]{:S(2)}) collective-permute-start(bf16[8,96,128]{2,1,0:T(8,128)(2,1)} %get-tuple-element.50), channel_id=1, source_target_pairs={{0,16},{1,17},{2,18},{3,19},{4,20},{5,21},{6,22},{7,23},{8,24},{9,... | collective-permute-start | bytes 589832 | tf_op jit(solution)/shard_map/ppermute | solution.py:369
  8.5 2.6 %pack_main.1 = bf16[32,192,128]{2,1,0:T(8,128)(2,1)} custom-call(bf16[1,384,1536]{2,1,0:T(8,128)(2,1)} %first.3, bf16[1,1536,384]{2,1,0:T(8,128)(2,1)} %second.3), custom_call_target="tpu_custom_call" | custom-call | bytes 2359296 | tf_op jit(solution)/shard_map/pack_main/pallas_call | solution.py:490
  11.1 6.1 %all-to-all-start = ((bf16[32,192,128]{2,1,0:T(8,128)(2,1)}), bf16[32,192,128]{2,1,0:T(8,128)(2,1)S(1)}, u32[]{:S(2)}, u32[]{:S(2)}) async-start(bf16[32,192,128]{2,1,0:T(8,128)(2,1)} %pack_main.1), calls=%async_computation | async-start | bytes 3145728 | tf_op jit(solution)/shard_map/all_to_all | solution.py:573
  17.2 1.5 copy.10.image
  19.0 5.2 %collective-permute-done.1.refs_2_ = bf16[8,96,128]{2,1,0:T(8,128)(2,1)S(1)} collective-permute-done((bf16[8,96,128]{2,1,0:T(8,128)(2,1)}, bf16[8,96,128]{2,1,0:T(8,128)(2,1)S(1)}, u32[]{:S(2)}, u32[]{:S(2)}) %collective-permute-start.1) | collective-permute-done | bytes 196640 | tf_op jit(solution)/shard_map/ppermute | solution.py:369
  25.0 2.5 %collective-permute-start.3 = (bf16[4,2,96,128]{3,2,1,0:T(8,128)(2,1)S(1)}, bf16[4,2,96,128]{3,2,1,0:T(8,128)(2,1)S(1)}, u32[]{:S(2)}, u32[]{:S(2)}) collective-permute-start(bf16[4,2,96,128]{3,2,1,0:T(8,128)(2,1)S(1)} %get-tuple-element.53), channel_id=1, source_target_pairs={{0,2},{1,3},{2,0},{3,1},{4,6},{5,7},{6,4},{7,5},{8,10},{9,11},{10,... | collective-permute-start | bytes 589832 | tf_op jit(solution)/shard_map/ppermute | solution.py:369
  27.5 1.7 collective-permute-start.4
  29.1 23.1 %score.1 = (bf16[32,192,128]{2,1,0:T(8,128)(2,1)}, bf16[8,96,128]{2,1,0:T(8,128)(2,1)S(1)}, bf16[8,96,128]{2,1,0:T(8,128)(2,1)}, bf16[8,96,128]{2,1,0:T(8,128)(2,1)}, bf16[8,96,128]{2,1,0:T(8,128)(2,1)}) custom-call(s32[8]{0:T(128)S(1)} %bitcast.6, s32[1]{0:T(128)} %bitcast.me, bf16[8,197,384]{2,1,0:T(8,128)(2,1)S(1)} %copy.10.image, ...), custom_call_target="tpu_custom_call" | custom-call | flops 9814671360 | bytes 7139328 | tf_op jit(solution)/shard_map/score/pallas_call | solution.py:129
  52.9 6.9 %all-to-all-done.main.params = bf16[32,192,128]{2,1,0:T(8,128)(2,1)S(1)} async-done(((bf16[32,192,128]{2,1,0:T(8,128)(2,1)}), bf16[32,192,128]{2,1,0:T(8,128)(2,1)S(1)}, u32[]{:S(2)}, u32[]{:S(2)}) %all-to-all-start) | async-done | bytes 1572896 | tf_op jit(solution)/shard_map/all_to_all | solution.py:573
  59.7 9.3 %collective-permute-start.7 = (bf16[8,96,128]{2,1,0:T(8,128)(2,1)}, bf16[8,96,128]{2,1,0:T(8,128)(2,1)}, u32[]{:S(2)}, u32[]{:S(2)}) collective-permute-start(bf16[8,96,128]{2,1,0:T(8,128)(2,1)} %get-tuple-element.69), channel_id=1, source_target_pairs={{0,8},{1,9},{2,10},{3,11},{4,12},{5,13},{6,14},{7,15},{8,0},{9,1},... | collective-permute-start | bytes 589832 | tf_op jit(solution)/shard_map/ppermute | solution.py:369
  69.0 2.5 %collective-permute-start.8 = (bf16[8,96,128]{2,1,0:T(8,128)(2,1)}, bf16[8,96,128]{2,1,0:T(8,128)(2,1)}, u32[]{:S(2)}, u32[]{:S(2)}) collective-permute-start(bf16[8,96,128]{2,1,0:T(8,128)(2,1)} %get-tuple-element.70), channel_id=1, source_target_pairs={{0,16},{1,17},{2,18},{3,19},{4,20},{5,21},{6,22},{7,23},{8,24},{9,... | collective-permute-start | bytes 589832 | tf_op jit(solution)/shard_map/ppermute | solution.py:369
  71.5 1.5 collective-permute-start.9
  73.0 5.3 %all-to-all-start.1 = ((bf16[32,192,128]{2,1,0:T(8,128)(2,1)}), bf16[32,192,128]{2,1,0:T(8,128)(2,1)S(1)}, u32[]{:S(2)}, u32[]{:S(2)}) async-start(bf16[32,192,128]{2,1,0:T(8,128)(2,1)} %get-tuple-element.81), calls=%async_computation.1 | async-start | bytes 3145728 | tf_op jit(solution)/shard_map/all_to_all | solution.py:573
  78.3 1.1 core.3
  79.5 1.8 collective-permute-done.9.refs_3_
  82.2 1.2 plane.4
  83.4 1.5 collective-permute-start.17
  84.9 2.1 collective-permute-start.18
  87.0 2.2 gram.1
  89.2 1.2 collective-permute-done.10
  90.4 2.9 %collective-permute-start.13 = (f32[8,128]{1,0:T(8,128)S(1)}, f32[8,128]{1,0:T(8,128)S(1)}, u32[]{:S(2)}, u32[]{:S(2)}) collective-permute-start(f32[8,128]{1,0:T(8,128)S(1)} %add.25), channel_id=1, source_target_pairs={{0,6},{1,7},{2,4},{3,5},{4,2},{5,3},{6,0},{7,1},{8,14},{9,15},{10,... | collective-permute-start | bytes 12296 | tf_op jit(solution)/shard_map/ppermute | solution.py:205
  93.3 11.0 %collective-permute-done.17.refs_1_ = bf16[4,2,96,128]{3,2,1,0:T(8,128)(2,1)S(1)} collective-permute-done((bf16[4,2,96,128]{3,2,1,0:T(8,128)(2,1)S(1)}, bf16[4,2,96,128]{3,2,1,0:T(8,128)(2,1)S(1)}, u32[]{:S(2)}, u32[]{:S(2)}) %collective-permute-start.17) | collective-permute-done | bytes 196640 | tf_op jit(solution)/shard_map/ppermute | solution.py:369
  104.4 3.4 %collective-permute-done.11 = f32[8,128]{1,0:T(8,128)S(1)} collective-permute-done((f32[8,128]{1,0:T(8,128)S(1)}, f32[8,128]{1,0:T(8,128)S(1)}, u32[]{:S(2)}, u32[]{:S(2)}) %collective-permute-start.11) | collective-permute-done | bytes 4128 | tf_op jit(solution)/shard_map/ppermute | solution.py:205
  107.9 1.3 collective-permute-start.16
  109.2 6.2 %collective-permute-start.15 = (f32[8,128]{1,0:T(8,128)S(1)}, f32[8,128]{1,0:T(8,128)S(1)}, u32[]{:S(2)}, u32[]{:S(2)}) collective-permute-start(f32[8,128]{1,0:T(8,128)S(1)} %add_add_fusion.1), channel_id=1, source_target_pairs={{0,16},{1,17},{2,18},{3,19},{4,20},{5,21},{6,22},{7,23},{8,24},{9,... | collective-permute-start | bytes 12296 | tf_op jit(solution)/shard_map/ppermute | solution.py:205
  117.1 1.9 collective-permute-done.14
  119.1 2.4 %mix_side.1 = (bf16[512,512]{1,0:T(8,128)(2,1)S(1)}, bf16[8,192,128]{2,1,0:T(8,128)(2,1)S(1)}, bf16[8,192,128]{2,1,0:T(8,128)(2,1)}, bf16[8,192,128]{2,1,0:T(8,128)(2,1)}, bf16[8,192,128]{2,1,0:T(8,128)(2,1)}) custom-call(f32[1]{0:T(128)S(6)} %copy.12.scale, s32[1]{0:T(128)} %bitcast.me, f32[8,128]{1,0:T(8,128)S(1)} %add_add_fusion.packed, ...), custom_call_target="tpu_custom_call" | custom-call | flops 805306368 | bytes 3145728 | tf_op jit(solution)/shard_map/mix_side/pallas_call | solution.py:270
  123.0 1.4 collective-permute-start.21
  124.4 2.0 collective-permute-start.22
  126.5 1.0 collective-permute-start.23
  127.4 1.0 copy-done.4
  128.5 3.2 %mix_main.1 = bf16[32,384,128]{2,1,0:T(8,128)(2,1)} custom-call(bf16[512,512]{1,0:T(8,128)(2,1)S(1)} %copy-done.4, bf16[32,192,128]{2,1,0:T(8,128)(2,1)S(1)} %all-to-all-done.1.scores, bf16[32,192,128]{2,1,0:T(8,128)(2,1)S(1)} %all-to-all-done.main.params), custom_call_target="tpu_custom_call" | custom-call | flops 1610612736 | bytes 6291456 | tf_op jit(solution)/shard_map/mix_main/pallas_call | solution.py:315
  131.7 4.7 %all-to-all-start.2 = ((bf16[32,384,128]{2,1,0:T(8,128)(2,1)}), bf16[32,384,128]{2,1,0:T(8,128)(2,1)}, u32[]{:S(2)}, u32[]{:S(2)}) async-start(bf16[32,384,128]{2,1,0:T(8,128)(2,1)} %mix_main.1), calls=%async_computation.2 | async-start | bytes 6291456 | tf_op jit(solution)/shard_map/all_to_all | solution.py:573
  136.5 2.2 collective-permute-done.21.refs_1_
  138.7 20.1 %collective-permute-done.22.refs_2_ = bf16[8,192,128]{2,1,0:T(8,128)(2,1)} collective-permute-done((bf16[8,192,128]{2,1,0:T(8,128)(2,1)}, bf16[8,192,128]{2,1,0:T(8,128)(2,1)}, u32[]{:S(2)}, u32[]{:S(2)}) %collective-permute-start.22) | collective-permute-done | bytes 393248 | tf_op jit(solution)/shard_map/ppermute | solution.py:369
  158.8 1.2 plane.5
  160.0 1.9 collective-permute-start.24
  162.0 6.5 %collective-permute-start.25 = (bf16[4,2,192,128]{3,2,1,0:T(8,128)(2,1)S(1)}, bf16[4,2,192,128]{3,2,1,0:T(8,128)(2,1)S(1)}, u32[]{:S(2)}, u32[]{:S(2)}) collective-permute-start(bf16[4,2,192,128]{3,2,1,0:T(8,128)(2,1)S(1)} %get-tuple-element.88), channel_id=1, source_target_pairs={{0,4},{1,5},{2,6},{3,7},{4,0},{5,1},{6,2},{7,3},{8,12},{9,13},{10,... | collective-permute-start | bytes 1179656 | tf_op jit(solution)/shard_map/ppermute | solution.py:369
  168.5 1.4 collective-permute-start.26
  169.9 4.6 %collective-permute-done.24.refs_1_ = bf16[4,2,192,128]{3,2,1,0:T(8,128)(2,1)S(1)} collective-permute-done((bf16[4,2,192,128]{3,2,1,0:T(8,128)(2,1)S(1)}, bf16[4,2,192,128]{3,2,1,0:T(8,128)(2,1)S(1)}, u32[]{:S(2)}, u32[]{:S(2)}) %collective-permute-start.24) | collective-permute-done | bytes 393248 | tf_op jit(solution)/shard_map/ppermute | solution.py:369
  174.4 3.4 %collective-permute-done.25.refs_2_ = bf16[4,2,192,128]{3,2,1,0:T(8,128)(2,1)S(1)} collective-permute-done((bf16[4,2,192,128]{3,2,1,0:T(8,128)(2,1)S(1)}, bf16[4,2,192,128]{3,2,1,0:T(8,128)(2,1)S(1)}, u32[]{:S(2)}, u32[]{:S(2)}) %collective-permute-start.25) | collective-permute-done | bytes 393248 | tf_op jit(solution)/shard_map/ppermute | solution.py:369
  177.9 9.2 %collective-permute-done.26.refs_3_ = bf16[4,2,192,128]{3,2,1,0:T(8,128)(2,1)S(1)} collective-permute-done((bf16[4,2,192,128]{3,2,1,0:T(8,128)(2,1)S(1)}, bf16[4,2,192,128]{3,2,1,0:T(8,128)(2,1)S(1)}, u32[]{:S(2)}, u32[]{:S(2)}) %collective-permute-start.26) | collective-permute-done | bytes 393248 | tf_op jit(solution)/shard_map/ppermute | solution.py:369
  187.2 2.3 collective-permute-done.27.far
  189.6 1.2 copy-done
  190.8 36.4 %all-to-all-done.2.source = bf16[32,384,128]{2,1,0:T(8,128)(2,1)} async-done(((bf16[32,384,128]{2,1,0:T(8,128)(2,1)}), bf16[32,384,128]{2,1,0:T(8,128)(2,1)}, u32[]{:S(2)}, u32[]{:S(2)}) %all-to-all-start.2) | async-done | bytes 3145760 | tf_op jit(solution)/shard_map/all_to_all | solution.py:573
  227.2 5.0 %unpack.1 = (bf16[1,384,1536]{2,1,0:T(8,128)(2,1)}, bf16[1,1536,384]{2,1,0:T(8,128)(2,1)}, bf16[1,384,1536]{2,1,0:T(8,128)(2,1)}, bf16[1,1536,384]{2,1,0:T(8,128)(2,1)}) custom-call(bf16[32,384,128]{2,1,0:T(8,128)(2,1)} %all-to-all-done.2.source, bf16[32,192,128]{2,1,0:T(8,128)(2,1)} %copy-done), custom_call_target="tpu_custom_call" | custom-call | bytes 9437184 | tf_op jit(solution)/shard_map/unpack/pallas_call | solution.py:554
  (59 shorter events, 6.0 us)
Async XLA Ops:
  2.8 16.2 %collective-permute-start = (bf16[8,96,128]{2,1,0:T(8,128)(2,1)}, bf16[8,96,128]{2,1,0:T(8,128)(2,1)S(1)}, u32[]{:S(2)}, u32[]{:S(2)}) collective-permute-start(bf16[8,96,128]{2,1,0:T(8,128)(2,1)} %get-tuple-element.49), channel_id=1, source_target_pairs={{0,8},{1,9},{2,10},{3,11},{4,12},{5,13},{6,14},{7,15},{8,0},{9,1},... | collective-permute-start | bytes 589832 | tf_op jit(solution)/shard_map/ppermute | solution.py:369
  5.9 18.3 %collective-permute-start.1 = (bf16[8,96,128]{2,1,0:T(8,128)(2,1)}, bf16[8,96,128]{2,1,0:T(8,128)(2,1)S(1)}, u32[]{:S(2)}, u32[]{:S(2)}) collective-permute-start(bf16[8,96,128]{2,1,0:T(8,128)(2,1)} %get-tuple-element.50), channel_id=1, source_target_pairs={{0,16},{1,17},{2,18},{3,19},{4,20},{5,21},{6,22},{7,23},{8,24},{9,... | collective-permute-start | bytes 589832 | tf_op jit(solution)/shard_map/ppermute | solution.py:369
  8.4 15.7 %collective-permute-start.2 = (bf16[8,96,128]{2,1,0:T(8,128)(2,1)}, bf16[8,96,128]{2,1,0:T(8,128)(2,1)S(1)}, u32[]{:S(2)}, u32[]{:S(2)}) collective-permute-start(bf16[8,96,128]{2,1,0:T(8,128)(2,1)} %get-tuple-element.51), channel_id=1, source_target_pairs={{0,24},{1,25},{2,26},{3,27},{4,28},{5,29},{6,30},{7,31},{8,16},{9,... | collective-permute-start | bytes 589832 | tf_op jit(solution)/shard_map/ppermute | solution.py:369
  11.1 48.7 %all-to-all-start = ((bf16[32,192,128]{2,1,0:T(8,128)(2,1)}), bf16[32,192,128]{2,1,0:T(8,128)(2,1)S(1)}, u32[]{:S(2)}, u32[]{:S(2)}) async-start(bf16[32,192,128]{2,1,0:T(8,128)(2,1)} %pack_main.1), calls=%async_computation | async-start | bytes 3145728 | tf_op jit(solution)/shard_map/all_to_all | solution.py:573
  17.1 1.6 copy-start.11
  18.8 5.4 %copy-start.5 = (bf16[8,96,128]{2,1,0:T(8,128)(2,1)S(1)}, bf16[8,96,128]{2,1,0:T(8,128)(2,1)}, u32[]{:S(2)}) copy-start(bf16[8,96,128]{2,1,0:T(8,128)(2,1)} %get-tuple-element.48.refs_0_) | copy-start | bytes 589828
  24.2 5.0 %copy-start.1 = (bf16[1,384,1536]{2,1,0:T(8,128)(2,1)S(1)}, bf16[1,384,1536]{2,1,0:T(8,128)(2,1)}, u32[]{:S(2)}) copy-start(bf16[1,384,1536]{2,1,0:T(8,128)(2,1)} %first.3) | copy-start | bytes 3538948
  24.2 5.0 %copy-start.2 = (bf16[1,1536,384]{2,1,0:T(8,128)(2,1)S(1)}, bf16[1,1536,384]{2,1,0:T(8,128)(2,1)}, u32[]{:S(2)}) copy-start(bf16[1,1536,384]{2,1,0:T(8,128)(2,1)} %second.3) | copy-start | bytes 3538948
  24.2 5.0 %copy-start.6 = (s32[1,8]{1,0:T(1,128)S(1)}, s32[1,8]{1,0:T(1,128)}, u32[]{:S(2)}) copy-start(s32[1,8]{1,0:T(1,128)} %param.10) | copy-start | bytes 100
  25.0 46.5 %collective-permute-start.3 = (bf16[4,2,96,128]{3,2,1,0:T(8,128)(2,1)S(1)}, bf16[4,2,96,128]{3,2,1,0:T(8,128)(2,1)S(1)}, u32[]{:S(2)}, u32[]{:S(2)}) collective-permute-start(bf16[4,2,96,128]{3,2,1,0:T(8,128)(2,1)S(1)} %get-tuple-element.53), channel_id=1, source_target_pairs={{0,2},{1,3},{2,0},{3,1},{4,6},{5,7},{6,4},{7,5},{8,10},{9,11},{10,... | collective-permute-start | bytes 589832 | tf_op jit(solution)/shard_map/ppermute | solution.py:369
  27.5 50.8 %collective-permute-start.4 = (bf16[4,2,96,128]{3,2,1,0:T(8,128)(2,1)}, bf16[4,2,96,128]{3,2,1,0:T(8,128)(2,1)}, u32[]{:S(2)}, u32[]{:S(2)}) collective-permute-start(bf16[4,2,96,128]{3,2,1,0:T(8,128)(2,1)} %get-tuple-element.54), channel_id=1, source_target_pairs={{0,4},{1,5},{2,6},{3,7},{4,0},{5,1},{6,2},{7,3},{8,12},{9,13},{10,... | collective-permute-start | bytes 589832 | tf_op jit(solution)/shard_map/ppermute | solution.py:369
  29.1 49.1 %collective-permute-start.5 = (bf16[4,2,96,128]{3,2,1,0:T(8,128)(2,1)}, bf16[4,2,96,128]{3,2,1,0:T(8,128)(2,1)}, u32[]{:S(2)}, u32[]{:S(2)}) collective-permute-start(bf16[4,2,96,128]{3,2,1,0:T(8,128)(2,1)} %get-tuple-element.55), channel_id=1, source_target_pairs={{0,6},{1,7},{2,4},{3,5},{4,2},{5,3},{6,0},{7,1},{8,14},{9,15},{10,... | collective-permute-start | bytes 589832 | tf_op jit(solution)/shard_map/ppermute | solution.py:369
  52.2 0.7 copy-start.9
  59.7 19.7 %collective-permute-start.7 = (bf16[8,96,128]{2,1,0:T(8,128)(2,1)}, bf16[8,96,128]{2,1,0:T(8,128)(2,1)}, u32[]{:S(2)}, u32[]{:S(2)}) collective-permute-start(bf16[8,96,128]{2,1,0:T(8,128)(2,1)} %get-tuple-element.69), channel_id=1, source_target_pairs={{0,8},{1,9},{2,10},{3,11},{4,12},{5,13},{6,14},{7,15},{8,0},{9,1},... | collective-permute-start | bytes 589832 | tf_op jit(solution)/shard_map/ppermute | solution.py:369
  69.0 10.5 %collective-permute-start.8 = (bf16[8,96,128]{2,1,0:T(8,128)(2,1)}, bf16[8,96,128]{2,1,0:T(8,128)(2,1)}, u32[]{:S(2)}, u32[]{:S(2)}) collective-permute-start(bf16[8,96,128]{2,1,0:T(8,128)(2,1)} %get-tuple-element.70), channel_id=1, source_target_pairs={{0,16},{1,17},{2,18},{3,19},{4,20},{5,21},{6,22},{7,23},{8,24},{9,... | collective-permute-start | bytes 589832 | tf_op jit(solution)/shard_map/ppermute | solution.py:369
  71.5 9.7 %collective-permute-start.9 = (bf16[8,96,128]{2,1,0:T(8,128)(2,1)}, bf16[8,96,128]{2,1,0:T(8,128)(2,1)}, u32[]{:S(2)}, u32[]{:S(2)}) collective-permute-start(bf16[8,96,128]{2,1,0:T(8,128)(2,1)} %get-tuple-element.71), channel_id=1, source_target_pairs={{0,24},{1,25},{2,26},{3,27},{4,28},{5,29},{6,30},{7,31},{8,16},{9,... | collective-permute-start | bytes 589832 | tf_op jit(solution)/shard_map/ppermute | solution.py:369
  73.0 54.4 %all-to-all-start.1 = ((bf16[32,192,128]{2,1,0:T(8,128)(2,1)}), bf16[32,192,128]{2,1,0:T(8,128)(2,1)S(1)}, u32[]{:S(2)}, u32[]{:S(2)}) async-start(bf16[32,192,128]{2,1,0:T(8,128)(2,1)} %get-tuple-element.81), calls=%async_computation.1 | async-start | bytes 3145728 | tf_op jit(solution)/shard_map/all_to_all | solution.py:573
  79.3 7.6 %collective-permute-start.6 = (bf16[4,4,96,128]{3,2,1,0:T(8,128)(2,1)S(1)}, bf16[4,4,96,128]{3,2,1,0:T(8,128)(2,1)S(1)}, u32[]{:S(2)}, u32[]{:S(2)}) collective-permute-start(bf16[4,4,96,128]{3,2,1,0:T(8,128)(2,1)S(1)} %get-tuple-element.64), channel_id=1, source_target_pairs={{0,1},{1,0},{2,3},{3,2},{4,5},{5,4},{6,7},{7,6},{8,9},{9,8},{10,11... | collective-permute-start | bytes 1179656 | tf_op jit(solution)/shard_map/ppermute | solution.py:369
  81.3 0.9 copy-start.10
  83.4 20.9 %collective-permute-start.17 = (bf16[4,2,96,128]{3,2,1,0:T(8,128)(2,1)S(1)}, bf16[4,2,96,128]{3,2,1,0:T(8,128)(2,1)S(1)}, u32[]{:S(2)}, u32[]{:S(2)}) collective-permute-start(bf16[4,2,96,128]{3,2,1,0:T(8,128)(2,1)S(1)} %get-tuple-element.75), channel_id=1, source_target_pairs={{0,2},{1,3},{2,0},{3,1},{4,6},{5,7},{6,4},{7,5},{8,10},{9,11},{10,... | collective-permute-start | bytes 589832 | tf_op jit(solution)/shard_map/ppermute | solution.py:369
  84.9 19.4 %collective-permute-start.18 = (bf16[4,2,96,128]{3,2,1,0:T(8,128)(2,1)S(1)}, bf16[4,2,96,128]{3,2,1,0:T(8,128)(2,1)S(1)}, u32[]{:S(2)}, u32[]{:S(2)}) collective-permute-start(bf16[4,2,96,128]{3,2,1,0:T(8,128)(2,1)S(1)} %get-tuple-element.76), channel_id=1, source_target_pairs={{0,4},{1,5},{2,6},{3,7},{4,0},{5,1},{6,2},{7,3},{8,12},{9,13},{10,... | collective-permute-start | bytes 589832 | tf_op jit(solution)/shard_map/ppermute | solution.py:369
  87.0 17.3 %collective-permute-start.19 = (bf16[4,2,96,128]{3,2,1,0:T(8,128)(2,1)S(1)}, bf16[4,2,96,128]{3,2,1,0:T(8,128)(2,1)S(1)}, u32[]{:S(2)}, u32[]{:S(2)}) collective-permute-start(bf16[4,2,96,128]{3,2,1,0:T(8,128)(2,1)S(1)} %get-tuple-element.77), channel_id=1, source_target_pairs={{0,6},{1,7},{2,4},{3,5},{4,2},{5,3},{6,0},{7,1},{8,14},{9,15},{10,... | collective-permute-start | bytes 589832 | tf_op jit(solution)/shard_map/ppermute | solution.py:369
  89.2 1.2 collective-permute-start.10
  90.4 14.1 %collective-permute-start.13 = (f32[8,128]{1,0:T(8,128)S(1)}, f32[8,128]{1,0:T(8,128)S(1)}, u32[]{:S(2)}, u32[]{:S(2)}) collective-permute-start(f32[8,128]{1,0:T(8,128)S(1)} %add.25), channel_id=1, source_target_pairs={{0,6},{1,7},{2,4},{3,5},{4,2},{5,3},{6,0},{7,1},{8,14},{9,15},{10,... | collective-permute-start | bytes 12296 | tf_op jit(solution)/shard_map/ppermute | solution.py:205
  93.3 11.1 %collective-permute-start.12 = (f32[8,128]{1,0:T(8,128)S(1)}, f32[8,128]{1,0:T(8,128)S(1)}, u32[]{:S(2)}, u32[]{:S(2)}) collective-permute-start(f32[8,128]{1,0:T(8,128)S(1)} %add.25), channel_id=1, source_target_pairs={{0,4},{1,5},{2,6},{3,7},{4,0},{5,1},{6,2},{7,3},{8,12},{9,13},{10,... | collective-permute-start | bytes 12296 | tf_op jit(solution)/shard_map/ppermute | solution.py:205
  104.3 3.6 %collective-permute-start.11 = (f32[8,128]{1,0:T(8,128)S(1)}, f32[8,128]{1,0:T(8,128)S(1)}, u32[]{:S(2)}, u32[]{:S(2)}) collective-permute-start(f32[8,128]{1,0:T(8,128)S(1)} %add.25), channel_id=1, source_target_pairs={{0,2},{1,3},{2,0},{3,1},{4,6},{5,7},{6,4},{7,5},{8,10},{9,11},{10,... | collective-permute-start | bytes 12296 | tf_op jit(solution)/shard_map/ppermute | solution.py:205
  104.3 14.7 %collective-permute-start.20 = (bf16[4,4,96,128]{3,2,1,0:T(8,128)(2,1)S(1)}, bf16[4,4,96,128]{3,2,1,0:T(8,128)(2,1)S(1)}, u32[]{:S(2)}, u32[]{:S(2)}) collective-permute-start(bf16[4,4,96,128]{3,2,1,0:T(8,128)(2,1)S(1)} %get-tuple-element.79), channel_id=1, source_target_pairs={{0,1},{1,0},{2,3},{3,2},{4,5},{5,4},{6,7},{7,6},{8,9},{9,8},{10,11... | collective-permute-start | bytes 1179656 | tf_op jit(solution)/shard_map/ppermute | solution.py:369
  107.9 8.7 %collective-permute-start.16 = (f32[8,128]{1,0:T(8,128)S(1)}, f32[8,128]{1,0:T(8,128)S(1)}, u32[]{:S(2)}, u32[]{:S(2)}) collective-permute-start(f32[8,128]{1,0:T(8,128)S(1)} %add_add_fusion.1), channel_id=1, source_target_pairs={{0,24},{1,25},{2,26},{3,27},{4,28},{5,29},{6,30},{7,31},{8,16},{9,... | collective-permute-start | bytes 12296 | tf_op jit(solution)/shard_map/ppermute | solution.py:205
  109.2 7.9 %collective-permute-start.15 = (f32[8,128]{1,0:T(8,128)S(1)}, f32[8,128]{1,0:T(8,128)S(1)}, u32[]{:S(2)}, u32[]{:S(2)}) collective-permute-start(f32[8,128]{1,0:T(8,128)S(1)} %add_add_fusion.1), channel_id=1, source_target_pairs={{0,16},{1,17},{2,18},{3,19},{4,20},{5,21},{6,22},{7,23},{8,24},{9,... | collective-permute-start | bytes 12296 | tf_op jit(solution)/shard_map/ppermute | solution.py:205
  115.4 3.6 %collective-permute-start.14 = (f32[8,128]{1,0:T(8,128)S(1)}, f32[8,128]{1,0:T(8,128)S(1)}, u32[]{:S(2)}, u32[]{:S(2)}) collective-permute-start(f32[8,128]{1,0:T(8,128)S(1)} %add_add_fusion.1), channel_id=1, source_target_pairs={{0,8},{1,9},{2,10},{3,11},{4,12},{5,13},{6,14},{7,15},{8,0},{9,1},... | collective-permute-start | bytes 12296 | tf_op jit(solution)/shard_map/ppermute | solution.py:205
  121.5 0.8 copy-start.3
  122.3 0.8 copy-start.7
  123.0 15.6 %collective-permute-start.21 = (bf16[8,192,128]{2,1,0:T(8,128)(2,1)}, bf16[8,192,128]{2,1,0:T(8,128)(2,1)S(1)}, u32[]{:S(2)}, u32[]{:S(2)}) collective-permute-start(bf16[8,192,128]{2,1,0:T(8,128)(2,1)} %get-tuple-element.83), channel_id=1, source_target_pairs={{0,8},{1,9},{2,10},{3,11},{4,12},{5,13},{6,14},{7,15},{8,0},{9,1},... | collective-permute-start | bytes 1179656 | tf_op jit(solution)/shard_map/ppermute | solution.py:369
  124.4 34.4 %collective-permute-start.22 = (bf16[8,192,128]{2,1,0:T(8,128)(2,1)}, bf16[8,192,128]{2,1,0:T(8,128)(2,1)}, u32[]{:S(2)}, u32[]{:S(2)}) collective-permute-start(bf16[8,192,128]{2,1,0:T(8,128)(2,1)} %get-tuple-element.84), channel_id=1, source_target_pairs={{0,16},{1,17},{2,18},{3,19},{4,20},{5,21},{6,22},{7,23},{8,24},{9,... | collective-permute-start | bytes 1179656 | tf_op jit(solution)/shard_map/ppermute | solution.py:369
  126.5 32.4 %collective-permute-start.23 = (bf16[8,192,128]{2,1,0:T(8,128)(2,1)}, bf16[8,192,128]{2,1,0:T(8,128)(2,1)}, u32[]{:S(2)}, u32[]{:S(2)}) collective-permute-start(bf16[8,192,128]{2,1,0:T(8,128)(2,1)} %get-tuple-element.85), channel_id=1, source_target_pairs={{0,24},{1,25},{2,26},{3,27},{4,28},{5,29},{6,30},{7,31},{8,16},{9,... | collective-permute-start | bytes 1179656 | tf_op jit(solution)/shard_map/ppermute | solution.py:369
  127.4 1.0 copy-start.4
  131.7 27.1 %copy-start.8 = (bf16[8,192,128]{2,1,0:T(8,128)(2,1)S(1)}, bf16[8,192,128]{2,1,0:T(8,128)(2,1)}, u32[]{:S(2)}) copy-start(bf16[8,192,128]{2,1,0:T(8,128)(2,1)} %copy-done.7) | copy-start | bytes 1179652
  131.7 95.4 %all-to-all-start.2 = ((bf16[32,384,128]{2,1,0:T(8,128)(2,1)}), bf16[32,384,128]{2,1,0:T(8,128)(2,1)}, u32[]{:S(2)}, u32[]{:S(2)}) async-start(bf16[32,384,128]{2,1,0:T(8,128)(2,1)} %mix_main.1), calls=%async_computation.2 | async-start | bytes 6291456 | tf_op jit(solution)/shard_map/all_to_all | solution.py:573
  160.0 14.4 %collective-permute-start.24 = (bf16[4,2,192,128]{3,2,1,0:T(8,128)(2,1)S(1)}, bf16[4,2,192,128]{3,2,1,0:T(8,128)(2,1)S(1)}, u32[]{:S(2)}, u32[]{:S(2)}) collective-permute-start(bf16[4,2,192,128]{3,2,1,0:T(8,128)(2,1)S(1)} %get-tuple-element.87), channel_id=1, source_target_pairs={{0,2},{1,3},{2,0},{3,1},{4,6},{5,7},{6,4},{7,5},{8,10},{9,11},{10,... | collective-permute-start | bytes 1179656 | tf_op jit(solution)/shard_map/ppermute | solution.py:369
  162.0 15.9 %collective-permute-start.25 = (bf16[4,2,192,128]{3,2,1,0:T(8,128)(2,1)S(1)}, bf16[4,2,192,128]{3,2,1,0:T(8,128)(2,1)S(1)}, u32[]{:S(2)}, u32[]{:S(2)}) collective-permute-start(bf16[4,2,192,128]{3,2,1,0:T(8,128)(2,1)S(1)} %get-tuple-element.88), channel_id=1, source_target_pairs={{0,4},{1,5},{2,6},{3,7},{4,0},{5,1},{6,2},{7,3},{8,12},{9,13},{10,... | collective-permute-start | bytes 1179656 | tf_op jit(solution)/shard_map/ppermute | solution.py:369
  168.5 18.6 %collective-permute-start.26 = (bf16[4,2,192,128]{3,2,1,0:T(8,128)(2,1)S(1)}, bf16[4,2,192,128]{3,2,1,0:T(8,128)(2,1)S(1)}, u32[]{:S(2)}, u32[]{:S(2)}) collective-permute-start(bf16[4,2,192,128]{3,2,1,0:T(8,128)(2,1)S(1)} %get-tuple-element.89), channel_id=1, source_target_pairs={{0,6},{1,7},{2,4},{3,5},{4,2},{5,3},{6,0},{7,1},{8,14},{9,15},{10,... | collective-permute-start | bytes 1179656 | tf_op jit(solution)/shard_map/ppermute | solution.py:369
  187.1 2.4 %collective-permute-start.27 = (bf16[4,4,192,128]{3,2,1,0:T(8,128)(2,1)S(1)}, bf16[4,4,192,128]{3,2,1,0:T(8,128)(2,1)S(1)}, u32[]{:S(2)}, u32[]{:S(2)}) collective-permute-start(bf16[4,4,192,128]{3,2,1,0:T(8,128)(2,1)S(1)} %get-tuple-element.91), channel_id=1, source_target_pairs={{0,1},{1,0},{2,3},{3,2},{4,5},{5,4},{6,7},{7,6},{8,9},{9,8},{10,11... | collective-permute-start | bytes 2359304 | tf_op jit(solution)/shard_map/ppermute | solution.py:369
  189.6 1.2 copy-start

commit v14 on v13

--- a/solution.py
+++ b/solution.py
@@ -22,7 +22,7 @@
 SIDE = 2 * EDGE
 GROUPS = range(D // LANES)
 ROWS = SIDE * len(GROUPS)
-MAIN = 2 * SIDE
+MAIN = ROWS - EDGE
 REST = ROWS - MAIN
 PLANES = 4
 PLANE = BLOCKS // PLANES
@@ -248,8 +248,8 @@
     ksum = jnp.sum(full, axis=1, keepdims=True)
     mixer = full.astype(jnp.bfloat16)
     mixing[...] = mixer
-    count = SIDE // TILE // 2
-    for start in range(0, SIDE, count * TILE):
+    count = REST // TILE
+    for start in range(0, REST, count * TILE):
         at = [start + q * TILE for q in range(count)]
         got = jnp.concatenate([rows_of(scores, r) for r in at], axis=1)
         own = jnp.concatenate([rows_of(params, r) for r in at], axis=1)
@@ -286,10 +286,10 @@
     members = params.shape[0]
     mixer = mixing[...]
     ksum = jnp.sum(mixer.astype(jnp.float32), axis=1, keepdims=True)
-    groups = MAIN // SIDE
     copies = []
     for r in range(0, SIDE, TILE):
-        at = [g * SIDE + r for g in range(groups)]
+        at = [g * SIDE + r for g in GROUPS if g * SIDE + r < MAIN]
+        groups = len(at)
         got = jnp.concatenate([rows_of(scores, x) for x in at], axis=1)
         own = jnp.concatenate([rows_of(params, x) for x in at], axis=1)
         both = mix(mixer, ksum, got, own)
@@ -417,21 +417,14 @@
 TALL = FF // STEPS
 
 
-def pack_side_kernel(me, first, second, *refs):
-    outs, (wide, tall, side, loads) = refs[:PLANES], refs[PLANES:]
-    copies = [pltpu.make_async_copy(second.at[0, :, pl.ds(D - LANES, LANES)], tall, loads.at[COLS])]
-    for c in range(COLS):
-        here = first.at[0, :, pl.ds((c + 1) * D - LANES, LANES)]
-        copies.append(pltpu.make_async_copy(here, wide.at[c], loads.at[c]))
-    for copy in copies:
-        copy.start()
-    for copy in copies:
-        copy.wait()
-    for b in range(BLOCKS):
-        r = b // COLS * EDGE
-        side[b, 0:EDGE, :] = wide[b % COLS, r : r + EDGE, :]
-        side[b, EDGE:REST, :] = tall[b * EDGE : (b + 1) * EDGE, :]
-    by_plane(me, side, outs)
+def pack_side_kernel(me, second, *refs):
+    outs, (tall, load) = refs[:PLANES], refs[PLANES:]
+    copy = pltpu.make_async_copy(second.at[0, :, pl.ds(D - LANES, LANES)], tall, load)
+    copy.start()
+    copy.wait()
+    for k in range(BLOCKS):
+        here = pl.ds(pl.multiple_of((k ^ me[0]) * EDGE, EDGE), EDGE)
+        outs[k // PLANE][k % PLANE] = tall[here, :]
 
 
 def pack_main_kernel(first, second, out, wide, tall, packed, loads, stores):
@@ -456,13 +449,13 @@
         for copy in load(d):
             copy.wait()
         for c in range(COLS):
-            for g in range(MAIN // SIDE):
-                b, at = d * COLS + c, g * SIDE
-                lanes = g * LANES
+            for g in GROUPS:
+                b, at, lanes = d * COLS + c, g * SIDE, g * LANES
                 packed[b, at : at + EDGE, :] = wide[d, :, c * D + lanes : c * D + lanes + LANES]
-                packed[b, at + EDGE : at + SIDE, :] = tall[
-                    d, c * EDGE : (c + 1) * EDGE, lanes : lanes + LANES
-                ]
+                if at + EDGE < MAIN:
+                    packed[b, at + EDGE : at + SIDE, :] = tall[
+                        d, c * EDGE : (c + 1) * EDGE, lanes : lanes + LANES
+                    ]
         store(d).start()
     for d in range(STEPS):
         store(d).wait()
@@ -476,17 +469,12 @@
     side = pl.pallas_call(
         pack_side_kernel,
         out_shape=side_shapes(REST),
-        in_specs=[pl.BlockSpec(memory_space=pltpu.SMEM)] + anywhere * 2,
-        scratch_shapes=[
-            pltpu.VMEM((COLS, D, LANES), bf),
-            pltpu.VMEM((FF, LANES), bf),
-            pltpu.VMEM((BLOCKS, REST, LANES), bf),
-            pltpu.SemaphoreType.DMA((COLS + 1,)),
-        ],
+        in_specs=[pl.BlockSpec(memory_space=pltpu.SMEM)] + anywhere,
+        scratch_shapes=[pltpu.VMEM((FF, LANES), bf), pltpu.SemaphoreType.DMA],
         compiler_params=params,
         cost_estimate=cost,
         name="pack_side",
-    )(me, first, second)
+    )(me, second)
     main = pl.pallas_call(
         pack_main_kernel,
         out_shape=pltpu.HBM((BLOCKS, MAIN, LANES), bf),
@@ -506,13 +494,7 @@
     return main, side
 
 
-def unpack_kernel(source, side, first_a, second_a, first_s, second_s, *refs):
-    main, wide, tall, loads, stores = refs
-
-    def load(d):
-        here = pl.ds(d * COLS, COLS)
-        return pltpu.make_async_copy(source.at[here], main.at[here], loads.at[d])
-
+def unpack_kernel(main, side, first_a, second_a, first_s, second_s, wide, tall, stores):
     def store(which, d):
         first, second = ((first_a, second_a), (first_s, second_s))[which]
         return (
@@ -524,23 +506,16 @@
             ),
         )
 
-    for d in range(STEPS):
-        load(d).start()
-    for d in range(STEPS):
-        load(d).wait()
-        for which in range(2):
+    for which in range(2):
+        for d in range(STEPS):
             for c in range(COLS):
                 for g in GROUPS:
-                    b, at = d * COLS + c, g * SIDE
-                    if at < MAIN:
-                        ref, at = main, which * MAIN + at
-                    else:
-                        ref, at = side, which * REST + at - MAIN
+                    b, at = d * COLS + c, which * MAIN + g * SIDE
                     lanes = slice(c * D + g * LANES, c * D + (g + 1) * LANES)
-                    wide[which, d, :, lanes] = ref[b, at : at + EDGE, :]
+                    wide[which, d, :, lanes] = main[b, at : at + EDGE, :]
+                    ref, at = (main, at + EDGE) if g * SIDE + EDGE < MAIN else (side, which * REST)
                     lanes = slice(g * LANES, (g + 1) * LANES)
-                    here = slice(c * EDGE, (c + 1) * EDGE)
-                    tall[which, d, here, lanes] = ref[b, at + EDGE : at + SIDE, :]
+                    tall[which, d, c * EDGE : (c + 1) * EDGE, lanes] = ref[b, at : at + EDGE, :]
             for copy in store(which, d):
                 copy.start()
     for which in range(2):
@@ -554,16 +529,14 @@
     return pl.pallas_call(
         unpack_kernel,
         out_shape=(pltpu.HBM((1, D, FF), bf), pltpu.HBM((1, FF, D), bf)) * 2,
-        in_specs=[pl.BlockSpec(memory_space=pl.ANY), pl.BlockSpec(memory_space=pltpu.VMEM)],
+        in_specs=[pl.BlockSpec(memory_space=pltpu.VMEM)] * 2,
         out_specs=(pl.BlockSpec(memory_space=pl.ANY),) * 4,
         scratch_shapes=[
-            pltpu.VMEM((BLOCKS, 2 * MAIN, LANES), bf),
             pltpu.VMEM((2, STEPS, EDGE, FF), bf),
             pltpu.VMEM((2, STEPS, TALL, D), bf),
-            pltpu.SemaphoreType.DMA((STEPS,)),
             pltpu.SemaphoreType.DMA((2, 2, STEPS)),
         ],
-        compiler_params=pltpu.CompilerParams(vmem_limit_bytes=57 * 1024 * 1024),
+        compiler_params=pltpu.CompilerParams(vmem_limit_bytes=24 * 1024 * 1024),
         cost_estimate=pl.CostEstimate(flops=0, bytes_accessed=16 * D * FF, transcendentals=0),
         name="unpack",
     )(main, side)

time: 233 us -> 230 us (0.987)
  waiting for transfers between devices: 110 us -> 135 us
  starting transfers between devices: 68.2 us -> 48.5 us
  local copies, waits for them, and re-layouts: 7.22 us -> 2.83 us
  Pallas kernels: 45.2 us -> 41.4 us
    ppermute x7, waiting for transfers between devices: 7.07 us -> 26.1 us  [add_over(): lax.ppermute(value, AXES, [(i, i ^ bit) for i in range(members)])]
    ppermute x21, starting transfers between devices: 41.1 us -> 25.8 us  [swap(): return lax.ppermute(value, AXES, pairs)]
    all_to_all x3, waiting for transfers between devices: 43.2 us -> 55.6 us  [exchange(): return lax.all_to_all(blocks, AXES, split_axis=0, concat_axis=0, tiled=True)]
    ppermute x21, waiting for transfers between devices: 59.7 us -> 53.6 us  [swap(): return lax.ppermute(value, AXES, pairs)]
    unnamed x26 -> x18, local copies, waits for them, and re-layouts: 7.22 us -> 2.83 us
    pallas_call x9, Pallas kernels: 4.62 us -> 0.34 us  [regroup(): pl.pallas_call(body, out_shape=shapes, in_specs=[pl.BlockSpec(memory_spac...]
    ppermute x7, starting transfers between devices: 11 us -> 7.94 us  [add_over(): lax.ppermute(value, AXES, [(i, i ^ bit) for i in range(members)])]
  transfers between devices with their start and end apart: 31 -> 31, of which waited for: 15 -> 13; matrix products, arithmetic and copies ran while one was open for 1% -> 0% of each run, Pallas kernels for 16% -> 15%
where the time goes in v14:
time: 230 us
  waiting for transfers between devices  135 us (59%)
  starting transfers between devices  48.5 us (21%)
  Pallas kernels  41.4 us (18%)
  local copies, waits for them, and re-layouts  2.83 us (1%)
    all_to_all x3, waiting for transfers between devices, exchange(): return lax.all_to_all(blocks, AXES, split_axis=0, concat_axis=0, tiled=True)  55.6 us
    ppermute x21, waiting for transfers between devices, swap(): return lax.ppermute(value, AXES, pairs)  53.6 us
    ppermute x7, waiting for transfers between devices, add_over(): lax.ppermute(value, AXES, [(i, i ^ bit) for i in range(members)])  26.1 us
    ppermute x21, starting transfers between devices, swap(): return lax.ppermute(value, AXES, pairs)  25.8 us
    pallas_call x1, Pallas kernels, particle_scores(): pl.pallas_call(functools.partial(score_kernel, DATA / count), out_shape=(...  23 us
    all_to_all x3, starting transfers between devices, exchange(): return lax.all_to_all(blocks, AXES, split_axis=0, concat_axis=0, tiled=True)  14.7 us
    ppermute x7, starting transfers between devices, add_over(): lax.ppermute(value, AXES, [(i, i ^ bit) for i in range(members)])  7.94 us
    pallas_call x1, Pallas kernels, mix_main(): pl.pallas_call(mix_main_kernel, out_shape=pltpu.HBM((members, 2 * MAIN, L...  5.14 us
  transfers between devices with their start and end apart: 31, of which 13 were waited for; matrix products, arithmetic and copies ran while one was open for 0% of the time, Pallas kernels for 15%

profile of v14, /device:TPU:0, one launch (start us, length us, event | category | flops | bytes accessed | tf_op | source)
XLA Modules:
  0.0 229.7 jit_solution(17444932398233086316)
XLA Ops:
  0.6 1.8 pack_side.1
  2.4 3.1 %collective-permute-start = (bf16[8,48,128]{2,1,0:T(8,128)(2,1)}, bf16[8,48,128]{2,1,0:T(8,128)(2,1)S(1)}, u32[]{:S(2)}, u32[]{:S(2)}) collective-permute-start(bf16[8,48,128]{2,1,0:T(8,128)(2,1)} %get-tuple-element.49), channel_id=1, source_target_pairs={{0,8},{1,9},{2,10},{3,11},{4,12},{5,13},{6,14},{7,15},{8,0},{9,1},... | collective-permute-start | bytes 294920 | tf_op jit(solution)/shard_map/ppermute | solution.py:369
  5.5 2.6 %collective-permute-start.1 = (bf16[8,48,128]{2,1,0:T(8,128)(2,1)}, bf16[8,48,128]{2,1,0:T(8,128)(2,1)S(1)}, u32[]{:S(2)}, u32[]{:S(2)}) collective-permute-start(bf16[8,48,128]{2,1,0:T(8,128)(2,1)} %get-tuple-element.50), channel_id=1, source_target_pairs={{0,16},{1,17},{2,18},{3,19},{4,20},{5,21},{6,22},{7,23},{8,24},{9,... | collective-permute-start | bytes 294920 | tf_op jit(solution)/shard_map/ppermute | solution.py:369
  8.1 2.6 %pack_main.1 = bf16[32,240,128]{2,1,0:T(8,128)(2,1)} custom-call(bf16[1,384,1536]{2,1,0:T(8,128)(2,1)} %first.1, bf16[1,1536,384]{2,1,0:T(8,128)(2,1)} %second.3), custom_call_target="tpu_custom_call" | custom-call | bytes 2359296 | tf_op jit(solution)/shard_map/pack_main/pallas_call | solution.py:478
  10.8 6.1 %all-to-all-start = ((bf16[32,240,128]{2,1,0:T(8,128)(2,1)}), bf16[32,240,128]{2,1,0:T(8,128)(2,1)S(1)}, u32[]{:S(2)}, u32[]{:S(2)}) async-start(bf16[32,240,128]{2,1,0:T(8,128)(2,1)} %pack_main.1), calls=%async_computation | async-start | bytes 3932160 | tf_op jit(solution)/shard_map/all_to_all | solution.py:546
  16.9 0.2 copy.10.image
  17.0 1.1 copy-done.7
  18.3 0.7 copy-done.2
  19.1 1.8 collective-permute-start.3
  20.9 1.5 collective-permute-start.4
  22.4 0.3 collective-permute-start.5
  22.6 23.0 %score.1 = (bf16[32,240,128]{2,1,0:T(8,128)(2,1)}, bf16[8,48,128]{2,1,0:T(8,128)(2,1)S(1)}, bf16[8,48,128]{2,1,0:T(8,128)(2,1)S(1)}, bf16[8,48,128]{2,1,0:T(8,128)(2,1)S(1)}, bf16[8,48,128]{2,1,0:T(8,128)(2,1)S(1)}) custom-call(s32[8]{0:T(128)S(1)} %bitcast.6, s32[1]{0:T(128)} %bitcast.me, bf16[8,197,384]{2,1,0:T(8,128)(2,1)S(1)} %copy.10.image, ...), custom_call_target="tpu_custom_call" | custom-call | flops 9814671360 | bytes 7139328 | tf_op jit(solution)/shard_map/score/pallas_call | solution.py:129
  45.8 17.0 %all-to-all-done.main.params = bf16[32,240,128]{2,1,0:T(8,128)(2,1)S(1)} async-done(((bf16[32,240,128]{2,1,0:T(8,128)(2,1)}), bf16[32,240,128]{2,1,0:T(8,128)(2,1)S(1)}, u32[]{:S(2)}, u32[]{:S(2)}) %all-to-all-start) | async-done | bytes 1966112 | tf_op jit(solution)/shard_map/all_to_all | solution.py:546
  62.8 2.0 collective-permute-start.8
  64.8 2.3 %collective-permute-start.9 = (bf16[8,48,128]{2,1,0:T(8,128)(2,1)S(1)}, bf16[8,48,128]{2,1,0:T(8,128)(2,1)S(1)}, u32[]{:S(2)}, u32[]{:S(2)}) collective-permute-start(bf16[8,48,128]{2,1,0:T(8,128)(2,1)S(1)} %get-tuple-element.71), channel_id=1, source_target_pairs={{0,24},{1,25},{2,26},{3,27},{4,28},{5,29},{6,30},{7,31},{8,16},{9,... | collective-permute-start | bytes 294920 | tf_op jit(solution)/shard_map/ppermute | solution.py:369
  67.2 4.3 %all-to-all-start.1 = ((bf16[32,240,128]{2,1,0:T(8,128)(2,1)}), bf16[32,240,128]{2,1,0:T(8,128)(2,1)}, u32[]{:S(2)}, u32[]{:S(2)}) async-start(bf16[32,240,128]{2,1,0:T(8,128)(2,1)} %get-tuple-element.81), calls=%async_computation.1 | async-start | bytes 3932160 | tf_op jit(solution)/shard_map/all_to_all | solution.py:546
  71.6 2.0 collective-permute-done.8.refs_2_
  73.6 2.2 gram.1
  75.8 1.2 collective-permute-done.10
  77.0 2.1 collective-permute-start.13
  79.1 0.6 collective-permute-start.12
  79.8 0.7 collective-permute-start.11
  80.5 1.3 collective-permute-start.17
  81.8 1.4 collective-permute-start.18
  83.2 3.1 %collective-permute-done.13 = f32[8,128]{1,0:T(8,128)S(1)} collective-permute-done((f32[8,128]{1,0:T(8,128)S(1)}, f32[8,128]{1,0:T(8,128)S(1)}, u32[]{:S(2)}, u32[]{:S(2)}) %collective-permute-start.13) | collective-permute-done | bytes 4128 | tf_op jit(solution)/shard_map/ppermute | solution.py:205
  86.2 1.4 collective-permute-start.19
  87.6 3.8 %collective-permute-start.16 = (f32[8,128]{1,0:T(8,128)S(1)}, f32[8,128]{1,0:T(8,128)S(1)}, u32[]{:S(2)}, u32[]{:S(2)}) collective-permute-start(f32[8,128]{1,0:T(8,128)S(1)} %add_add_fusion.1), channel_id=1, source_target_pairs={{0,24},{1,25},{2,26},{3,27},{4,28},{5,29},{6,30},{7,31},{8,16},{9,... | collective-permute-start | bytes 12296 | tf_op jit(solution)/shard_map/ppermute | solution.py:205
  91.4 0.7 collective-permute-start.14
  92.7 2.9 %collective-permute-done.19.refs_3_ = bf16[4,2,48,128]{3,2,1,0:T(8,128)(2,1)S(1)} collective-permute-done((bf16[4,2,48,128]{3,2,1,0:T(8,128)(2,1)S(1)}, bf16[4,2,48,128]{3,2,1,0:T(8,128)(2,1)S(1)}, u32[]{:S(2)}, u32[]{:S(2)}) %collective-permute-start.19) | collective-permute-done | bytes 98336 | tf_op jit(solution)/shard_map/ppermute | solution.py:369
  95.7 12.1 %collective-permute-done.16 = f32[8,128]{1,0:T(8,128)S(1)} collective-permute-done((f32[8,128]{1,0:T(8,128)S(1)}, f32[8,128]{1,0:T(8,128)S(1)}, u32[]{:S(2)}, u32[]{:S(2)}) %collective-permute-start.16) | collective-permute-done | bytes 4128 | tf_op jit(solution)/shard_map/ppermute | solution.py:205
  107.8 9.7 %collective-permute-done.15 = f32[8,128]{1,0:T(8,128)S(1)} collective-permute-done((f32[8,128]{1,0:T(8,128)S(1)}, f32[8,128]{1,0:T(8,128)S(1)}, u32[]{:S(2)}, u32[]{:S(2)}) %collective-permute-start.15) | collective-permute-done | bytes 4128 | tf_op jit(solution)/shard_map/ppermute | solution.py:205
  117.6 1.7 mix_side.1
  119.3 0.7 copy-done.4
  120.0 0.5 collective-permute-start.21
  120.5 2.3 collective-permute-start.22
  122.8 1.6 collective-permute-start.23
  124.4 5.1 %mix_main.1 = bf16[32,480,128]{2,1,0:T(8,128)(2,1)} custom-call(bf16[512,512]{1,0:T(8,128)(2,1)S(1)} %get-tuple-element.80.mixing, bf16[32,240,128]{2,1,0:T(8,128)(2,1)} %all-to-all-done.1.scores, bf16[32,240,128]{2,1,0:T(8,128)(2,1)S(1)} %all-to-all-done.main.params), custom_call_target="tpu_custom_call" | custom-call | flops 2013265920 | bytes 7864320 | tf_op jit(solution)/shard_map/mix_main/pallas_call | solution.py:315
  129.5 4.3 %all-to-all-start.2 = ((bf16[32,480,128]{2,1,0:T(8,128)(2,1)}), bf16[32,480,128]{2,1,0:T(8,128)(2,1)}, u32[]{:S(2)}, u32[]{:S(2)}) async-start(bf16[32,480,128]{2,1,0:T(8,128)(2,1)} %mix_main.1), calls=%async_computation.2 | async-start | bytes 7864320 | tf_op jit(solution)/shard_map/all_to_all | solution.py:546
  133.9 3.8 %collective-permute-done.22.refs_2_ = bf16[8,96,128]{2,1,0:T(8,128)(2,1)S(1)} collective-permute-done((bf16[8,96,128]{2,1,0:T(8,128)(2,1)S(1)}, bf16[8,96,128]{2,1,0:T(8,128)(2,1)S(1)}, u32[]{:S(2)}, u32[]{:S(2)}) %collective-permute-start.22) | collective-permute-done | bytes 196640 | tf_op jit(solution)/shard_map/ppermute | solution.py:369
  137.7 1.5 collective-permute-start.24
  139.2 1.5 collective-permute-start.25
  140.7 0.5 collective-permute-start.26
  141.3 21.8 %collective-permute-done.24.refs_1_ = bf16[4,2,96,128]{3,2,1,0:T(8,128)(2,1)S(1)} collective-permute-done((bf16[4,2,96,128]{3,2,1,0:T(8,128)(2,1)S(1)}, bf16[4,2,96,128]{3,2,1,0:T(8,128)(2,1)S(1)}, u32[]{:S(2)}, u32[]{:S(2)}) %collective-permute-start.24) | collective-permute-done | bytes 196640 | tf_op jit(solution)/shard_map/ppermute | solution.py:369
  163.0 6.7 %collective-permute-done.25.refs_2_ = bf16[4,2,96,128]{3,2,1,0:T(8,128)(2,1)S(1)} collective-permute-done((bf16[4,2,96,128]{3,2,1,0:T(8,128)(2,1)S(1)}, bf16[4,2,96,128]{3,2,1,0:T(8,128)(2,1)S(1)}, u32[]{:S(2)}, u32[]{:S(2)}) %collective-permute-start.25) | collective-permute-done | bytes 196640 | tf_op jit(solution)/shard_map/ppermute | solution.py:369
  169.7 14.7 %collective-permute-done.26.refs_3_ = bf16[4,2,96,128]{3,2,1,0:T(8,128)(2,1)S(1)} collective-permute-done((bf16[4,2,96,128]{3,2,1,0:T(8,128)(2,1)S(1)}, bf16[4,2,96,128]{3,2,1,0:T(8,128)(2,1)S(1)}, u32[]{:S(2)}, u32[]{:S(2)}) %collective-permute-start.26) | collective-permute-done | bytes 196640 | tf_op jit(solution)/shard_map/ppermute | solution.py:369
  184.5 1.7 collective-permute-done.27.far
  186.3 38.6 %all-to-all-done.2.main = bf16[32,480,128]{2,1,0:T(8,128)(2,1)} async-done(((bf16[32,480,128]{2,1,0:T(8,128)(2,1)}), bf16[32,480,128]{2,1,0:T(8,128)(2,1)}, u32[]{:S(2)}, u32[]{:S(2)}) %all-to-all-start.2) | async-done | bytes 3932192 | tf_op jit(solution)/shard_map/all_to_all | solution.py:546
  224.9 4.6 %unpack.1 = (bf16[1,384,1536]{2,1,0:T(8,128)(2,1)}, bf16[1,1536,384]{2,1,0:T(8,128)(2,1)}, bf16[1,384,1536]{2,1,0:T(8,128)(2,1)}, bf16[1,1536,384]{2,1,0:T(8,128)(2,1)}) custom-call(bf16[32,480,128]{2,1,0:T(8,128)(2,1)} %all-to-all-done.2.main, bf16[32,96,128]{2,1,0:T(8,128)(2,1)S(1)} %settle.5.side), custom_call_target="tpu_custom_call" | custom-call | bytes 9437184 | tf_op jit(solution)/shard_map/unpack/pallas_call | solution.py:529
  (51 shorter events, 0.8 us)
Async XLA Ops:
  2.4 15.9 %collective-permute-start = (bf16[8,48,128]{2,1,0:T(8,128)(2,1)}, bf16[8,48,128]{2,1,0:T(8,128)(2,1)S(1)}, u32[]{:S(2)}, u32[]{:S(2)}) collective-permute-start(bf16[8,48,128]{2,1,0:T(8,128)(2,1)} %get-tuple-element.49), channel_id=1, source_target_pairs={{0,8},{1,9},{2,10},{3,11},{4,12},{5,13},{6,14},{7,15},{8,0},{9,1},... | collective-permute-start | bytes 294920 | tf_op jit(solution)/shard_map/ppermute | solution.py:369
  5.5 12.8 %collective-permute-start.1 = (bf16[8,48,128]{2,1,0:T(8,128)(2,1)}, bf16[8,48,128]{2,1,0:T(8,128)(2,1)S(1)}, u32[]{:S(2)}, u32[]{:S(2)}) collective-permute-start(bf16[8,48,128]{2,1,0:T(8,128)(2,1)} %get-tuple-element.50), channel_id=1, source_target_pairs={{0,16},{1,17},{2,18},{3,19},{4,20},{5,21},{6,22},{7,23},{8,24},{9,... | collective-permute-start | bytes 294920 | tf_op jit(solution)/shard_map/ppermute | solution.py:369
  8.1 10.2 %collective-permute-start.2 = (bf16[8,48,128]{2,1,0:T(8,128)(2,1)}, bf16[8,48,128]{2,1,0:T(8,128)(2,1)S(1)}, u32[]{:S(2)}, u32[]{:S(2)}) collective-permute-start(bf16[8,48,128]{2,1,0:T(8,128)(2,1)} %get-tuple-element.51), channel_id=1, source_target_pairs={{0,24},{1,25},{2,26},{3,27},{4,28},{5,29},{6,30},{7,31},{8,16},{9,... | collective-permute-start | bytes 294920 | tf_op jit(solution)/shard_map/ppermute | solution.py:369
  10.8 6.1 %copy-start.6 = (bf16[8,197,384]{2,0,1:T(8,128)(2,1)S(1)}, bf16[8,197,384]{2,0,1:T(8,128)(2,1)}, u32[]{:S(2)}) copy-start(bf16[8,197,384]{2,0,1:T(8,128)(2,1)} %param.8) | copy-start | bytes 3631108
  10.8 52.0 %all-to-all-start = ((bf16[32,240,128]{2,1,0:T(8,128)(2,1)}), bf16[32,240,128]{2,1,0:T(8,128)(2,1)S(1)}, u32[]{:S(2)}, u32[]{:S(2)}) async-start(bf16[32,240,128]{2,1,0:T(8,128)(2,1)} %pack_main.1), calls=%async_computation | async-start | bytes 3932160 | tf_op jit(solution)/shard_map/all_to_all | solution.py:546
  16.9 1.3 copy-start.7
  18.1 0.9 copy-start.2
  19.0 3.6 %copy-start = (bf16[1,1536,384]{2,1,0:T(8,128)(2,1)S(1)}, bf16[1,1536,384]{2,1,0:T(8,128)(2,1)}, u32[]{:S(2)}) copy-start(bf16[1,1536,384]{2,1,0:T(8,128)(2,1)} %second.3) | copy-start | bytes 3538948
  19.0 3.6 %copy-start.1 = (bf16[1,384,1536]{2,1,0:T(8,128)(2,1)S(1)}, bf16[1,384,1536]{2,1,0:T(8,128)(2,1)}, u32[]{:S(2)}) copy-start(bf16[1,384,1536]{2,1,0:T(8,128)(2,1)} %first.1) | copy-start | bytes 3538948
  19.0 3.6 %copy-start.3 = (s32[1,8]{1,0:T(1,128)S(1)}, s32[1,8]{1,0:T(1,128)}, u32[]{:S(2)}) copy-start(s32[1,8]{1,0:T(1,128)} %param.10) | copy-start | bytes 100
  19.1 26.6 %collective-permute-start.3 = (bf16[4,2,48,128]{3,2,1,0:T(8,128)(2,1)S(1)}, bf16[4,2,48,128]{3,2,1,0:T(8,128)(2,1)S(1)}, u32[]{:S(2)}, u32[]{:S(2)}) collective-permute-start(bf16[4,2,48,128]{3,2,1,0:T(8,128)(2,1)S(1)} %get-tuple-element.53), channel_id=1, source_target_pairs={{0,2},{1,3},{2,0},{3,1},{4,6},{5,7},{6,4},{7,5},{8,10},{9,11},{10,... | collective-permute-start | bytes 294920 | tf_op jit(solution)/shard_map/ppermute | solution.py:369
  20.9 24.8 %collective-permute-start.4 = (bf16[4,2,48,128]{3,2,1,0:T(8,128)(2,1)S(1)}, bf16[4,2,48,128]{3,2,1,0:T(8,128)(2,1)S(1)}, u32[]{:S(2)}, u32[]{:S(2)}) collective-permute-start(bf16[4,2,48,128]{3,2,1,0:T(8,128)(2,1)S(1)} %get-tuple-element.54), channel_id=1, source_target_pairs={{0,4},{1,5},{2,6},{3,7},{4,0},{5,1},{6,2},{7,3},{8,12},{9,13},{10,... | collective-permute-start | bytes 294920 | tf_op jit(solution)/shard_map/ppermute | solution.py:369
  22.4 23.3 %collective-permute-start.5 = (bf16[4,2,48,128]{3,2,1,0:T(8,128)(2,1)S(1)}, bf16[4,2,48,128]{3,2,1,0:T(8,128)(2,1)S(1)}, u32[]{:S(2)}, u32[]{:S(2)}) collective-permute-start(bf16[4,2,48,128]{3,2,1,0:T(8,128)(2,1)S(1)} %get-tuple-element.55), channel_id=1, source_target_pairs={{0,6},{1,7},{2,4},{3,5},{4,2},{5,3},{6,0},{7,1},{8,14},{9,15},{10,... | collective-permute-start | bytes 294920 | tf_op jit(solution)/shard_map/ppermute | solution.py:369
  45.7 25.8 %collective-permute-start.6 = (bf16[4,4,48,128]{3,2,1,0:T(8,128)(2,1)S(1)}, bf16[4,4,48,128]{3,2,1,0:T(8,128)(2,1)S(1)}, u32[]{:S(2)}, u32[]{:S(2)}) collective-permute-start(bf16[4,4,48,128]{3,2,1,0:T(8,128)(2,1)S(1)} %get-tuple-element.64), channel_id=1, source_target_pairs={{0,1},{1,0},{2,3},{3,2},{4,5},{5,4},{6,7},{7,6},{8,9},{9,8},{10,11... | collective-permute-start | bytes 589832 | tf_op jit(solution)/shard_map/ppermute | solution.py:369
  62.8 8.8 %collective-permute-start.7 = (bf16[8,48,128]{2,1,0:T(8,128)(2,1)S(1)}, bf16[8,48,128]{2,1,0:T(8,128)(2,1)S(1)}, u32[]{:S(2)}, u32[]{:S(2)}) collective-permute-start(bf16[8,48,128]{2,1,0:T(8,128)(2,1)S(1)} %get-tuple-element.69), channel_id=1, source_target_pairs={{0,8},{1,9},{2,10},{3,11},{4,12},{5,13},{6,14},{7,15},{8,0},{9,1},... | collective-permute-start | bytes 294920 | tf_op jit(solution)/shard_map/ppermute | solution.py:369
  62.8 10.8 %collective-permute-start.8 = (bf16[8,48,128]{2,1,0:T(8,128)(2,1)S(1)}, bf16[8,48,128]{2,1,0:T(8,128)(2,1)S(1)}, u32[]{:S(2)}, u32[]{:S(2)}) collective-permute-start(bf16[8,48,128]{2,1,0:T(8,128)(2,1)S(1)} %get-tuple-element.70), channel_id=1, source_target_pairs={{0,16},{1,17},{2,18},{3,19},{4,20},{5,21},{6,22},{7,23},{8,24},{9,... | collective-permute-start | bytes 294920 | tf_op jit(solution)/shard_map/ppermute | solution.py:369
  64.8 8.8 %collective-permute-start.9 = (bf16[8,48,128]{2,1,0:T(8,128)(2,1)S(1)}, bf16[8,48,128]{2,1,0:T(8,128)(2,1)S(1)}, u32[]{:S(2)}, u32[]{:S(2)}) collective-permute-start(bf16[8,48,128]{2,1,0:T(8,128)(2,1)S(1)} %get-tuple-element.71), channel_id=1, source_target_pairs={{0,24},{1,25},{2,26},{3,27},{4,28},{5,29},{6,30},{7,31},{8,16},{9,... | collective-permute-start | bytes 294920 | tf_op jit(solution)/shard_map/ppermute | solution.py:369
  67.2 57.2 %all-to-all-start.1 = ((bf16[32,240,128]{2,1,0:T(8,128)(2,1)}), bf16[32,240,128]{2,1,0:T(8,128)(2,1)}, u32[]{:S(2)}, u32[]{:S(2)}) async-start(bf16[32,240,128]{2,1,0:T(8,128)(2,1)} %get-tuple-element.81), calls=%async_computation.1 | async-start | bytes 3932160 | tf_op jit(solution)/shard_map/all_to_all | solution.py:546
  75.8 1.2 collective-permute-start.10
  77.0 9.2 %collective-permute-start.13 = (f32[8,128]{1,0:T(8,128)S(1)}, f32[8,128]{1,0:T(8,128)S(1)}, u32[]{:S(2)}, u32[]{:S(2)}) collective-permute-start(f32[8,128]{1,0:T(8,128)S(1)} %add.25), channel_id=1, source_target_pairs={{0,6},{1,7},{2,4},{3,5},{4,2},{5,3},{6,0},{7,1},{8,14},{9,15},{10,... | collective-permute-start | bytes 12296 | tf_op jit(solution)/shard_map/ppermute | solution.py:205
  79.1 8.5 %collective-permute-start.12 = (f32[8,128]{1,0:T(8,128)S(1)}, f32[8,128]{1,0:T(8,128)S(1)}, u32[]{:S(2)}, u32[]{:S(2)}) collective-permute-start(f32[8,128]{1,0:T(8,128)S(1)} %add.25), channel_id=1, source_target_pairs={{0,4},{1,5},{2,6},{3,7},{4,0},{5,1},{6,2},{7,3},{8,12},{9,13},{10,... | collective-permute-start | bytes 12296 | tf_op jit(solution)/shard_map/ppermute | solution.py:205
  79.8 7.8 %collective-permute-start.11 = (f32[8,128]{1,0:T(8,128)S(1)}, f32[8,128]{1,0:T(8,128)S(1)}, u32[]{:S(2)}, u32[]{:S(2)}) collective-permute-start(f32[8,128]{1,0:T(8,128)S(1)} %add.25), channel_id=1, source_target_pairs={{0,2},{1,3},{2,0},{3,1},{4,6},{5,7},{6,4},{7,5},{8,10},{9,11},{10,... | collective-permute-start | bytes 12296 | tf_op jit(solution)/shard_map/ppermute | solution.py:205
  80.5 10.9 %collective-permute-start.17 = (bf16[4,2,48,128]{3,2,1,0:T(8,128)(2,1)S(1)}, bf16[4,2,48,128]{3,2,1,0:T(8,128)(2,1)S(1)}, u32[]{:S(2)}, u32[]{:S(2)}) collective-permute-start(bf16[4,2,48,128]{3,2,1,0:T(8,128)(2,1)S(1)} %get-tuple-element.75), channel_id=1, source_target_pairs={{0,2},{1,3},{2,0},{3,1},{4,6},{5,7},{6,4},{7,5},{8,10},{9,11},{10,... | collective-permute-start | bytes 294920 | tf_op jit(solution)/shard_map/ppermute | solution.py:369
  81.8 10.9 %collective-permute-start.18 = (bf16[4,2,48,128]{3,2,1,0:T(8,128)(2,1)S(1)}, bf16[4,2,48,128]{3,2,1,0:T(8,128)(2,1)S(1)}, u32[]{:S(2)}, u32[]{:S(2)}) collective-permute-start(bf16[4,2,48,128]{3,2,1,0:T(8,128)(2,1)S(1)} %get-tuple-element.76), channel_id=1, source_target_pairs={{0,4},{1,5},{2,6},{3,7},{4,0},{5,1},{6,2},{7,3},{8,12},{9,13},{10,... | collective-permute-start | bytes 294920 | tf_op jit(solution)/shard_map/ppermute | solution.py:369
  86.2 9.4 %collective-permute-start.19 = (bf16[4,2,48,128]{3,2,1,0:T(8,128)(2,1)S(1)}, bf16[4,2,48,128]{3,2,1,0:T(8,128)(2,1)S(1)}, u32[]{:S(2)}, u32[]{:S(2)}) collective-permute-start(bf16[4,2,48,128]{3,2,1,0:T(8,128)(2,1)S(1)} %get-tuple-element.77), channel_id=1, source_target_pairs={{0,6},{1,7},{2,4},{3,5},{4,2},{5,3},{6,0},{7,1},{8,14},{9,15},{10,... | collective-permute-start | bytes 294920 | tf_op jit(solution)/shard_map/ppermute | solution.py:369
  87.6 20.2 %collective-permute-start.16 = (f32[8,128]{1,0:T(8,128)S(1)}, f32[8,128]{1,0:T(8,128)S(1)}, u32[]{:S(2)}, u32[]{:S(2)}) collective-permute-start(f32[8,128]{1,0:T(8,128)S(1)} %add_add_fusion.1), channel_id=1, source_target_pairs={{0,24},{1,25},{2,26},{3,27},{4,28},{5,29},{6,30},{7,31},{8,16},{9,... | collective-permute-start | bytes 12296 | tf_op jit(solution)/shard_map/ppermute | solution.py:205
  91.4 26.2 %collective-permute-start.15 = (f32[8,128]{1,0:T(8,128)S(1)}, f32[8,128]{1,0:T(8,128)S(1)}, u32[]{:S(2)}, u32[]{:S(2)}) collective-permute-start(f32[8,128]{1,0:T(8,128)S(1)} %add_add_fusion.1), channel_id=1, source_target_pairs={{0,16},{1,17},{2,18},{3,19},{4,20},{5,21},{6,22},{7,23},{8,24},{9,... | collective-permute-start | bytes 12296 | tf_op jit(solution)/shard_map/ppermute | solution.py:205
  91.4 26.2 %collective-permute-start.14 = (f32[8,128]{1,0:T(8,128)S(1)}, f32[8,128]{1,0:T(8,128)S(1)}, u32[]{:S(2)}, u32[]{:S(2)}) collective-permute-start(f32[8,128]{1,0:T(8,128)S(1)} %add_add_fusion.1), channel_id=1, source_target_pairs={{0,8},{1,9},{2,10},{3,11},{4,12},{5,13},{6,14},{7,15},{8,0},{9,1},... | collective-permute-start | bytes 12296 | tf_op jit(solution)/shard_map/ppermute | solution.py:205
  95.7 21.9 %collective-permute-start.20 = (bf16[4,4,48,128]{3,2,1,0:T(8,128)(2,1)S(1)}, bf16[4,4,48,128]{3,2,1,0:T(8,128)(2,1)S(1)}, u32[]{:S(2)}, u32[]{:S(2)}) collective-permute-start(bf16[4,4,48,128]{3,2,1,0:T(8,128)(2,1)S(1)} %get-tuple-element.79), channel_id=1, source_target_pairs={{0,1},{1,0},{2,3},{3,2},{4,5},{5,4},{6,7},{7,6},{8,9},{9,8},{10,11... | collective-permute-start | bytes 589832 | tf_op jit(solution)/shard_map/ppermute | solution.py:369
  119.3 0.7 copy-start.4
  120.0 13.9 %collective-permute-start.21 = (bf16[8,96,128]{2,1,0:T(8,128)(2,1)}, bf16[8,96,128]{2,1,0:T(8,128)(2,1)S(1)}, u32[]{:S(2)}, u32[]{:S(2)}) collective-permute-start(bf16[8,96,128]{2,1,0:T(8,128)(2,1)} %get-tuple-element.83), channel_id=1, source_target_pairs={{0,8},{1,9},{2,10},{3,11},{4,12},{5,13},{6,14},{7,15},{8,0},{9,1},... | collective-permute-start | bytes 589832 | tf_op jit(solution)/shard_map/ppermute | solution.py:369
  120.5 17.2 %collective-permute-start.22 = (bf16[8,96,128]{2,1,0:T(8,128)(2,1)S(1)}, bf16[8,96,128]{2,1,0:T(8,128)(2,1)S(1)}, u32[]{:S(2)}, u32[]{:S(2)}) collective-permute-start(bf16[8,96,128]{2,1,0:T(8,128)(2,1)S(1)} %get-tuple-element.84), channel_id=1, source_target_pairs={{0,16},{1,17},{2,18},{3,19},{4,20},{5,21},{6,22},{7,23},{8,24},{9,... | collective-permute-start | bytes 589832 | tf_op jit(solution)/shard_map/ppermute | solution.py:369
  122.8 14.9 %collective-permute-start.23 = (bf16[8,96,128]{2,1,0:T(8,128)(2,1)S(1)}, bf16[8,96,128]{2,1,0:T(8,128)(2,1)S(1)}, u32[]{:S(2)}, u32[]{:S(2)}) collective-permute-start(bf16[8,96,128]{2,1,0:T(8,128)(2,1)S(1)} %get-tuple-element.85), channel_id=1, source_target_pairs={{0,24},{1,25},{2,26},{3,27},{4,28},{5,29},{6,30},{7,31},{8,16},{9,... | collective-permute-start | bytes 589832 | tf_op jit(solution)/shard_map/ppermute | solution.py:369
  129.5 8.1 %copy-start.5 = (bf16[8,96,128]{2,1,0:T(8,128)(2,1)S(1)}, bf16[8,96,128]{2,1,0:T(8,128)(2,1)}, u32[]{:S(2)}) copy-start(bf16[8,96,128]{2,1,0:T(8,128)(2,1)} %copy-done.4) | copy-start | bytes 589828
  129.5 95.4 %all-to-all-start.2 = ((bf16[32,480,128]{2,1,0:T(8,128)(2,1)}), bf16[32,480,128]{2,1,0:T(8,128)(2,1)}, u32[]{:S(2)}, u32[]{:S(2)}) async-start(bf16[32,480,128]{2,1,0:T(8,128)(2,1)} %mix_main.1), calls=%async_computation.2 | async-start | bytes 7864320 | tf_op jit(solution)/shard_map/all_to_all | solution.py:546
  137.7 25.3 %collective-permute-start.24 = (bf16[4,2,96,128]{3,2,1,0:T(8,128)(2,1)S(1)}, bf16[4,2,96,128]{3,2,1,0:T(8,128)(2,1)S(1)}, u32[]{:S(2)}, u32[]{:S(2)}) collective-permute-start(bf16[4,2,96,128]{3,2,1,0:T(8,128)(2,1)S(1)} %get-tuple-element.87), channel_id=1, source_target_pairs={{0,2},{1,3},{2,0},{3,1},{4,6},{5,7},{6,4},{7,5},{8,10},{9,11},{10,... | collective-permute-start | bytes 589832 | tf_op jit(solution)/shard_map/ppermute | solution.py:369
  139.2 30.5 %collective-permute-start.25 = (bf16[4,2,96,128]{3,2,1,0:T(8,128)(2,1)S(1)}, bf16[4,2,96,128]{3,2,1,0:T(8,128)(2,1)S(1)}, u32[]{:S(2)}, u32[]{:S(2)}) collective-permute-start(bf16[4,2,96,128]{3,2,1,0:T(8,128)(2,1)S(1)} %get-tuple-element.88), channel_id=1, source_target_pairs={{0,4},{1,5},{2,6},{3,7},{4,0},{5,1},{6,2},{7,3},{8,12},{9,13},{10,... | collective-permute-start | bytes 589832 | tf_op jit(solution)/shard_map/ppermute | solution.py:369
  140.7 43.7 %collective-permute-start.26 = (bf16[4,2,96,128]{3,2,1,0:T(8,128)(2,1)S(1)}, bf16[4,2,96,128]{3,2,1,0:T(8,128)(2,1)S(1)}, u32[]{:S(2)}, u32[]{:S(2)}) collective-permute-start(bf16[4,2,96,128]{3,2,1,0:T(8,128)(2,1)S(1)} %get-tuple-element.89), channel_id=1, source_target_pairs={{0,6},{1,7},{2,4},{3,5},{4,2},{5,3},{6,0},{7,1},{8,14},{9,15},{10,... | collective-permute-start | bytes 589832 | tf_op jit(solution)/shard_map/ppermute | solution.py:369
  184.5 1.8 collective-permute-start.27

commit v15 on v14

--- a/solution.py
+++ b/solution.py
@@ -24,6 +24,8 @@
 ROWS = SIDE * len(GROUPS)
 MAIN = ROWS - EDGE
 REST = ROWS - MAIN
+PMAIN = MAIN - TILE
+PREST = ROWS - PMAIN
 PLANES = 4
 PLANE = BLOCKS // PLANES
 LONG = 10**11
@@ -52,13 +54,13 @@
         outs[k // PLANE][k % PLANE] = side[k ^ me[0]]
 
 
+def rows_of(main, side, at):
+    ref, at = (main, at) if at < main.shape[1] else (side, at - main.shape[1])
+    return ref[:, at : at + TILE, :].reshape(ref.shape[0] * TILE, LANES)
+
+
 def tile(main, side, r):
-    parts = []
-    for g in GROUPS:
-        at = g * SIDE + r
-        ref, at = (main, at) if at < MAIN else (side, at - MAIN)
-        parts.append(ref[:, at : at + TILE, :].reshape(ref.shape[0] * TILE, LANES))
-    return jnp.concatenate(parts, axis=1)
+    return jnp.concatenate([rows_of(main, side, g * SIDE + r) for g in GROUPS], axis=1)
 
 
 def score_kernel(
@@ -237,10 +239,6 @@
     return both.astype(jnp.bfloat16)
 
 
-def rows_of(ref, at):
-    return ref[:, at : at + TILE, :].reshape(ref.shape[0] * TILE, LANES)
-
-
 def mix_side_kernel(scale, me, packed, scores, params, mixing, *refs):
     outs, side = refs[:PLANES], refs[PLANES]
     members = params.shape[0]
@@ -248,16 +246,13 @@
     ksum = jnp.sum(full, axis=1, keepdims=True)
     mixer = full.astype(jnp.bfloat16)
     mixing[...] = mixer
-    count = REST // TILE
-    for start in range(0, REST, count * TILE):
-        at = [start + q * TILE for q in range(count)]
-        got = jnp.concatenate([rows_of(scores, r) for r in at], axis=1)
-        own = jnp.concatenate([rows_of(params, r) for r in at], axis=1)
-        both = mix(mixer, ksum, got, own)
-        for q in range(2 * count):
-            part = both[:, q * LANES : (q + 1) * LANES].reshape(members, TILE, LANES)
-            r = q // count * REST + at[q % count]
-            side[:, r : r + TILE, :] = part
+    at = range(0, REST, TILE)
+    got = jnp.concatenate([rows_of(scores, None, r) for r in at], axis=1)
+    own = jnp.concatenate([rows_of(params, None, PREST - REST + r) for r in at], axis=1)
+    both = mix(mixer, ksum, got, own)
+    for q in range(2 * len(at)):
+        part = both[:, q * LANES : (q + 1) * LANES].reshape(members, TILE, LANES)
+        side[:, q * TILE : (q + 1) * TILE, :] = part
     by_plane(me, side, outs)
 
 
@@ -282,7 +277,7 @@
     )(scale, me, packed, scores, params)
 
 
-def mix_main_kernel(mixing, scores, params, out, mixed, stores):
+def mix_main_kernel(mixing, scores, params, side_params, out, mixed, stores):
     members = params.shape[0]
     mixer = mixing[...]
     ksum = jnp.sum(mixer.astype(jnp.float32), axis=1, keepdims=True)
@@ -290,8 +285,8 @@
     for r in range(0, SIDE, TILE):
         at = [g * SIDE + r for g in GROUPS if g * SIDE + r < MAIN]
         groups = len(at)
-        got = jnp.concatenate([rows_of(scores, x) for x in at], axis=1)
-        own = jnp.concatenate([rows_of(params, x) for x in at], axis=1)
+        got = jnp.concatenate([rows_of(scores, None, x) for x in at], axis=1)
+        own = jnp.concatenate([rows_of(params, side_params, x) for x in at], axis=1)
         both = mix(mixer, ksum, got, own)
         for q in range(2 * groups):
             part = both[:, q * LANES : (q + 1) * LANES].reshape(members, TILE, LANES)
@@ -308,14 +303,14 @@
         copy.wait()
 
 
-def mix_main(mixing, scores, params):
+def mix_main(mixing, scores, params, side_params):
     members = params.shape[0]
     wide = members * TILE
     vmem = pl.BlockSpec(memory_space=pltpu.VMEM)
     return pl.pallas_call(
         mix_main_kernel,
         out_shape=pltpu.HBM((members, 2 * MAIN, LANES), jnp.bfloat16),
-        in_specs=[vmem] * 3,
+        in_specs=[vmem] * 4,
         out_specs=pl.BlockSpec(memory_space=pl.ANY),
         scratch_shapes=[
             pltpu.VMEM((members, 2 * MAIN, LANES), jnp.bfloat16),
@@ -328,7 +323,7 @@
             transcendentals=0,
         ),
         name="mix_main",
-    )(mixing, scores, params)
+    )(mixing, scores, params, side_params)
 
 
 def plane_kernel(*refs):
@@ -417,14 +412,23 @@
 TALL = FF // STEPS
 
 
-def pack_side_kernel(me, second, *refs):
-    outs, (tall, load) = refs[:PLANES], refs[PLANES:]
-    copy = pltpu.make_async_copy(second.at[0, :, pl.ds(D - LANES, LANES)], tall, load)
-    copy.start()
-    copy.wait()
+def pack_side_kernel(me, first, second, *refs):
+    outs, (wide, tall, loads) = refs[:PLANES], refs[PLANES:]
+    copies = [pltpu.make_async_copy(second.at[0, :, pl.ds(D - LANES, LANES)], tall, loads.at[COLS])]
+    for c in range(COLS):
+        here = first.at[0, :, pl.ds((c + 1) * D - LANES, LANES)]
+        copies.append(pltpu.make_async_copy(here, wide.at[c], loads.at[c]))
+    for copy in copies:
+        copy.start()
+    for copy in copies:
+        copy.wait()
+    more = PREST - EDGE
     for k in range(BLOCKS):
-        here = pl.ds(pl.multiple_of((k ^ me[0]) * EDGE, EDGE), EDGE)
-        outs[k // PLANE][k % PLANE] = tall[here, :]
+        b = k ^ me[0]
+        here = pl.ds(pl.multiple_of(b // COLS * EDGE + EDGE - more, TILE), more)
+        outs[k // PLANE][k % PLANE, 0:more, :] = wide[b % COLS, here, :]
+        here = pl.ds(pl.multiple_of(b * EDGE, EDGE), EDGE)
+        outs[k // PLANE][k % PLANE, more:PREST, :] = tall[here, :]
 
 
 def pack_main_kernel(first, second, out, wide, tall, packed, loads, stores):
@@ -451,8 +455,11 @@
         for c in range(COLS):
             for g in GROUPS:
                 b, at, lanes = d * COLS + c, g * SIDE, g * LANES
-                packed[b, at : at + EDGE, :] = wide[d, :, c * D + lanes : c * D + lanes + LANES]
-                if at + EDGE < MAIN:
+                end = min(EDGE, PMAIN - at)
+                packed[b, at : at + end, :] = wide[
+                    d, 0:end, c * D + lanes : c * D + lanes + LANES
+                ]
+                if at + EDGE < PMAIN:
                     packed[b, at + EDGE : at + SIDE, :] = tall[
                         d, c * EDGE : (c + 1) * EDGE, lanes : lanes + LANES
                     ]
@@ -468,22 +475,26 @@
     cost = pl.CostEstimate(flops=0, bytes_accessed=4 * D * FF, transcendentals=0)
     side = pl.pallas_call(
         pack_side_kernel,
-        out_shape=side_shapes(REST),
-        in_specs=[pl.BlockSpec(memory_space=pltpu.SMEM)] + anywhere,
-        scratch_shapes=[pltpu.VMEM((FF, LANES), bf), pltpu.SemaphoreType.DMA],
+        out_shape=side_shapes(PREST),
+        in_specs=[pl.BlockSpec(memory_space=pltpu.SMEM)] + anywhere * 2,
+        scratch_shapes=[
+            pltpu.VMEM((COLS, D, LANES), bf),
+            pltpu.VMEM((FF, LANES), bf),
+            pltpu.SemaphoreType.DMA((COLS + 1,)),
+        ],
         compiler_params=params,
         cost_estimate=cost,
         name="pack_side",
-    )(me, second)
+    )(me, first, second)
     main = pl.pallas_call(
         pack_main_kernel,
-        out_shape=pltpu.HBM((BLOCKS, MAIN, LANES), bf),
+        out_shape=pltpu.HBM((BLOCKS, PMAIN, LANES), bf),
         in_specs=anywhere * 2,
         out_specs=anywhere[0],
         scratch_shapes=[
             pltpu.VMEM((STEPS, EDGE, FF), bf),
             pltpu.VMEM((STEPS, TALL, D), bf),
-            pltpu.VMEM((BLOCKS, MAIN, LANES), bf),
+            pltpu.VMEM((BLOCKS, PMAIN, LANES), bf),
             pltpu.SemaphoreType.DMA((2, STEPS)),
             pltpu.SemaphoreType.DMA((STEPS,)),
         ],
@@ -537,7 +548,7 @@
             pltpu.SemaphoreType.DMA((2, 2, STEPS)),
         ],
         compiler_params=pltpu.CompilerParams(vmem_limit_bytes=24 * 1024 * 1024),
-        cost_estimate=pl.CostEstimate(flops=0, bytes_accessed=16 * D * FF, transcendentals=0),
+        cost_estimate=pl.CostEstimate(flops=0, bytes_accessed=LONG // 100, transcendentals=0),
         name="unpack",
     )(main, side)
 
@@ -572,7 +583,7 @@
         for bits in ((1,), (2, 4, 6), (8, 16, 24)):
             packed = add_over(packed, members, bits)
         mixing, *side = mix_side(kernel_scale, me, packed, side_scores, side_params)
-        main = mix_main(mixing, scores, params)
+        main = mix_main(mixing, scores, params, side_params)
         side = in_order(across_chips(in_plane(across_planes(side))), me)
         return from_blocks(exchange(main), side)
     cut = (members, BLOCKS * ROWS // members, LANES)

time: 230 us -> 230 us (level)
  waiting for transfers between devices: 135 us -> 121 us
  starting transfers between devices: 48.5 us -> 56.9 us
  local copies, waits for them, and re-layouts: 2.83 us -> 7.39 us
    ppermute x7, waiting for transfers between devices: 26.1 us -> 19.8 us  [add_over(): lax.ppermute(value, AXES, [(i, i ^ bit) for i in range(members)])]
    ppermute x7, starting transfers between devices: 7.94 us -> 14.1 us  [add_over(): lax.ppermute(value, AXES, [(i, i ^ bit) for i in range(members)])]
    ppermute x21, waiting for transfers between devices: 53.6 us -> 48.5 us  [swap(): return lax.ppermute(value, AXES, pairs)]
    unnamed x18 -> x26, local copies, waits for them, and re-layouts: 2.83 us -> 7.39 us
    all_to_all x3, waiting for transfers between devices: 55.6 us -> 52.6 us  [exchange(): return lax.all_to_all(blocks, AXES, split_axis=0, concat_axis=0, tiled=True)]
  transfers between devices with their start and end apart: 31 -> 31, of which waited for: 13 -> 11; matrix products, arithmetic and copies ran while one was open for 0% -> 1% of each run, Pallas kernels for 15% -> 15%
where the time goes in v15:
time: 230 us; the launch traced here: 229 us
  waiting for transfers between devices  121 us (53%)
  starting transfers between devices  56.9 us (25%)
  Pallas kernels  42.3 us (18%)
  local copies, waits for them, and re-layouts  7.39 us (3%)
    all_to_all x3, waiting for transfers between devices, exchange(): return lax.all_to_all(blocks, AXES, split_axis=0, concat_axis=0, tiled=True)  52.6 us
    ppermute x21, waiting for transfers between devices, swap(): return lax.ppermute(value, AXES, pairs)  48.5 us
    ppermute x21, starting transfers between devices, swap(): return lax.ppermute(value, AXES, pairs)  27.9 us
    pallas_call x1, Pallas kernels, particle_scores(): pl.pallas_call(functools.partial(score_kernel, DATA / count), out_shape=(...  23 us
    ppermute x7, waiting for transfers between devices, add_over(): lax.ppermute(value, AXES, [(i, i ^ bit) for i in range(members)])  19.8 us
    all_to_all x3, starting transfers between devices, exchange(): return lax.all_to_all(blocks, AXES, split_axis=0, concat_axis=0, tiled=True)  14.8 us
    ppermute x7, starting transfers between devices, add_over(): lax.ppermute(value, AXES, [(i, i ^ bit) for i in range(members)])  14.1 us
    unnamed x26, local copies, waits for them, and re-layouts  7.39 us
  transfers between devices with their start and end apart: 31, of which 11 were waited for; matrix products, arithmetic and copies ran while one was open for 1% of the time, Pallas kernels for 15%

profile of v15, /device:TPU:0, one launch (start us, length us, event | category | flops | bytes accessed | tf_op | source)
XLA Modules:
  0.0 229.2 jit_solution(5605761995324168580)
XLA Ops:
  0.6 2.2 pack_side.1
  2.9 3.1 %collective-permute-start = (bf16[8,64,128]{2,1,0:T(8,128)(2,1)}, bf16[8,64,128]{2,1,0:T(8,128)(2,1)S(1)}, u32[]{:S(2)}, u32[]{:S(2)}) collective-permute-start(bf16[8,64,128]{2,1,0:T(8,128)(2,1)} %get-tuple-element.49), channel_id=1, source_target_pairs={{0,8},{1,9},{2,10},{3,11},{4,12},{5,13},{6,14},{7,15},{8,0},{9,1},... | collective-permute-start | bytes 393224 | tf_op jit(solution)/shard_map/ppermute | solution.py:364
  5.9 2.6 %collective-permute-start.1 = (bf16[8,64,128]{2,1,0:T(8,128)(2,1)}, bf16[8,64,128]{2,1,0:T(8,128)(2,1)S(1)}, u32[]{:S(2)}, u32[]{:S(2)}) collective-permute-start(bf16[8,64,128]{2,1,0:T(8,128)(2,1)} %get-tuple-element.50), channel_id=1, source_target_pairs={{0,16},{1,17},{2,18},{3,19},{4,20},{5,21},{6,22},{7,23},{8,24},{9,... | collective-permute-start | bytes 393224 | tf_op jit(solution)/shard_map/ppermute | solution.py:364
  8.5 2.6 %pack_main.1 = bf16[32,224,128]{2,1,0:T(8,128)(2,1)} custom-call(bf16[1,384,1536]{2,1,0:T(8,128)(2,1)} %first.3, bf16[1,1536,384]{2,1,0:T(8,128)(2,1)} %second.3), custom_call_target="tpu_custom_call" | custom-call | bytes 2359296 | tf_op jit(solution)/shard_map/pack_main/pallas_call | solution.py:489
  11.2 6.1 %all-to-all-start = ((bf16[32,224,128]{2,1,0:T(8,128)(2,1)}), bf16[32,224,128]{2,1,0:T(8,128)(2,1)S(1)}, u32[]{:S(2)}, u32[]{:S(2)}) async-start(bf16[32,224,128]{2,1,0:T(8,128)(2,1)} %pack_main.1), calls=%async_computation | async-start | bytes 3670016 | tf_op jit(solution)/shard_map/all_to_all | solution.py:557
  17.3 1.5 copy.10.image
  19.1 0.7 copy-done.5
  19.9 1.8 collective-permute-start.3
  21.7 1.5 collective-permute-start.4
  23.4 23.0 %score.1 = (bf16[32,240,128]{2,1,0:T(8,128)(2,1)}, bf16[8,48,128]{2,1,0:T(8,128)(2,1)S(1)}, bf16[8,48,128]{2,1,0:T(8,128)(2,1)}, bf16[8,48,128]{2,1,0:T(8,128)(2,1)S(1)}, bf16[8,48,128]{2,1,0:T(8,128)(2,1)S(1)}) custom-call(s32[8]{0:T(128)S(1)} %bitcast.6, s32[1]{0:T(128)} %bitcast.me, bf16[8,197,384]{2,1,0:T(8,128)(2,1)S(1)} %copy.10.image, ...), custom_call_target="tpu_custom_call" | custom-call | flops 9814671360 | bytes 7139328 | tf_op jit(solution)/shard_map/score/pallas_call | solution.py:131
  47.1 13.3 %all-to-all-done.main.params = bf16[32,224,128]{2,1,0:T(8,128)(2,1)S(1)} async-done(((bf16[32,224,128]{2,1,0:T(8,128)(2,1)}), bf16[32,224,128]{2,1,0:T(8,128)(2,1)S(1)}, u32[]{:S(2)}, u32[]{:S(2)}) %all-to-all-start) | async-done | bytes 1835040 | tf_op jit(solution)/shard_map/all_to_all | solution.py:557
  60.4 1.2 copy-done
  61.6 2.5 %collective-permute-start.8 = (bf16[8,48,128]{2,1,0:T(8,128)(2,1)S(1)}, bf16[8,48,128]{2,1,0:T(8,128)(2,1)}, u32[]{:S(2)}, u32[]{:S(2)}) collective-permute-start(bf16[8,48,128]{2,1,0:T(8,128)(2,1)S(1)} %get-tuple-element.70), channel_id=1, source_target_pairs={{0,16},{1,17},{2,18},{3,19},{4,20},{5,21},{6,22},{7,23},{8,24},{9,... | collective-permute-start | bytes 294920 | tf_op jit(solution)/shard_map/ppermute | solution.py:364
  64.1 1.9 collective-permute-start.9
  66.0 4.7 %all-to-all-start.1 = ((bf16[32,240,128]{2,1,0:T(8,128)(2,1)}), bf16[32,240,128]{2,1,0:T(8,128)(2,1)S(1)}, u32[]{:S(2)}, u32[]{:S(2)}) async-start(bf16[32,240,128]{2,1,0:T(8,128)(2,1)} %get-tuple-element.81), calls=%async_computation.1 | async-start | bytes 3932160 | tf_op jit(solution)/shard_map/all_to_all | solution.py:557
  70.8 1.0 collective-permute-done.9.refs_3_
  71.8 0.9 copy-done.10
  72.7 1.0 plane.4
  73.7 2.2 gram.1
  75.9 1.2 collective-permute-done.10
  77.1 2.0 collective-permute-start.11
  79.1 1.4 collective-permute-start.12
  80.6 2.0 collective-permute-start.17
  82.6 1.4 collective-permute-start.18
  84.0 2.8 %collective-permute-start.19 = (bf16[4,2,48,128]{3,2,1,0:T(8,128)(2,1)S(1)}, bf16[4,2,48,128]{3,2,1,0:T(8,128)(2,1)S(1)}, u32[]{:S(2)}, u32[]{:S(2)}) collective-permute-start(bf16[4,2,48,128]{3,2,1,0:T(8,128)(2,1)S(1)} %get-tuple-element.77), channel_id=1, source_target_pairs={{0,6},{1,7},{2,4},{3,5},{4,2},{5,3},{6,0},{7,1},{8,14},{9,15},{10,... | collective-permute-start | bytes 294920 | tf_op jit(solution)/shard_map/ppermute | solution.py:364
  86.8 0.6 collective-permute-start.14
  87.4 2.5 %collective-permute-start.15 = (f32[8,128]{1,0:T(8,128)S(1)}, f32[8,128]{1,0:T(8,128)S(1)}, u32[]{:S(2)}, u32[]{:S(2)}) collective-permute-start(f32[8,128]{1,0:T(8,128)S(1)} %add_add_fusion.1), channel_id=1, source_target_pairs={{0,16},{1,17},{2,18},{3,19},{4,20},{5,21},{6,22},{7,23},{8,24},{9,... | collective-permute-start | bytes 12296 | tf_op jit(solution)/shard_map/ppermute | solution.py:207
  89.9 7.6 %collective-permute-start.16 = (f32[8,128]{1,0:T(8,128)S(1)}, f32[8,128]{1,0:T(8,128)S(1)}, u32[]{:S(2)}, u32[]{:S(2)}) collective-permute-start(f32[8,128]{1,0:T(8,128)S(1)} %add_add_fusion.1), channel_id=1, source_target_pairs={{0,24},{1,25},{2,26},{3,27},{4,28},{5,29},{6,30},{7,31},{8,16},{9,... | collective-permute-start | bytes 12296 | tf_op jit(solution)/shard_map/ppermute | solution.py:207
  98.2 5.1 %collective-permute-done.14 = f32[8,128]{1,0:T(8,128)S(1)} collective-permute-done((f32[8,128]{1,0:T(8,128)S(1)}, f32[8,128]{1,0:T(8,128)S(1)}, u32[]{:S(2)}, u32[]{:S(2)}) %collective-permute-start.14) | collective-permute-done | bytes 4128 | tf_op jit(solution)/shard_map/ppermute | solution.py:207
  103.3 13.5 %collective-permute-done.15 = f32[8,128]{1,0:T(8,128)S(1)} collective-permute-done((f32[8,128]{1,0:T(8,128)S(1)}, f32[8,128]{1,0:T(8,128)S(1)}, u32[]{:S(2)}, u32[]{:S(2)}) %collective-permute-start.15) | collective-permute-done | bytes 4128 | tf_op jit(solution)/shard_map/ppermute | solution.py:207
  116.9 1.7 mix_side.1
  118.6 0.7 copy-done.7
  119.3 0.6 collective-permute-start.21
  119.9 1.6 collective-permute-start.22
  121.5 2.2 collective-permute-start.23
  123.7 1.5 copy-done.2
  125.2 3.6 %mix_main.1 = bf16[32,480,128]{2,1,0:T(8,128)(2,1)} custom-call(bf16[512,512]{1,0:T(8,128)(2,1)S(1)} %get-tuple-element.80.mixing, bf16[32,240,128]{2,1,0:T(8,128)(2,1)S(1)} %all-to-all-done.1.scores, bf16[32,224,128]{2,1,0:T(8,128)(2,1)S(1)} %copy-done.2, bf16[32,64,128]{2,1,0:T(8,128)(2,1)S(1)} %settle.3.side.params.side_params), custom_call_target="tpu_custom_call" | custom-call | flops 2013265920 | bytes 7864320 | tf_op jit(solution)/shard_map/mix_main/pallas_call | solution.py:310
  128.8 4.1 %all-to-all-start.2 = ((bf16[32,480,128]{2,1,0:T(8,128)(2,1)}), bf16[32,480,128]{2,1,0:T(8,128)(2,1)}, u32[]{:S(2)}, u32[]{:S(2)}) async-start(bf16[32,480,128]{2,1,0:T(8,128)(2,1)} %mix_main.1), calls=%async_computation.2 | async-start | bytes 7864320 | tf_op jit(solution)/shard_map/all_to_all | solution.py:557
  132.9 4.5 %collective-permute-done.22.refs_2_ = bf16[8,96,128]{2,1,0:T(8,128)(2,1)} collective-permute-done((bf16[8,96,128]{2,1,0:T(8,128)(2,1)}, bf16[8,96,128]{2,1,0:T(8,128)(2,1)}, u32[]{:S(2)}, u32[]{:S(2)}) %collective-permute-start.22) | collective-permute-done | bytes 196640 | tf_op jit(solution)/shard_map/ppermute | solution.py:364
  137.4 1.1 plane.5
  138.4 1.5 collective-permute-start.24
  139.9 1.5 collective-permute-start.25
  142.0 20.1 %collective-permute-done.24.refs_1_ = bf16[4,2,96,128]{3,2,1,0:T(8,128)(2,1)S(1)} collective-permute-done((bf16[4,2,96,128]{3,2,1,0:T(8,128)(2,1)S(1)}, bf16[4,2,96,128]{3,2,1,0:T(8,128)(2,1)S(1)}, u32[]{:S(2)}, u32[]{:S(2)}) %collective-permute-start.24) | collective-permute-done | bytes 196640 | tf_op jit(solution)/shard_map/ppermute | solution.py:364
  162.0 6.1 %collective-permute-done.25.refs_2_ = bf16[4,2,96,128]{3,2,1,0:T(8,128)(2,1)S(1)} collective-permute-done((bf16[4,2,96,128]{3,2,1,0:T(8,128)(2,1)S(1)}, bf16[4,2,96,128]{3,2,1,0:T(8,128)(2,1)S(1)}, u32[]{:S(2)}, u32[]{:S(2)}) %collective-permute-start.25) | collective-permute-done | bytes 196640 | tf_op jit(solution)/shard_map/ppermute | solution.py:364
  168.2 15.1 %collective-permute-done.26.refs_3_ = bf16[4,2,96,128]{3,2,1,0:T(8,128)(2,1)S(1)} collective-permute-done((bf16[4,2,96,128]{3,2,1,0:T(8,128)(2,1)S(1)}, bf16[4,2,96,128]{3,2,1,0:T(8,128)(2,1)S(1)}, u32[]{:S(2)}, u32[]{:S(2)}) %collective-permute-start.26) | collective-permute-done | bytes 196640 | tf_op jit(solution)/shard_map/ppermute | solution.py:364
  183.4 1.7 collective-permute-done.27.far
  185.1 39.3 %all-to-all-done.2.main = bf16[32,480,128]{2,1,0:T(8,128)(2,1)} async-done(((bf16[32,480,128]{2,1,0:T(8,128)(2,1)}), bf16[32,480,128]{2,1,0:T(8,128)(2,1)}, u32[]{:S(2)}, u32[]{:S(2)}) %all-to-all-start.2) | async-done | bytes 3932192 | tf_op jit(solution)/shard_map/all_to_all | solution.py:557
  224.4 4.6 %unpack.1 = (bf16[1,384,1536]{2,1,0:T(8,128)(2,1)}, bf16[1,1536,384]{2,1,0:T(8,128)(2,1)}, bf16[1,384,1536]{2,1,0:T(8,128)(2,1)}, bf16[1,1536,384]{2,1,0:T(8,128)(2,1)}) custom-call(bf16[32,480,128]{2,1,0:T(8,128)(2,1)} %all-to-all-done.2.main, bf16[32,96,128]{2,1,0:T(8,128)(2,1)S(1)} %settle.5.side), custom_call_target="tpu_custom_call" | custom-call | bytes 1000000000 | tf_op jit(solution)/shard_map/unpack/pallas_call | solution.py:540
  (59 shorter events, 2.2 us)
Async XLA Ops:
  2.9 16.2 %collective-permute-start = (bf16[8,64,128]{2,1,0:T(8,128)(2,1)}, bf16[8,64,128]{2,1,0:T(8,128)(2,1)S(1)}, u32[]{:S(2)}, u32[]{:S(2)}) collective-permute-start(bf16[8,64,128]{2,1,0:T(8,128)(2,1)} %get-tuple-element.49), channel_id=1, source_target_pairs={{0,8},{1,9},{2,10},{3,11},{4,12},{5,13},{6,14},{7,15},{8,0},{9,1},... | collective-permute-start | bytes 393224 | tf_op jit(solution)/shard_map/ppermute | solution.py:364
  5.9 13.1 %collective-permute-start.1 = (bf16[8,64,128]{2,1,0:T(8,128)(2,1)}, bf16[8,64,128]{2,1,0:T(8,128)(2,1)S(1)}, u32[]{:S(2)}, u32[]{:S(2)}) collective-permute-start(bf16[8,64,128]{2,1,0:T(8,128)(2,1)} %get-tuple-element.50), channel_id=1, source_target_pairs={{0,16},{1,17},{2,18},{3,19},{4,20},{5,21},{6,22},{7,23},{8,24},{9,... | collective-permute-start | bytes 393224 | tf_op jit(solution)/shard_map/ppermute | solution.py:364
  8.5 10.6 %collective-permute-start.2 = (bf16[8,64,128]{2,1,0:T(8,128)(2,1)}, bf16[8,64,128]{2,1,0:T(8,128)(2,1)S(1)}, u32[]{:S(2)}, u32[]{:S(2)}) collective-permute-start(bf16[8,64,128]{2,1,0:T(8,128)(2,1)} %get-tuple-element.51), channel_id=1, source_target_pairs={{0,24},{1,25},{2,26},{3,27},{4,28},{5,29},{6,30},{7,31},{8,16},{9,... | collective-permute-start | bytes 393224 | tf_op jit(solution)/shard_map/ppermute | solution.py:364
  11.2 49.2 %all-to-all-start = ((bf16[32,224,128]{2,1,0:T(8,128)(2,1)}), bf16[32,224,128]{2,1,0:T(8,128)(2,1)S(1)}, u32[]{:S(2)}, u32[]{:S(2)}) async-start(bf16[32,224,128]{2,1,0:T(8,128)(2,1)} %pack_main.1), calls=%async_computation | async-start | bytes 3670016 | tf_op jit(solution)/shard_map/all_to_all | solution.py:557
  17.3 1.6 copy-start.11
  18.9 0.9 copy-start.5
  19.8 3.6 %copy-start.3 = (bf16[1,384,1536]{2,1,0:T(8,128)(2,1)S(1)}, bf16[1,384,1536]{2,1,0:T(8,128)(2,1)}, u32[]{:S(2)}) copy-start(bf16[1,384,1536]{2,1,0:T(8,128)(2,1)} %first.3) | copy-start | bytes 3538948
  19.8 3.6 %copy-start.4 = (bf16[1,1536,384]{2,1,0:T(8,128)(2,1)S(1)}, bf16[1,1536,384]{2,1,0:T(8,128)(2,1)}, u32[]{:S(2)}) copy-start(bf16[1,1536,384]{2,1,0:T(8,128)(2,1)} %second.3) | copy-start | bytes 3538948
  19.8 3.6 %copy-start.6 = (s32[1,8]{1,0:T(1,128)S(1)}, s32[1,8]{1,0:T(1,128)}, u32[]{:S(2)}) copy-start(s32[1,8]{1,0:T(1,128)} %param.10) | copy-start | bytes 100
  19.9 26.6 %collective-permute-start.3 = (bf16[4,2,64,128]{3,2,1,0:T(8,128)(2,1)S(1)}, bf16[4,2,64,128]{3,2,1,0:T(8,128)(2,1)S(1)}, u32[]{:S(2)}, u32[]{:S(2)}) collective-permute-start(bf16[4,2,64,128]{3,2,1,0:T(8,128)(2,1)S(1)} %get-tuple-element.53), channel_id=1, source_target_pairs={{0,2},{1,3},{2,0},{3,1},{4,6},{5,7},{6,4},{7,5},{8,10},{9,11},{10,... | collective-permute-start | bytes 393224 | tf_op jit(solution)/shard_map/ppermute | solution.py:364
  21.7 24.8 %collective-permute-start.4 = (bf16[4,2,64,128]{3,2,1,0:T(8,128)(2,1)S(1)}, bf16[4,2,64,128]{3,2,1,0:T(8,128)(2,1)S(1)}, u32[]{:S(2)}, u32[]{:S(2)}) collective-permute-start(bf16[4,2,64,128]{3,2,1,0:T(8,128)(2,1)S(1)} %get-tuple-element.54), channel_id=1, source_target_pairs={{0,4},{1,5},{2,6},{3,7},{4,0},{5,1},{6,2},{7,3},{8,12},{9,13},{10,... | collective-permute-start | bytes 393224 | tf_op jit(solution)/shard_map/ppermute | solution.py:364
  23.2 23.3 %collective-permute-start.5 = (bf16[4,2,64,128]{3,2,1,0:T(8,128)(2,1)S(1)}, bf16[4,2,64,128]{3,2,1,0:T(8,128)(2,1)S(1)}, u32[]{:S(2)}, u32[]{:S(2)}) collective-permute-start(bf16[4,2,64,128]{3,2,1,0:T(8,128)(2,1)S(1)} %get-tuple-element.55), channel_id=1, source_target_pairs={{0,6},{1,7},{2,4},{3,5},{4,2},{5,3},{6,0},{7,1},{8,14},{9,15},{10,... | collective-permute-start | bytes 393224 | tf_op jit(solution)/shard_map/ppermute | solution.py:364
  46.4 0.6 copy-start.9
  47.1 23.6 %collective-permute-start.6 = (bf16[4,4,64,128]{3,2,1,0:T(8,128)(2,1)S(1)}, bf16[4,4,64,128]{3,2,1,0:T(8,128)(2,1)S(1)}, u32[]{:S(2)}, u32[]{:S(2)}) collective-permute-start(bf16[4,4,64,128]{3,2,1,0:T(8,128)(2,1)S(1)} %get-tuple-element.64), channel_id=1, source_target_pairs={{0,1},{1,0},{2,3},{3,2},{4,5},{5,4},{6,7},{7,6},{8,9},{9,8},{10,11... | collective-permute-start | bytes 786440 | tf_op jit(solution)/shard_map/ppermute | solution.py:364
  60.4 1.2 copy-start
  61.6 9.2 %collective-permute-start.7 = (bf16[8,48,128]{2,1,0:T(8,128)(2,1)}, bf16[8,48,128]{2,1,0:T(8,128)(2,1)}, u32[]{:S(2)}, u32[]{:S(2)}) collective-permute-start(bf16[8,48,128]{2,1,0:T(8,128)(2,1)} %get-tuple-element.69), channel_id=1, source_target_pairs={{0,8},{1,9},{2,10},{3,11},{4,12},{5,13},{6,14},{7,15},{8,0},{9,1},... | collective-permute-start | bytes 294920 | tf_op jit(solution)/shard_map/ppermute | solution.py:364
  61.6 9.2 %collective-permute-start.8 = (bf16[8,48,128]{2,1,0:T(8,128)(2,1)S(1)}, bf16[8,48,128]{2,1,0:T(8,128)(2,1)}, u32[]{:S(2)}, u32[]{:S(2)}) collective-permute-start(bf16[8,48,128]{2,1,0:T(8,128)(2,1)S(1)} %get-tuple-element.70), channel_id=1, source_target_pairs={{0,16},{1,17},{2,18},{3,19},{4,20},{5,21},{6,22},{7,23},{8,24},{9,... | collective-permute-start | bytes 294920 | tf_op jit(solution)/shard_map/ppermute | solution.py:364
  64.1 7.7 %collective-permute-start.9 = (bf16[8,48,128]{2,1,0:T(8,128)(2,1)S(1)}, bf16[8,48,128]{2,1,0:T(8,128)(2,1)}, u32[]{:S(2)}, u32[]{:S(2)}) collective-permute-start(bf16[8,48,128]{2,1,0:T(8,128)(2,1)S(1)} %get-tuple-element.71), channel_id=1, source_target_pairs={{0,24},{1,25},{2,26},{3,27},{4,28},{5,29},{6,30},{7,31},{8,16},{9,... | collective-permute-start | bytes 294920 | tf_op jit(solution)/shard_map/ppermute | solution.py:364
  66.0 57.7 %all-to-all-start.1 = ((bf16[32,240,128]{2,1,0:T(8,128)(2,1)}), bf16[32,240,128]{2,1,0:T(8,128)(2,1)S(1)}, u32[]{:S(2)}, u32[]{:S(2)}) async-start(bf16[32,240,128]{2,1,0:T(8,128)(2,1)} %get-tuple-element.81), calls=%async_computation.1 | async-start | bytes 3932160 | tf_op jit(solution)/shard_map/all_to_all | solution.py:557
  70.8 3.0 %copy-start.1 = (bf16[32,224,128]{2,1,0:T(8,128)(2,1)S(1)}, bf16[32,224,128]{2,1,0:T(8,128)(2,1)}, u32[]{:S(2)}) copy-start(bf16[32,224,128]{2,1,0:T(8,128)(2,1)} %copy-done) | copy-start | bytes 5505028
  71.8 0.9 copy-start.10
  75.9 1.2 collective-permute-start.10
  77.1 6.9 %collective-permute-start.11 = (f32[8,128]{1,0:T(8,128)S(1)}, f32[8,128]{1,0:T(8,128)S(1)}, u32[]{:S(2)}, u32[]{:S(2)}) collective-permute-start(f32[8,128]{1,0:T(8,128)S(1)} %add.25), channel_id=1, source_target_pairs={{0,2},{1,3},{2,0},{3,1},{4,6},{5,7},{6,4},{7,5},{8,10},{9,11},{10,... | collective-permute-start | bytes 12296 | tf_op jit(solution)/shard_map/ppermute | solution.py:207
  79.1 7.7 %collective-permute-start.12 = (f32[8,128]{1,0:T(8,128)S(1)}, f32[8,128]{1,0:T(8,128)S(1)}, u32[]{:S(2)}, u32[]{:S(2)}) collective-permute-start(f32[8,128]{1,0:T(8,128)S(1)} %add.25), channel_id=1, source_target_pairs={{0,4},{1,5},{2,6},{3,7},{4,0},{5,1},{6,2},{7,3},{8,12},{9,13},{10,... | collective-permute-start | bytes 12296 | tf_op jit(solution)/shard_map/ppermute | solution.py:207
  80.5 6.3 %collective-permute-start.13 = (f32[8,128]{1,0:T(8,128)S(1)}, f32[8,128]{1,0:T(8,128)S(1)}, u32[]{:S(2)}, u32[]{:S(2)}) collective-permute-start(f32[8,128]{1,0:T(8,128)S(1)} %add.25), channel_id=1, source_target_pairs={{0,6},{1,7},{2,4},{3,5},{4,2},{5,3},{6,0},{7,1},{8,14},{9,15},{10,... | collective-permute-start | bytes 12296 | tf_op jit(solution)/shard_map/ppermute | solution.py:207
  80.6 9.3 %collective-permute-start.17 = (bf16[4,2,48,128]{3,2,1,0:T(8,128)(2,1)S(1)}, bf16[4,2,48,128]{3,2,1,0:T(8,128)(2,1)S(1)}, u32[]{:S(2)}, u32[]{:S(2)}) collective-permute-start(bf16[4,2,48,128]{3,2,1,0:T(8,128)(2,1)S(1)} %get-tuple-element.75), channel_id=1, source_target_pairs={{0,2},{1,3},{2,0},{3,1},{4,6},{5,7},{6,4},{7,5},{8,10},{9,11},{10,... | collective-permute-start | bytes 294920 | tf_op jit(solution)/shard_map/ppermute | solution.py:364
  82.6 15.5 %collective-permute-start.18 = (bf16[4,2,48,128]{3,2,1,0:T(8,128)(2,1)S(1)}, bf16[4,2,48,128]{3,2,1,0:T(8,128)(2,1)S(1)}, u32[]{:S(2)}, u32[]{:S(2)}) collective-permute-start(bf16[4,2,48,128]{3,2,1,0:T(8,128)(2,1)S(1)} %get-tuple-element.76), channel_id=1, source_target_pairs={{0,4},{1,5},{2,6},{3,7},{4,0},{5,1},{6,2},{7,3},{8,12},{9,13},{10,... | collective-permute-start | bytes 294920 | tf_op jit(solution)/shard_map/ppermute | solution.py:364
  84.0 14.1 %collective-permute-start.19 = (bf16[4,2,48,128]{3,2,1,0:T(8,128)(2,1)S(1)}, bf16[4,2,48,128]{3,2,1,0:T(8,128)(2,1)S(1)}, u32[]{:S(2)}, u32[]{:S(2)}) collective-permute-start(bf16[4,2,48,128]{3,2,1,0:T(8,128)(2,1)S(1)} %get-tuple-element.77), channel_id=1, source_target_pairs={{0,6},{1,7},{2,4},{3,5},{4,2},{5,3},{6,0},{7,1},{8,14},{9,15},{10,... | collective-permute-start | bytes 294920 | tf_op jit(solution)/shard_map/ppermute | solution.py:364
  86.8 16.5 %collective-permute-start.14 = (f32[8,128]{1,0:T(8,128)S(1)}, f32[8,128]{1,0:T(8,128)S(1)}, u32[]{:S(2)}, u32[]{:S(2)}) collective-permute-start(f32[8,128]{1,0:T(8,128)S(1)} %add_add_fusion.1), channel_id=1, source_target_pairs={{0,8},{1,9},{2,10},{3,11},{4,12},{5,13},{6,14},{7,15},{8,0},{9,1},... | collective-permute-start | bytes 12296 | tf_op jit(solution)/shard_map/ppermute | solution.py:207
  87.4 29.4 %collective-permute-start.15 = (f32[8,128]{1,0:T(8,128)S(1)}, f32[8,128]{1,0:T(8,128)S(1)}, u32[]{:S(2)}, u32[]{:S(2)}) collective-permute-start(f32[8,128]{1,0:T(8,128)S(1)} %add_add_fusion.1), channel_id=1, source_target_pairs={{0,16},{1,17},{2,18},{3,19},{4,20},{5,21},{6,22},{7,23},{8,24},{9,... | collective-permute-start | bytes 12296 | tf_op jit(solution)/shard_map/ppermute | solution.py:207
  89.9 26.9 %collective-permute-start.16 = (f32[8,128]{1,0:T(8,128)S(1)}, f32[8,128]{1,0:T(8,128)S(1)}, u32[]{:S(2)}, u32[]{:S(2)}) collective-permute-start(f32[8,128]{1,0:T(8,128)S(1)} %add_add_fusion.1), channel_id=1, source_target_pairs={{0,24},{1,25},{2,26},{3,27},{4,28},{5,29},{6,30},{7,31},{8,16},{9,... | collective-permute-start | bytes 12296 | tf_op jit(solution)/shard_map/ppermute | solution.py:207
  98.1 18.7 %collective-permute-start.20 = (bf16[4,4,48,128]{3,2,1,0:T(8,128)(2,1)S(1)}, bf16[4,4,48,128]{3,2,1,0:T(8,128)(2,1)S(1)}, u32[]{:S(2)}, u32[]{:S(2)}) collective-permute-start(bf16[4,4,48,128]{3,2,1,0:T(8,128)(2,1)S(1)} %get-tuple-element.79), channel_id=1, source_target_pairs={{0,1},{1,0},{2,3},{3,2},{4,5},{5,4},{6,7},{7,6},{8,9},{9,8},{10,11... | collective-permute-start | bytes 589832 | tf_op jit(solution)/shard_map/ppermute | solution.py:364
  118.6 0.7 copy-start.7
  119.3 13.6 %collective-permute-start.21 = (bf16[8,96,128]{2,1,0:T(8,128)(2,1)}, bf16[8,96,128]{2,1,0:T(8,128)(2,1)S(1)}, u32[]{:S(2)}, u32[]{:S(2)}) collective-permute-start(bf16[8,96,128]{2,1,0:T(8,128)(2,1)} %get-tuple-element.83), channel_id=1, source_target_pairs={{0,8},{1,9},{2,10},{3,11},{4,12},{5,13},{6,14},{7,15},{8,0},{9,1},... | collective-permute-start | bytes 589832 | tf_op jit(solution)/shard_map/ppermute | solution.py:364
  119.9 17.5 %collective-permute-start.22 = (bf16[8,96,128]{2,1,0:T(8,128)(2,1)}, bf16[8,96,128]{2,1,0:T(8,128)(2,1)}, u32[]{:S(2)}, u32[]{:S(2)}) collective-permute-start(bf16[8,96,128]{2,1,0:T(8,128)(2,1)} %get-tuple-element.84), channel_id=1, source_target_pairs={{0,16},{1,17},{2,18},{3,19},{4,20},{5,21},{6,22},{7,23},{8,24},{9,... | collective-permute-start | bytes 589832 | tf_op jit(solution)/shard_map/ppermute | solution.py:364
  121.5 15.9 %collective-permute-start.23 = (bf16[8,96,128]{2,1,0:T(8,128)(2,1)S(1)}, bf16[8,96,128]{2,1,0:T(8,128)(2,1)}, u32[]{:S(2)}, u32[]{:S(2)}) collective-permute-start(bf16[8,96,128]{2,1,0:T(8,128)(2,1)S(1)} %get-tuple-element.85), channel_id=1, source_target_pairs={{0,24},{1,25},{2,26},{3,27},{4,28},{5,29},{6,30},{7,31},{8,16},{9,... | collective-permute-start | bytes 589832 | tf_op jit(solution)/shard_map/ppermute | solution.py:364
  123.7 1.5 copy-start.2
  128.8 8.6 %copy-start.8 = (bf16[8,96,128]{2,1,0:T(8,128)(2,1)S(1)}, bf16[8,96,128]{2,1,0:T(8,128)(2,1)}, u32[]{:S(2)}) copy-start(bf16[8,96,128]{2,1,0:T(8,128)(2,1)} %copy-done.7) | copy-start | bytes 589828
  128.8 95.6 %all-to-all-start.2 = ((bf16[32,480,128]{2,1,0:T(8,128)(2,1)}), bf16[32,480,128]{2,1,0:T(8,128)(2,1)}, u32[]{:S(2)}, u32[]{:S(2)}) async-start(bf16[32,480,128]{2,1,0:T(8,128)(2,1)} %mix_main.1), calls=%async_computation.2 | async-start | bytes 7864320 | tf_op jit(solution)/shard_map/all_to_all | solution.py:557
  138.4 23.6 %collective-permute-start.24 = (bf16[4,2,96,128]{3,2,1,0:T(8,128)(2,1)S(1)}, bf16[4,2,96,128]{3,2,1,0:T(8,128)(2,1)S(1)}, u32[]{:S(2)}, u32[]{:S(2)}) collective-permute-start(bf16[4,2,96,128]{3,2,1,0:T(8,128)(2,1)S(1)} %get-tuple-element.87), channel_id=1, source_target_pairs={{0,2},{1,3},{2,0},{3,1},{4,6},{5,7},{6,4},{7,5},{8,10},{9,11},{10,... | collective-permute-start | bytes 589832 | tf_op jit(solution)/shard_map/ppermute | solution.py:364
  139.9 28.3 %collective-permute-start.25 = (bf16[4,2,96,128]{3,2,1,0:T(8,128)(2,1)S(1)}, bf16[4,2,96,128]{3,2,1,0:T(8,128)(2,1)S(1)}, u32[]{:S(2)}, u32[]{:S(2)}) collective-permute-start(bf16[4,2,96,128]{3,2,1,0:T(8,128)(2,1)S(1)} %get-tuple-element.88), channel_id=1, source_target_pairs={{0,4},{1,5},{2,6},{3,7},{4,0},{5,1},{6,2},{7,3},{8,12},{9,13},{10,... | collective-permute-start | bytes 589832 | tf_op jit(solution)/shard_map/ppermute | solution.py:364
  141.4 41.8 %collective-permute-start.26 = (bf16[4,2,96,128]{3,2,1,0:T(8,128)(2,1)S(1)}, bf16[4,2,96,128]{3,2,1,0:T(8,128)(2,1)S(1)}, u32[]{:S(2)}, u32[]{:S(2)}) collective-permute-start(bf16[4,2,96,128]{3,2,1,0:T(8,128)(2,1)S(1)} %get-tuple-element.89), channel_id=1, source_target_pairs={{0,6},{1,7},{2,4},{3,5},{4,2},{5,3},{6,0},{7,1},{8,14},{9,15},{10,... | collective-permute-start | bytes 589832 | tf_op jit(solution)/shard_map/ppermute | solution.py:364
  183.3 1.8 collective-permute-start.27

commit v16 on v15

--- a/solution.py
+++ b/solution.py
@@ -22,10 +22,8 @@
 SIDE = 2 * EDGE
 GROUPS = range(D // LANES)
 ROWS = SIDE * len(GROUPS)
-MAIN = ROWS - EDGE
-REST = ROWS - MAIN
-PMAIN = MAIN - TILE
-PREST = ROWS - PMAIN
+REST = EDGE + TILE
+MAIN = ROWS - REST
 PLANES = 4
 PLANE = BLOCKS // PLANES
 LONG = 10**11
@@ -37,16 +35,21 @@
 
 def dot(a, b, dims):
     return lax.dot_general(a, b, (dims, ((), ())), preferred_element_type=jnp.float32)
+
+
+def in_main(at):
+    return max(0, min(EDGE, MAIN - at))
 
 
 def put(main, side, block, row, value):
     for g in GROUPS:
         at = g * SIDE + row
         part = value[:, g * LANES : (g + 1) * LANES]
-        if at >= MAIN:
-            side[block, at - MAIN : at - MAIN + EDGE, :] = part
-        else:
-            main[block, at : at + EDGE, :] = part
+        n = in_main(at)
+        if n:
+            main[block, at : at + n, :] = part[:n]
+        if n < EDGE:
+            side[block, at + n - MAIN : at + EDGE - MAIN, :] = part[n:]
 
 
 def by_plane(me, side, outs):
@@ -248,7 +251,7 @@
     mixing[...] = mixer
     at = range(0, REST, TILE)
     got = jnp.concatenate([rows_of(scores, None, r) for r in at], axis=1)
-    own = jnp.concatenate([rows_of(params, None, PREST - REST + r) for r in at], axis=1)
+    own = jnp.concatenate([rows_of(params, None, r) for r in at], axis=1)
     both = mix(mixer, ksum, got, own)
     for q in range(2 * len(at)):
         part = both[:, q * LANES : (q + 1) * LANES].reshape(members, TILE, LANES)
@@ -422,13 +425,13 @@
         copy.start()
     for copy in copies:
         copy.wait()
-    more = PREST - EDGE
+    more = REST - EDGE
     for k in range(BLOCKS):
         b = k ^ me[0]
         here = pl.ds(pl.multiple_of(b // COLS * EDGE + EDGE - more, TILE), more)
         outs[k // PLANE][k % PLANE, 0:more, :] = wide[b % COLS, here, :]
         here = pl.ds(pl.multiple_of(b * EDGE, EDGE), EDGE)
-        outs[k // PLANE][k % PLANE, more:PREST, :] = tall[here, :]
+        outs[k // PLANE][k % PLANE, more:REST, :] = tall[here, :]
 
 
 def pack_main_kernel(first, second, out, wide, tall, packed, loads, stores):
@@ -455,11 +458,11 @@
         for c in range(COLS):
             for g in GROUPS:
                 b, at, lanes = d * COLS + c, g * SIDE, g * LANES
-                end = min(EDGE, PMAIN - at)
+                end = in_main(at)
                 packed[b, at : at + end, :] = wide[
                     d, 0:end, c * D + lanes : c * D + lanes + LANES
                 ]
-                if at + EDGE < PMAIN:
+                if at + EDGE < MAIN:
                     packed[b, at + EDGE : at + SIDE, :] = tall[
                         d, c * EDGE : (c + 1) * EDGE, lanes : lanes + LANES
                     ]
@@ -475,7 +478,7 @@
     cost = pl.CostEstimate(flops=0, bytes_accessed=4 * D * FF, transcendentals=0)
     side = pl.pallas_call(
         pack_side_kernel,
-        out_shape=side_shapes(PREST),
+        out_shape=side_shapes(REST),
         in_specs=[pl.BlockSpec(memory_space=pltpu.SMEM)] + anywhere * 2,
         scratch_shapes=[
             pltpu.VMEM((COLS, D, LANES), bf),
@@ -488,13 +491,13 @@
     )(me, first, second)
     main = pl.pallas_call(
         pack_main_kernel,
-        out_shape=pltpu.HBM((BLOCKS, PMAIN, LANES), bf),
+        out_shape=pltpu.HBM((BLOCKS, MAIN, LANES), bf),
         in_specs=anywhere * 2,
         out_specs=anywhere[0],
         scratch_shapes=[
             pltpu.VMEM((STEPS, EDGE, FF), bf),
             pltpu.VMEM((STEPS, TALL, D), bf),
-            pltpu.VMEM((BLOCKS, PMAIN, LANES), bf),
+            pltpu.VMEM((BLOCKS, MAIN, LANES), bf),
             pltpu.SemaphoreType.DMA((2, STEPS)),
             pltpu.SemaphoreType.DMA((STEPS,)),
         ],
@@ -503,6 +506,12 @@
         name="pack_main",
     )(first, second)
     return main, side
+
+
+def pieces(main, side, which, at):
+    n = in_main(at)
+    found = [(0, n, main, which * MAIN + at), (n, EDGE - n, side, which * REST + at + n - MAIN)]
+    return [piece for piece in found if piece[1]]
 
 
 def unpack_kernel(main, side, first_a, second_a, first_s, second_s, wide, tall, stores):
@@ -521,12 +530,14 @@
         for d in range(STEPS):
             for c in range(COLS):
                 for g in GROUPS:
-                    b, at = d * COLS + c, which * MAIN + g * SIDE
+                    b = d * COLS + c
                     lanes = slice(c * D + g * LANES, c * D + (g + 1) * LANES)
-                    wide[which, d, :, lanes] = main[b, at : at + EDGE, :]
-                    ref, at = (main, at + EDGE) if g * SIDE + EDGE < MAIN else (side, which * REST)
+                    for row, n, ref, at in pieces(main, side, which, g * SIDE):
+                        wide[which, d, row : row + n, lanes] = ref[b, at : at + n, :]
                     lanes = slice(g * LANES, (g + 1) * LANES)
-                    tall[which, d, c * EDGE : (c + 1) * EDGE, lanes] = ref[b, at : at + EDGE, :]
+                    for row, n, ref, at in pieces(main, side, which, g * SIDE + EDGE):
+                        here = slice(c * EDGE + row, c * EDGE + row + n)
+                        tall[which, d, here, lanes] = ref[b, at : at + n, :]
             for copy in store(which, d):
                 copy.start()
     for which in range(2):
@@ -548,7 +559,7 @@
             pltpu.SemaphoreType.DMA((2, 2, STEPS)),
         ],
         compiler_params=pltpu.CompilerParams(vmem_limit_bytes=24 * 1024 * 1024),
-        cost_estimate=pl.CostEstimate(flops=0, bytes_accessed=LONG // 100, transcendentals=0),
+        cost_estimate=pl.CostEstimate(flops=0, bytes_accessed=16 * D * FF, transcendentals=0),
         name="unpack",
     )(main, side)
 

time: 230 us -> 229 us (level)
  local copies, waits for them, and re-layouts: 7.39 us -> 3.22 us
    ppermute x7, waiting for transfers between devices: 19.8 us -> 11.8 us  [add_over(): lax.ppermute(value, AXES, [(i, i ^ bit) for i in range(members)])]
    ppermute x21, waiting for transfers between devices: 48.5 us -> 53.7 us  [swap(): return lax.ppermute(value, AXES, pairs)]
    all_to_all x3, waiting for transfers between devices: 52.6 us -> 57.7 us  [exchange(): return lax.all_to_all(blocks, AXES, split_axis=0, concat_axis=0, tiled=True)]
    unnamed x26 -> x16, local copies, waits for them, and re-layouts: 7.39 us -> 3.22 us
  transfers between devices with their start and end apart: 31 -> 31, of which waited for: 11 -> 13; matrix products, arithmetic and copies ran while one was open for 1% -> 1% of each run, Pallas kernels for 15% -> 16%
where the time goes in v16:
time: 229 us
  waiting for transfers between devices  123 us (54%)
  starting transfers between devices  57.7 us (25%)
  Pallas kernels  42.9 us (19%)
  local copies, waits for them, and re-layouts  3.22 us (1%)
    all_to_all x3, waiting for transfers between devices, exchange(): return lax.all_to_all(blocks, AXES, split_axis=0, concat_axis=0, tiled=True)  57.7 us
    ppermute x21, waiting for transfers between devices, swap(): return lax.ppermute(value, AXES, pairs)  53.7 us
    ppermute x21, starting transfers between devices, swap(): return lax.ppermute(value, AXES, pairs)  29.3 us
    pallas_call x1, Pallas kernels, particle_scores(): pl.pallas_call(functools.partial(score_kernel, DATA / count), out_shape=(...  22.9 us
    all_to_all x3, starting transfers between devices, exchange(): return lax.all_to_all(blocks, AXES, split_axis=0, concat_axis=0, tiled=True)  15 us
    ppermute x7, starting transfers between devices, add_over(): lax.ppermute(value, AXES, [(i, i ^ bit) for i in range(members)])  13.4 us
    ppermute x7, waiting for transfers between devices, add_over(): lax.ppermute(value, AXES, [(i, i ^ bit) for i in range(members)])  11.8 us
    pallas_call x1, Pallas kernels, mix_main(): pl.pallas_call(mix_main_kernel, out_shape=pltpu.HBM((members, 2 * MAIN, L...  5.05 us
  transfers between devices with their start and end apart: 31, of which 13 were waited for; matrix products, arithmetic and copies ran while one was open for 1% of the time, Pallas kernels for 16%

profile of v16, /device:TPU:0, one launch (start us, length us, event | category | flops | bytes accessed | tf_op | source)
XLA Modules:
  0.0 228.7 jit_solution(11468106966209529256)
XLA Ops:
  0.6 2.2 pack_side.1
  2.9 3.1 %collective-permute-start = (bf16[8,64,128]{2,1,0:T(8,128)(2,1)}, bf16[8,64,128]{2,1,0:T(8,128)(2,1)S(1)}, u32[]{:S(2)}, u32[]{:S(2)}) collective-permute-start(bf16[8,64,128]{2,1,0:T(8,128)(2,1)} %get-tuple-element.49), channel_id=1, source_target_pairs={{0,8},{1,9},{2,10},{3,11},{4,12},{5,13},{6,14},{7,15},{8,0},{9,1},... | collective-permute-start | bytes 393224 | tf_op jit(solution)/shard_map/ppermute | solution.py:367
  5.9 2.6 %collective-permute-start.1 = (bf16[8,64,128]{2,1,0:T(8,128)(2,1)}, bf16[8,64,128]{2,1,0:T(8,128)(2,1)S(1)}, u32[]{:S(2)}, u32[]{:S(2)}) collective-permute-start(bf16[8,64,128]{2,1,0:T(8,128)(2,1)} %get-tuple-element.50), channel_id=1, source_target_pairs={{0,16},{1,17},{2,18},{3,19},{4,20},{5,21},{6,22},{7,23},{8,24},{9,... | collective-permute-start | bytes 393224 | tf_op jit(solution)/shard_map/ppermute | solution.py:367
  8.5 2.6 %pack_main.1 = bf16[32,224,128]{2,1,0:T(8,128)(2,1)} custom-call(bf16[1,384,1536]{2,1,0:T(8,128)(2,1)} %first.3, bf16[1,1536,384]{2,1,0:T(8,128)(2,1)} %second.3), custom_call_target="tpu_custom_call" | custom-call | bytes 2359296 | tf_op jit(solution)/shard_map/pack_main/pallas_call | solution.py:492
  11.2 6.1 %all-to-all-start = ((bf16[32,224,128]{2,1,0:T(8,128)(2,1)}), bf16[32,224,128]{2,1,0:T(8,128)(2,1)S(1)}, u32[]{:S(2)}, u32[]{:S(2)}) async-start(bf16[32,224,128]{2,1,0:T(8,128)(2,1)} %pack_main.1), calls=%async_computation | async-start | bytes 3670016 | tf_op jit(solution)/shard_map/all_to_all | solution.py:568
  17.3 1.5 copy.10.image
  19.1 0.7 copy-done.2
  19.9 1.8 collective-permute-start.3
  21.7 1.5 collective-permute-start.4
  23.4 22.9 %score.1 = (bf16[32,224,128]{2,1,0:T(8,128)(2,1)}, bf16[8,64,128]{2,1,0:T(8,128)(2,1)S(1)}, bf16[8,64,128]{2,1,0:T(8,128)(2,1)S(1)}, bf16[8,64,128]{2,1,0:T(8,128)(2,1)S(1)}, bf16[8,64,128]{2,1,0:T(8,128)(2,1)S(1)}) custom-call(s32[8]{0:T(128)S(1)} %bitcast.6, s32[1]{0:T(128)} %bitcast.me, bf16[8,197,384]{2,1,0:T(8,128)(2,1)S(1)} %copy.10.image, ...), custom_call_target="tpu_custom_call" | custom-call | flops 9814671360 | bytes 7139328 | tf_op jit(solution)/shard_map/score/pallas_call | solution.py:134
  46.4 14.0 %all-to-all-done.main.params = bf16[32,224,128]{2,1,0:T(8,128)(2,1)S(1)} async-done(((bf16[32,224,128]{2,1,0:T(8,128)(2,1)}), bf16[32,224,128]{2,1,0:T(8,128)(2,1)S(1)}, u32[]{:S(2)}, u32[]{:S(2)}) %all-to-all-start) | async-done | bytes 1835040 | tf_op jit(solution)/shard_map/all_to_all | solution.py:568
  60.4 2.5 %collective-permute-start.8 = (bf16[8,64,128]{2,1,0:T(8,128)(2,1)S(1)}, bf16[8,64,128]{2,1,0:T(8,128)(2,1)S(1)}, u32[]{:S(2)}, u32[]{:S(2)}) collective-permute-start(bf16[8,64,128]{2,1,0:T(8,128)(2,1)S(1)} %get-tuple-element.70), channel_id=1, source_target_pairs={{0,16},{1,17},{2,18},{3,19},{4,20},{5,21},{6,22},{7,23},{8,24},{9,... | collective-permute-start | bytes 393224 | tf_op jit(solution)/shard_map/ppermute | solution.py:367
  62.9 1.9 collective-permute-start.9
  64.8 4.8 %all-to-all-start.1 = ((bf16[32,224,128]{2,1,0:T(8,128)(2,1)}), bf16[32,224,128]{2,1,0:T(8,128)(2,1)}, u32[]{:S(2)}, u32[]{:S(2)}) async-start(bf16[32,224,128]{2,1,0:T(8,128)(2,1)} %get-tuple-element.81), calls=%async_computation.1 | async-start | bytes 3670016 | tf_op jit(solution)/shard_map/all_to_all | solution.py:568
  69.8 3.4 %collective-permute-done.8.refs_2_ = bf16[8,64,128]{2,1,0:T(8,128)(2,1)S(1)} collective-permute-done((bf16[8,64,128]{2,1,0:T(8,128)(2,1)S(1)}, bf16[8,64,128]{2,1,0:T(8,128)(2,1)S(1)}, u32[]{:S(2)}, u32[]{:S(2)}) %collective-permute-start.8) | collective-permute-done | bytes 131104 | tf_op jit(solution)/shard_map/ppermute | solution.py:367
  73.2 1.5 collective-permute-start.17
  74.7 1.7 collective-permute-start.18
  76.4 0.4 collective-permute-start.19
  76.8 2.2 gram.1
  79.0 1.2 collective-permute-done.10
  80.2 1.4 collective-permute-start.11
  81.6 1.7 collective-permute-start.12
  83.3 2.1 collective-permute-done.17.refs_1_
  85.3 1.9 collective-permute-start.13
  87.2 0.4 collective-permute-done.18.refs_2_
  87.6 7.6 %collective-permute-done.19.refs_3_ = bf16[4,2,64,128]{3,2,1,0:T(8,128)(2,1)S(1)} collective-permute-done((bf16[4,2,64,128]{3,2,1,0:T(8,128)(2,1)S(1)}, bf16[4,2,64,128]{3,2,1,0:T(8,128)(2,1)S(1)}, u32[]{:S(2)}, u32[]{:S(2)}) %collective-permute-start.19) | collective-permute-done | bytes 131104 | tf_op jit(solution)/shard_map/ppermute | solution.py:367
  95.4 6.0 %collective-permute-start.14 = (f32[8,128]{1,0:T(8,128)S(1)}, f32[8,128]{1,0:T(8,128)S(1)}, u32[]{:S(2)}, u32[]{:S(2)}) collective-permute-start(f32[8,128]{1,0:T(8,128)S(1)} %add_add_fusion.1), channel_id=1, source_target_pairs={{0,8},{1,9},{2,10},{3,11},{4,12},{5,13},{6,14},{7,15},{8,0},{9,1},... | collective-permute-start | bytes 12296 | tf_op jit(solution)/shard_map/ppermute | solution.py:210
  101.3 0.6 collective-permute-start.15
  101.9 1.9 collective-permute-start.16
  104.4 10.6 %collective-permute-done.15 = f32[8,128]{1,0:T(8,128)S(1)} collective-permute-done((f32[8,128]{1,0:T(8,128)S(1)}, f32[8,128]{1,0:T(8,128)S(1)}, u32[]{:S(2)}, u32[]{:S(2)}) %collective-permute-start.15) | collective-permute-done | bytes 4128 | tf_op jit(solution)/shard_map/ppermute | solution.py:210
  115.1 1.9 mix_side.1
  117.0 0.7 copy-done.4
  117.7 0.5 collective-permute-start.21
  118.3 2.2 collective-permute-start.22
  120.5 1.6 collective-permute-start.23
  122.1 5.0 %mix_main.1 = bf16[32,448,128]{2,1,0:T(8,128)(2,1)} custom-call(bf16[512,512]{1,0:T(8,128)(2,1)S(1)} %get-tuple-element.80.mixing, bf16[32,224,128]{2,1,0:T(8,128)(2,1)} %all-to-all-done.1.scores, bf16[32,224,128]{2,1,0:T(8,128)(2,1)S(1)} %all-to-all-done.main.params, bf16[32,64,128]{2,1,0:T(8,128)(2,1)S(1)} %settle.3.side.params.side_params), custom_call_target="tpu_custom_call" | custom-call | flops 1879048192 | bytes 7340032 | tf_op jit(solution)/shard_map/mix_main/pallas_call | solution.py:313
  127.2 4.1 %all-to-all-start.2 = ((bf16[32,448,128]{2,1,0:T(8,128)(2,1)}), bf16[32,448,128]{2,1,0:T(8,128)(2,1)}, u32[]{:S(2)}, u32[]{:S(2)}) async-start(bf16[32,448,128]{2,1,0:T(8,128)(2,1)} %mix_main.1), calls=%async_computation.2 | async-start | bytes 7340032 | tf_op jit(solution)/shard_map/all_to_all | solution.py:568
  131.3 8.6 %collective-permute-done.22.refs_2_ = bf16[8,128,128]{2,1,0:T(8,128)(2,1)} collective-permute-done((bf16[8,128,128]{2,1,0:T(8,128)(2,1)}, bf16[8,128,128]{2,1,0:T(8,128)(2,1)}, u32[]{:S(2)}, u32[]{:S(2)}) %collective-permute-start.22) | collective-permute-done | bytes 262176 | tf_op jit(solution)/shard_map/ppermute | solution.py:367
  140.0 1.1 plane.5
  141.1 5.3 %collective-permute-start.24 = (bf16[4,2,128,128]{3,2,1,0:T(8,128)(2,1)S(1)}, bf16[4,2,128,128]{3,2,1,0:T(8,128)(2,1)S(1)}, u32[]{:S(2)}, u32[]{:S(2)}) collective-permute-start(bf16[4,2,128,128]{3,2,1,0:T(8,128)(2,1)S(1)} %get-tuple-element.87), channel_id=1, source_target_pairs={{0,2},{1,3},{2,0},{3,1},{4,6},{5,7},{6,4},{7,5},{8,10},{9,11},{10,... | collective-permute-start | bytes 786440 | tf_op jit(solution)/shard_map/ppermute | solution.py:367
  146.4 2.0 collective-permute-start.25
  148.3 0.3 collective-permute-start.26
  148.6 9.8 %collective-permute-done.24.refs_1_ = bf16[4,2,128,128]{3,2,1,0:T(8,128)(2,1)S(1)} collective-permute-done((bf16[4,2,128,128]{3,2,1,0:T(8,128)(2,1)S(1)}, bf16[4,2,128,128]{3,2,1,0:T(8,128)(2,1)S(1)}, u32[]{:S(2)}, u32[]{:S(2)}) %collective-permute-start.24) | collective-permute-done | bytes 262176 | tf_op jit(solution)/shard_map/ppermute | solution.py:367
  158.4 6.4 %collective-permute-done.25.refs_2_ = bf16[4,2,128,128]{3,2,1,0:T(8,128)(2,1)S(1)} collective-permute-done((bf16[4,2,128,128]{3,2,1,0:T(8,128)(2,1)S(1)}, bf16[4,2,128,128]{3,2,1,0:T(8,128)(2,1)S(1)}, u32[]{:S(2)}, u32[]{:S(2)}) %collective-permute-start.25) | collective-permute-done | bytes 262176 | tf_op jit(solution)/shard_map/ppermute | solution.py:367
  164.8 13.4 %collective-permute-done.26.refs_3_ = bf16[4,2,128,128]{3,2,1,0:T(8,128)(2,1)S(1)} collective-permute-done((bf16[4,2,128,128]{3,2,1,0:T(8,128)(2,1)S(1)}, bf16[4,2,128,128]{3,2,1,0:T(8,128)(2,1)S(1)}, u32[]{:S(2)}, u32[]{:S(2)}) %collective-permute-start.26) | collective-permute-done | bytes 262176 | tf_op jit(solution)/shard_map/ppermute | solution.py:367
  178.4 1.9 collective-permute-done.27.far
  180.4 43.6 %all-to-all-done.2.main = bf16[32,448,128]{2,1,0:T(8,128)(2,1)} async-done(((bf16[32,448,128]{2,1,0:T(8,128)(2,1)}), bf16[32,448,128]{2,1,0:T(8,128)(2,1)}, u32[]{:S(2)}, u32[]{:S(2)}) %all-to-all-start.2) | async-done | bytes 3670048 | tf_op jit(solution)/shard_map/all_to_all | solution.py:568
  224.0 4.5 %unpack.1 = (bf16[1,384,1536]{2,1,0:T(8,128)(2,1)}, bf16[1,1536,384]{2,1,0:T(8,128)(2,1)}, bf16[1,384,1536]{2,1,0:T(8,128)(2,1)}, bf16[1,1536,384]{2,1,0:T(8,128)(2,1)}) custom-call(bf16[32,448,128]{2,1,0:T(8,128)(2,1)} %all-to-all-done.2.main, bf16[32,128,128]{2,1,0:T(8,128)(2,1)S(1)} %settle.5.side), custom_call_target="tpu_custom_call" | custom-call | bytes 9437184 | tf_op jit(solution)/shard_map/unpack/pallas_call | solution.py:551
  (49 shorter events, 1.2 us)
Async XLA Ops:
  2.9 16.2 %collective-permute-start = (bf16[8,64,128]{2,1,0:T(8,128)(2,1)}, bf16[8,64,128]{2,1,0:T(8,128)(2,1)S(1)}, u32[]{:S(2)}, u32[]{:S(2)}) collective-permute-start(bf16[8,64,128]{2,1,0:T(8,128)(2,1)} %get-tuple-element.49), channel_id=1, source_target_pairs={{0,8},{1,9},{2,10},{3,11},{4,12},{5,13},{6,14},{7,15},{8,0},{9,1},... | collective-permute-start | bytes 393224 | tf_op jit(solution)/shard_map/ppermute | solution.py:367
  5.9 13.1 %collective-permute-start.1 = (bf16[8,64,128]{2,1,0:T(8,128)(2,1)}, bf16[8,64,128]{2,1,0:T(8,128)(2,1)S(1)}, u32[]{:S(2)}, u32[]{:S(2)}) collective-permute-start(bf16[8,64,128]{2,1,0:T(8,128)(2,1)} %get-tuple-element.50), channel_id=1, source_target_pairs={{0,16},{1,17},{2,18},{3,19},{4,20},{5,21},{6,22},{7,23},{8,24},{9,... | collective-permute-start | bytes 393224 | tf_op jit(solution)/shard_map/ppermute | solution.py:367
  8.5 10.6 %collective-permute-start.2 = (bf16[8,64,128]{2,1,0:T(8,128)(2,1)}, bf16[8,64,128]{2,1,0:T(8,128)(2,1)S(1)}, u32[]{:S(2)}, u32[]{:S(2)}) collective-permute-start(bf16[8,64,128]{2,1,0:T(8,128)(2,1)} %get-tuple-element.51), channel_id=1, source_target_pairs={{0,24},{1,25},{2,26},{3,27},{4,28},{5,29},{6,30},{7,31},{8,16},{9,... | collective-permute-start | bytes 393224 | tf_op jit(solution)/shard_map/ppermute | solution.py:367
  11.2 49.2 %all-to-all-start = ((bf16[32,224,128]{2,1,0:T(8,128)(2,1)}), bf16[32,224,128]{2,1,0:T(8,128)(2,1)S(1)}, u32[]{:S(2)}, u32[]{:S(2)}) async-start(bf16[32,224,128]{2,1,0:T(8,128)(2,1)} %pack_main.1), calls=%async_computation | async-start | bytes 3670016 | tf_op jit(solution)/shard_map/all_to_all | solution.py:568
  17.3 1.6 copy-start.6
  18.9 0.9 copy-start.2
  19.8 3.6 %copy-start = (bf16[1,384,1536]{2,1,0:T(8,128)(2,1)S(1)}, bf16[1,384,1536]{2,1,0:T(8,128)(2,1)}, u32[]{:S(2)}) copy-start(bf16[1,384,1536]{2,1,0:T(8,128)(2,1)} %first.3) | copy-start | bytes 3538948
  19.8 3.6 %copy-start.1 = (bf16[1,1536,384]{2,1,0:T(8,128)(2,1)S(1)}, bf16[1,1536,384]{2,1,0:T(8,128)(2,1)}, u32[]{:S(2)}) copy-start(bf16[1,1536,384]{2,1,0:T(8,128)(2,1)} %second.3) | copy-start | bytes 3538948
  19.8 3.6 %copy-start.3 = (s32[1,8]{1,0:T(1,128)S(1)}, s32[1,8]{1,0:T(1,128)}, u32[]{:S(2)}) copy-start(s32[1,8]{1,0:T(1,128)} %param.10) | copy-start | bytes 100
  19.9 43.0 %collective-permute-start.3 = (bf16[4,2,64,128]{3,2,1,0:T(8,128)(2,1)S(1)}, bf16[4,2,64,128]{3,2,1,0:T(8,128)(2,1)S(1)}, u32[]{:S(2)}, u32[]{:S(2)}) collective-permute-start(bf16[4,2,64,128]{3,2,1,0:T(8,128)(2,1)S(1)} %get-tuple-element.53), channel_id=1, source_target_pairs={{0,2},{1,3},{2,0},{3,1},{4,6},{5,7},{6,4},{7,5},{8,10},{9,11},{10,... | collective-permute-start | bytes 393224 | tf_op jit(solution)/shard_map/ppermute | solution.py:367
  21.7 47.9 %collective-permute-start.4 = (bf16[4,2,64,128]{3,2,1,0:T(8,128)(2,1)S(1)}, bf16[4,2,64,128]{3,2,1,0:T(8,128)(2,1)S(1)}, u32[]{:S(2)}, u32[]{:S(2)}) collective-permute-start(bf16[4,2,64,128]{3,2,1,0:T(8,128)(2,1)S(1)} %get-tuple-element.54), channel_id=1, source_target_pairs={{0,4},{1,5},{2,6},{3,7},{4,0},{5,1},{6,2},{7,3},{8,12},{9,13},{10,... | collective-permute-start | bytes 393224 | tf_op jit(solution)/shard_map/ppermute | solution.py:367
  23.2 46.5 %collective-permute-start.5 = (bf16[4,2,64,128]{3,2,1,0:T(8,128)(2,1)S(1)}, bf16[4,2,64,128]{3,2,1,0:T(8,128)(2,1)S(1)}, u32[]{:S(2)}, u32[]{:S(2)}) collective-permute-start(bf16[4,2,64,128]{3,2,1,0:T(8,128)(2,1)S(1)} %get-tuple-element.55), channel_id=1, source_target_pairs={{0,6},{1,7},{2,4},{3,5},{4,2},{5,3},{6,0},{7,1},{8,14},{9,15},{10,... | collective-permute-start | bytes 393224 | tf_op jit(solution)/shard_map/ppermute | solution.py:367
  60.4 9.4 %collective-permute-start.7 = (bf16[8,64,128]{2,1,0:T(8,128)(2,1)S(1)}, bf16[8,64,128]{2,1,0:T(8,128)(2,1)S(1)}, u32[]{:S(2)}, u32[]{:S(2)}) collective-permute-start(bf16[8,64,128]{2,1,0:T(8,128)(2,1)S(1)} %get-tuple-element.69), channel_id=1, source_target_pairs={{0,8},{1,9},{2,10},{3,11},{4,12},{5,13},{6,14},{7,15},{8,0},{9,1},... | collective-permute-start | bytes 393224 | tf_op jit(solution)/shard_map/ppermute | solution.py:367
  60.4 12.8 %collective-permute-start.8 = (bf16[8,64,128]{2,1,0:T(8,128)(2,1)S(1)}, bf16[8,64,128]{2,1,0:T(8,128)(2,1)S(1)}, u32[]{:S(2)}, u32[]{:S(2)}) collective-permute-start(bf16[8,64,128]{2,1,0:T(8,128)(2,1)S(1)} %get-tuple-element.70), channel_id=1, source_target_pairs={{0,16},{1,17},{2,18},{3,19},{4,20},{5,21},{6,22},{7,23},{8,24},{9,... | collective-permute-start | bytes 393224 | tf_op jit(solution)/shard_map/ppermute | solution.py:367
  62.9 10.3 %collective-permute-start.9 = (bf16[8,64,128]{2,1,0:T(8,128)(2,1)S(1)}, bf16[8,64,128]{2,1,0:T(8,128)(2,1)S(1)}, u32[]{:S(2)}, u32[]{:S(2)}) collective-permute-start(bf16[8,64,128]{2,1,0:T(8,128)(2,1)S(1)} %get-tuple-element.71), channel_id=1, source_target_pairs={{0,24},{1,25},{2,26},{3,27},{4,28},{5,29},{6,30},{7,31},{8,16},{9,... | collective-permute-start | bytes 393224 | tf_op jit(solution)/shard_map/ppermute | solution.py:367
  64.8 57.3 %all-to-all-start.1 = ((bf16[32,224,128]{2,1,0:T(8,128)(2,1)}), bf16[32,224,128]{2,1,0:T(8,128)(2,1)}, u32[]{:S(2)}, u32[]{:S(2)}) async-start(bf16[32,224,128]{2,1,0:T(8,128)(2,1)} %get-tuple-element.81), calls=%async_computation.1 | async-start | bytes 3670016 | tf_op jit(solution)/shard_map/all_to_all | solution.py:568
  69.7 7.1 %collective-permute-start.6 = (bf16[4,4,64,128]{3,2,1,0:T(8,128)(2,1)S(1)}, bf16[4,4,64,128]{3,2,1,0:T(8,128)(2,1)S(1)}, u32[]{:S(2)}, u32[]{:S(2)}) collective-permute-start(bf16[4,4,64,128]{3,2,1,0:T(8,128)(2,1)S(1)} %get-tuple-element.64), channel_id=1, source_target_pairs={{0,1},{1,0},{2,3},{3,2},{4,5},{5,4},{6,7},{7,6},{8,9},{9,8},{10,11... | collective-permute-start | bytes 786440 | tf_op jit(solution)/shard_map/ppermute | solution.py:367
  73.2 12.1 %collective-permute-start.17 = (bf16[4,2,64,128]{3,2,1,0:T(8,128)(2,1)S(1)}, bf16[4,2,64,128]{3,2,1,0:T(8,128)(2,1)S(1)}, u32[]{:S(2)}, u32[]{:S(2)}) collective-permute-start(bf16[4,2,64,128]{3,2,1,0:T(8,128)(2,1)S(1)} %get-tuple-element.75), channel_id=1, source_target_pairs={{0,2},{1,3},{2,0},{3,1},{4,6},{5,7},{6,4},{7,5},{8,10},{9,11},{10,... | collective-permute-start | bytes 393224 | tf_op jit(solution)/shard_map/ppermute | solution.py:367
  74.7 12.9 %collective-permute-start.18 = (bf16[4,2,64,128]{3,2,1,0:T(8,128)(2,1)S(1)}, bf16[4,2,64,128]{3,2,1,0:T(8,128)(2,1)S(1)}, u32[]{:S(2)}, u32[]{:S(2)}) collective-permute-start(bf16[4,2,64,128]{3,2,1,0:T(8,128)(2,1)S(1)} %get-tuple-element.76), channel_id=1, source_target_pairs={{0,4},{1,5},{2,6},{3,7},{4,0},{5,1},{6,2},{7,3},{8,12},{9,13},{10,... | collective-permute-start | bytes 393224 | tf_op jit(solution)/shard_map/ppermute | solution.py:367
  76.4 18.8 %collective-permute-start.19 = (bf16[4,2,64,128]{3,2,1,0:T(8,128)(2,1)S(1)}, bf16[4,2,64,128]{3,2,1,0:T(8,128)(2,1)S(1)}, u32[]{:S(2)}, u32[]{:S(2)}) collective-permute-start(bf16[4,2,64,128]{3,2,1,0:T(8,128)(2,1)S(1)} %get-tuple-element.77), channel_id=1, source_target_pairs={{0,6},{1,7},{2,4},{3,5},{4,2},{5,3},{6,0},{7,1},{8,14},{9,15},{10,... | collective-permute-start | bytes 393224 | tf_op jit(solution)/shard_map/ppermute | solution.py:367
  79.0 1.2 collective-permute-start.10
  80.2 15.1 %collective-permute-start.11 = (f32[8,128]{1,0:T(8,128)S(1)}, f32[8,128]{1,0:T(8,128)S(1)}, u32[]{:S(2)}, u32[]{:S(2)}) collective-permute-start(f32[8,128]{1,0:T(8,128)S(1)} %add.25), channel_id=1, source_target_pairs={{0,2},{1,3},{2,0},{3,1},{4,6},{5,7},{6,4},{7,5},{8,10},{9,11},{10,... | collective-permute-start | bytes 12296 | tf_op jit(solution)/shard_map/ppermute | solution.py:210
  81.6 13.7 %collective-permute-start.12 = (f32[8,128]{1,0:T(8,128)S(1)}, f32[8,128]{1,0:T(8,128)S(1)}, u32[]{:S(2)}, u32[]{:S(2)}) collective-permute-start(f32[8,128]{1,0:T(8,128)S(1)} %add.25), channel_id=1, source_target_pairs={{0,4},{1,5},{2,6},{3,7},{4,0},{5,1},{6,2},{7,3},{8,12},{9,13},{10,... | collective-permute-start | bytes 12296 | tf_op jit(solution)/shard_map/ppermute | solution.py:210
  85.3 10.0 %collective-permute-start.13 = (f32[8,128]{1,0:T(8,128)S(1)}, f32[8,128]{1,0:T(8,128)S(1)}, u32[]{:S(2)}, u32[]{:S(2)}) collective-permute-start(f32[8,128]{1,0:T(8,128)S(1)} %add.25), channel_id=1, source_target_pairs={{0,6},{1,7},{2,4},{3,5},{4,2},{5,3},{6,0},{7,1},{8,14},{9,15},{10,... | collective-permute-start | bytes 12296 | tf_op jit(solution)/shard_map/ppermute | solution.py:210
  95.2 19.8 %collective-permute-start.20 = (bf16[4,4,64,128]{3,2,1,0:T(8,128)(2,1)S(1)}, bf16[4,4,64,128]{3,2,1,0:T(8,128)(2,1)S(1)}, u32[]{:S(2)}, u32[]{:S(2)}) collective-permute-start(bf16[4,4,64,128]{3,2,1,0:T(8,128)(2,1)S(1)} %get-tuple-element.79), channel_id=1, source_target_pairs={{0,1},{1,0},{2,3},{3,2},{4,5},{5,4},{6,7},{7,6},{8,9},{9,8},{10,11... | collective-permute-start | bytes 786440 | tf_op jit(solution)/shard_map/ppermute | solution.py:367
  95.4 9.1 %collective-permute-start.14 = (f32[8,128]{1,0:T(8,128)S(1)}, f32[8,128]{1,0:T(8,128)S(1)}, u32[]{:S(2)}, u32[]{:S(2)}) collective-permute-start(f32[8,128]{1,0:T(8,128)S(1)} %add_add_fusion.1), channel_id=1, source_target_pairs={{0,8},{1,9},{2,10},{3,11},{4,12},{5,13},{6,14},{7,15},{8,0},{9,1},... | collective-permute-start | bytes 12296 | tf_op jit(solution)/shard_map/ppermute | solution.py:210
  101.3 13.7 %collective-permute-start.15 = (f32[8,128]{1,0:T(8,128)S(1)}, f32[8,128]{1,0:T(8,128)S(1)}, u32[]{:S(2)}, u32[]{:S(2)}) collective-permute-start(f32[8,128]{1,0:T(8,128)S(1)} %add_add_fusion.1), channel_id=1, source_target_pairs={{0,16},{1,17},{2,18},{3,19},{4,20},{5,21},{6,22},{7,23},{8,24},{9,... | collective-permute-start | bytes 12296 | tf_op jit(solution)/shard_map/ppermute | solution.py:210
  101.9 13.2 %collective-permute-start.16 = (f32[8,128]{1,0:T(8,128)S(1)}, f32[8,128]{1,0:T(8,128)S(1)}, u32[]{:S(2)}, u32[]{:S(2)}) collective-permute-start(f32[8,128]{1,0:T(8,128)S(1)} %add_add_fusion.1), channel_id=1, source_target_pairs={{0,24},{1,25},{2,26},{3,27},{4,28},{5,29},{6,30},{7,31},{8,16},{9,... | collective-permute-start | bytes 12296 | tf_op jit(solution)/shard_map/ppermute | solution.py:210
  117.0 0.7 copy-start.4
  117.7 13.6 %collective-permute-start.21 = (bf16[8,128,128]{2,1,0:T(8,128)(2,1)}, bf16[8,128,128]{2,1,0:T(8,128)(2,1)S(1)}, u32[]{:S(2)}, u32[]{:S(2)}) collective-permute-start(bf16[8,128,128]{2,1,0:T(8,128)(2,1)} %get-tuple-element.83), channel_id=1, source_target_pairs={{0,8},{1,9},{2,10},{3,11},{4,12},{5,13},{6,14},{7,15},{8,0},{9,1},... | collective-permute-start | bytes 786440 | tf_op jit(solution)/shard_map/ppermute | solution.py:367
  118.3 21.7 %collective-permute-start.22 = (bf16[8,128,128]{2,1,0:T(8,128)(2,1)}, bf16[8,128,128]{2,1,0:T(8,128)(2,1)}, u32[]{:S(2)}, u32[]{:S(2)}) collective-permute-start(bf16[8,128,128]{2,1,0:T(8,128)(2,1)} %get-tuple-element.84), channel_id=1, source_target_pairs={{0,16},{1,17},{2,18},{3,19},{4,20},{5,21},{6,22},{7,23},{8,24},{9,... | collective-permute-start | bytes 786440 | tf_op jit(solution)/shard_map/ppermute | solution.py:367
  120.5 19.5 %collective-permute-start.23 = (bf16[8,128,128]{2,1,0:T(8,128)(2,1)S(1)}, bf16[8,128,128]{2,1,0:T(8,128)(2,1)}, u32[]{:S(2)}, u32[]{:S(2)}) collective-permute-start(bf16[8,128,128]{2,1,0:T(8,128)(2,1)S(1)} %get-tuple-element.85), channel_id=1, source_target_pairs={{0,24},{1,25},{2,26},{3,27},{4,28},{5,29},{6,30},{7,31},{8,16},{9,... | collective-permute-start | bytes 786440 | tf_op jit(solution)/shard_map/ppermute | solution.py:367
  127.2 12.8 %copy-start.5 = (bf16[8,128,128]{2,1,0:T(8,128)(2,1)S(1)}, bf16[8,128,128]{2,1,0:T(8,128)(2,1)}, u32[]{:S(2)}) copy-start(bf16[8,128,128]{2,1,0:T(8,128)(2,1)} %copy-done.4) | copy-start | bytes 786436
  127.2 96.8 %all-to-all-start.2 = ((bf16[32,448,128]{2,1,0:T(8,128)(2,1)}), bf16[32,448,128]{2,1,0:T(8,128)(2,1)}, u32[]{:S(2)}, u32[]{:S(2)}) async-start(bf16[32,448,128]{2,1,0:T(8,128)(2,1)} %mix_main.1), calls=%async_computation.2 | async-start | bytes 7340032 | tf_op jit(solution)/shard_map/all_to_all | solution.py:568
  141.1 17.4 %collective-permute-start.24 = (bf16[4,2,128,128]{3,2,1,0:T(8,128)(2,1)S(1)}, bf16[4,2,128,128]{3,2,1,0:T(8,128)(2,1)S(1)}, u32[]{:S(2)}, u32[]{:S(2)}) collective-permute-start(bf16[4,2,128,128]{3,2,1,0:T(8,128)(2,1)S(1)} %get-tuple-element.87), channel_id=1, source_target_pairs={{0,2},{1,3},{2,0},{3,1},{4,6},{5,7},{6,4},{7,5},{8,10},{9,11},{10,... | collective-permute-start | bytes 786440 | tf_op jit(solution)/shard_map/ppermute | solution.py:367
  146.4 18.4 %collective-permute-start.25 = (bf16[4,2,128,128]{3,2,1,0:T(8,128)(2,1)S(1)}, bf16[4,2,128,128]{3,2,1,0:T(8,128)(2,1)S(1)}, u32[]{:S(2)}, u32[]{:S(2)}) collective-permute-start(bf16[4,2,128,128]{3,2,1,0:T(8,128)(2,1)S(1)} %get-tuple-element.88), channel_id=1, source_target_pairs={{0,4},{1,5},{2,6},{3,7},{4,0},{5,1},{6,2},{7,3},{8,12},{9,13},{10,... | collective-permute-start | bytes 786440 | tf_op jit(solution)/shard_map/ppermute | solution.py:367
  148.3 29.9 %collective-permute-start.26 = (bf16[4,2,128,128]{3,2,1,0:T(8,128)(2,1)S(1)}, bf16[4,2,128,128]{3,2,1,0:T(8,128)(2,1)S(1)}, u32[]{:S(2)}, u32[]{:S(2)}) collective-permute-start(bf16[4,2,128,128]{3,2,1,0:T(8,128)(2,1)S(1)} %get-tuple-element.89), channel_id=1, source_target_pairs={{0,6},{1,7},{2,4},{3,5},{4,2},{5,3},{6,0},{7,1},{8,14},{9,15},{10,... | collective-permute-start | bytes 786440 | tf_op jit(solution)/shard_map/ppermute | solution.py:367
  178.3 2.0 collective-permute-start.27

commit v17 on v16

--- a/solution.py
+++ b/solution.py
@@ -587,11 +587,14 @@
     )
     if tiled:
         side_params = in_order(after(side_params, side_scores[0]), me)
-        scores = exchange(scores)
-        side_scores = in_plane(across_planes(after(side_scores, params)))
-        packed = distances(*after((params, side_params), side_scores[0]))
+        side_scores = across_planes(after(side_scores, params))
+        packed = distances(params, side_params)
+        got = [swap(packed, z * PLANE) for z in range(1, PLANES)]
+        scores = exchange(after(scores, packed))
+        side_scores = in_plane(side_scores)
+        packed = sum(after(got, side_scores[0]), packed)
         side_scores = in_order(across_chips(side_scores), me)
-        for bits in ((1,), (2, 4, 6), (8, 16, 24)):
+        for bits in ((2, 4, 6), (1,)):
             packed = add_over(packed, members, bits)
         mixing, *side = mix_side(kernel_scale, me, packed, side_scores, side_params)
         main = mix_main(mixing, scores, params, side_params)

time: 229 us -> 238 us (1.039)
  waiting for transfers between devices: 123 us -> 135 us
  starting transfers between devices: 57.7 us -> 53.7 us
    ppermute x21 -> x24, waiting for transfers between devices: 53.7 us -> 72.4 us  [swap(): return lax.ppermute(value, AXES, pairs)]
    ppermute x7 -> x4, starting transfers between devices: 13.4 us -> 3.56 us  [add_over(): lax.ppermute(value, AXES, [(i, i ^ bit) for i in range(members)])]
    ppermute x7 -> x4, waiting for transfers between devices: 11.8 us -> 4.4 us  [add_over(): lax.ppermute(value, AXES, [(i, i ^ bit) for i in range(members)])]
    ppermute x21 -> x24, starting transfers between devices: 29.3 us -> 35.5 us  [swap(): return lax.ppermute(value, AXES, pairs)]
  transfers between devices with their start and end apart: 31 -> 31, of which waited for: 13 -> 15; matrix products, arithmetic and copies ran while one was open for 1% -> 1% of each run, Pallas kernels for 16% -> 16%
where the time goes in v17:
time: 238 us
  waiting for transfers between devices  135 us (57%)
  starting transfers between devices  53.7 us (23%)
  Pallas kernels  43.9 us (18%)
  local copies, waits for them, and re-layouts  3.82 us (2%)
    ppermute x24, waiting for transfers between devices, swap(): return lax.ppermute(value, AXES, pairs)  72.4 us
    all_to_all x3, waiting for transfers between devices, exchange(): return lax.all_to_all(blocks, AXES, split_axis=0, concat_axis=0, tiled=True)  57.7 us
    ppermute x24, starting transfers between devices, swap(): return lax.ppermute(value, AXES, pairs)  35.5 us
    pallas_call x1, Pallas kernels, particle_scores(): pl.pallas_call(functools.partial(score_kernel, DATA / count), out_shape=(...  23 us
    all_to_all x3, starting transfers between devices, exchange(): return lax.all_to_all(blocks, AXES, split_axis=0, concat_axis=0, tiled=True)  14.6 us
    pallas_call x1, Pallas kernels, mix_main(): pl.pallas_call(mix_main_kernel, out_shape=pltpu.HBM((members, 2 * MAIN, L...  5.02 us
  transfers between devices with their start and end apart: 31, of which 15 were waited for; matrix products, arithmetic and copies ran while one was open for 1% of the time, Pallas kernels for 16%

profile of v17, /device:TPU:0, one launch (start us, length us, event | category | flops | bytes accessed | tf_op | source)
XLA Modules:
  0.0 237.6 jit_solution(3003019431731664687)
XLA Ops:
  0.6 2.2 pack_side.1
  2.9 3.1 %collective-permute-start = (bf16[8,64,128]{2,1,0:T(8,128)(2,1)}, bf16[8,64,128]{2,1,0:T(8,128)(2,1)S(1)}, u32[]{:S(2)}, u32[]{:S(2)}) collective-permute-start(bf16[8,64,128]{2,1,0:T(8,128)(2,1)} %get-tuple-element.51), channel_id=1, source_target_pairs={{0,8},{1,9},{2,10},{3,11},{4,12},{5,13},{6,14},{7,15},{8,0},{9,1},... | collective-permute-start | bytes 393224 | tf_op jit(solution)/shard_map/ppermute | solution.py:367
  5.9 2.6 %collective-permute-start.1 = (bf16[8,64,128]{2,1,0:T(8,128)(2,1)}, bf16[8,64,128]{2,1,0:T(8,128)(2,1)S(1)}, u32[]{:S(2)}, u32[]{:S(2)}) collective-permute-start(bf16[8,64,128]{2,1,0:T(8,128)(2,1)} %get-tuple-element.52), channel_id=1, source_target_pairs={{0,16},{1,17},{2,18},{3,19},{4,20},{5,21},{6,22},{7,23},{8,24},{9,... | collective-permute-start | bytes 393224 | tf_op jit(solution)/shard_map/ppermute | solution.py:367
  8.5 2.6 %pack_main.1 = bf16[32,224,128]{2,1,0:T(8,128)(2,1)} custom-call(bf16[1,384,1536]{2,1,0:T(8,128)(2,1)} %first.3, bf16[1,1536,384]{2,1,0:T(8,128)(2,1)} %second.3), custom_call_target="tpu_custom_call" | custom-call | bytes 2359296 | tf_op jit(solution)/shard_map/pack_main/pallas_call | solution.py:492
  11.2 6.1 %all-to-all-start = ((bf16[32,224,128]{2,1,0:T(8,128)(2,1)}), bf16[32,224,128]{2,1,0:T(8,128)(2,1)S(1)}, u32[]{:S(2)}, u32[]{:S(2)}) async-start(bf16[32,224,128]{2,1,0:T(8,128)(2,1)} %pack_main.1), calls=%async_computation | async-start | bytes 3670016 | tf_op jit(solution)/shard_map/all_to_all | solution.py:568
  17.3 1.5 copy.10.image
  19.1 0.7 copy-done.2
  19.9 1.8 collective-permute-start.3
  21.7 1.5 collective-permute-start.4
  23.4 23.0 %score.1 = (bf16[32,224,128]{2,1,0:T(8,128)(2,1)}, bf16[8,64,128]{2,1,0:T(8,128)(2,1)S(1)}, bf16[8,64,128]{2,1,0:T(8,128)(2,1)S(1)}, bf16[8,64,128]{2,1,0:T(8,128)(2,1)S(1)}, bf16[8,64,128]{2,1,0:T(8,128)(2,1)S(1)}) custom-call(s32[8]{0:T(128)S(1)} %bitcast.6, s32[1]{0:T(128)} %bitcast.me, bf16[8,197,384]{2,1,0:T(8,128)(2,1)S(1)} %copy.10.image, ...), custom_call_target="tpu_custom_call" | custom-call | flops 9814671360 | bytes 7139328 | tf_op jit(solution)/shard_map/score/pallas_call | solution.py:134
  46.4 0.6 copy-done.6
  47.0 13.4 %all-to-all-done.main.params = bf16[32,224,128]{2,1,0:T(8,128)(2,1)S(1)} async-done(((bf16[32,224,128]{2,1,0:T(8,128)(2,1)}), bf16[32,224,128]{2,1,0:T(8,128)(2,1)S(1)}, u32[]{:S(2)}, u32[]{:S(2)}) %all-to-all-start) | async-done | bytes 1835040 | tf_op jit(solution)/shard_map/all_to_all | solution.py:568
  60.4 2.5 %collective-permute-start.11 = (bf16[8,64,128]{2,1,0:T(8,128)(2,1)S(1)}, bf16[8,64,128]{2,1,0:T(8,128)(2,1)}, u32[]{:S(2)}, u32[]{:S(2)}) collective-permute-start(bf16[8,64,128]{2,1,0:T(8,128)(2,1)S(1)} %get-tuple-element.72), channel_id=1, source_target_pairs={{0,16},{1,17},{2,18},{3,19},{4,20},{5,21},{6,22},{7,23},{8,24},{9,... | collective-permute-start | bytes 393224 | tf_op jit(solution)/shard_map/ppermute | solution.py:367
  62.9 1.9 collective-permute-start.12
  64.8 2.2 gram.1
  67.0 4.8 %all-to-all-start.1 = ((bf16[32,224,128]{2,1,0:T(8,128)(2,1)}), bf16[32,224,128]{2,1,0:T(8,128)(2,1)}, u32[]{:S(2)}, u32[]{:S(2)}) async-start(bf16[32,224,128]{2,1,0:T(8,128)(2,1)} %get-tuple-element.85), calls=%async_computation.1 | async-start | bytes 3670016 | tf_op jit(solution)/shard_map/all_to_all | solution.py:568
  71.8 1.5 collective-permute-done.11.refs_2_
  73.3 1.1 plane.4
  74.4 1.5 collective-permute-start.17
  75.9 1.6 collective-permute-start.18
  77.9 3.0 %collective-permute-start.7 = (f32[8,128]{1,0:T(8,128)S(1)}, f32[8,128]{1,0:T(8,128)S(1)}, u32[]{:S(2)}, u32[]{:S(2)}) collective-permute-start(f32[8,128]{1,0:T(8,128)S(1)} %gram.1), channel_id=1, source_target_pairs={{0,8},{1,9},{2,10},{3,11},{4,12},{5,13},{6,14},{7,15},{8,0},{9,1},... | collective-permute-start | bytes 12296 | tf_op jit(solution)/shard_map/ppermute | solution.py:367
  80.9 2.3 collective-permute-start.8
  83.2 18.8 %collective-permute-done.7 = f32[8,128]{1,0:T(8,128)S(1)} collective-permute-done((f32[8,128]{1,0:T(8,128)S(1)}, f32[8,128]{1,0:T(8,128)S(1)}, u32[]{:S(2)}, u32[]{:S(2)}) %collective-permute-start.7) | collective-permute-done | bytes 4128 | tf_op jit(solution)/shard_map/ppermute | solution.py:367
  102.0 3.5 %collective-permute-start.9 = (f32[8,128]{1,0:T(8,128)S(1)}, f32[8,128]{1,0:T(8,128)S(1)}, u32[]{:S(2)}, u32[]{:S(2)}) collective-permute-start(f32[8,128]{1,0:T(8,128)S(1)} %gram.1), channel_id=1, source_target_pairs={{0,24},{1,25},{2,26},{3,27},{4,28},{5,29},{6,30},{7,31},{8,16},{9,... | collective-permute-start | bytes 12296 | tf_op jit(solution)/shard_map/ppermute | solution.py:367
  105.5 9.6 %collective-permute-done.8 = f32[8,128]{1,0:T(8,128)S(1)} collective-permute-done((f32[8,128]{1,0:T(8,128)S(1)}, f32[8,128]{1,0:T(8,128)S(1)}, u32[]{:S(2)}, u32[]{:S(2)}) %collective-permute-start.8) | collective-permute-done | bytes 4128 | tf_op jit(solution)/shard_map/ppermute | solution.py:367
  115.3 1.4 collective-permute-start.13
  116.7 1.5 collective-permute-start.14
  118.2 0.6 collective-permute-start.15
  119.0 1.4 collective-permute-done.14
  120.3 2.4 %collective-permute-done.15 = f32[8,128]{1,0:T(8,128)S(1)} collective-permute-done((f32[8,128]{1,0:T(8,128)S(1)}, f32[8,128]{1,0:T(8,128)S(1)}, u32[]{:S(2)}, u32[]{:S(2)}) %collective-permute-start.15) | collective-permute-done | bytes 4128 | tf_op jit(solution)/shard_map/ppermute | solution.py:210
  124.0 1.9 mix_side.1
  125.9 0.7 copy-done.4
  126.6 0.5 collective-permute-start.21
  127.1 2.0 collective-permute-start.22
  129.1 1.8 collective-permute-start.23
  130.9 5.0 %mix_main.1 = bf16[32,448,128]{2,1,0:T(8,128)(2,1)} custom-call(bf16[512,512]{1,0:T(8,128)(2,1)S(1)} %get-tuple-element.83.mixing, bf16[32,224,128]{2,1,0:T(8,128)(2,1)} %all-to-all-done.1.scores, bf16[32,224,128]{2,1,0:T(8,128)(2,1)S(1)} %all-to-all-done.main.params, bf16[32,64,128]{2,1,0:T(8,128)(2,1)S(1)} %settle.3.side.params.side_params), custom_call_target="tpu_custom_call" | custom-call | flops 1879048192 | bytes 7340032 | tf_op jit(solution)/shard_map/mix_main/pallas_call | solution.py:313
  136.0 3.7 %all-to-all-start.2 = ((bf16[32,448,128]{2,1,0:T(8,128)(2,1)}), bf16[32,448,128]{2,1,0:T(8,128)(2,1)}, u32[]{:S(2)}, u32[]{:S(2)}) async-start(bf16[32,448,128]{2,1,0:T(8,128)(2,1)} %mix_main.1), calls=%async_computation.2 | async-start | bytes 7340032 | tf_op jit(solution)/shard_map/all_to_all | solution.py:568
  139.9 8.8 %collective-permute-done.22.refs_2_ = bf16[8,128,128]{2,1,0:T(8,128)(2,1)} collective-permute-done((bf16[8,128,128]{2,1,0:T(8,128)(2,1)}, bf16[8,128,128]{2,1,0:T(8,128)(2,1)}, u32[]{:S(2)}, u32[]{:S(2)}) %collective-permute-start.22) | collective-permute-done | bytes 262176 | tf_op jit(solution)/shard_map/ppermute | solution.py:367
  148.8 1.1 plane.5
  149.9 1.9 collective-permute-start.24
  151.7 1.8 collective-permute-start.25
  153.6 1.4 collective-permute-start.26
  154.9 12.5 %collective-permute-done.24.refs_1_ = bf16[4,2,128,128]{3,2,1,0:T(8,128)(2,1)S(1)} collective-permute-done((bf16[4,2,128,128]{3,2,1,0:T(8,128)(2,1)S(1)}, bf16[4,2,128,128]{3,2,1,0:T(8,128)(2,1)S(1)}, u32[]{:S(2)}, u32[]{:S(2)}) %collective-permute-start.24) | collective-permute-done | bytes 262176 | tf_op jit(solution)/shard_map/ppermute | solution.py:367
  167.4 5.0 %collective-permute-done.25.refs_2_ = bf16[4,2,128,128]{3,2,1,0:T(8,128)(2,1)S(1)} collective-permute-done((bf16[4,2,128,128]{3,2,1,0:T(8,128)(2,1)S(1)}, bf16[4,2,128,128]{3,2,1,0:T(8,128)(2,1)S(1)}, u32[]{:S(2)}, u32[]{:S(2)}) %collective-permute-start.25) | collective-permute-done | bytes 262176 | tf_op jit(solution)/shard_map/ppermute | solution.py:367
  172.4 14.0 %collective-permute-done.26.refs_3_ = bf16[4,2,128,128]{3,2,1,0:T(8,128)(2,1)S(1)} collective-permute-done((bf16[4,2,128,128]{3,2,1,0:T(8,128)(2,1)S(1)}, bf16[4,2,128,128]{3,2,1,0:T(8,128)(2,1)S(1)}, u32[]{:S(2)}, u32[]{:S(2)}) %collective-permute-start.26) | collective-permute-done | bytes 262176 | tf_op jit(solution)/shard_map/ppermute | solution.py:367
  186.6 1.9 collective-permute-done.27.far
  188.5 44.4 %all-to-all-done.2.main = bf16[32,448,128]{2,1,0:T(8,128)(2,1)} async-done(((bf16[32,448,128]{2,1,0:T(8,128)(2,1)}), bf16[32,448,128]{2,1,0:T(8,128)(2,1)}, u32[]{:S(2)}, u32[]{:S(2)}) %all-to-all-start.2) | async-done | bytes 3670048 | tf_op jit(solution)/shard_map/all_to_all | solution.py:568
  232.9 4.5 %unpack.1 = (bf16[1,384,1536]{2,1,0:T(8,128)(2,1)}, bf16[1,1536,384]{2,1,0:T(8,128)(2,1)}, bf16[1,384,1536]{2,1,0:T(8,128)(2,1)}, bf16[1,1536,384]{2,1,0:T(8,128)(2,1)}) custom-call(bf16[32,448,128]{2,1,0:T(8,128)(2,1)} %all-to-all-done.2.main, bf16[32,128,128]{2,1,0:T(8,128)(2,1)S(1)} %settle.5.side), custom_call_target="tpu_custom_call" | custom-call | bytes 9437184 | tf_op jit(solution)/shard_map/unpack/pallas_call | solution.py:551
  (53 shorter events, 2.3 us)
Async XLA Ops:
  2.9 16.2 %collective-permute-start = (bf16[8,64,128]{2,1,0:T(8,128)(2,1)}, bf16[8,64,128]{2,1,0:T(8,128)(2,1)S(1)}, u32[]{:S(2)}, u32[]{:S(2)}) collective-permute-start(bf16[8,64,128]{2,1,0:T(8,128)(2,1)} %get-tuple-element.51), channel_id=1, source_target_pairs={{0,8},{1,9},{2,10},{3,11},{4,12},{5,13},{6,14},{7,15},{8,0},{9,1},... | collective-permute-start | bytes 393224 | tf_op jit(solution)/shard_map/ppermute | solution.py:367
  5.9 13.1 %collective-permute-start.1 = (bf16[8,64,128]{2,1,0:T(8,128)(2,1)}, bf16[8,64,128]{2,1,0:T(8,128)(2,1)S(1)}, u32[]{:S(2)}, u32[]{:S(2)}) collective-permute-start(bf16[8,64,128]{2,1,0:T(8,128)(2,1)} %get-tuple-element.52), channel_id=1, source_target_pairs={{0,16},{1,17},{2,18},{3,19},{4,20},{5,21},{6,22},{7,23},{8,24},{9,... | collective-permute-start | bytes 393224 | tf_op jit(solution)/shard_map/ppermute | solution.py:367
  8.5 10.6 %collective-permute-start.2 = (bf16[8,64,128]{2,1,0:T(8,128)(2,1)}, bf16[8,64,128]{2,1,0:T(8,128)(2,1)S(1)}, u32[]{:S(2)}, u32[]{:S(2)}) collective-permute-start(bf16[8,64,128]{2,1,0:T(8,128)(2,1)} %get-tuple-element.53), channel_id=1, source_target_pairs={{0,24},{1,25},{2,26},{3,27},{4,28},{5,29},{6,30},{7,31},{8,16},{9,... | collective-permute-start | bytes 393224 | tf_op jit(solution)/shard_map/ppermute | solution.py:367
  11.2 49.2 %all-to-all-start = ((bf16[32,224,128]{2,1,0:T(8,128)(2,1)}), bf16[32,224,128]{2,1,0:T(8,128)(2,1)S(1)}, u32[]{:S(2)}, u32[]{:S(2)}) async-start(bf16[32,224,128]{2,1,0:T(8,128)(2,1)} %pack_main.1), calls=%async_computation | async-start | bytes 3670016 | tf_op jit(solution)/shard_map/all_to_all | solution.py:568
  17.3 1.6 copy-start.8
  18.9 0.9 copy-start.2
  19.8 3.6 %copy-start = (bf16[1,384,1536]{2,1,0:T(8,128)(2,1)S(1)}, bf16[1,384,1536]{2,1,0:T(8,128)(2,1)}, u32[]{:S(2)}) copy-start(bf16[1,384,1536]{2,1,0:T(8,128)(2,1)} %first.3) | copy-start | bytes 3538948
  19.8 3.6 %copy-start.1 = (bf16[1,1536,384]{2,1,0:T(8,128)(2,1)S(1)}, bf16[1,1536,384]{2,1,0:T(8,128)(2,1)}, u32[]{:S(2)}) copy-start(bf16[1,1536,384]{2,1,0:T(8,128)(2,1)} %second.3) | copy-start | bytes 3538948
  19.8 3.6 %copy-start.3 = (s32[1,8]{1,0:T(1,128)S(1)}, s32[1,8]{1,0:T(1,128)}, u32[]{:S(2)}) copy-start(s32[1,8]{1,0:T(1,128)} %param.10) | copy-start | bytes 100
  19.9 26.5 %collective-permute-start.3 = (bf16[4,2,64,128]{3,2,1,0:T(8,128)(2,1)S(1)}, bf16[4,2,64,128]{3,2,1,0:T(8,128)(2,1)S(1)}, u32[]{:S(2)}, u32[]{:S(2)}) collective-permute-start(bf16[4,2,64,128]{3,2,1,0:T(8,128)(2,1)S(1)} %get-tuple-element.55), channel_id=1, source_target_pairs={{0,2},{1,3},{2,0},{3,1},{4,6},{5,7},{6,4},{7,5},{8,10},{9,11},{10,... | collective-permute-start | bytes 393224 | tf_op jit(solution)/shard_map/ppermute | solution.py:367
  21.7 24.7 %collective-permute-start.4 = (bf16[4,2,64,128]{3,2,1,0:T(8,128)(2,1)S(1)}, bf16[4,2,64,128]{3,2,1,0:T(8,128)(2,1)S(1)}, u32[]{:S(2)}, u32[]{:S(2)}) collective-permute-start(bf16[4,2,64,128]{3,2,1,0:T(8,128)(2,1)S(1)} %get-tuple-element.56), channel_id=1, source_target_pairs={{0,4},{1,5},{2,6},{3,7},{4,0},{5,1},{6,2},{7,3},{8,12},{9,13},{10,... | collective-permute-start | bytes 393224 | tf_op jit(solution)/shard_map/ppermute | solution.py:367
  23.1 23.2 %collective-permute-start.5 = (bf16[4,2,64,128]{3,2,1,0:T(8,128)(2,1)S(1)}, bf16[4,2,64,128]{3,2,1,0:T(8,128)(2,1)S(1)}, u32[]{:S(2)}, u32[]{:S(2)}) collective-permute-start(bf16[4,2,64,128]{3,2,1,0:T(8,128)(2,1)S(1)} %get-tuple-element.57), channel_id=1, source_target_pairs={{0,6},{1,7},{2,4},{3,5},{4,2},{5,3},{6,0},{7,1},{8,14},{9,15},{10,... | collective-permute-start | bytes 393224 | tf_op jit(solution)/shard_map/ppermute | solution.py:367
  46.4 0.7 copy-start.6
  47.0 17.8 %collective-permute-start.6 = (bf16[4,4,64,128]{3,2,1,0:T(8,128)(2,1)S(1)}, bf16[4,4,64,128]{3,2,1,0:T(8,128)(2,1)S(1)}, u32[]{:S(2)}, u32[]{:S(2)}) collective-permute-start(bf16[4,4,64,128]{3,2,1,0:T(8,128)(2,1)S(1)} %get-tuple-element.66), channel_id=1, source_target_pairs={{0,1},{1,0},{2,3},{3,2},{4,5},{5,4},{6,7},{7,6},{8,9},{9,8},{10,11... | collective-permute-start | bytes 786440 | tf_op jit(solution)/shard_map/ppermute | solution.py:367
  60.4 11.4 %collective-permute-start.10 = (bf16[8,64,128]{2,1,0:T(8,128)(2,1)S(1)}, bf16[8,64,128]{2,1,0:T(8,128)(2,1)}, u32[]{:S(2)}, u32[]{:S(2)}) collective-permute-start(bf16[8,64,128]{2,1,0:T(8,128)(2,1)S(1)} %get-tuple-element.71), channel_id=1, source_target_pairs={{0,8},{1,9},{2,10},{3,11},{4,12},{5,13},{6,14},{7,15},{8,0},{9,1},... | collective-permute-start | bytes 393224 | tf_op jit(solution)/shard_map/ppermute | solution.py:367
  60.4 12.9 %collective-permute-start.11 = (bf16[8,64,128]{2,1,0:T(8,128)(2,1)S(1)}, bf16[8,64,128]{2,1,0:T(8,128)(2,1)}, u32[]{:S(2)}, u32[]{:S(2)}) collective-permute-start(bf16[8,64,128]{2,1,0:T(8,128)(2,1)S(1)} %get-tuple-element.72), channel_id=1, source_target_pairs={{0,16},{1,17},{2,18},{3,19},{4,20},{5,21},{6,22},{7,23},{8,24},{9,... | collective-permute-start | bytes 393224 | tf_op jit(solution)/shard_map/ppermute | solution.py:367
  62.9 10.4 %collective-permute-start.12 = (bf16[8,64,128]{2,1,0:T(8,128)(2,1)S(1)}, bf16[8,64,128]{2,1,0:T(8,128)(2,1)}, u32[]{:S(2)}, u32[]{:S(2)}) collective-permute-start(bf16[8,64,128]{2,1,0:T(8,128)(2,1)S(1)} %get-tuple-element.73), channel_id=1, source_target_pairs={{0,24},{1,25},{2,26},{3,27},{4,28},{5,29},{6,30},{7,31},{8,16},{9,... | collective-permute-start | bytes 393224 | tf_op jit(solution)/shard_map/ppermute | solution.py:367
  67.0 6.3 %copy-start.7 = (bf16[8,64,128]{2,1,0:T(8,128)(2,1)S(1)}, bf16[8,64,128]{2,1,0:T(8,128)(2,1)}, u32[]{:S(2)}) copy-start(bf16[8,64,128]{2,1,0:T(8,128)(2,1)} %copy-done.6) | copy-start | bytes 393220
  67.0 64.0 %all-to-all-start.1 = ((bf16[32,224,128]{2,1,0:T(8,128)(2,1)}), bf16[32,224,128]{2,1,0:T(8,128)(2,1)}, u32[]{:S(2)}, u32[]{:S(2)}) async-start(bf16[32,224,128]{2,1,0:T(8,128)(2,1)} %get-tuple-element.85), calls=%async_computation.1 | async-start | bytes 3670016 | tf_op jit(solution)/shard_map/all_to_all | solution.py:568
  74.4 40.8 %collective-permute-start.17 = (bf16[4,2,64,128]{3,2,1,0:T(8,128)(2,1)S(1)}, bf16[4,2,64,128]{3,2,1,0:T(8,128)(2,1)S(1)}, u32[]{:S(2)}, u32[]{:S(2)}) collective-permute-start(bf16[4,2,64,128]{3,2,1,0:T(8,128)(2,1)S(1)} %get-tuple-element.78), channel_id=1, source_target_pairs={{0,2},{1,3},{2,0},{3,1},{4,6},{5,7},{6,4},{7,5},{8,10},{9,11},{10,... | collective-permute-start | bytes 393224 | tf_op jit(solution)/shard_map/ppermute | solution.py:367
  75.9 39.3 %collective-permute-start.18 = (bf16[4,2,64,128]{3,2,1,0:T(8,128)(2,1)S(1)}, bf16[4,2,64,128]{3,2,1,0:T(8,128)(2,1)S(1)}, u32[]{:S(2)}, u32[]{:S(2)}) collective-permute-start(bf16[4,2,64,128]{3,2,1,0:T(8,128)(2,1)S(1)} %get-tuple-element.79), channel_id=1, source_target_pairs={{0,4},{1,5},{2,6},{3,7},{4,0},{5,1},{6,2},{7,3},{8,12},{9,13},{10,... | collective-permute-start | bytes 393224 | tf_op jit(solution)/shard_map/ppermute | solution.py:367
  77.5 37.6 %collective-permute-start.19 = (bf16[4,2,64,128]{3,2,1,0:T(8,128)(2,1)S(1)}, bf16[4,2,64,128]{3,2,1,0:T(8,128)(2,1)S(1)}, u32[]{:S(2)}, u32[]{:S(2)}) collective-permute-start(bf16[4,2,64,128]{3,2,1,0:T(8,128)(2,1)S(1)} %get-tuple-element.80), channel_id=1, source_target_pairs={{0,6},{1,7},{2,4},{3,5},{4,2},{5,3},{6,0},{7,1},{8,14},{9,15},{10,... | collective-permute-start | bytes 393224 | tf_op jit(solution)/shard_map/ppermute | solution.py:367
  77.9 24.1 %collective-permute-start.7 = (f32[8,128]{1,0:T(8,128)S(1)}, f32[8,128]{1,0:T(8,128)S(1)}, u32[]{:S(2)}, u32[]{:S(2)}) collective-permute-start(f32[8,128]{1,0:T(8,128)S(1)} %gram.1), channel_id=1, source_target_pairs={{0,8},{1,9},{2,10},{3,11},{4,12},{5,13},{6,14},{7,15},{8,0},{9,1},... | collective-permute-start | bytes 12296 | tf_op jit(solution)/shard_map/ppermute | solution.py:367
  80.9 34.2 %collective-permute-start.8 = (f32[8,128]{1,0:T(8,128)S(1)}, f32[8,128]{1,0:T(8,128)S(1)}, u32[]{:S(2)}, u32[]{:S(2)}) collective-permute-start(f32[8,128]{1,0:T(8,128)S(1)} %gram.1), channel_id=1, source_target_pairs={{0,16},{1,17},{2,18},{3,19},{4,20},{5,21},{6,22},{7,23},{8,24},{9,... | collective-permute-start | bytes 12296 | tf_op jit(solution)/shard_map/ppermute | solution.py:367
  102.0 13.1 %collective-permute-start.9 = (f32[8,128]{1,0:T(8,128)S(1)}, f32[8,128]{1,0:T(8,128)S(1)}, u32[]{:S(2)}, u32[]{:S(2)}) collective-permute-start(f32[8,128]{1,0:T(8,128)S(1)} %gram.1), channel_id=1, source_target_pairs={{0,24},{1,25},{2,26},{3,27},{4,28},{5,29},{6,30},{7,31},{8,16},{9,... | collective-permute-start | bytes 12296 | tf_op jit(solution)/shard_map/ppermute | solution.py:367
  115.2 8.7 %collective-permute-start.20 = (bf16[4,4,64,128]{3,2,1,0:T(8,128)(2,1)S(1)}, bf16[4,4,64,128]{3,2,1,0:T(8,128)(2,1)S(1)}, u32[]{:S(2)}, u32[]{:S(2)}) collective-permute-start(bf16[4,4,64,128]{3,2,1,0:T(8,128)(2,1)S(1)} %get-tuple-element.82), channel_id=1, source_target_pairs={{0,1},{1,0},{2,3},{3,2},{4,5},{5,4},{6,7},{7,6},{8,9},{9,8},{10,11... | collective-permute-start | bytes 786440 | tf_op jit(solution)/shard_map/ppermute | solution.py:367
  115.3 3.7 %collective-permute-start.13 = (f32[8,128]{1,0:T(8,128)S(1)}, f32[8,128]{1,0:T(8,128)S(1)}, u32[]{:S(2)}, u32[]{:S(2)}) collective-permute-start(f32[8,128]{1,0:T(8,128)S(1)} %add_add_fusion.1), channel_id=1, source_target_pairs={{0,2},{1,3},{2,0},{3,1},{4,6},{5,7},{6,4},{7,5},{8,10},{9,11},{10,... | collective-permute-start | bytes 12296 | tf_op jit(solution)/shard_map/ppermute | solution.py:210
  116.7 3.6 %collective-permute-start.14 = (f32[8,128]{1,0:T(8,128)S(1)}, f32[8,128]{1,0:T(8,128)S(1)}, u32[]{:S(2)}, u32[]{:S(2)}) collective-permute-start(f32[8,128]{1,0:T(8,128)S(1)} %add_add_fusion.1), channel_id=1, source_target_pairs={{0,4},{1,5},{2,6},{3,7},{4,0},{5,1},{6,2},{7,3},{8,12},{9,13},{10,... | collective-permute-start | bytes 12296 | tf_op jit(solution)/shard_map/ppermute | solution.py:210
  118.2 4.5 %collective-permute-start.15 = (f32[8,128]{1,0:T(8,128)S(1)}, f32[8,128]{1,0:T(8,128)S(1)}, u32[]{:S(2)}, u32[]{:S(2)}) collective-permute-start(f32[8,128]{1,0:T(8,128)S(1)} %add_add_fusion.1), channel_id=1, source_target_pairs={{0,6},{1,7},{2,4},{3,5},{4,2},{5,3},{6,0},{7,1},{8,14},{9,15},{10,... | collective-permute-start | bytes 12296 | tf_op jit(solution)/shard_map/ppermute | solution.py:210
  122.7 1.2 collective-permute-start.16
  125.9 0.7 copy-start.4
  126.6 13.4 %collective-permute-start.21 = (bf16[8,128,128]{2,1,0:T(8,128)(2,1)}, bf16[8,128,128]{2,1,0:T(8,128)(2,1)S(1)}, u32[]{:S(2)}, u32[]{:S(2)}) collective-permute-start(bf16[8,128,128]{2,1,0:T(8,128)(2,1)} %get-tuple-element.87), channel_id=1, source_target_pairs={{0,8},{1,9},{2,10},{3,11},{4,12},{5,13},{6,14},{7,15},{8,0},{9,1},... | collective-permute-start | bytes 786440 | tf_op jit(solution)/shard_map/ppermute | solution.py:367
  127.1 21.7 %collective-permute-start.22 = (bf16[8,128,128]{2,1,0:T(8,128)(2,1)}, bf16[8,128,128]{2,1,0:T(8,128)(2,1)}, u32[]{:S(2)}, u32[]{:S(2)}) collective-permute-start(bf16[8,128,128]{2,1,0:T(8,128)(2,1)} %get-tuple-element.88), channel_id=1, source_target_pairs={{0,16},{1,17},{2,18},{3,19},{4,20},{5,21},{6,22},{7,23},{8,24},{9,... | collective-permute-start | bytes 786440 | tf_op jit(solution)/shard_map/ppermute | solution.py:367
  129.1 19.6 %collective-permute-start.23 = (bf16[8,128,128]{2,1,0:T(8,128)(2,1)S(1)}, bf16[8,128,128]{2,1,0:T(8,128)(2,1)}, u32[]{:S(2)}, u32[]{:S(2)}) collective-permute-start(bf16[8,128,128]{2,1,0:T(8,128)(2,1)S(1)} %get-tuple-element.89), channel_id=1, source_target_pairs={{0,24},{1,25},{2,26},{3,27},{4,28},{5,29},{6,30},{7,31},{8,16},{9,... | collective-permute-start | bytes 786440 | tf_op jit(solution)/shard_map/ppermute | solution.py:367
  136.0 12.8 %copy-start.5 = (bf16[8,128,128]{2,1,0:T(8,128)(2,1)S(1)}, bf16[8,128,128]{2,1,0:T(8,128)(2,1)}, u32[]{:S(2)}) copy-start(bf16[8,128,128]{2,1,0:T(8,128)(2,1)} %copy-done.4) | copy-start | bytes 786436
  136.0 96.9 %all-to-all-start.2 = ((bf16[32,448,128]{2,1,0:T(8,128)(2,1)}), bf16[32,448,128]{2,1,0:T(8,128)(2,1)}, u32[]{:S(2)}, u32[]{:S(2)}) async-start(bf16[32,448,128]{2,1,0:T(8,128)(2,1)} %mix_main.1), calls=%async_computation.2 | async-start | bytes 7340032 | tf_op jit(solution)/shard_map/all_to_all | solution.py:568
  149.9 17.5 %collective-permute-start.24 = (bf16[4,2,128,128]{3,2,1,0:T(8,128)(2,1)S(1)}, bf16[4,2,128,128]{3,2,1,0:T(8,128)(2,1)S(1)}, u32[]{:S(2)}, u32[]{:S(2)}) collective-permute-start(bf16[4,2,128,128]{3,2,1,0:T(8,128)(2,1)S(1)} %get-tuple-element.91), channel_id=1, source_target_pairs={{0,2},{1,3},{2,0},{3,1},{4,6},{5,7},{6,4},{7,5},{8,10},{9,11},{10,... | collective-permute-start | bytes 786440 | tf_op jit(solution)/shard_map/ppermute | solution.py:367
  151.7 20.7 %collective-permute-start.25 = (bf16[4,2,128,128]{3,2,1,0:T(8,128)(2,1)S(1)}, bf16[4,2,128,128]{3,2,1,0:T(8,128)(2,1)S(1)}, u32[]{:S(2)}, u32[]{:S(2)}) collective-permute-start(bf16[4,2,128,128]{3,2,1,0:T(8,128)(2,1)S(1)} %get-tuple-element.92), channel_id=1, source_target_pairs={{0,4},{1,5},{2,6},{3,7},{4,0},{5,1},{6,2},{7,3},{8,12},{9,13},{10,... | collective-permute-start | bytes 786440 | tf_op jit(solution)/shard_map/ppermute | solution.py:367
  153.6 32.8 %collective-permute-start.26 = (bf16[4,2,128,128]{3,2,1,0:T(8,128)(2,1)S(1)}, bf16[4,2,128,128]{3,2,1,0:T(8,128)(2,1)S(1)}, u32[]{:S(2)}, u32[]{:S(2)}) collective-permute-start(bf16[4,2,128,128]{3,2,1,0:T(8,128)(2,1)S(1)} %get-tuple-element.93), channel_id=1, source_target_pairs={{0,6},{1,7},{2,4},{3,5},{4,2},{5,3},{6,0},{7,1},{8,14},{9,15},{10,... | collective-permute-start | bytes 786440 | tf_op jit(solution)/shard_map/ppermute | solution.py:367
  186.5 2.0 collective-permute-start.27

commit v18 on v17

--- a/solution.py
+++ b/solution.py
@@ -590,9 +590,9 @@
         side_scores = across_planes(after(side_scores, params))
         packed = distances(params, side_params)
         got = [swap(packed, z * PLANE) for z in range(1, PLANES)]
-        scores = exchange(after(scores, packed))
-        side_scores = in_plane(side_scores)
-        packed = sum(after(got, side_scores[0]), packed)
+        scores = exchange(scores)
+        side_scores = in_plane(after(side_scores, got))
+        packed = sum(got, packed)
         side_scores = in_order(across_chips(side_scores), me)
         for bits in ((2, 4, 6), (1,)):
             packed = add_over(packed, members, bits)

time: 238 us -> 227 us (0.954)
  waiting for transfers between devices: 135 us -> 128 us
  starting transfers between devices: 53.7 us -> 49.3 us
    ppermute x24, waiting for transfers between devices: 72.4 us -> 65 us  [swap(): return lax.ppermute(value, AXES, pairs)]
    ppermute x24, starting transfers between devices: 35.5 us -> 31.9 us  [swap(): return lax.ppermute(value, AXES, pairs)]
    all_to_all x3, waiting for transfers between devices: 57.7 us -> 60.6 us  [exchange(): return lax.all_to_all(blocks, AXES, split_axis=0, concat_axis=0, tiled=True)]
  transfers between devices with their start and end apart: 31 -> 31, of which waited for: 15 -> 16; matrix products, arithmetic and copies ran while one was open for 1% -> 1% of each run, Pallas kernels for 16% -> 16%
where the time goes in v18:
time: 227 us
  waiting for transfers between devices  128 us (56%)
  starting transfers between devices  49.3 us (22%)
  Pallas kernels  43.9 us (19%)
  local copies, waits for them, and re-layouts  3.82 us (2%)
    ppermute x24, waiting for transfers between devices, swap(): return lax.ppermute(value, AXES, pairs)  65 us
    all_to_all x3, waiting for transfers between devices, exchange(): return lax.all_to_all(blocks, AXES, split_axis=0, concat_axis=0, tiled=True)  60.6 us
    ppermute x24, starting transfers between devices, swap(): return lax.ppermute(value, AXES, pairs)  31.9 us
    pallas_call x1, Pallas kernels, particle_scores(): pl.pallas_call(functools.partial(score_kernel, DATA / count), out_shape=(...  22.9 us
    all_to_all x3, starting transfers between devices, exchange(): return lax.all_to_all(blocks, AXES, split_axis=0, concat_axis=0, tiled=True)  13.9 us
    pallas_call x1, Pallas kernels, mix_main(): pl.pallas_call(mix_main_kernel, out_shape=pltpu.HBM((members, 2 * MAIN, L...  5.03 us
  transfers between devices with their start and end apart: 31, of which 16 were waited for; matrix products, arithmetic and copies ran while one was open for 1% of the time, Pallas kernels for 16%

profile of v18, /device:TPU:0, one launch (start us, length us, event | category | flops | bytes accessed | tf_op | source)
XLA Modules:
  0.0 226.8 jit_solution(8685986890708162938)
XLA Ops:
  0.6 2.2 pack_side.1
  2.9 3.1 %collective-permute-start = (bf16[8,64,128]{2,1,0:T(8,128)(2,1)}, bf16[8,64,128]{2,1,0:T(8,128)(2,1)S(1)}, u32[]{:S(2)}, u32[]{:S(2)}) collective-permute-start(bf16[8,64,128]{2,1,0:T(8,128)(2,1)} %get-tuple-element.51), channel_id=1, source_target_pairs={{0,8},{1,9},{2,10},{3,11},{4,12},{5,13},{6,14},{7,15},{8,0},{9,1},... | collective-permute-start | bytes 393224 | tf_op jit(solution)/shard_map/ppermute | solution.py:367
  5.9 2.6 %collective-permute-start.1 = (bf16[8,64,128]{2,1,0:T(8,128)(2,1)}, bf16[8,64,128]{2,1,0:T(8,128)(2,1)S(1)}, u32[]{:S(2)}, u32[]{:S(2)}) collective-permute-start(bf16[8,64,128]{2,1,0:T(8,128)(2,1)} %get-tuple-element.52), channel_id=1, source_target_pairs={{0,16},{1,17},{2,18},{3,19},{4,20},{5,21},{6,22},{7,23},{8,24},{9,... | collective-permute-start | bytes 393224 | tf_op jit(solution)/shard_map/ppermute | solution.py:367
  8.5 2.6 %pack_main.1 = bf16[32,224,128]{2,1,0:T(8,128)(2,1)} custom-call(bf16[1,384,1536]{2,1,0:T(8,128)(2,1)} %first.3, bf16[1,1536,384]{2,1,0:T(8,128)(2,1)} %second.3), custom_call_target="tpu_custom_call" | custom-call | bytes 2359296 | tf_op jit(solution)/shard_map/pack_main/pallas_call | solution.py:492
  11.2 6.1 %all-to-all-start = ((bf16[32,224,128]{2,1,0:T(8,128)(2,1)}), bf16[32,224,128]{2,1,0:T(8,128)(2,1)S(1)}, u32[]{:S(2)}, u32[]{:S(2)}) async-start(bf16[32,224,128]{2,1,0:T(8,128)(2,1)} %pack_main.1), calls=%async_computation | async-start | bytes 3670016 | tf_op jit(solution)/shard_map/all_to_all | solution.py:568
  17.3 1.5 copy.10.image
  19.1 0.7 copy-done.2
  19.9 1.8 collective-permute-start.3
  21.7 1.5 collective-permute-start.4
  23.1 0.3 collective-permute-start.5
  23.4 22.9 %score.1 = (bf16[32,224,128]{2,1,0:T(8,128)(2,1)}, bf16[8,64,128]{2,1,0:T(8,128)(2,1)S(1)}, bf16[8,64,128]{2,1,0:T(8,128)(2,1)S(1)}, bf16[8,64,128]{2,1,0:T(8,128)(2,1)S(1)}, bf16[8,64,128]{2,1,0:T(8,128)(2,1)S(1)}) custom-call(s32[8]{0:T(128)S(1)} %bitcast.6, s32[1]{0:T(128)} %bitcast.me, bf16[8,197,384]{2,1,0:T(8,128)(2,1)S(1)} %copy.10.image, ...), custom_call_target="tpu_custom_call" | custom-call | flops 9814671360 | bytes 7139328 | tf_op jit(solution)/shard_map/score/pallas_call | solution.py:134
  46.4 0.6 copy-done.6
  47.0 13.4 %all-to-all-done.main.params = bf16[32,224,128]{2,1,0:T(8,128)(2,1)S(1)} async-done(((bf16[32,224,128]{2,1,0:T(8,128)(2,1)}), bf16[32,224,128]{2,1,0:T(8,128)(2,1)S(1)}, u32[]{:S(2)}, u32[]{:S(2)}) %all-to-all-start) | async-done | bytes 1835040 | tf_op jit(solution)/shard_map/all_to_all | solution.py:568
  60.4 2.5 %collective-permute-start.15 = (bf16[8,64,128]{2,1,0:T(8,128)(2,1)S(1)}, bf16[8,64,128]{2,1,0:T(8,128)(2,1)}, u32[]{:S(2)}, u32[]{:S(2)}) collective-permute-start(bf16[8,64,128]{2,1,0:T(8,128)(2,1)S(1)} %get-tuple-element.72), channel_id=1, source_target_pairs={{0,16},{1,17},{2,18},{3,19},{4,20},{5,21},{6,22},{7,23},{8,24},{9,... | collective-permute-start | bytes 393224 | tf_op jit(solution)/shard_map/ppermute | solution.py:367
  62.9 1.9 collective-permute-start.16
  64.8 2.2 gram.1
  67.0 2.5 %collective-permute-start.8 = (f32[8,128]{1,0:T(8,128)S(1)}, f32[8,128]{1,0:T(8,128)S(1)}, u32[]{:S(2)}, u32[]{:S(2)}) collective-permute-start(f32[8,128]{1,0:T(8,128)S(1)} %gram.1), channel_id=1, source_target_pairs={{0,16},{1,17},{2,18},{3,19},{4,20},{5,21},{6,22},{7,23},{8,24},{9,... | collective-permute-start | bytes 12296 | tf_op jit(solution)/shard_map/ppermute | solution.py:367
  69.5 1.5 collective-permute-done.7
  71.0 1.9 collective-permute-start.9
  72.9 4.1 %all-to-all-start.1 = ((bf16[32,224,128]{2,1,0:T(8,128)(2,1)}), bf16[32,224,128]{2,1,0:T(8,128)(2,1)}, u32[]{:S(2)}, u32[]{:S(2)}) async-start(bf16[32,224,128]{2,1,0:T(8,128)(2,1)} %get-tuple-element.85), calls=%async_computation.1 | async-start | bytes 3670016 | tf_op jit(solution)/shard_map/all_to_all | solution.py:568
  77.1 1.1 plane.4
  78.2 1.6 collective-permute-start.17
  79.8 1.5 collective-permute-start.18
  81.3 0.5 collective-permute-start.19
  81.8 11.8 %collective-permute-done.17.refs_1_ = bf16[4,2,64,128]{3,2,1,0:T(8,128)(2,1)S(1)} collective-permute-done((bf16[4,2,64,128]{3,2,1,0:T(8,128)(2,1)S(1)}, bf16[4,2,64,128]{3,2,1,0:T(8,128)(2,1)S(1)}, u32[]{:S(2)}, u32[]{:S(2)}) %collective-permute-start.17) | collective-permute-done | bytes 131104 | tf_op jit(solution)/shard_map/ppermute | solution.py:367
  93.6 2.8 %collective-permute-done.18.refs_2_ = bf16[4,2,64,128]{3,2,1,0:T(8,128)(2,1)S(1)} collective-permute-done((bf16[4,2,64,128]{3,2,1,0:T(8,128)(2,1)S(1)}, bf16[4,2,64,128]{3,2,1,0:T(8,128)(2,1)S(1)}, u32[]{:S(2)}, u32[]{:S(2)}) %collective-permute-start.18) | collective-permute-done | bytes 131104 | tf_op jit(solution)/shard_map/ppermute | solution.py:367
  96.4 6.7 %collective-permute-done.19.refs_3_ = bf16[4,2,64,128]{3,2,1,0:T(8,128)(2,1)S(1)} collective-permute-done((bf16[4,2,64,128]{3,2,1,0:T(8,128)(2,1)S(1)}, bf16[4,2,64,128]{3,2,1,0:T(8,128)(2,1)S(1)}, u32[]{:S(2)}, u32[]{:S(2)}) %collective-permute-start.19) | collective-permute-done | bytes 131104 | tf_op jit(solution)/shard_map/ppermute | solution.py:367
  103.3 0.9 collective-permute-start.11
  104.2 2.6 %collective-permute-start.12 = (f32[8,128]{1,0:T(8,128)S(1)}, f32[8,128]{1,0:T(8,128)S(1)}, u32[]{:S(2)}, u32[]{:S(2)}) collective-permute-start(f32[8,128]{1,0:T(8,128)S(1)} %add_add_fusion.1), channel_id=1, source_target_pairs={{0,6},{1,7},{2,4},{3,5},{4,2},{5,3},{6,0},{7,1},{8,14},{9,15},{10,... | collective-permute-start | bytes 12296 | tf_op jit(solution)/shard_map/ppermute | solution.py:210
  107.0 1.7 collective-permute-done.12
  109.3 0.5 collective-permute-done.13
  109.9 1.9 mix_side.1
  111.8 0.7 copy-done.4
  112.5 3.5 %collective-permute-start.22 = (bf16[8,128,128]{2,1,0:T(8,128)(2,1)}, bf16[8,128,128]{2,1,0:T(8,128)(2,1)}, u32[]{:S(2)}, u32[]{:S(2)}) collective-permute-start(bf16[8,128,128]{2,1,0:T(8,128)(2,1)} %get-tuple-element.88), channel_id=1, source_target_pairs={{0,16},{1,17},{2,18},{3,19},{4,20},{5,21},{6,22},{7,23},{8,24},{9,... | collective-permute-start | bytes 786440 | tf_op jit(solution)/shard_map/ppermute | solution.py:367
  116.0 0.8 collective-permute-start.23
  116.9 3.7 %all-to-all-done.1.scores = bf16[32,224,128]{2,1,0:T(8,128)(2,1)} async-done(((bf16[32,224,128]{2,1,0:T(8,128)(2,1)}), bf16[32,224,128]{2,1,0:T(8,128)(2,1)}, u32[]{:S(2)}, u32[]{:S(2)}) %all-to-all-start.1) | async-done | bytes 1835040 | tf_op jit(solution)/shard_map/all_to_all | solution.py:568
  120.6 5.0 %mix_main.1 = bf16[32,448,128]{2,1,0:T(8,128)(2,1)} custom-call(bf16[512,512]{1,0:T(8,128)(2,1)S(1)} %get-tuple-element.84.mixing, bf16[32,224,128]{2,1,0:T(8,128)(2,1)} %all-to-all-done.1.scores, bf16[32,224,128]{2,1,0:T(8,128)(2,1)S(1)} %all-to-all-done.main.params, bf16[32,64,128]{2,1,0:T(8,128)(2,1)S(1)} %settle.3.side.params.side_params), custom_call_target="tpu_custom_call" | custom-call | flops 1879048192 | bytes 7340032 | tf_op jit(solution)/shard_map/mix_main/pallas_call | solution.py:313
  125.7 3.7 %all-to-all-start.2 = ((bf16[32,448,128]{2,1,0:T(8,128)(2,1)}), bf16[32,448,128]{2,1,0:T(8,128)(2,1)}, u32[]{:S(2)}, u32[]{:S(2)}) async-start(bf16[32,448,128]{2,1,0:T(8,128)(2,1)} %mix_main.1), calls=%async_computation.2 | async-start | bytes 7340032 | tf_op jit(solution)/shard_map/all_to_all | solution.py:568
  129.4 10.5 %collective-permute-done.22.refs_2_ = bf16[8,128,128]{2,1,0:T(8,128)(2,1)} collective-permute-done((bf16[8,128,128]{2,1,0:T(8,128)(2,1)}, bf16[8,128,128]{2,1,0:T(8,128)(2,1)}, u32[]{:S(2)}, u32[]{:S(2)}) %collective-permute-start.22) | collective-permute-done | bytes 262176 | tf_op jit(solution)/shard_map/ppermute | solution.py:367
  139.9 1.1 plane.5
  141.0 2.8 %collective-permute-start.24 = (bf16[4,2,128,128]{3,2,1,0:T(8,128)(2,1)S(1)}, bf16[4,2,128,128]{3,2,1,0:T(8,128)(2,1)S(1)}, u32[]{:S(2)}, u32[]{:S(2)}) collective-permute-start(bf16[4,2,128,128]{3,2,1,0:T(8,128)(2,1)S(1)} %get-tuple-element.91), channel_id=1, source_target_pairs={{0,2},{1,3},{2,0},{3,1},{4,6},{5,7},{6,4},{7,5},{8,10},{9,11},{10,... | collective-permute-start | bytes 786440 | tf_op jit(solution)/shard_map/ppermute | solution.py:367
  143.8 2.9 %collective-permute-start.25 = (bf16[4,2,128,128]{3,2,1,0:T(8,128)(2,1)S(1)}, bf16[4,2,128,128]{3,2,1,0:T(8,128)(2,1)S(1)}, u32[]{:S(2)}, u32[]{:S(2)}) collective-permute-start(bf16[4,2,128,128]{3,2,1,0:T(8,128)(2,1)S(1)} %get-tuple-element.92), channel_id=1, source_target_pairs={{0,4},{1,5},{2,6},{3,7},{4,0},{5,1},{6,2},{7,3},{8,12},{9,13},{10,... | collective-permute-start | bytes 786440 | tf_op jit(solution)/shard_map/ppermute | solution.py:367
  146.7 10.2 %collective-permute-done.24.refs_1_ = bf16[4,2,128,128]{3,2,1,0:T(8,128)(2,1)S(1)} collective-permute-done((bf16[4,2,128,128]{3,2,1,0:T(8,128)(2,1)S(1)}, bf16[4,2,128,128]{3,2,1,0:T(8,128)(2,1)S(1)}, u32[]{:S(2)}, u32[]{:S(2)}) %collective-permute-start.24) | collective-permute-done | bytes 262176 | tf_op jit(solution)/shard_map/ppermute | solution.py:367
  156.9 4.7 %collective-permute-done.25.refs_2_ = bf16[4,2,128,128]{3,2,1,0:T(8,128)(2,1)S(1)} collective-permute-done((bf16[4,2,128,128]{3,2,1,0:T(8,128)(2,1)S(1)}, bf16[4,2,128,128]{3,2,1,0:T(8,128)(2,1)S(1)}, u32[]{:S(2)}, u32[]{:S(2)}) %collective-permute-start.25) | collective-permute-done | bytes 262176 | tf_op jit(solution)/shard_map/ppermute | solution.py:367
  161.7 14.8 %collective-permute-done.26.refs_3_ = bf16[4,2,128,128]{3,2,1,0:T(8,128)(2,1)S(1)} collective-permute-done((bf16[4,2,128,128]{3,2,1,0:T(8,128)(2,1)S(1)}, bf16[4,2,128,128]{3,2,1,0:T(8,128)(2,1)S(1)}, u32[]{:S(2)}, u32[]{:S(2)}) %collective-permute-start.26) | collective-permute-done | bytes 262176 | tf_op jit(solution)/shard_map/ppermute | solution.py:367
  176.6 1.9 collective-permute-done.27.far
  178.6 43.5 %all-to-all-done.2.main = bf16[32,448,128]{2,1,0:T(8,128)(2,1)} async-done(((bf16[32,448,128]{2,1,0:T(8,128)(2,1)}), bf16[32,448,128]{2,1,0:T(8,128)(2,1)}, u32[]{:S(2)}, u32[]{:S(2)}) %all-to-all-start.2) | async-done | bytes 3670048 | tf_op jit(solution)/shard_map/all_to_all | solution.py:568
  222.1 4.5 %unpack.1 = (bf16[1,384,1536]{2,1,0:T(8,128)(2,1)}, bf16[1,1536,384]{2,1,0:T(8,128)(2,1)}, bf16[1,384,1536]{2,1,0:T(8,128)(2,1)}, bf16[1,1536,384]{2,1,0:T(8,128)(2,1)}) custom-call(bf16[32,448,128]{2,1,0:T(8,128)(2,1)} %all-to-all-done.2.main, bf16[32,128,128]{2,1,0:T(8,128)(2,1)S(1)} %settle.5.side), custom_call_target="tpu_custom_call" | custom-call | bytes 9437184 | tf_op jit(solution)/shard_map/unpack/pallas_call | solution.py:551
  (53 shorter events, 1.1 us)
Async XLA Ops:
  2.9 16.2 %collective-permute-start = (bf16[8,64,128]{2,1,0:T(8,128)(2,1)}, bf16[8,64,128]{2,1,0:T(8,128)(2,1)S(1)}, u32[]{:S(2)}, u32[]{:S(2)}) collective-permute-start(bf16[8,64,128]{2,1,0:T(8,128)(2,1)} %get-tuple-element.51), channel_id=1, source_target_pairs={{0,8},{1,9},{2,10},{3,11},{4,12},{5,13},{6,14},{7,15},{8,0},{9,1},... | collective-permute-start | bytes 393224 | tf_op jit(solution)/shard_map/ppermute | solution.py:367
  5.9 13.1 %collective-permute-start.1 = (bf16[8,64,128]{2,1,0:T(8,128)(2,1)}, bf16[8,64,128]{2,1,0:T(8,128)(2,1)S(1)}, u32[]{:S(2)}, u32[]{:S(2)}) collective-permute-start(bf16[8,64,128]{2,1,0:T(8,128)(2,1)} %get-tuple-element.52), channel_id=1, source_target_pairs={{0,16},{1,17},{2,18},{3,19},{4,20},{5,21},{6,22},{7,23},{8,24},{9,... | collective-permute-start | bytes 393224 | tf_op jit(solution)/shard_map/ppermute | solution.py:367
  8.5 10.6 %collective-permute-start.2 = (bf16[8,64,128]{2,1,0:T(8,128)(2,1)}, bf16[8,64,128]{2,1,0:T(8,128)(2,1)S(1)}, u32[]{:S(2)}, u32[]{:S(2)}) collective-permute-start(bf16[8,64,128]{2,1,0:T(8,128)(2,1)} %get-tuple-element.53), channel_id=1, source_target_pairs={{0,24},{1,25},{2,26},{3,27},{4,28},{5,29},{6,30},{7,31},{8,16},{9,... | collective-permute-start | bytes 393224 | tf_op jit(solution)/shard_map/ppermute | solution.py:367
  11.2 49.2 %all-to-all-start = ((bf16[32,224,128]{2,1,0:T(8,128)(2,1)}), bf16[32,224,128]{2,1,0:T(8,128)(2,1)S(1)}, u32[]{:S(2)}, u32[]{:S(2)}) async-start(bf16[32,224,128]{2,1,0:T(8,128)(2,1)} %pack_main.1), calls=%async_computation | async-start | bytes 3670016 | tf_op jit(solution)/shard_map/all_to_all | solution.py:568
  17.3 1.6 copy-start.8
  18.9 0.9 copy-start.2
  19.8 3.6 %copy-start = (bf16[1,384,1536]{2,1,0:T(8,128)(2,1)S(1)}, bf16[1,384,1536]{2,1,0:T(8,128)(2,1)}, u32[]{:S(2)}) copy-start(bf16[1,384,1536]{2,1,0:T(8,128)(2,1)} %first.3) | copy-start | bytes 3538948
  19.8 3.6 %copy-start.1 = (bf16[1,1536,384]{2,1,0:T(8,128)(2,1)S(1)}, bf16[1,1536,384]{2,1,0:T(8,128)(2,1)}, u32[]{:S(2)}) copy-start(bf16[1,1536,384]{2,1,0:T(8,128)(2,1)} %second.3) | copy-start | bytes 3538948
  19.8 3.6 %copy-start.3 = (s32[1,8]{1,0:T(1,128)S(1)}, s32[1,8]{1,0:T(1,128)}, u32[]{:S(2)}) copy-start(s32[1,8]{1,0:T(1,128)} %param.10) | copy-start | bytes 100
  19.9 26.5 %collective-permute-start.3 = (bf16[4,2,64,128]{3,2,1,0:T(8,128)(2,1)S(1)}, bf16[4,2,64,128]{3,2,1,0:T(8,128)(2,1)S(1)}, u32[]{:S(2)}, u32[]{:S(2)}) collective-permute-start(bf16[4,2,64,128]{3,2,1,0:T(8,128)(2,1)S(1)} %get-tuple-element.55), channel_id=1, source_target_pairs={{0,2},{1,3},{2,0},{3,1},{4,6},{5,7},{6,4},{7,5},{8,10},{9,11},{10,... | collective-permute-start | bytes 393224 | tf_op jit(solution)/shard_map/ppermute | solution.py:367
  21.7 24.7 %collective-permute-start.4 = (bf16[4,2,64,128]{3,2,1,0:T(8,128)(2,1)S(1)}, bf16[4,2,64,128]{3,2,1,0:T(8,128)(2,1)S(1)}, u32[]{:S(2)}, u32[]{:S(2)}) collective-permute-start(bf16[4,2,64,128]{3,2,1,0:T(8,128)(2,1)S(1)} %get-tuple-element.56), channel_id=1, source_target_pairs={{0,4},{1,5},{2,6},{3,7},{4,0},{5,1},{6,2},{7,3},{8,12},{9,13},{10,... | collective-permute-start | bytes 393224 | tf_op jit(solution)/shard_map/ppermute | solution.py:367
  23.1 23.2 %collective-permute-start.5 = (bf16[4,2,64,128]{3,2,1,0:T(8,128)(2,1)S(1)}, bf16[4,2,64,128]{3,2,1,0:T(8,128)(2,1)S(1)}, u32[]{:S(2)}, u32[]{:S(2)}) collective-permute-start(bf16[4,2,64,128]{3,2,1,0:T(8,128)(2,1)S(1)} %get-tuple-element.57), channel_id=1, source_target_pairs={{0,6},{1,7},{2,4},{3,5},{4,2},{5,3},{6,0},{7,1},{8,14},{9,15},{10,... | collective-permute-start | bytes 393224 | tf_op jit(solution)/shard_map/ppermute | solution.py:367
  46.4 0.7 copy-start.6
  47.0 17.8 %collective-permute-start.6 = (bf16[4,4,64,128]{3,2,1,0:T(8,128)(2,1)S(1)}, bf16[4,4,64,128]{3,2,1,0:T(8,128)(2,1)S(1)}, u32[]{:S(2)}, u32[]{:S(2)}) collective-permute-start(bf16[4,4,64,128]{3,2,1,0:T(8,128)(2,1)S(1)} %get-tuple-element.66), channel_id=1, source_target_pairs={{0,1},{1,0},{2,3},{3,2},{4,5},{5,4},{6,7},{7,6},{8,9},{9,8},{10,11... | collective-permute-start | bytes 786440 | tf_op jit(solution)/shard_map/ppermute | solution.py:367
  60.4 16.7 %collective-permute-start.14 = (bf16[8,64,128]{2,1,0:T(8,128)(2,1)S(1)}, bf16[8,64,128]{2,1,0:T(8,128)(2,1)}, u32[]{:S(2)}, u32[]{:S(2)}) collective-permute-start(bf16[8,64,128]{2,1,0:T(8,128)(2,1)S(1)} %get-tuple-element.71), channel_id=1, source_target_pairs={{0,8},{1,9},{2,10},{3,11},{4,12},{5,13},{6,14},{7,15},{8,0},{9,1},... | collective-permute-start | bytes 393224 | tf_op jit(solution)/shard_map/ppermute | solution.py:367
  60.4 16.7 %collective-permute-start.15 = (bf16[8,64,128]{2,1,0:T(8,128)(2,1)S(1)}, bf16[8,64,128]{2,1,0:T(8,128)(2,1)}, u32[]{:S(2)}, u32[]{:S(2)}) collective-permute-start(bf16[8,64,128]{2,1,0:T(8,128)(2,1)S(1)} %get-tuple-element.72), channel_id=1, source_target_pairs={{0,16},{1,17},{2,18},{3,19},{4,20},{5,21},{6,22},{7,23},{8,24},{9,... | collective-permute-start | bytes 393224 | tf_op jit(solution)/shard_map/ppermute | solution.py:367
  62.9 14.2 %collective-permute-start.16 = (bf16[8,64,128]{2,1,0:T(8,128)(2,1)S(1)}, bf16[8,64,128]{2,1,0:T(8,128)(2,1)}, u32[]{:S(2)}, u32[]{:S(2)}) collective-permute-start(bf16[8,64,128]{2,1,0:T(8,128)(2,1)S(1)} %get-tuple-element.73), channel_id=1, source_target_pairs={{0,24},{1,25},{2,26},{3,27},{4,28},{5,29},{6,30},{7,31},{8,16},{9,... | collective-permute-start | bytes 393224 | tf_op jit(solution)/shard_map/ppermute | solution.py:367
  67.0 4.0 %collective-permute-start.7 = (f32[8,128]{1,0:T(8,128)S(1)}, f32[8,128]{1,0:T(8,128)S(1)}, u32[]{:S(2)}, u32[]{:S(2)}) collective-permute-start(f32[8,128]{1,0:T(8,128)S(1)} %gram.1), channel_id=1, source_target_pairs={{0,8},{1,9},{2,10},{3,11},{4,12},{5,13},{6,14},{7,15},{8,0},{9,1},... | collective-permute-start | bytes 12296 | tf_op jit(solution)/shard_map/ppermute | solution.py:367
  67.0 10.1 %collective-permute-start.8 = (f32[8,128]{1,0:T(8,128)S(1)}, f32[8,128]{1,0:T(8,128)S(1)}, u32[]{:S(2)}, u32[]{:S(2)}) collective-permute-start(f32[8,128]{1,0:T(8,128)S(1)} %gram.1), channel_id=1, source_target_pairs={{0,16},{1,17},{2,18},{3,19},{4,20},{5,21},{6,22},{7,23},{8,24},{9,... | collective-permute-start | bytes 12296 | tf_op jit(solution)/shard_map/ppermute | solution.py:367
  71.0 6.1 %collective-permute-start.9 = (f32[8,128]{1,0:T(8,128)S(1)}, f32[8,128]{1,0:T(8,128)S(1)}, u32[]{:S(2)}, u32[]{:S(2)}) collective-permute-start(f32[8,128]{1,0:T(8,128)S(1)} %gram.1), channel_id=1, source_target_pairs={{0,24},{1,25},{2,26},{3,27},{4,28},{5,29},{6,30},{7,31},{8,16},{9,... | collective-permute-start | bytes 12296 | tf_op jit(solution)/shard_map/ppermute | solution.py:367
  72.9 4.2 %copy-start.7 = (bf16[8,64,128]{2,1,0:T(8,128)(2,1)S(1)}, bf16[8,64,128]{2,1,0:T(8,128)(2,1)}, u32[]{:S(2)}) copy-start(bf16[8,64,128]{2,1,0:T(8,128)(2,1)} %copy-done.6) | copy-start | bytes 393220
  72.9 47.7 %all-to-all-start.1 = ((bf16[32,224,128]{2,1,0:T(8,128)(2,1)}), bf16[32,224,128]{2,1,0:T(8,128)(2,1)}, u32[]{:S(2)}, u32[]{:S(2)}) async-start(bf16[32,224,128]{2,1,0:T(8,128)(2,1)} %get-tuple-element.85), calls=%async_computation.1 | async-start | bytes 3670016 | tf_op jit(solution)/shard_map/all_to_all | solution.py:568
  78.2 15.3 %collective-permute-start.17 = (bf16[4,2,64,128]{3,2,1,0:T(8,128)(2,1)S(1)}, bf16[4,2,64,128]{3,2,1,0:T(8,128)(2,1)S(1)}, u32[]{:S(2)}, u32[]{:S(2)}) collective-permute-start(bf16[4,2,64,128]{3,2,1,0:T(8,128)(2,1)S(1)} %get-tuple-element.79), channel_id=1, source_target_pairs={{0,2},{1,3},{2,0},{3,1},{4,6},{5,7},{6,4},{7,5},{8,10},{9,11},{10,... | collective-permute-start | bytes 393224 | tf_op jit(solution)/shard_map/ppermute | solution.py:367
  79.8 16.6 %collective-permute-start.18 = (bf16[4,2,64,128]{3,2,1,0:T(8,128)(2,1)S(1)}, bf16[4,2,64,128]{3,2,1,0:T(8,128)(2,1)S(1)}, u32[]{:S(2)}, u32[]{:S(2)}) collective-permute-start(bf16[4,2,64,128]{3,2,1,0:T(8,128)(2,1)S(1)} %get-tuple-element.80), channel_id=1, source_target_pairs={{0,4},{1,5},{2,6},{3,7},{4,0},{5,1},{6,2},{7,3},{8,12},{9,13},{10,... | collective-permute-start | bytes 393224 | tf_op jit(solution)/shard_map/ppermute | solution.py:367
  81.3 21.8 %collective-permute-start.19 = (bf16[4,2,64,128]{3,2,1,0:T(8,128)(2,1)S(1)}, bf16[4,2,64,128]{3,2,1,0:T(8,128)(2,1)S(1)}, u32[]{:S(2)}, u32[]{:S(2)}) collective-permute-start(bf16[4,2,64,128]{3,2,1,0:T(8,128)(2,1)S(1)} %get-tuple-element.81), channel_id=1, source_target_pairs={{0,6},{1,7},{2,4},{3,5},{4,2},{5,3},{6,0},{7,1},{8,14},{9,15},{10,... | collective-permute-start | bytes 393224 | tf_op jit(solution)/shard_map/ppermute | solution.py:367
  103.1 6.7 %collective-permute-start.20 = (bf16[4,4,64,128]{3,2,1,0:T(8,128)(2,1)S(1)}, bf16[4,4,64,128]{3,2,1,0:T(8,128)(2,1)S(1)}, u32[]{:S(2)}, u32[]{:S(2)}) collective-permute-start(bf16[4,4,64,128]{3,2,1,0:T(8,128)(2,1)S(1)} %get-tuple-element.83), channel_id=1, source_target_pairs={{0,1},{1,0},{2,3},{3,2},{4,5},{5,4},{6,7},{7,6},{8,9},{9,8},{10,11... | collective-permute-start | bytes 786440 | tf_op jit(solution)/shard_map/ppermute | solution.py:367
  103.2 3.7 %collective-permute-start.10 = (f32[8,128]{1,0:T(8,128)S(1)}, f32[8,128]{1,0:T(8,128)S(1)}, u32[]{:S(2)}, u32[]{:S(2)}) collective-permute-start(f32[8,128]{1,0:T(8,128)S(1)} %add_add_fusion.1), channel_id=1, source_target_pairs={{0,2},{1,3},{2,0},{3,1},{4,6},{5,7},{6,4},{7,5},{8,10},{9,11},{10,... | collective-permute-start | bytes 12296 | tf_op jit(solution)/shard_map/ppermute | solution.py:210
  103.3 3.7 %collective-permute-start.11 = (f32[8,128]{1,0:T(8,128)S(1)}, f32[8,128]{1,0:T(8,128)S(1)}, u32[]{:S(2)}, u32[]{:S(2)}) collective-permute-start(f32[8,128]{1,0:T(8,128)S(1)} %add_add_fusion.1), channel_id=1, source_target_pairs={{0,4},{1,5},{2,6},{3,7},{4,0},{5,1},{6,2},{7,3},{8,12},{9,13},{10,... | collective-permute-start | bytes 12296 | tf_op jit(solution)/shard_map/ppermute | solution.py:210
  104.2 4.5 %collective-permute-start.12 = (f32[8,128]{1,0:T(8,128)S(1)}, f32[8,128]{1,0:T(8,128)S(1)}, u32[]{:S(2)}, u32[]{:S(2)}) collective-permute-start(f32[8,128]{1,0:T(8,128)S(1)} %add_add_fusion.1), channel_id=1, source_target_pairs={{0,6},{1,7},{2,4},{3,5},{4,2},{5,3},{6,0},{7,1},{8,14},{9,15},{10,... | collective-permute-start | bytes 12296 | tf_op jit(solution)/shard_map/ppermute | solution.py:210
  108.7 1.2 collective-permute-start.13
  111.8 0.7 copy-start.4
  112.5 16.9 %collective-permute-start.21 = (bf16[8,128,128]{2,1,0:T(8,128)(2,1)}, bf16[8,128,128]{2,1,0:T(8,128)(2,1)S(1)}, u32[]{:S(2)}, u32[]{:S(2)}) collective-permute-start(bf16[8,128,128]{2,1,0:T(8,128)(2,1)} %get-tuple-element.87), channel_id=1, source_target_pairs={{0,8},{1,9},{2,10},{3,11},{4,12},{5,13},{6,14},{7,15},{8,0},{9,1},... | collective-permute-start | bytes 786440 | tf_op jit(solution)/shard_map/ppermute | solution.py:367
  112.5 27.4 %collective-permute-start.22 = (bf16[8,128,128]{2,1,0:T(8,128)(2,1)}, bf16[8,128,128]{2,1,0:T(8,128)(2,1)}, u32[]{:S(2)}, u32[]{:S(2)}) collective-permute-start(bf16[8,128,128]{2,1,0:T(8,128)(2,1)} %get-tuple-element.88), channel_id=1, source_target_pairs={{0,16},{1,17},{2,18},{3,19},{4,20},{5,21},{6,22},{7,23},{8,24},{9,... | collective-permute-start | bytes 786440 | tf_op jit(solution)/shard_map/ppermute | solution.py:367
  116.0 23.9 %collective-permute-start.23 = (bf16[8,128,128]{2,1,0:T(8,128)(2,1)S(1)}, bf16[8,128,128]{2,1,0:T(8,128)(2,1)}, u32[]{:S(2)}, u32[]{:S(2)}) collective-permute-start(bf16[8,128,128]{2,1,0:T(8,128)(2,1)S(1)} %get-tuple-element.89), channel_id=1, source_target_pairs={{0,24},{1,25},{2,26},{3,27},{4,28},{5,29},{6,30},{7,31},{8,16},{9,... | collective-permute-start | bytes 786440 | tf_op jit(solution)/shard_map/ppermute | solution.py:367
  125.6 14.3 %copy-start.5 = (bf16[8,128,128]{2,1,0:T(8,128)(2,1)S(1)}, bf16[8,128,128]{2,1,0:T(8,128)(2,1)}, u32[]{:S(2)}) copy-start(bf16[8,128,128]{2,1,0:T(8,128)(2,1)} %copy-done.4) | copy-start | bytes 786436
  125.7 96.4 %all-to-all-start.2 = ((bf16[32,448,128]{2,1,0:T(8,128)(2,1)}), bf16[32,448,128]{2,1,0:T(8,128)(2,1)}, u32[]{:S(2)}, u32[]{:S(2)}) async-start(bf16[32,448,128]{2,1,0:T(8,128)(2,1)} %mix_main.1), calls=%async_computation.2 | async-start | bytes 7340032 | tf_op jit(solution)/shard_map/all_to_all | solution.py:568
  141.0 15.9 %collective-permute-start.24 = (bf16[4,2,128,128]{3,2,1,0:T(8,128)(2,1)S(1)}, bf16[4,2,128,128]{3,2,1,0:T(8,128)(2,1)S(1)}, u32[]{:S(2)}, u32[]{:S(2)}) collective-permute-start(bf16[4,2,128,128]{3,2,1,0:T(8,128)(2,1)S(1)} %get-tuple-element.91), channel_id=1, source_target_pairs={{0,2},{1,3},{2,0},{3,1},{4,6},{5,7},{6,4},{7,5},{8,10},{9,11},{10,... | collective-permute-start | bytes 786440 | tf_op jit(solution)/shard_map/ppermute | solution.py:367
  143.8 17.9 %collective-permute-start.25 = (bf16[4,2,128,128]{3,2,1,0:T(8,128)(2,1)S(1)}, bf16[4,2,128,128]{3,2,1,0:T(8,128)(2,1)S(1)}, u32[]{:S(2)}, u32[]{:S(2)}) collective-permute-start(bf16[4,2,128,128]{3,2,1,0:T(8,128)(2,1)S(1)} %get-tuple-element.92), channel_id=1, source_target_pairs={{0,4},{1,5},{2,6},{3,7},{4,0},{5,1},{6,2},{7,3},{8,12},{9,13},{10,... | collective-permute-start | bytes 786440 | tf_op jit(solution)/shard_map/ppermute | solution.py:367
  146.7 29.7 %collective-permute-start.26 = (bf16[4,2,128,128]{3,2,1,0:T(8,128)(2,1)S(1)}, bf16[4,2,128,128]{3,2,1,0:T(8,128)(2,1)S(1)}, u32[]{:S(2)}, u32[]{:S(2)}) collective-permute-start(bf16[4,2,128,128]{3,2,1,0:T(8,128)(2,1)S(1)} %get-tuple-element.93), channel_id=1, source_target_pairs={{0,6},{1,7},{2,4},{3,5},{4,2},{5,3},{6,0},{7,1},{8,14},{9,15},{10,... | collective-permute-start | bytes 786440 | tf_op jit(solution)/shard_map/ppermute | solution.py:367
  176.5 2.0 collective-permute-start.27

commit v19 on v18

--- a/solution.py
+++ b/solution.py
@@ -22,7 +22,7 @@
 SIDE = 2 * EDGE
 GROUPS = range(D // LANES)
 ROWS = SIDE * len(GROUPS)
-REST = EDGE + TILE
+REST = EDGE + 2 * TILE
 MAIN = ROWS - REST
 PLANES = 4
 PLANE = BLOCKS // PLANES

time: 227 us -> 234 us (1.031)
  local copies, waits for them, and re-layouts: 3.82 us -> 9.96 us
  starting transfers between devices: 49.3 us -> 52.6 us
  Pallas kernels: 43.9 us -> 40.8 us
    ppermute x24, waiting for transfers between devices: 65 us -> 73.5 us  [swap(): return lax.ppermute(value, AXES, pairs)]
    all_to_all x3, waiting for transfers between devices: 60.6 us -> 52.1 us  [exchange(): return lax.all_to_all(blocks, AXES, split_axis=0, concat_axis=0, tiled=True)]
    unnamed x20 -> x36, local copies, waits for them, and re-layouts: 3.82 us -> 9.96 us
    all_to_all x3, starting transfers between devices: 13.9 us -> 16.4 us  [exchange(): return lax.all_to_all(blocks, AXES, split_axis=0, concat_axis=0, tiled=True)]
  transfers between devices with their start and end apart: 31 -> 31, of which waited for: 16 -> 16; matrix products, arithmetic and copies ran while one was open for 1% -> 0% of each run, Pallas kernels for 16% -> 15%
where the time goes in v19:
time: 234 us
  waiting for transfers between devices  128 us (55%)
  starting transfers between devices  52.6 us (22%)
  Pallas kernels  40.8 us (17%)
  local copies, waits for them, and re-layouts  9.96 us (4%)
    ppermute x24, waiting for transfers between devices, swap(): return lax.ppermute(value, AXES, pairs)  73.5 us
    all_to_all x3, waiting for transfers between devices, exchange(): return lax.all_to_all(blocks, AXES, split_axis=0, concat_axis=0, tiled=True)  52.1 us
    ppermute x24, starting transfers between devices, swap(): return lax.ppermute(value, AXES, pairs)  32.6 us
    pallas_call x1, Pallas kernels, particle_scores(): pl.pallas_call(functools.partial(score_kernel, DATA / count), out_shape=(...  23.1 us
    all_to_all x3, starting transfers between devices, exchange(): return lax.all_to_all(blocks, AXES, split_axis=0, concat_axis=0, tiled=True)  16.4 us
    unnamed x36, local copies, waits for them, and re-layouts  9.96 us
  transfers between devices with their start and end apart: 31, of which 16 were waited for; matrix products, arithmetic and copies ran while one was open for 0% of the time, Pallas kernels for 15%

profile of v19, /device:TPU:0, one launch (start us, length us, event | category | flops | bytes accessed | tf_op | source)
XLA Modules:
  0.0 233.6 jit_solution(3348458279288918815)
XLA Ops:
  0.6 2.3 pack_side.1
  2.9 3.1 %collective-permute-start = (bf16[8,80,128]{2,1,0:T(8,128)(2,1)}, bf16[8,80,128]{2,1,0:T(8,128)(2,1)S(1)}, u32[]{:S(2)}, u32[]{:S(2)}) collective-permute-start(bf16[8,80,128]{2,1,0:T(8,128)(2,1)} %get-tuple-element.51), channel_id=1, source_target_pairs={{0,8},{1,9},{2,10},{3,11},{4,12},{5,13},{6,14},{7,15},{8,0},{9,1},... | collective-permute-start | bytes 491528 | tf_op jit(solution)/shard_map/ppermute | solution.py:367
  6.0 2.6 %collective-permute-start.1 = (bf16[8,80,128]{2,1,0:T(8,128)(2,1)}, bf16[8,80,128]{2,1,0:T(8,128)(2,1)S(1)}, u32[]{:S(2)}, u32[]{:S(2)}) collective-permute-start(bf16[8,80,128]{2,1,0:T(8,128)(2,1)} %get-tuple-element.52), channel_id=1, source_target_pairs={{0,16},{1,17},{2,18},{3,19},{4,20},{5,21},{6,22},{7,23},{8,24},{9,... | collective-permute-start | bytes 491528 | tf_op jit(solution)/shard_map/ppermute | solution.py:367
  8.6 2.6 %pack_main.1 = bf16[32,208,128]{2,1,0:T(8,128)(2,1)} custom-call(bf16[1,384,1536]{2,1,0:T(8,128)(2,1)} %first.3, bf16[1,1536,384]{2,1,0:T(8,128)(2,1)} %second.3), custom_call_target="tpu_custom_call" | custom-call | bytes 2359296 | tf_op jit(solution)/shard_map/pack_main/pallas_call | solution.py:492
  11.2 6.1 %all-to-all-start = ((bf16[32,208,128]{2,1,0:T(8,128)(2,1)}), bf16[32,208,128]{2,1,0:T(8,128)(2,1)S(1)}, u32[]{:S(2)}, u32[]{:S(2)}) async-start(bf16[32,208,128]{2,1,0:T(8,128)(2,1)} %pack_main.1), calls=%async_computation | async-start | bytes 3407872 | tf_op jit(solution)/shard_map/all_to_all | solution.py:568
  17.5 1.1 copy-done.16
  18.8 2.5 %collective-permute-done.1.refs_2_ = bf16[8,80,128]{2,1,0:T(8,128)(2,1)S(1)} collective-permute-done((bf16[8,80,128]{2,1,0:T(8,128)(2,1)}, bf16[8,80,128]{2,1,0:T(8,128)(2,1)S(1)}, u32[]{:S(2)}, u32[]{:S(2)}) %collective-permute-start.1) | collective-permute-done | bytes 163872 | tf_op jit(solution)/shard_map/ppermute | solution.py:367
  21.3 1.6 collective-permute-start.3
  22.9 1.5 collective-permute-start.4
  24.9 23.1 %score.1 = (bf16[32,208,128]{2,1,0:T(8,128)(2,1)}, bf16[8,80,128]{2,1,0:T(8,128)(2,1)S(1)}, bf16[8,80,128]{2,1,0:T(8,128)(2,1)}, bf16[8,80,128]{2,1,0:T(8,128)(2,1)}, bf16[8,80,128]{2,1,0:T(8,128)(2,1)}) custom-call(s32[8]{0:T(128)S(1)} %bitcast.6, s32[1]{0:T(128)} %bitcast.me, bf16[8,197,384]{2,1,0:T(8,128)(2,1)S(1)} %copy.10.image, ...), custom_call_target="tpu_custom_call" | custom-call | flops 9814671360 | bytes 7139328 | tf_op jit(solution)/shard_map/score/pallas_call | solution.py:134
  48.6 11.2 %all-to-all-done.main.params = bf16[32,208,128]{2,1,0:T(8,128)(2,1)S(1)} async-done(((bf16[32,208,128]{2,1,0:T(8,128)(2,1)}), bf16[32,208,128]{2,1,0:T(8,128)(2,1)S(1)}, u32[]{:S(2)}, u32[]{:S(2)}) %all-to-all-start) | async-done | bytes 1703968 | tf_op jit(solution)/shard_map/all_to_all | solution.py:568
  60.4 2.5 %collective-permute-start.15 = (bf16[8,80,128]{2,1,0:T(8,128)(2,1)}, bf16[8,80,128]{2,1,0:T(8,128)(2,1)}, u32[]{:S(2)}, u32[]{:S(2)}) collective-permute-start(bf16[8,80,128]{2,1,0:T(8,128)(2,1)} %get-tuple-element.72), channel_id=1, source_target_pairs={{0,16},{1,17},{2,18},{3,19},{4,20},{5,21},{6,22},{7,23},{8,24},{9,... | collective-permute-start | bytes 491528 | tf_op jit(solution)/shard_map/ppermute | solution.py:367
  62.9 1.4 collective-permute-start.16
  64.3 2.2 gram.1
  66.5 2.5 %collective-permute-start.9 = (f32[8,128]{1,0:T(8,128)S(1)}, f32[8,128]{1,0:T(8,128)S(1)}, u32[]{:S(2)}, u32[]{:S(2)}) collective-permute-start(f32[8,128]{1,0:T(8,128)S(1)} %gram.1), channel_id=1, source_target_pairs={{0,24},{1,25},{2,26},{3,27},{4,28},{5,29},{6,30},{7,31},{8,16},{9,... | collective-permute-start | bytes 12296 | tf_op jit(solution)/shard_map/ppermute | solution.py:367
  69.0 7.3 %collective-permute-done.9 = f32[8,128]{1,0:T(8,128)S(1)} collective-permute-done((f32[8,128]{1,0:T(8,128)S(1)}, f32[8,128]{1,0:T(8,128)S(1)}, u32[]{:S(2)}, u32[]{:S(2)}) %collective-permute-start.9) | collective-permute-done | bytes 4128 | tf_op jit(solution)/shard_map/ppermute | solution.py:367
  76.3 3.4 %collective-permute-start.7 = (f32[8,128]{1,0:T(8,128)S(1)}, f32[8,128]{1,0:T(8,128)S(1)}, u32[]{:S(2)}, u32[]{:S(2)}) collective-permute-start(f32[8,128]{1,0:T(8,128)S(1)} %gram.1), channel_id=1, source_target_pairs={{0,8},{1,9},{2,10},{3,11},{4,12},{5,13},{6,14},{7,15},{8,0},{9,1},... | collective-permute-start | bytes 12296 | tf_op jit(solution)/shard_map/ppermute | solution.py:367
  79.7 6.3 %all-to-all-start.1 = ((bf16[32,208,128]{2,1,0:T(8,128)(2,1)}), bf16[32,208,128]{2,1,0:T(8,128)(2,1)S(1)}, u32[]{:S(2)}, u32[]{:S(2)}) async-start(bf16[32,208,128]{2,1,0:T(8,128)(2,1)} %get-tuple-element.85), calls=%async_computation.1 | async-start | bytes 3407872 | tf_op jit(solution)/shard_map/all_to_all | solution.py:568
  86.9 1.1 plane.4
  88.1 1.7 collective-permute-start.17
  89.7 1.5 collective-permute-start.18
  91.6 11.1 %collective-permute-done.17.refs_1_ = bf16[4,2,80,128]{3,2,1,0:T(8,128)(2,1)S(1)} collective-permute-done((bf16[4,2,80,128]{3,2,1,0:T(8,128)(2,1)S(1)}, bf16[4,2,80,128]{3,2,1,0:T(8,128)(2,1)S(1)}, u32[]{:S(2)}, u32[]{:S(2)}) %collective-permute-start.17) | collective-permute-done | bytes 163872 | tf_op jit(solution)/shard_map/ppermute | solution.py:367
  102.7 3.2 %collective-permute-done.18.refs_2_ = bf16[4,2,80,128]{3,2,1,0:T(8,128)(2,1)S(1)} collective-permute-done((bf16[4,2,80,128]{3,2,1,0:T(8,128)(2,1)S(1)}, bf16[4,2,80,128]{3,2,1,0:T(8,128)(2,1)S(1)}, u32[]{:S(2)}, u32[]{:S(2)}) %collective-permute-start.18) | collective-permute-done | bytes 163872 | tf_op jit(solution)/shard_map/ppermute | solution.py:367
  105.9 6.5 %collective-permute-done.19.refs_3_ = bf16[4,2,80,128]{3,2,1,0:T(8,128)(2,1)S(1)} collective-permute-done((bf16[4,2,80,128]{3,2,1,0:T(8,128)(2,1)S(1)}, bf16[4,2,80,128]{3,2,1,0:T(8,128)(2,1)S(1)}, u32[]{:S(2)}, u32[]{:S(2)}) %collective-permute-start.19) | collective-permute-done | bytes 163872 | tf_op jit(solution)/shard_map/ppermute | solution.py:367
  113.0 1.8 collective-permute-start.11
  114.8 1.3 collective-permute-start.10
  116.1 1.1 collective-permute-done.12
  117.1 1.3 collective-permute-done.10
  119.7 2.2 mix_side.1
  124.4 1.8 collective-permute-start.22
  126.2 1.6 collective-permute-start.23
  127.8 1.1 copy-done.6
  128.9 1.0 copy-done.8
  129.9 3.2 %mix_main.1 = bf16[32,416,128]{2,1,0:T(8,128)(2,1)} custom-call(bf16[512,512]{1,0:T(8,128)(2,1)S(1)} %copy-done.8, bf16[32,208,128]{2,1,0:T(8,128)(2,1)S(1)} %all-to-all-done.1.scores, bf16[32,208,128]{2,1,0:T(8,128)(2,1)S(1)} %all-to-all-done.main.params, bf16[32,80,128]{2,1,0:T(8,128)(2,1)S(1)} %copy-done.6), custom_call_target="tpu_custom_call" | custom-call | flops 1744830464 | bytes 6815744 | tf_op jit(solution)/shard_map/mix_main/pallas_call | solution.py:313
  133.1 4.1 %all-to-all-start.2 = ((bf16[32,416,128]{2,1,0:T(8,128)(2,1)}), bf16[32,416,128]{2,1,0:T(8,128)(2,1)S(1)}, u32[]{:S(2)}, u32[]{:S(2)}) async-start(bf16[32,416,128]{2,1,0:T(8,128)(2,1)} %mix_main.1), calls=%async_computation.2 | async-start | bytes 6815744 | tf_op jit(solution)/shard_map/all_to_all | solution.py:568
  137.2 2.8 %collective-permute-done.21.refs_1_ = bf16[8,160,128]{2,1,0:T(8,128)(2,1)} collective-permute-done((bf16[8,160,128]{2,1,0:T(8,128)(2,1)}, bf16[8,160,128]{2,1,0:T(8,128)(2,1)}, u32[]{:S(2)}, u32[]{:S(2)}) %collective-permute-start.21) | collective-permute-done | bytes 327712 | tf_op jit(solution)/shard_map/ppermute | solution.py:367
  140.0 10.3 %collective-permute-done.22.refs_2_ = bf16[8,160,128]{2,1,0:T(8,128)(2,1)} collective-permute-done((bf16[8,160,128]{2,1,0:T(8,128)(2,1)}, bf16[8,160,128]{2,1,0:T(8,128)(2,1)}, u32[]{:S(2)}, u32[]{:S(2)}) %collective-permute-start.22) | collective-permute-done | bytes 327712 | tf_op jit(solution)/shard_map/ppermute | solution.py:367
  151.3 1.3 plane.5
  152.5 2.1 collective-permute-start.24
  154.6 2.1 collective-permute-start.25
  157.5 12.5 %collective-permute-done.24.refs_1_ = bf16[4,2,160,128]{3,2,1,0:T(8,128)(2,1)S(1)} collective-permute-done((bf16[4,2,160,128]{3,2,1,0:T(8,128)(2,1)S(1)}, bf16[4,2,160,128]{3,2,1,0:T(8,128)(2,1)S(1)}, u32[]{:S(2)}, u32[]{:S(2)}) %collective-permute-start.24) | collective-permute-done | bytes 327712 | tf_op jit(solution)/shard_map/ppermute | solution.py:367
  170.0 2.5 %collective-permute-done.25.refs_2_ = bf16[4,2,160,128]{3,2,1,0:T(8,128)(2,1)S(1)} collective-permute-done((bf16[4,2,160,128]{3,2,1,0:T(8,128)(2,1)S(1)}, bf16[4,2,160,128]{3,2,1,0:T(8,128)(2,1)S(1)}, u32[]{:S(2)}, u32[]{:S(2)}) %collective-permute-start.25) | collective-permute-done | bytes 327712 | tf_op jit(solution)/shard_map/ppermute | solution.py:367
  172.6 12.8 %collective-permute-done.26.refs_3_ = bf16[4,2,160,128]{3,2,1,0:T(8,128)(2,1)S(1)} collective-permute-done((bf16[4,2,160,128]{3,2,1,0:T(8,128)(2,1)S(1)}, bf16[4,2,160,128]{3,2,1,0:T(8,128)(2,1)S(1)}, u32[]{:S(2)}, u32[]{:S(2)}) %collective-permute-start.26) | collective-permute-done | bytes 327712 | tf_op jit(solution)/shard_map/ppermute | solution.py:367
  185.5 2.1 collective-permute-done.27.far
  187.7 1.1 copy-done
  188.8 40.9 %all-to-all-done.2.main = bf16[32,416,128]{2,1,0:T(8,128)(2,1)S(1)} async-done(((bf16[32,416,128]{2,1,0:T(8,128)(2,1)}), bf16[32,416,128]{2,1,0:T(8,128)(2,1)S(1)}, u32[]{:S(2)}, u32[]{:S(2)}) %all-to-all-start.2) | async-done | bytes 3407904 | tf_op jit(solution)/shard_map/all_to_all | solution.py:568
  229.6 1.3 copy-done.1
  230.9 2.5 %unpack.1 = (bf16[1,384,1536]{2,1,0:T(8,128)(2,1)}, bf16[1,1536,384]{2,1,0:T(8,128)(2,1)}, bf16[1,384,1536]{2,1,0:T(8,128)(2,1)}, bf16[1,1536,384]{2,1,0:T(8,128)(2,1)}) custom-call(bf16[32,416,128]{2,1,0:T(8,128)(2,1)S(1)} %all-to-all-done.2.main, bf16[32,160,128]{2,1,0:T(8,128)(2,1)S(1)} %copy-done.1), custom_call_target="tpu_custom_call" | custom-call | bytes 9437184 | tf_op jit(solution)/shard_map/unpack/pallas_call | solution.py:551
  (69 shorter events, 9.2 us)
Async XLA Ops:
  2.9 15.9 %collective-permute-start = (bf16[8,80,128]{2,1,0:T(8,128)(2,1)}, bf16[8,80,128]{2,1,0:T(8,128)(2,1)S(1)}, u32[]{:S(2)}, u32[]{:S(2)}) collective-permute-start(bf16[8,80,128]{2,1,0:T(8,128)(2,1)} %get-tuple-element.51), channel_id=1, source_target_pairs={{0,8},{1,9},{2,10},{3,11},{4,12},{5,13},{6,14},{7,15},{8,0},{9,1},... | collective-permute-start | bytes 491528 | tf_op jit(solution)/shard_map/ppermute | solution.py:367
  6.0 15.3 %collective-permute-start.1 = (bf16[8,80,128]{2,1,0:T(8,128)(2,1)}, bf16[8,80,128]{2,1,0:T(8,128)(2,1)S(1)}, u32[]{:S(2)}, u32[]{:S(2)}) collective-permute-start(bf16[8,80,128]{2,1,0:T(8,128)(2,1)} %get-tuple-element.52), channel_id=1, source_target_pairs={{0,16},{1,17},{2,18},{3,19},{4,20},{5,21},{6,22},{7,23},{8,24},{9,... | collective-permute-start | bytes 491528 | tf_op jit(solution)/shard_map/ppermute | solution.py:367
  8.6 12.7 %collective-permute-start.2 = (bf16[8,80,128]{2,1,0:T(8,128)(2,1)}, bf16[8,80,128]{2,1,0:T(8,128)(2,1)S(1)}, u32[]{:S(2)}, u32[]{:S(2)}) collective-permute-start(bf16[8,80,128]{2,1,0:T(8,128)(2,1)} %get-tuple-element.53), channel_id=1, source_target_pairs={{0,24},{1,25},{2,26},{3,27},{4,28},{5,29},{6,30},{7,31},{8,16},{9,... | collective-permute-start | bytes 491528 | tf_op jit(solution)/shard_map/ppermute | solution.py:367
  11.2 6.1 %copy-start.15 = (bf16[8,197,384]{2,0,1:T(8,128)(2,1)S(1)}, bf16[8,197,384]{2,0,1:T(8,128)(2,1)}, u32[]{:S(2)}) copy-start(bf16[8,197,384]{2,0,1:T(8,128)(2,1)} %param.8) | copy-start | bytes 3631108
  11.2 48.6 %all-to-all-start = ((bf16[32,208,128]{2,1,0:T(8,128)(2,1)}), bf16[32,208,128]{2,1,0:T(8,128)(2,1)S(1)}, u32[]{:S(2)}, u32[]{:S(2)}) async-start(bf16[32,208,128]{2,1,0:T(8,128)(2,1)} %pack_main.1), calls=%async_computation | async-start | bytes 3407872 | tf_op jit(solution)/shard_map/all_to_all | solution.py:568
  17.3 1.3 copy-start.16
  18.6 2.7 %copy-start.9 = (bf16[8,80,128]{2,1,0:T(8,128)(2,1)S(1)}, bf16[8,80,128]{2,1,0:T(8,128)(2,1)}, u32[]{:S(2)}) copy-start(bf16[8,80,128]{2,1,0:T(8,128)(2,1)} %get-tuple-element.50.refs_0_) | copy-start | bytes 491524
  21.3 3.6 %copy-start.2 = (bf16[1,384,1536]{2,1,0:T(8,128)(2,1)S(1)}, bf16[1,384,1536]{2,1,0:T(8,128)(2,1)}, u32[]{:S(2)}) copy-start(bf16[1,384,1536]{2,1,0:T(8,128)(2,1)} %first.3) | copy-start | bytes 3538948
  21.3 3.6 %copy-start.3 = (bf16[1,1536,384]{2,1,0:T(8,128)(2,1)S(1)}, bf16[1,1536,384]{2,1,0:T(8,128)(2,1)}, u32[]{:S(2)}) copy-start(bf16[1,1536,384]{2,1,0:T(8,128)(2,1)} %second.3) | copy-start | bytes 3538948
  21.3 3.6 %copy-start.10 = (s32[1,8]{1,0:T(1,128)S(1)}, s32[1,8]{1,0:T(1,128)}, u32[]{:S(2)}) copy-start(s32[1,8]{1,0:T(1,128)} %param.10) | copy-start | bytes 100
  21.3 26.6 %collective-permute-start.3 = (bf16[4,2,80,128]{3,2,1,0:T(8,128)(2,1)S(1)}, bf16[4,2,80,128]{3,2,1,0:T(8,128)(2,1)S(1)}, u32[]{:S(2)}, u32[]{:S(2)}) collective-permute-start(bf16[4,2,80,128]{3,2,1,0:T(8,128)(2,1)S(1)} %get-tuple-element.55), channel_id=1, source_target_pairs={{0,2},{1,3},{2,0},{3,1},{4,6},{5,7},{6,4},{7,5},{8,10},{9,11},{10,... | collective-permute-start | bytes 491528 | tf_op jit(solution)/shard_map/ppermute | solution.py:367
  22.9 25.1 %collective-permute-start.4 = (bf16[4,2,80,128]{3,2,1,0:T(8,128)(2,1)S(1)}, bf16[4,2,80,128]{3,2,1,0:T(8,128)(2,1)S(1)}, u32[]{:S(2)}, u32[]{:S(2)}) collective-permute-start(bf16[4,2,80,128]{3,2,1,0:T(8,128)(2,1)S(1)} %get-tuple-element.56), channel_id=1, source_target_pairs={{0,4},{1,5},{2,6},{3,7},{4,0},{5,1},{6,2},{7,3},{8,12},{9,13},{10,... | collective-permute-start | bytes 491528 | tf_op jit(solution)/shard_map/ppermute | solution.py:367
  24.4 23.6 %collective-permute-start.5 = (bf16[4,2,80,128]{3,2,1,0:T(8,128)(2,1)S(1)}, bf16[4,2,80,128]{3,2,1,0:T(8,128)(2,1)S(1)}, u32[]{:S(2)}, u32[]{:S(2)}) collective-permute-start(bf16[4,2,80,128]{3,2,1,0:T(8,128)(2,1)S(1)} %get-tuple-element.57), channel_id=1, source_target_pairs={{0,6},{1,7},{2,4},{3,5},{4,2},{5,3},{6,0},{7,1},{8,14},{9,15},{10,... | collective-permute-start | bytes 491528 | tf_op jit(solution)/shard_map/ppermute | solution.py:367
  48.0 0.7 copy-start.13
  48.6 15.6 %collective-permute-start.6 = (bf16[4,4,80,128]{3,2,1,0:T(8,128)(2,1)S(1)}, bf16[4,4,80,128]{3,2,1,0:T(8,128)(2,1)S(1)}, u32[]{:S(2)}, u32[]{:S(2)}) collective-permute-start(bf16[4,4,80,128]{3,2,1,0:T(8,128)(2,1)S(1)} %get-tuple-element.66), channel_id=1, source_target_pairs={{0,1},{1,0},{2,3},{3,2},{4,5},{5,4},{6,7},{7,6},{8,9},{9,8},{10,11... | collective-permute-start | bytes 983048 | tf_op jit(solution)/shard_map/ppermute | solution.py:367
  59.9 26.1 %collective-permute-start.14 = (bf16[8,80,128]{2,1,0:T(8,128)(2,1)}, bf16[8,80,128]{2,1,0:T(8,128)(2,1)}, u32[]{:S(2)}, u32[]{:S(2)}) collective-permute-start(bf16[8,80,128]{2,1,0:T(8,128)(2,1)} %get-tuple-element.71), channel_id=1, source_target_pairs={{0,8},{1,9},{2,10},{3,11},{4,12},{5,13},{6,14},{7,15},{8,0},{9,1},... | collective-permute-start | bytes 491528 | tf_op jit(solution)/shard_map/ppermute | solution.py:367
  60.4 25.6 %collective-permute-start.15 = (bf16[8,80,128]{2,1,0:T(8,128)(2,1)}, bf16[8,80,128]{2,1,0:T(8,128)(2,1)}, u32[]{:S(2)}, u32[]{:S(2)}) collective-permute-start(bf16[8,80,128]{2,1,0:T(8,128)(2,1)} %get-tuple-element.72), channel_id=1, source_target_pairs={{0,16},{1,17},{2,18},{3,19},{4,20},{5,21},{6,22},{7,23},{8,24},{9,... | collective-permute-start | bytes 491528 | tf_op jit(solution)/shard_map/ppermute | solution.py:367
  62.9 23.1 %collective-permute-start.16 = (bf16[8,80,128]{2,1,0:T(8,128)(2,1)}, bf16[8,80,128]{2,1,0:T(8,128)(2,1)}, u32[]{:S(2)}, u32[]{:S(2)}) collective-permute-start(bf16[8,80,128]{2,1,0:T(8,128)(2,1)} %get-tuple-element.73), channel_id=1, source_target_pairs={{0,24},{1,25},{2,26},{3,27},{4,28},{5,29},{6,30},{7,31},{8,16},{9,... | collective-permute-start | bytes 491528 | tf_op jit(solution)/shard_map/ppermute | solution.py:367
  64.3 2.2 copy-start.4
  66.5 9.8 %collective-permute-start.9 = (f32[8,128]{1,0:T(8,128)S(1)}, f32[8,128]{1,0:T(8,128)S(1)}, u32[]{:S(2)}, u32[]{:S(2)}) collective-permute-start(f32[8,128]{1,0:T(8,128)S(1)} %gram.1), channel_id=1, source_target_pairs={{0,24},{1,25},{2,26},{3,27},{4,28},{5,29},{6,30},{7,31},{8,16},{9,... | collective-permute-start | bytes 12296 | tf_op jit(solution)/shard_map/ppermute | solution.py:367
  69.0 17.0 %collective-permute-start.8 = (f32[8,128]{1,0:T(8,128)S(1)}, f32[8,128]{1,0:T(8,128)S(1)}, u32[]{:S(2)}, u32[]{:S(2)}) collective-permute-start(f32[8,128]{1,0:T(8,128)S(1)} %gram.1), channel_id=1, source_target_pairs={{0,16},{1,17},{2,18},{3,19},{4,20},{5,21},{6,22},{7,23},{8,24},{9,... | collective-permute-start | bytes 12296 | tf_op jit(solution)/shard_map/ppermute | solution.py:367
  76.3 9.7 %collective-permute-start.7 = (f32[8,128]{1,0:T(8,128)S(1)}, f32[8,128]{1,0:T(8,128)S(1)}, u32[]{:S(2)}, u32[]{:S(2)}) collective-permute-start(f32[8,128]{1,0:T(8,128)S(1)} %gram.1), channel_id=1, source_target_pairs={{0,8},{1,9},{2,10},{3,11},{4,12},{5,13},{6,14},{7,15},{8,0},{9,1},... | collective-permute-start | bytes 12296 | tf_op jit(solution)/shard_map/ppermute | solution.py:367
  79.7 48.1 %all-to-all-start.1 = ((bf16[32,208,128]{2,1,0:T(8,128)(2,1)}), bf16[32,208,128]{2,1,0:T(8,128)(2,1)S(1)}, u32[]{:S(2)}, u32[]{:S(2)}) async-start(bf16[32,208,128]{2,1,0:T(8,128)(2,1)} %get-tuple-element.85), calls=%async_computation.1 | async-start | bytes 3407872 | tf_op jit(solution)/shard_map/all_to_all | solution.py:568
  86.0 0.9 copy-start.14
  88.1 31.6 %copy-start.5 = (bf16[32,80,128]{2,1,0:T(8,128)(2,1)S(1)}, bf16[32,80,128]{2,1,0:T(8,128)(2,1)}, u32[]{:S(2)}) copy-start(bf16[32,80,128]{2,1,0:T(8,128)(2,1)} %copy-done.4) | copy-start | bytes 1966084
  88.1 14.7 %collective-permute-start.17 = (bf16[4,2,80,128]{3,2,1,0:T(8,128)(2,1)S(1)}, bf16[4,2,80,128]{3,2,1,0:T(8,128)(2,1)S(1)}, u32[]{:S(2)}, u32[]{:S(2)}) collective-permute-start(bf16[4,2,80,128]{3,2,1,0:T(8,128)(2,1)S(1)} %get-tuple-element.79), channel_id=1, source_target_pairs={{0,2},{1,3},{2,0},{3,1},{4,6},{5,7},{6,4},{7,5},{8,10},{9,11},{10,... | collective-permute-start | bytes 491528 | tf_op jit(solution)/shard_map/ppermute | solution.py:367
  89.7 16.2 %collective-permute-start.18 = (bf16[4,2,80,128]{3,2,1,0:T(8,128)(2,1)S(1)}, bf16[4,2,80,128]{3,2,1,0:T(8,128)(2,1)S(1)}, u32[]{:S(2)}, u32[]{:S(2)}) collective-permute-start(bf16[4,2,80,128]{3,2,1,0:T(8,128)(2,1)S(1)} %get-tuple-element.80), channel_id=1, source_target_pairs={{0,4},{1,5},{2,6},{3,7},{4,0},{5,1},{6,2},{7,3},{8,12},{9,13},{10,... | collective-permute-start | bytes 491528 | tf_op jit(solution)/shard_map/ppermute | solution.py:367
  91.2 21.2 %collective-permute-start.19 = (bf16[4,2,80,128]{3,2,1,0:T(8,128)(2,1)S(1)}, bf16[4,2,80,128]{3,2,1,0:T(8,128)(2,1)S(1)}, u32[]{:S(2)}, u32[]{:S(2)}) collective-permute-start(bf16[4,2,80,128]{3,2,1,0:T(8,128)(2,1)S(1)} %get-tuple-element.81), channel_id=1, source_target_pairs={{0,6},{1,7},{2,4},{3,5},{4,2},{5,3},{6,0},{7,1},{8,14},{9,15},{10,... | collective-permute-start | bytes 491528 | tf_op jit(solution)/shard_map/ppermute | solution.py:367
  112.4 7.2 %collective-permute-start.20 = (bf16[4,4,80,128]{3,2,1,0:T(8,128)(2,1)S(1)}, bf16[4,4,80,128]{3,2,1,0:T(8,128)(2,1)S(1)}, u32[]{:S(2)}, u32[]{:S(2)}) collective-permute-start(bf16[4,4,80,128]{3,2,1,0:T(8,128)(2,1)S(1)} %get-tuple-element.83), channel_id=1, source_target_pairs={{0,1},{1,0},{2,3},{3,2},{4,5},{5,4},{6,7},{7,6},{8,9},{9,8},{10,11... | collective-permute-start | bytes 983048 | tf_op jit(solution)/shard_map/ppermute | solution.py:367
  112.5 4.6 %collective-permute-start.12 = (f32[8,128]{1,0:T(8,128)S(1)}, f32[8,128]{1,0:T(8,128)S(1)}, u32[]{:S(2)}, u32[]{:S(2)}) collective-permute-start(f32[8,128]{1,0:T(8,128)S(1)} %add_add_fusion.1), channel_id=1, source_target_pairs={{0,6},{1,7},{2,4},{3,5},{4,2},{5,3},{6,0},{7,1},{8,14},{9,15},{10,... | collective-permute-start | bytes 12296 | tf_op jit(solution)/shard_map/ppermute | solution.py:210
  113.0 4.1 %collective-permute-start.11 = (f32[8,128]{1,0:T(8,128)S(1)}, f32[8,128]{1,0:T(8,128)S(1)}, u32[]{:S(2)}, u32[]{:S(2)}) collective-permute-start(f32[8,128]{1,0:T(8,128)S(1)} %add_add_fusion.1), channel_id=1, source_target_pairs={{0,4},{1,5},{2,6},{3,7},{4,0},{5,1},{6,2},{7,3},{8,12},{9,13},{10,... | collective-permute-start | bytes 12296 | tf_op jit(solution)/shard_map/ppermute | solution.py:210
  114.8 3.6 %collective-permute-start.10 = (f32[8,128]{1,0:T(8,128)S(1)}, f32[8,128]{1,0:T(8,128)S(1)}, u32[]{:S(2)}, u32[]{:S(2)}) collective-permute-start(f32[8,128]{1,0:T(8,128)S(1)} %add_add_fusion.1), channel_id=1, source_target_pairs={{0,2},{1,3},{2,0},{3,1},{4,6},{5,7},{6,4},{7,5},{8,10},{9,11},{10,... | collective-permute-start | bytes 12296 | tf_op jit(solution)/shard_map/ppermute | solution.py:210
  118.4 1.2 collective-permute-start.13
  121.8 0.8 copy-start.7
  122.6 0.7 copy-start.11
  123.4 16.6 %collective-permute-start.21 = (bf16[8,160,128]{2,1,0:T(8,128)(2,1)}, bf16[8,160,128]{2,1,0:T(8,128)(2,1)}, u32[]{:S(2)}, u32[]{:S(2)}) collective-permute-start(bf16[8,160,128]{2,1,0:T(8,128)(2,1)} %get-tuple-element.87), channel_id=1, source_target_pairs={{0,8},{1,9},{2,10},{3,11},{4,12},{5,13},{6,14},{7,15},{8,0},{9,1},... | collective-permute-start | bytes 983048 | tf_op jit(solution)/shard_map/ppermute | solution.py:367
  124.4 25.9 %collective-permute-start.22 = (bf16[8,160,128]{2,1,0:T(8,128)(2,1)}, bf16[8,160,128]{2,1,0:T(8,128)(2,1)}, u32[]{:S(2)}, u32[]{:S(2)}) collective-permute-start(bf16[8,160,128]{2,1,0:T(8,128)(2,1)} %get-tuple-element.88), channel_id=1, source_target_pairs={{0,16},{1,17},{2,18},{3,19},{4,20},{5,21},{6,22},{7,23},{8,24},{9,... | collective-permute-start | bytes 983048 | tf_op jit(solution)/shard_map/ppermute | solution.py:367
  126.2 24.1 %collective-permute-start.23 = (bf16[8,160,128]{2,1,0:T(8,128)(2,1)}, bf16[8,160,128]{2,1,0:T(8,128)(2,1)}, u32[]{:S(2)}, u32[]{:S(2)}) collective-permute-start(bf16[8,160,128]{2,1,0:T(8,128)(2,1)} %get-tuple-element.89), channel_id=1, source_target_pairs={{0,24},{1,25},{2,26},{3,27},{4,28},{5,29},{6,30},{7,31},{8,16},{9,... | collective-permute-start | bytes 983048 | tf_op jit(solution)/shard_map/ppermute | solution.py:367
  127.8 1.1 copy-start.6
  128.8 1.0 copy-start.8
  133.1 96.5 %all-to-all-start.2 = ((bf16[32,416,128]{2,1,0:T(8,128)(2,1)}), bf16[32,416,128]{2,1,0:T(8,128)(2,1)S(1)}, u32[]{:S(2)}, u32[]{:S(2)}) async-start(bf16[32,416,128]{2,1,0:T(8,128)(2,1)} %mix_main.1), calls=%async_computation.2 | async-start | bytes 6815744 | tf_op jit(solution)/shard_map/all_to_all | solution.py:568
  150.3 1.0 copy-start.12
  152.5 17.5 %collective-permute-start.24 = (bf16[4,2,160,128]{3,2,1,0:T(8,128)(2,1)S(1)}, bf16[4,2,160,128]{3,2,1,0:T(8,128)(2,1)S(1)}, u32[]{:S(2)}, u32[]{:S(2)}) collective-permute-start(bf16[4,2,160,128]{3,2,1,0:T(8,128)(2,1)S(1)} %get-tuple-element.91), channel_id=1, source_target_pairs={{0,2},{1,3},{2,0},{3,1},{4,6},{5,7},{6,4},{7,5},{8,10},{9,11},{10,... | collective-permute-start | bytes 983048 | tf_op jit(solution)/shard_map/ppermute | solution.py:367
  154.6 17.9 %collective-permute-start.25 = (bf16[4,2,160,128]{3,2,1,0:T(8,128)(2,1)S(1)}, bf16[4,2,160,128]{3,2,1,0:T(8,128)(2,1)S(1)}, u32[]{:S(2)}, u32[]{:S(2)}) collective-permute-start(bf16[4,2,160,128]{3,2,1,0:T(8,128)(2,1)S(1)} %get-tuple-element.92), channel_id=1, source_target_pairs={{0,4},{1,5},{2,6},{3,7},{4,0},{5,1},{6,2},{7,3},{8,12},{9,13},{10,... | collective-permute-start | bytes 983048 | tf_op jit(solution)/shard_map/ppermute | solution.py:367
  156.8 28.6 %collective-permute-start.26 = (bf16[4,2,160,128]{3,2,1,0:T(8,128)(2,1)S(1)}, bf16[4,2,160,128]{3,2,1,0:T(8,128)(2,1)S(1)}, u32[]{:S(2)}, u32[]{:S(2)}) collective-permute-start(bf16[4,2,160,128]{3,2,1,0:T(8,128)(2,1)S(1)} %get-tuple-element.93), channel_id=1, source_target_pairs={{0,6},{1,7},{2,4},{3,5},{4,2},{5,3},{6,0},{7,1},{8,14},{9,15},{10,... | collective-permute-start | bytes 983048 | tf_op jit(solution)/shard_map/ppermute | solution.py:367
  185.4 2.2 collective-permute-start.27
  187.7 1.1 copy-start
  229.6 1.3 copy-start.1
